TPU v7x, 32 devices: a whole 2x2x4 slice. The times are simulated.
32 devices in a mesh: section: 2 (over core), dp: 4 (over z), ctx: 4 (over y, x).
Axes of the slice: x: 2, y: 2, z: 4, core: 2. Of those that a mesh axis runs over, the one named last changes fastest.
Arguments:
- inputs: bfloat16 [2, 4, 1024, 768], P(None, 'dp', 'ctx'), may hold values from -6 to 6
- lengths: int32 [2, 4], P(None, 'dp'), may hold values from 1 to 1024, as said below
- cotangent: bfloat16 [2, 4, 1024, 768], P(None, 'dp', 'ctx'), may hold values from -6 to 6
- first_gain: bfloat16 [2, 768], P('section'), may hold values from 0.5 to 1.5
- joint_weight: bfloat16 [2, 768, 2304], P('section'), may hold values from -0.21875 to 0.21875
- pre_mix: float32 [2, 12, 12], P('section'), may hold values from -1.75 to 1.75
- post_mix: float32 [2, 12, 12], P('section'), may hold values from -1.75 to 1.75
- mixer_weight: bfloat16 [2, 768, 768], P('section'), may hold values from -0.875 to 0.875
- second_gain: bfloat16 [2, 768], P('section'), may hold values from 0.5 to 1.5
- up_weight: bfloat16 [2, 768, 3072], P('section'), may hold values from -0.21875 to 0.21875
- down_weight: bfloat16 [2, 3072, 768], P('section'), may hold values from -0.109375 to 0.109375
Outputs:
- section_ends: bfloat16 [2, 2, 4, 1024, 768], P('section', None, 'dp', 'ctx')
- first_grad: float32 [2, 768], P('section', ('dp', 'ctx'))
- joint_grad: float32 [2, 768, 2304], P('section', ('dp', 'ctx'))
- premix_grad: float32 [2, 12, 12], P('section')
- postmix_grad: float32 [2, 12, 12], P('section')
- mixer_grad: float32 [2, 768, 768], P('section', ('dp', 'ctx'))
- second_grad: float32 [2, 768], P('section', ('dp', 'ctx'))
- up_grad: float32 [2, 768, 3072], P('section', ('dp', 'ctx'))
- down_grad: float32 [2, 3072, 768], P('section', ('dp', 'ctx'))
Inputs may be any that keep to these rules, and one draw needn't show every extreme that they name: For each index of dp, of the rows it holds (one per micro-batch, 2 in all) one has length 1024; the others lean towards short lengths.
All inputs are finite; a program needn't handle non-finite values.
Results may differ from a plain program's by a relative error of at most 0.024.
Values may be sent and summed in bfloat16 or wider, within the bound.
No kernel may reach another device: no remote copies, remote signals or barrier semaphores. Data moves between devices by JAX's collectives and lax.ppermute only.
A program may use at most 320 MiB of HBM per device.

v0:
```python
import jax
import jax.numpy as jnp
from jax import lax
from jax.sharding import PartitionSpec as P

HEADS = 12
HEAD = 64


HIGHEST = lax.Precision.HIGHEST
eps = 1e-06


def shifted(x, axis, by):
    count = lax.axis_size(axis)
    pairs = [(i, i + by) for i in range(count) if 0 <= i + by < count]
    return lax.ppermute(x, axis, pairs)


def dense(left_side, right_side):
    return jnp.dot(left_side, right_side, preferred_element_type=jnp.float32)


def dense_tn(left_side, right_side):
    return lax.dot_general(
        left_side, right_side, (((0,), (0,)), ((), ())), preferred_element_type=jnp.float32
    )


def dense_nt(left_side, right_side):
    return lax.dot_general(
        left_side, right_side, (((1,), (1,)), ((), ())), preferred_element_type=jnp.float32
    )


def rms_parts(values, gain):
    inverse = lax.rsqrt(jnp.mean(values * values, axis=-1, keepdims=True) + eps)
    return (inverse, values * inverse * gain)


def rms_back(grad_normed, values, inverse, gain):
    unit = values * inverse
    gain_grad = jnp.sum(grad_normed * unit, axis=0)
    scaled = grad_normed * gain
    return (inverse * (scaled - unit * jnp.mean(scaled * unit, axis=-1, keepdims=True)), gain_grad)


def attend(query, kv_all, premix, postmix, allowed):
    row_count, seq_total, double_width = kv_all.shape
    model_width = double_width // 2
    key_heads = kv_all[:, :, :model_width].reshape(row_count, seq_total, HEADS, HEAD)
    value_heads = kv_all[:, :, model_width:].reshape(row_count, seq_total, HEADS, HEAD)
    query_heads = query.reshape(row_count, -1, HEADS, HEAD)
    scores = (
        jnp.einsum("rche,rshe->rhcs", query_heads, key_heads, preferred_element_type=jnp.float32)
        * 0.125
    )
    logits = jnp.einsum("gh,rgcs->rhcs", premix, scores, precision=HIGHEST)
    logits = jnp.where(allowed, logits, -1e30)
    highest = jnp.max(logits, axis=-1, keepdims=True)
    exponent = jnp.exp(logits - highest)
    total = jnp.sum(exponent, axis=-1, keepdims=True)
    attention = exponent / total
    mixed_low = jnp.einsum("gh,rgcs->rhcs", postmix, attention, precision=HIGHEST).astype(
        jnp.bfloat16
    )
    attended = jnp.einsum(
        "rhcs,rshe->rche", mixed_low, value_heads, preferred_element_type=jnp.float32
    )
    return (
        key_heads,
        value_heads,
        query_heads,
        scores,
        attention,
        mixed_low,
        highest[..., 0],
        total[..., 0],
        attended.reshape(-1, model_width),
    )


def local(
    inputs,
    lengths,
    cotangent,
    first_gain,
    joint_weight,
    pre_mix,
    post_mix,
    mixer_weight,
    second_gain,
    up_weight,
    down_weight,
):
    section_id = lax.axis_index("section")
    micro_count, row_count, local_len, model_width = inputs.shape
    seq_total = local_len * lax.axis_size("ctx")
    gain_a = first_gain[0].astype(jnp.float32)
    joint_w = joint_weight[0]
    premix = pre_mix[0]
    postmix = post_mix[0]
    mixer_w = mixer_weight[0]
    gain_b = second_gain[0].astype(jnp.float32)
    upward_w = up_weight[0]
    downward_w = down_weight[0]
    query_place = lax.axis_index("ctx") * local_len + jnp.arange(local_len)
    key_place = jnp.arange(seq_total)

    def allowed_for(row_lengths):
        return (key_place[None, None, None, :] <= query_place[None, None, :, None]) & (
            key_place[None, None, None, :] < row_lengths[:, None, None, None]
        )

    def front_half(block_in):
        values = block_in.reshape(-1, model_width).astype(jnp.float32)
        inverse, normed = rms_parts(values, gain_a)
        normed_low = normed.astype(jnp.bfloat16)
        joint_out = dense(normed_low, joint_w).astype(jnp.bfloat16)
        kv_local = joint_out[:, model_width:].reshape(row_count, local_len, 2 * model_width)
        return (values, inverse, normed_low, joint_out[:, :model_width], kv_local)

    def rest_half(values, attended):
        attended_low = attended.astype(jnp.bfloat16)
        hidden = values + dense(attended_low, mixer_w)
        inverse_two, normed_two = rms_parts(hidden, gain_b)
        normed_two_low = normed_two.astype(jnp.bfloat16)
        upward = dense(normed_two_low, upward_w)
        active_low = jax.nn.gelu(upward, approximate=True).astype(jnp.bfloat16)
        output = hidden + dense(active_low, downward_w)
        return (attended_low, hidden, inverse_two, normed_two_low, upward, active_low, output)

    kept_count = 1
    kept_init = jnp.zeros((kept_count, row_count, seq_total, 2 * model_width), jnp.bfloat16)
    stash_init = jnp.zeros_like(inputs)
    ends_init = jnp.zeros_like(inputs)
    recv_init = jnp.zeros((row_count, local_len, model_width), jnp.bfloat16)

    def forward_tick(moment, carry):
        received, stash, kept, ends_local = carry
        micro_index = jnp.clip(moment - section_id, 0, micro_count - 1)
        is_live = (moment - section_id >= 0) & (moment - section_id < micro_count)
        fresh = lax.dynamic_index_in_dim(inputs, micro_index, 0, keepdims=False)
        block_in = jnp.where(section_id == 0, fresh, received)
        values, inverse, normed_low, query, kv_local = front_half(block_in)
        kv_all = lax.all_gather(kv_local, "ctx", axis=1, tiled=True)
        row_lengths = lax.dynamic_index_in_dim(lengths, micro_index, 0, keepdims=False)
        attended = attend(query, kv_all, premix, postmix, allowed_for(row_lengths))[-1]
        output = rest_half(values, attended)[-1]
        result = output.astype(jnp.bfloat16).reshape(row_count, local_len, model_width)
        received = shifted(result, "section", 1)
        old_stash = lax.dynamic_index_in_dim(stash, micro_index, 0, keepdims=False)
        stash = lax.dynamic_update_index_in_dim(
            stash, jnp.where(is_live, block_in, old_stash), micro_index, 0
        )
        old_end = lax.dynamic_index_in_dim(ends_local, micro_index, 0, keepdims=False)
        new_end = jnp.where(is_live & (section_id == 1), result, old_end)
        ends_local = lax.dynamic_update_index_in_dim(ends_local, new_end, micro_index, 0)
        return (received, stash, kept, ends_local)

    received, stash, kept, ends_local = lax.fori_loop(
        0, micro_count + 1, forward_tick, (recv_init, stash_init, kept_init, ends_init)
    )
    big_shapes = (
        gain_a.shape,
        joint_w.shape,
        mixer_w.shape,
        gain_b.shape,
        upward_w.shape,
        downward_w.shape,
    )
    grad_init = tuple((jnp.zeros(shape_w, jnp.float32) for shape_w in big_shapes))
    mix_init = (jnp.zeros(premix.shape, jnp.float32), jnp.zeros(postmix.shape, jnp.float32))

    def backward_tick(moment, carry):
        received, grad_sums, mix_sums, ends_local = carry
        micro_index = jnp.clip(moment - 1 + section_id, 0, micro_count - 1)
        is_live = (moment - 1 + section_id >= 0) & (moment - 1 + section_id < micro_count)
        cot_block = lax.dynamic_index_in_dim(cotangent, micro_index, 0, keepdims=False)
        grad_out = (
            jnp.where(section_id == 1, cot_block, received)
            .astype(jnp.float32)
            .reshape(-1, model_width)
        )
        block_in = lax.dynamic_index_in_dim(stash, micro_index, 0, keepdims=False)
        values, inverse, normed_low, query, kv_local = front_half(block_in)
        kv_all = lax.all_gather(kv_local, "ctx", axis=1, tiled=True)
        row_lengths = lax.dynamic_index_in_dim(lengths, micro_index, 0, keepdims=False)
        (
            key_heads,
            value_heads,
            query_heads,
            scores,
            attention,
            mixed_low,
            highest,
            total,
            attended,
        ) = attend(query, kv_all, premix, postmix, allowed_for(row_lengths))
        attended_low, hidden, inverse_two, normed_two_low, upward, active_low, output = rest_half(
            values, attended
        )
        grad_low = grad_out.astype(jnp.bfloat16)
        down_term = dense_tn(active_low, grad_low)
        grad_active = dense_nt(grad_low, downward_w)
        gelu_out, gelu_pull = jax.vjp(
            lambda upward_in: jax.nn.gelu(upward_in, approximate=True), upward
        )
        grad_up = gelu_pull(grad_active)[0].astype(jnp.bfloat16)
        up_term = dense_tn(normed_two_low, grad_up)
        grad_norm_two, gain_b_term = rms_back(
            dense_nt(grad_up, upward_w), hidden, inverse_two, gain_b
        )
        grad_hidden = grad_out + grad_norm_two
        grad_hidden_low = grad_hidden.astype(jnp.bfloat16)
        mixer_term = dense_tn(attended_low, grad_hidden_low)
        grad_att = (
            dense_nt(grad_hidden_low, mixer_w)
            .astype(jnp.bfloat16)
            .reshape(row_count, local_len, HEADS, HEAD)
        )
        grad_mixed = jnp.einsum(
            "rche,rshe->rhcs", grad_att, value_heads, preferred_element_type=jnp.float32
        )
        postmix_term = jnp.einsum("rgcs,rhcs->gh", attention, grad_mixed, precision=HIGHEST)
        grad_attention = jnp.einsum("gh,rhcs->rgcs", postmix, grad_mixed, precision=HIGHEST)
        spread = jnp.sum(grad_attention * attention, axis=-1)
        grad_logits = attention * (grad_attention - spread[..., None])
        premix_term = jnp.einsum("rgcs,rhcs->gh", scores, grad_logits, precision=HIGHEST)
        grad_scores = jnp.einsum("gh,rhcs->rgcs", premix, grad_logits, precision=HIGHEST).astype(
            jnp.bfloat16
        )
        grad_query = (
            jnp.einsum(
                "rhcs,rshe->rche", grad_scores, key_heads, preferred_element_type=jnp.float32
            )
            * 0.125
        )
        grad_keys = (
            jnp.einsum(
                "rhcs,rche->rshe", grad_scores, query_heads, preferred_element_type=jnp.float32
            )
            * 0.125
        )
        grad_values = jnp.einsum(
            "rhcs,rche->rshe", mixed_low, grad_att, preferred_element_type=jnp.float32
        )
        grad_kv = jnp.concatenate(
            [
                grad_keys.reshape(row_count, seq_total, model_width),
                grad_values.reshape(row_count, seq_total, model_width),
            ],
            axis=-1,
        )
        grad_kv_local = lax.psum_scatter(
            grad_kv.astype(jnp.bfloat16), "ctx", scatter_dimension=1, tiled=True
        ).astype(jnp.float32)
        grad_joint = jnp.concatenate(
            [grad_query.reshape(-1, model_width), grad_kv_local.reshape(-1, 2 * model_width)],
            axis=-1,
        ).astype(jnp.bfloat16)
        joint_term = dense_tn(normed_low, grad_joint)
        grad_front, gain_a_term = rms_back(dense_nt(grad_joint, joint_w), values, inverse, gain_a)
        grad_in = grad_hidden + grad_front
        sent = grad_in.astype(jnp.bfloat16).reshape(row_count, local_len, model_width)
        received = shifted(sent, "section", -1)
        old_end = lax.dynamic_index_in_dim(ends_local, micro_index, 0, keepdims=False)
        new_end = jnp.where(is_live & (section_id == 0), sent, old_end)
        ends_local = lax.dynamic_update_index_in_dim(ends_local, new_end, micro_index, 0)
        live_scale = is_live.astype(jnp.float32)
        grad_terms = tuple(
            (
                term_w * live_scale
                for term_w in (gain_a_term, joint_term, mixer_term, gain_b_term, up_term, down_term)
            )
        )
        grad_sums = tuple((sum_w + term_w for sum_w, term_w in zip(grad_sums, grad_terms)))
        mix_sums = (mix_sums[0] + premix_term * live_scale, mix_sums[1] + postmix_term * live_scale)
        return (received, grad_sums, mix_sums, ends_local)

    received, grad_sums, mix_sums, ends_local = lax.fori_loop(
        0, micro_count + 1, backward_tick, (recv_init, grad_init, mix_init, ends_local)
    )
    shards = lax.psum_scatter(grad_sums, ("dp", "ctx"), scatter_dimension=0, tiled=True)
    mix_total = lax.psum((mix_sums[0], mix_sums[1]), ("dp", "ctx"))
    return (
        ends_local[None],
        shards[0][None],
        shards[1][None],
        mix_total[0][None],
        mix_total[1][None],
        shards[2][None],
        shards[3][None],
        shards[4][None],
        shards[5][None],
    )


def solution(mesh):
    in_specs = (
        P(None, "dp", "ctx", None),
        P(None, "dp"),
        P(None, "dp", "ctx", None),
        P("section", None),
        P("section", None, None),
        P("section", None, None),
        P("section", None, None),
        P("section", None, None),
        P("section", None),
        P("section", None, None),
        P("section", None, None),
    )
    out_specs = (
        P("section", None, "dp", "ctx", None),
        P("section", ("dp", "ctx")),
        P("section", ("dp", "ctx"), None),
        P("section", None, None),
        P("section", None, None),
        P("section", ("dp", "ctx"), None),
        P("section", ("dp", "ctx")),
        P("section", ("dp", "ctx"), None),
        P("section", ("dp", "ctx"), None),
    )
    return jax.shard_map(local, mesh=mesh, in_specs=in_specs, out_specs=out_specs, check_vma=False)
```

profile of v0, /device:TPU:0, one launch (start us, length us, event | category | flops | bytes accessed | tf_op | source)
XLA Modules:
  0.0 2360.2 jit_solution(9514920607811641386)
XLA Ops:
  13.9 496.4 %while.55 = (s32[]{:T(128)}, bf16[1,256,768]{2,1,0:T(8,128)(2,1)S(1)}, bf16[2,1,256,768]{3,2,1,0:T(8,128)(2,1)S(1)}, bf16[2,1,256,768]{3,2,1,0:T(8,128)(2,1)}, p...) while((s32[]{:T(128)}, ...), condition=%wide.region_5.6_spmd.clone.clone, body=%wide.region_0.5_spmd.clone.clone.sunk | while | flops 5378732032 | bytes 152048912 | solution.py:161
  24.8 41.9 %all-gather.11.cloned.1.call-done = bf16[1024,1536]{1,0:T(8,128)(2,1)} async-done(((bf16[256,1536]{1,0:T(8,128)(2,1)}), bf16[1024,1536]{1,0:T(8,128)(2,1)}) %all-gather.11.cloned.1.call-update) | async-done | bytes 3145744 | tf_op jit(solution)/shard_map/while/body/eval_jaxpr/all_gather | solution.py:146
  75.5 46.5 %bitcast_reduce_fusion.4 = (f32[12,256]{0,1:T(8,128)}, f32[256,1024,12]{1,2,0:T(8,128)}) fusion(pred[256,1024]{1,0:T(8,128)(4,1)} %fusion.320, f32[12,12]{0,1:T(8,128)S(1)} %copy-done.49, f32[12,256,1024]{2,1,0:T(8,128)S(1)} %broadcast_multiply_fusion.8), kind=kOutput, calls=%fused_computation.7.clone.1 | convolution fusion | flops 459273216 | bytes 25440832 | tf_op jit(solution)/shard_map/while/body/eval_jaxpr/gh,rgcs->rhcs/dot_general | solution.py:58
  189.2 39.2 %all-gather.11.cloned.1.call-done = bf16[1024,1536]{1,0:T(8,128)(2,1)} async-done(((bf16[256,1536]{1,0:T(8,128)(2,1)}), bf16[1024,1536]{1,0:T(8,128)(2,1)}) %all-gather.11.cloned.1.call-update) | async-done | bytes 3145744 | tf_op jit(solution)/shard_map/while/body/eval_jaxpr/all_gather | solution.py:146
  237.2 54.4 %bitcast_reduce_fusion.4 = (f32[12,256]{0,1:T(8,128)}, f32[256,1024,12]{1,2,0:T(8,128)}) fusion(pred[256,1024]{1,0:T(8,128)(4,1)} %fusion.320, f32[12,12]{0,1:T(8,128)S(1)} %copy-done.49, f32[12,256,1024]{2,1,0:T(8,128)S(1)} %broadcast_multiply_fusion.8), kind=kOutput, calls=%fused_computation.7.clone.1 | convolution fusion | flops 459273216 | bytes 25440832 | tf_op jit(solution)/shard_map/while/body/eval_jaxpr/gh,rgcs->rhcs/dot_general | solution.py:58
  358.8 39.2 %all-gather.11.cloned.1.call-done = bf16[1024,1536]{1,0:T(8,128)(2,1)} async-done(((bf16[256,1536]{1,0:T(8,128)(2,1)}), bf16[1024,1536]{1,0:T(8,128)(2,1)}) %all-gather.11.cloned.1.call-update) | async-done | bytes 3145744 | tf_op jit(solution)/shard_map/while/body/eval_jaxpr/all_gather | solution.py:146
  406.8 45.9 %bitcast_reduce_fusion.4 = (f32[12,256]{0,1:T(8,128)}, f32[256,1024,12]{1,2,0:T(8,128)}) fusion(pred[256,1024]{1,0:T(8,128)(4,1)} %fusion.320, f32[12,12]{0,1:T(8,128)S(1)} %copy-done.49, f32[12,256,1024]{2,1,0:T(8,128)S(1)} %broadcast_multiply_fusion.8), kind=kOutput, calls=%fused_computation.7.clone.1 | convolution fusion | flops 459273216 | bytes 25440832 | tf_op jit(solution)/shard_map/while/body/eval_jaxpr/gh,rgcs->rhcs/dot_general | solution.py:58
  510.4 1198.0 %while.56 = (s32[]{:T(128)}, bf16[1,256,768]{2,1,0:T(8,128)(2,1)S(1)}, f32[768]{0:T(1024)}, f32[768,2304]{1,0:T(8,128)}, f32[768,768]{1,0:T(8,128)}, /*index=5*/...) while((s32[]{:T(128)}, ...), condition=%wide.region_17.18_spmd.clone.clone, body=%wide.region_6.17_spmd.clone.clone.sunk | while | flops 14958455808 | bytes 780841536 | solution.py:281
  524.7 38.1 %all-gather.13.cloned.1.call-done = bf16[1024,1536]{1,0:T(8,128)(2,1)} async-done(((bf16[256,1536]{1,0:T(8,128)(2,1)}), bf16[1024,1536]{1,0:T(8,128)(2,1)}) %all-gather.13.cloned.1.call-update) | async-done | bytes 3145744 | tf_op jit(solution)/shard_map/while/body/eval_jaxpr/all_gather | solution.py:187
  573.6 44.7 %bitcast_reduce_fusion.5 = (f32[12,256]{0,1:T(8,128)S(1)}, f32[256,1024,12]{1,2,0:T(8,128)}) fusion(pred[256,1024]{1,0:T(8,128)(4,1)S(1)} %fusion.362, f32[12,12]{1,0:T(8,128)S(1)} %get-tuple-element.1848, f32[12,256,1024]{2,1,0:T(8,128)S(1)} %broadcast_multiply_fusion.9), kind=kOutput, calls=%fused_computation.94.clone.1 | convolution fusion | flops 459273216 | bytes 25440832 | tf_op jit(solution)/shard_map/while/body/eval_jaxpr/gh,rgcs->rhcs/dot_general | solution.py:58
  707.4 46.3 %fusion.369 = (f32[12,256]{0,1:T(8,128)}, f32[256,1024,12]{1,2,0:T(8,128)}) fusion(f32[12,256]{0,1:T(8,128)} %copy-done.31, f32[12,256]{0,1:T(8,128)S(1)} %get-tuple-element.1694, f32[256,1024,12]{1,2,0:T(8,128)} %get-tuple-element.1693, pred[256,1024]{1,0:T(8,128)(4,1)S(1)} %fusion.362, f32[12,12]{1,0:T(8,128)S(1)} %copy-done.56, ...), kind=kOutput, calls=%fused_computation.88.clone.1 | convolution fusion | flops 468710400 | bytes 38048320 | tf_op jit(solution)/shard_map/while/body/eval_jaxpr/gh,rhcs->rgcs/dot_general | solution.py:226
  916.1 39.0 %all-gather.13.cloned.1.call-done = bf16[1024,1536]{1,0:T(8,128)(2,1)} async-done(((bf16[256,1536]{1,0:T(8,128)(2,1)}), bf16[1024,1536]{1,0:T(8,128)(2,1)}) %all-gather.13.cloned.1.call-update) | async-done | bytes 3145744 | tf_op jit(solution)/shard_map/while/body/eval_jaxpr/all_gather | solution.py:187
  965.8 44.6 %bitcast_reduce_fusion.5 = (f32[12,256]{0,1:T(8,128)S(1)}, f32[256,1024,12]{1,2,0:T(8,128)}) fusion(pred[256,1024]{1,0:T(8,128)(4,1)S(1)} %fusion.362, f32[12,12]{1,0:T(8,128)S(1)} %get-tuple-element.1848, f32[12,256,1024]{2,1,0:T(8,128)S(1)} %broadcast_multiply_fusion.9), kind=kOutput, calls=%fused_computation.94.clone.1 | convolution fusion | flops 459273216 | bytes 25440832 | tf_op jit(solution)/shard_map/while/body/eval_jaxpr/gh,rgcs->rhcs/dot_general | solution.py:58
  1099.3 46.5 %fusion.369 = (f32[12,256]{0,1:T(8,128)}, f32[256,1024,12]{1,2,0:T(8,128)}) fusion(f32[12,256]{0,1:T(8,128)} %copy-done.31, f32[12,256]{0,1:T(8,128)S(1)} %get-tuple-element.1694, f32[256,1024,12]{1,2,0:T(8,128)} %get-tuple-element.1693, pred[256,1024]{1,0:T(8,128)(4,1)S(1)} %fusion.362, f32[12,12]{1,0:T(8,128)S(1)} %copy-done.56, ...), kind=kOutput, calls=%fused_computation.88.clone.1 | convolution fusion | flops 468710400 | bytes 38048320 | tf_op jit(solution)/shard_map/while/body/eval_jaxpr/gh,rhcs->rgcs/dot_general | solution.py:226
  1203.8 31.8 %fusion.375 = f32[12,12]{1,0:T(8,128)S(1)} fusion(f32[12,256,1024]{2,1,0:T(8,128)} %copy-done.1, f32[12,12]{1,0:T(8,128)S(1)} %copy-done.43, f32[]{:T(128)S(6)} %convert_element_type.455, pred[]{:T(512)S(6)} %compare.3, f32[12,256,1024]{2,0,1:T(8,128)} %fusion.374), kind=kOutput, calls=%fused_computation.147.clone.2 | convolution fusion | flops 452985280 | bytes 25166980 | tf_op jit(solution)/shard_map/while/body/eval_jaxpr/rgcs,rhcs->gh/dot_general | solution.py:225
  1316.6 39.2 %all-gather.13.cloned.1.call-done = bf16[1024,1536]{1,0:T(8,128)(2,1)} async-done(((bf16[256,1536]{1,0:T(8,128)(2,1)}), bf16[1024,1536]{1,0:T(8,128)(2,1)}) %all-gather.13.cloned.1.call-update) | async-done | bytes 3145744 | tf_op jit(solution)/shard_map/while/body/eval_jaxpr/all_gather | solution.py:187
  1366.6 44.6 %bitcast_reduce_fusion.5 = (f32[12,256]{0,1:T(8,128)S(1)}, f32[256,1024,12]{1,2,0:T(8,128)}) fusion(pred[256,1024]{1,0:T(8,128)(4,1)S(1)} %fusion.362, f32[12,12]{1,0:T(8,128)S(1)} %get-tuple-element.1848, f32[12,256,1024]{2,1,0:T(8,128)S(1)} %broadcast_multiply_fusion.9), kind=kOutput, calls=%fused_computation.94.clone.1 | convolution fusion | flops 459273216 | bytes 25440832 | tf_op jit(solution)/shard_map/while/body/eval_jaxpr/gh,rgcs->rhcs/dot_general | solution.py:58
  1500.3 46.3 %fusion.369 = (f32[12,256]{0,1:T(8,128)}, f32[256,1024,12]{1,2,0:T(8,128)}) fusion(f32[12,256]{0,1:T(8,128)} %copy-done.31, f32[12,256]{0,1:T(8,128)S(1)} %get-tuple-element.1694, f32[256,1024,12]{1,2,0:T(8,128)} %get-tuple-element.1693, pred[256,1024]{1,0:T(8,128)(4,1)S(1)} %fusion.362, f32[12,12]{1,0:T(8,128)S(1)} %copy-done.56, ...), kind=kOutput, calls=%fused_computation.88.clone.1 | convolution fusion | flops 468710400 | bytes 38048320 | tf_op jit(solution)/shard_map/while/body/eval_jaxpr/gh,rhcs->rgcs/dot_general | solution.py:226
  1604.8 31.8 %fusion.375 = f32[12,12]{1,0:T(8,128)S(1)} fusion(f32[12,256,1024]{2,1,0:T(8,128)} %copy-done.1, f32[12,12]{1,0:T(8,128)S(1)} %copy-done.43, f32[]{:T(128)S(6)} %convert_element_type.455, pred[]{:T(512)S(6)} %compare.3, f32[12,256,1024]{2,0,1:T(8,128)} %fusion.374), kind=kOutput, calls=%fused_computation.147.clone.2 | convolution fusion | flops 452985280 | bytes 25166980 | tf_op jit(solution)/shard_map/while/body/eval_jaxpr/rgcs,rhcs->gh/dot_general | solution.py:225
  1712.2 76.3 %all-reduce.2 = (f32[768]{0:T(1024)S(1)}, f32[1,12,12]{2,0,1:T(1,128)}, f32[1,12,12]{2,0,1:T(1,128)}, f32[768]{0:T(1024)S(1)}) all-reduce(f32[768]{0:T(1024)S(1)} %copy-done.55, f32[1,12,12]{2,0,1:T(1,128)S(1)} %broadcast_in_dim.196, ...), channel_id=5, replica_groups=mesh['section'=2,'dp'=4,'ctx'=4] {'dp','ctx'}, use_global_device_ids=true, to_apply=%region_18.19.clone | all-reduce | flops 1824 | bytes 14592
  1789.7 53.3 %reduce-scatter.8.cloned.1.call-done = f32[48,768]{1,0:T(8,128)} async-done(((f32[768,768]{1,0:T(8,128)}), f32[48,768]{1,0:T(8,128)}) %reduce-scatter.8.cloned.1.call-update) | async-done | bytes 147472 | tf_op jit(solution)/shard_map/reduce_scatter | solution.py:284
  1843.0 156.8 %reduce-scatter.6.cloned.1.call-done = f32[48,2304]{1,0:T(8,128)} async-done(((f32[768,2304]{1,0:T(8,128)}), f32[48,2304]{1,0:T(8,128)}) %reduce-scatter.6.cloned.1.call-update) | async-done | bytes 442384 | tf_op jit(solution)/shard_map/reduce_scatter | solution.py:284
  1999.8 176.7 %reduce-scatter.10.cloned.1.call-done = f32[48,3072]{1,0:T(8,128)} async-done(((f32[768,3072]{1,0:T(8,128)}), f32[48,3072]{1,0:T(8,128)}) %reduce-scatter.10.cloned.1.call-update) | async-done | bytes 589840 | tf_op jit(solution)/shard_map/reduce_scatter | solution.py:284
  2176.5 176.1 %reduce-scatter.12.cloned.1.call-done = f32[192,768]{1,0:T(8,128)} async-done(((f32[3072,768]{1,0:T(8,128)}), f32[192,768]{1,0:T(8,128)}) %reduce-scatter.12.cloned.1.call-update) | async-done | bytes 589840 | tf_op jit(solution)/shard_map/reduce_scatter | solution.py:284
  (669 shorter events, 973.3 us)
Async XLA Ops:
  13.9 496.5 %copy-start.42 = (f32[12,12]{1,0:T(8,128)S(1)}, f32[12,12]{1,0:T(8,128)}, u32[]{:S(2)}) copy-start(f32[12,12]{1,0:T(8,128)} %get-tuple-element.1788) | copy-start | bytes 1732
  14.2 52.5 %all-gather.11.cloned.1.call-start = ((), (), s32[]{:S(2)}) async-start(), calls=%async_computation.9 | async-start | bytes 3932160 | tf_op jit(solution)/shard_map/while/body/eval_jaxpr/all_gather | solution.py:146
  175.3 3.1 collective-permute-start
  178.6 49.8 %all-gather.11.cloned.1.call-start = ((), (), s32[]{:S(2)}) async-start(), calls=%async_computation.9 | async-start | bytes 3932160 | tf_op jit(solution)/shard_map/while/body/eval_jaxpr/all_gather | solution.py:146
  344.8 3.1 collective-permute-start
  348.2 49.8 %all-gather.11.cloned.1.call-start = ((), (), s32[]{:S(2)}) async-start(), calls=%async_computation.9 | async-start | bytes 3932160 | tf_op jit(solution)/shard_map/while/body/eval_jaxpr/all_gather | solution.py:146
  506.2 3.1 collective-permute-start
  514.2 48.5 %all-gather.13.cloned.1.call-start = ((), (), s32[]{:S(2)}) async-start(), calls=%async_computation.10 | async-start | bytes 3932160 | tf_op jit(solution)/shard_map/while/body/eval_jaxpr/all_gather | solution.py:187
  518.6 373.6 %reduce-scatter.14.cloned.1.call-start = ((), (), s32[]{:S(2)}) async-start(), calls=%async_computation.11 | async-start | bytes 3932160 | tf_op jit(solution)/shard_map/while/body/eval_jaxpr/reduce_scatter | solution.py:255
  573.6 44.7 %copy-start = (f32[12,256,1024]{2,1,0:T(8,128)}, f32[12,256,1024]{2,1,0:T(8,128)S(1)}, u32[]{:S(2)}) copy-start(f32[12,256,1024]{2,1,0:T(8,128)S(1)} %broadcast_multiply_fusion.9) | copy-start | bytes 37748740 | tf_op jit(solution)/shard_map/while
  618.3 46.9 %slice-start.3 = ((s8[4718592]{0:T(1024)(128)(4,1)}), s8[4194304]{0:T(1024)(128)(4,1)S(1)}, s32[]{:S(2)}) async-start(s8[4718592]{0:T(1024)(128)(4,1)} %bitcast.548), calls=%async_computation.15 | async-start | bytes 8388608 | tf_op jit(solution)/shard_map/while
  898.0 6.6 collective-permute-start.1
  905.6 49.4 %all-gather.13.cloned.1.call-start = ((), (), s32[]{:S(2)}) async-start(), calls=%async_computation.10 | async-start | bytes 3932160 | tf_op jit(solution)/shard_map/while/body/eval_jaxpr/all_gather | solution.py:187
  910.0 380.8 %reduce-scatter.14.cloned.1.call-start = ((), (), s32[]{:S(2)}) async-start(), calls=%async_computation.11 | async-start | bytes 3932160 | tf_op jit(solution)/shard_map/while/body/eval_jaxpr/reduce_scatter | solution.py:255
  1010.5 46.9 %slice-start.3 = ((s8[4718592]{0:T(1024)(128)(4,1)}), s8[4194304]{0:T(1024)(128)(4,1)S(1)}, s32[]{:S(2)}) async-start(s8[4718592]{0:T(1024)(128)(4,1)} %bitcast.548), calls=%async_computation.15 | async-start | bytes 8388608 | tf_op jit(solution)/shard_map/while
  1296.6 8.8 collective-permute-start.1
  1306.1 49.7 %all-gather.13.cloned.1.call-start = ((), (), s32[]{:S(2)}) async-start(), calls=%async_computation.10 | async-start | bytes 3932160 | tf_op jit(solution)/shard_map/while/body/eval_jaxpr/all_gather | solution.py:187
  1310.5 381.0 %reduce-scatter.14.cloned.1.call-start = ((), (), s32[]{:S(2)}) async-start(), calls=%async_computation.11 | async-start | bytes 3932160 | tf_op jit(solution)/shard_map/while/body/eval_jaxpr/reduce_scatter | solution.py:255
  1411.2 46.9 %slice-start.3 = ((s8[4718592]{0:T(1024)(128)(4,1)}), s8[4194304]{0:T(1024)(128)(4,1)S(1)}, s32[]{:S(2)}) async-start(s8[4718592]{0:T(1024)(128)(4,1)} %bitcast.548), calls=%async_computation.15 | async-start | bytes 8388608 | tf_op jit(solution)/shard_map/while
  1697.3 8.8 collective-permute-start.1
  1708.3 134.6 %reduce-scatter.8.cloned.1.call-start = ((), (), s32[]{:S(2)}) async-start(), calls=%async_computation.6 | async-start | bytes 2506752 | tf_op jit(solution)/shard_map/reduce_scatter | solution.py:284
  1708.9 290.8 %reduce-scatter.6.cloned.1.call-start = ((), (), s32[]{:S(2)}) async-start(), calls=%async_computation.5 | async-start | bytes 7520256 | tf_op jit(solution)/shard_map/reduce_scatter | solution.py:284
  1709.5 467.0 %reduce-scatter.10.cloned.1.call-start = ((), (), s32[]{:S(2)}) async-start(), calls=%async_computation.7 | async-start | bytes 10027008 | tf_op jit(solution)/shard_map/reduce_scatter | solution.py:284
  1710.1 642.5 %reduce-scatter.12.cloned.1.call-start = ((), (), s32[]{:S(2)}) async-start(), calls=%async_computation.8 | async-start | bytes 10027008 | tf_op jit(solution)/shard_map/reduce_scatter | solution.py:284
  (190 other events, 2167.6 us)
Sparse Core Ops, SparseCore 0:
  20.0 46.6 all-gather.10
  184.4 43.9 all-gather.10
  354.0 44.0 all-gather.10
  518.7 44.0 all-gather.12
  808.1 43.9 reduce-scatter.13
  910.1 44.9 all-gather.12
  1203.9 43.9 reduce-scatter.13
  1310.6 45.1 all-gather.12
  1604.8 43.9 reduce-scatter.13
Sparse Core Ops, SparseCore 1:
  1714.3 128.6 reduce-scatter.7
  1849.6 150.1 reduce-scatter.5
  2006.8 169.6 reduce-scatter.9
  2182.8 169.7 reduce-scatter.11
where the time goes:
time: 2360 us
  matrix products  1160 us (49%)
  waiting for transfers between devices  806 us (34%)
  other arithmetic  195 us (8%)
  local copies, waits for them, and re-layouts  83.1 us (4%)
  blocking collectives  76.3 us (3%)
    reduce_scatter x4, waiting for transfers between devices, local(): lax.psum_scatter(grad_sums, ('dp', 'ctx'), scatter_dimension=0, tiled=True)  563 us
    dot_general x6, matrix products, attend(): logits = jnp.einsum('gh,rgcs->rhcs', premix, scores, precision=HIGHEST)  281 us
    dot_general x6, matrix products, attend(): jnp.einsum('gh,rgcs->rhcs', postmix, attention, precision=HIGHEST)  174 us
    dot_general x3, matrix products, backward_tick(): jnp.einsum('gh,rhcs->rgcs', postmix, grad_mixed, precision=HIGHEST)  139 us
    all_gather x3, waiting for transfers between devices, forward_tick(): kv_all = lax.all_gather(kv_local, 'ctx', axis=1, tiled=True)  120 us
    all_gather x3, waiting for transfers between devices, backward_tick(): kv_all = lax.all_gather(kv_local, 'ctx', axis=1, tiled=True)  116 us
    dot_general x3, matrix products, backward_tick(): jnp.einsum('rgcs,rhcs->gh', attention, grad_mixed, precision=HIGHEST)  95.3 us
    dot_general x3, matrix products, backward_tick(): jnp.einsum('gh,rhcs->rgcs', premix, grad_logits, precision=HIGHEST)  88.5 us
  transfers between devices with their start and end apart: 19, of which 13 were waited for; matrix products, arithmetic and copies ran while one was open for 13% of the time, Pallas kernels for 0%

commit v1 on v0

v1 whole, which is shorter than its diff:
```python
import functools

import jax
import jax.numpy as jnp
from jax import lax
from jax.experimental import pallas as pl
from jax.experimental.pallas import tpu as pltpu
from jax.sharding import PartitionSpec as P

HEADS = 12
HEAD = 64
eps = 1e-06
MASKED = -1e30
f32 = jnp.float32
bf16 = jnp.bfloat16
VMEM_BYTES = 56 * 1024 * 1024


def dense(left_side, right_side):
    return jnp.dot(left_side, right_side, preferred_element_type=f32)


def dense_tn(left_side, right_side):
    return lax.dot_general(
        left_side, right_side, (((0,), (0,)), ((), ())), preferred_element_type=f32
    )


def dense_nt(left_side, right_side):
    return lax.dot_general(
        left_side, right_side, (((1,), (1,)), ((), ())), preferred_element_type=f32
    )


def forward_kernel(
    place, q_ref, k_ref, v_ref, pre_ref, post_ref, att_ref, u_ref, lse_ref, qp, logit, total, *, bq, bk
):
    step = pl.program_id(0)
    q_start = place[1 + step]
    length = place[0]
    q32 = q_ref[...].astype(f32)
    for h in range(HEADS):
        qp[pl.ds(h * bq, bq), :] = (q32 * pre_ref[h : h + 1, :]).astype(bf16)
    last = jnp.minimum(q_start + bq, length)
    blocks = (last + bk - 1) // bk
    rows = q_start + lax.broadcasted_iota(jnp.int32, (bq, bk), 0)

    def score(kb, top):
        k_blk = k_ref[pl.ds(pl.multiple_of(kb * bk, bk), bk), :]
        cols = kb * bk + lax.broadcasted_iota(jnp.int32, (bq, bk), 1)
        bias = jnp.where((cols <= rows) & (cols < length), 0.0, MASKED).astype(f32)
        tile = dense_nt(qp[...], k_blk)
        tile = (tile.reshape(HEADS, bq, bk) + bias[None]).reshape(HEADS * bq, bk)
        logit[kb] = tile
        return jnp.maximum(top, jnp.max(tile, axis=-1, keepdims=True))

    top = lax.fori_loop(0, blocks, score, jnp.full((HEADS * bq, 1), MASKED, f32))
    total[...] = jnp.zeros_like(total)

    def apply(kb, norm):
        e = jnp.exp(logit[kb] - top)
        v_blk = v_ref[pl.ds(pl.multiple_of(kb * bk, bk), bk), :]
        total[...] += dense(e.astype(bf16), v_blk)
        return norm + jnp.sum(e, axis=-1, keepdims=True)

    norm = lax.fori_loop(0, blocks, apply, jnp.zeros((HEADS * bq, 1), f32))
    scale = 1.0 / norm
    att = jnp.zeros((bq, q_ref.shape[1]), f32)
    for g in range(HEADS):
        u = total[pl.ds(g * bq, bq), :] * scale[g * bq : (g + 1) * bq]
        u_ref[pl.ds(g * bq, bq), :] = u.astype(bf16)
        att = att + u * post_ref[g : g + 1, :]
    att_ref[...] = att.astype(bf16)
    lse = jnp.broadcast_to(top + jnp.log(norm), (HEADS * bq, 128))
    lse_ref[0] = jnp.transpose(lse)[0:1, :]


def attention_forward(q, k, v, pre_vec, post_vec, place, bq, bk):
    count, width = q.shape
    seq = k.shape[0]
    steps = count // bq
    full = lambda i, place: (0, 0)
    return pl.pallas_call(
        functools.partial(forward_kernel, bq=bq, bk=bk),
        grid_spec=pltpu.PrefetchScalarGridSpec(
            num_scalar_prefetch=1,
            grid=(steps,),
            in_specs=[
                pl.BlockSpec((bq, width), lambda i, place: (i, 0)),
                pl.BlockSpec((seq, width), full),
                pl.BlockSpec((seq, width), full),
                pl.BlockSpec((HEADS, width), full),
                pl.BlockSpec((HEADS, width), full),
            ],
            out_specs=[
                pl.BlockSpec((bq, width), lambda i, place: (i, 0)),
                pl.BlockSpec((HEADS * bq, width), lambda i, place: (i, 0)),
                pl.BlockSpec((1, 1, HEADS * bq), lambda i, place: (i, 0, 0)),
            ],
            scratch_shapes=[
                pltpu.VMEM((HEADS * bq, width), bf16),
                pltpu.VMEM((seq // bk, HEADS * bq, bk), f32),
                pltpu.VMEM((HEADS * bq, width), f32),
            ],
        ),
        out_shape=[
            jax.ShapeDtypeStruct((count, width), bf16),
            jax.ShapeDtypeStruct((HEADS * count, width), bf16),
            jax.ShapeDtypeStruct((steps, 1, HEADS * bq), f32),
        ],
        compiler_params=pltpu.CompilerParams(vmem_limit_bytes=VMEM_BYTES),
        cost_estimate=pl.CostEstimate(
            flops=4 * HEADS * count * seq * width * 5 // 8,
            bytes_accessed=4 * seq * width + 2 * HEADS * count * width,
            transcendentals=HEADS * count * seq * 5 // 8,
        ),
    )(place, q, k, v, pre_vec, post_vec)


def backward_kernel(
    place, q_ref, datt_ref, u_ref, lse_ref, k_ref, kt_ref, v_ref, pre_ref, post_ref,
    dq_ref, dk_ref, dv_ref, pre_grad_ref, post_grad_ref,
    qp, dp, dk_sum, dv_sum, wt, delta, *, bq, bk,
):
    step = pl.program_id(0)
    q_start = place[1 + step]
    length = place[0]

    @pl.when(step == 0)
    def _():
        dk_sum[...] = jnp.zeros_like(dk_sum)
        dv_sum[...] = jnp.zeros_like(dv_sum)
        pre_grad_ref[...] = jnp.zeros_like(pre_grad_ref)
        post_grad_ref[...] = jnp.zeros_like(post_grad_ref)

    q32 = q_ref[...].astype(f32)
    datt = datt_ref[...].astype(f32)
    for h in range(HEADS):
        part = pl.ds(h * bq, bq)
        qp[part, :] = (q32 * pre_ref[h : h + 1, :]).astype(bf16)
        scaled = datt * post_ref[h : h + 1, :]
        dp[part, :] = scaled.astype(bf16)
        u = u_ref[part, :].astype(f32)
        spread = jnp.sum(scaled * u, axis=-1, keepdims=True)
        delta[part, :] = jnp.broadcast_to(spread, (bq, 128))
        post_grad_ref[h : h + 1, :] += jnp.sum(datt * u, axis=0, keepdims=True)
    spread = jnp.transpose(delta[...])[0:1, :]
    lse = lse_ref[0]
    wt[...] = jnp.zeros_like(wt)
    last = jnp.minimum(q_start + bq, length)
    blocks = (last + bk - 1) // bk
    cols = q_start + lax.broadcasted_iota(jnp.int32, (bk, HEADS * bq), 1) % bq

    def block(kb, carry):
        span = pl.ds(pl.multiple_of(kb * bk, bk), bk)
        rows = kb * bk + lax.broadcasted_iota(jnp.int32, (bk, HEADS * bq), 0)
        allowed = (rows <= cols) & (rows < length)
        logits = dense_nt(k_ref[span, :], qp[...])
        attention = jnp.exp(jnp.where(allowed, logits - lse, MASKED))
        grad = dense_nt(v_ref[span, :], dp[...])
        dlog = (attention * (grad - spread)).astype(bf16)
        dv_sum[span, :] += dense(attention.astype(bf16), dp[...])
        dk_sum[span, :] += dense(dlog, qp[...])
        wt[...] += dense(kt_ref[:, span], dlog)
        return carry

    lax.fori_loop(0, blocks, block, 0)
    w = jnp.transpose(wt[...])
    dq = jnp.zeros_like(q32)
    for h in range(HEADS):
        part = w[h * bq : (h + 1) * bq, :]
        dq = dq + part * pre_ref[h : h + 1, :]
        pre_grad_ref[h : h + 1, :] += jnp.sum(part * q32, axis=0, keepdims=True)
    dq_ref[...] = dq.astype(bf16)

    @pl.when(step == pl.num_programs(0) - 1)
    def _():
        dk_ref[...] = dk_sum[...].astype(bf16)
        dv_ref[...] = dv_sum[...].astype(bf16)


def attention_backward(q, datt, u, lse, k, kt, v, pre_vec, post_vec, place, bq, bk):
    count, width = q.shape
    seq = k.shape[0]
    steps = count // bq
    full = lambda i, place: (0, 0)
    row = lambda i, place: (i, 0)
    return pl.pallas_call(
        functools.partial(backward_kernel, bq=bq, bk=bk),
        grid_spec=pltpu.PrefetchScalarGridSpec(
            num_scalar_prefetch=1,
            grid=(steps,),
            in_specs=[
                pl.BlockSpec((bq, width), row),
                pl.BlockSpec((bq, width), row),
                pl.BlockSpec((HEADS * bq, width), row),
                pl.BlockSpec((1, 1, HEADS * bq), lambda i, place: (i, 0, 0)),
                pl.BlockSpec((seq, width), full),
                pl.BlockSpec((width, seq), full),
                pl.BlockSpec((seq, width), full),
                pl.BlockSpec((HEADS, width), full),
                pl.BlockSpec((HEADS, width), full),
            ],
            out_specs=[
                pl.BlockSpec((bq, width), row),
                pl.BlockSpec((seq, width), full),
                pl.BlockSpec((seq, width), full),
                pl.BlockSpec((HEADS, width), full),
                pl.BlockSpec((HEADS, width), full),
            ],
            scratch_shapes=[
                pltpu.VMEM((HEADS * bq, width), bf16),
                pltpu.VMEM((HEADS * bq, width), bf16),
                pltpu.VMEM((seq, width), f32),
                pltpu.VMEM((seq, width), f32),
                pltpu.VMEM((width, HEADS * bq), f32),
                pltpu.VMEM((HEADS * bq, 128), f32),
            ],
        ),
        out_shape=[
            jax.ShapeDtypeStruct((count, width), bf16),
            jax.ShapeDtypeStruct((seq, width), bf16),
            jax.ShapeDtypeStruct((seq, width), bf16),
            jax.ShapeDtypeStruct((HEADS, width), f32),
            jax.ShapeDtypeStruct((HEADS, width), f32),
        ],
        compiler_params=pltpu.CompilerParams(vmem_limit_bytes=VMEM_BYTES),
        cost_estimate=pl.CostEstimate(
            flops=10 * HEADS * count * seq * width * 5 // 8,
            bytes_accessed=10 * seq * width + 2 * HEADS * count * width,
            transcendentals=HEADS * count * seq * 5 // 8,
        ),
    )(place, q, datt, u, lse, k, kt, v, pre_vec, post_vec)


def swap_section(x):
    return lax.ppermute(x, "section", [(0, 1), (1, 0)])


def xor_permute(x, axis, by):
    return lax.ppermute(x, axis, [(i, i ^ by) for i in range(lax.axis_size(axis))])


def from_xor_order(x, index):
    places = range(x.shape[0])
    return jnp.concatenate([lax.dynamic_index_in_dim(x, index ^ i, 0) for i in places])


def reduce_scatter(block):
    dp_count, ctx_count = block.shape[:2]
    ctx, dp = lax.axis_index("ctx"), lax.axis_index("dp")
    bits = []
    bit = 1
    while bit < ctx_count:
        bits.append(bit)
        bit *= 2
    columns = block.shape[3]
    cut = (columns // 2 + 127) // 128 * 128
    halves = []
    for part, order in ((block[..., :cut], bits), (block[..., cut:], bits[::-1])):
        ids = list(range(len(bits)))
        part = part.reshape((dp_count,) + (2,) * len(bits) + part.shape[2:])
        left = list(bits[::-1])
        for bit in order:
            axis = 1 + left.index(bit)
            left.remove(bit)
            mine = (ctx // bit) % 2
            sent = lax.dynamic_index_in_dim(part, 1 - mine, axis, keepdims=False)
            kept = lax.dynamic_index_in_dim(part, mine, axis, keepdims=False)
            got = xor_permute(sent, "ctx", bit)
            part = (kept.astype(f32) + got.astype(f32)).astype(bf16)
        halves.append(part)
    whole = jnp.concatenate(halves, axis=-1)
    total = lax.dynamic_index_in_dim(whole, dp, 0, keepdims=False).astype(f32)
    for by in range(1, dp_count):
        sent = lax.dynamic_index_in_dim(whole, dp ^ by, 0, keepdims=False)
        total = total + xor_permute(sent, "dp", by).astype(f32)
    return total


def all_sum(vector):
    for axis in ("ctx", "dp"):
        bit = 1
        while bit < lax.axis_size(axis):
            vector = vector + xor_permute(vector, axis, bit)
            bit *= 2
    return vector


def local(
    inputs, lengths, cotangent, first_gain, joint_weight, pre_mix, post_mix,
    mixer_weight, second_gain, up_weight, down_weight,
):
    s = lax.axis_index("section")
    ctx = lax.axis_index("ctx")
    n = lax.axis_size("ctx")
    dp_count = lax.axis_size("dp")
    chips = n // 2
    micro_count, row_count, local_len, width = inputs.shape
    seq = local_len * n
    blk = local_len // 2
    m = ctx // chips
    xi = ctx % chips
    core = xi * 2 + s
    inputs = inputs.reshape(micro_count, 2, blk, width)
    cotangent = cotangent.reshape(micro_count, 2, blk, width)
    pick = lambda arr, i: lax.dynamic_index_in_dim(arr, i, 0, keepdims=False)

    mine = pick(inputs, m)
    pieces = []
    for d in range(1, n):
        target = m ^ (1 if d >= chips else 0)
        pieces.append(xor_permute(pick(pick(inputs, target), s), "ctx", d))
    own_half = jnp.stack([pick(mine, s)] + pieces)
    other_half = jnp.concatenate([pick(mine, 1 - s)[None], swap_section(jnp.stack(pieces))])
    first, second = jnp.where(s == 0, own_half, other_half), jnp.where(s == 0, other_half, own_half)
    x_all = from_xor_order(jnp.stack([first, second], axis=1), ctx).reshape(seq, width)

    both = []
    for w in (first_gain, joint_weight, pre_mix, post_mix, mixer_weight, second_gain, up_weight, down_weight):
        got = swap_section(w)
        both.append((jnp.where(s == 0, w[0], got[0]), jnp.where(s == 0, got[0], w[0])))
    gains_a, joints, premixes, postmixes, mixers, gains_b, ups, downs = both

    length = pick(lengths.reshape(-1), m)
    low_start = core * blk
    high_start = (2 * n - 1 - core) * blk
    bq = min(64, blk)
    bk = min(256, seq)
    per = blk // bq
    place = jnp.stack(
        [length]
        + [low_start + i * bq for i in range(per)]
        + [high_start + i * bq for i in range(per)]
    ).astype(jnp.int32)

    def own_rows(x):
        return jnp.concatenate(
            [
                lax.dynamic_slice_in_dim(x, low_start, blk, 0),
                lax.dynamic_slice_in_dim(x, high_start, blk, 0),
            ]
        )

    def gather_row(x):
        got = [x] + [xor_permute(x, "ctx", d) for d in range(1, chips)]
        own = jnp.stack(got)
        other = swap_section(own)
        first, second = jnp.where(s == 0, own, other), jnp.where(s == 0, other, own)
        cores = from_xor_order(jnp.stack([first, second], axis=1), xi).reshape(n, 2, blk, width)
        return jnp.concatenate([cores[i, 0] for i in range(n)] + [cores[n - 1 - i, 1] for i in range(n)])

    def scatter_row(x):
        parts = x.astype(bf16).reshape(2 * n, blk, width)
        cores = jnp.stack([parts[i if h == 0 else 2 * n - 1 - i] for i in range(n) for h in range(2)])
        cores = cores.reshape(chips, 2, 2, blk, width)
        kept = lax.dynamic_index_in_dim(cores, s, 1, keepdims=False)
        got = swap_section(lax.dynamic_index_in_dim(cores, 1 - s, 1, keepdims=False))
        chip = kept.astype(f32) + got.astype(f32)
        total = pick(chip, xi)
        low = chip.astype(bf16)
        for d in range(1, chips):
            total = total + xor_permute(pick(low, xi ^ d), "ctx", d).astype(f32)
        return total.reshape(2 * blk, width)

    def rms_parts(values, gain):
        inverse = lax.rsqrt(jnp.mean(values * values, axis=-1, keepdims=True) + eps)
        return inverse, (values * inverse * gain).astype(bf16)

    def forward(layer, x_own, normed_all, normed_own):
        gain_b = gains_b[layer].astype(f32)
        joint_w = joints[layer]
        pre_vec = 0.125 * jnp.repeat(premixes[layer].T, HEAD, axis=1)
        post_vec = jnp.repeat(postmixes[layer], HEAD, axis=1)
        q = dense(normed_own, joint_w[:, :width]).astype(bf16)
        k = dense(normed_all, joint_w[:, width : 2 * width]).astype(bf16)
        v = dense(normed_all, joint_w[:, 2 * width :]).astype(bf16)
        attended, u, lse = attention_forward(q, k, v, pre_vec, post_vec, place, bq, bk)
        hidden = x_own + dense(attended, mixers[layer])
        inverse_two, normed_two = rms_parts(hidden, gain_b)
        upward = dense(normed_two, ups[layer])
        active = jax.nn.gelu(upward, approximate=True).astype(bf16)
        output = hidden + dense(active, downs[layer])
        kept = (q, k, v, u, lse, attended, hidden, inverse_two, normed_two, upward, active, pre_vec, post_vec)
        return output, kept

    def chip_rows(x):
        return jnp.concatenate([x, swap_section(x)])

    def chip_product(left, right):
        half = right.shape[1] // 2
        kept = lax.dynamic_slice_in_dim(right, s * half, half, 1)
        got = swap_section(lax.dynamic_slice_in_dim(right, (1 - s) * half, half, 1))
        return dense_tn(chip_rows(left), jnp.concatenate([kept, got])).astype(bf16)

    def blocks_of(grad):
        return grad.reshape(dp_count, n, grad.shape[0] // (dp_count * n), grad.shape[1])

    def rms_back(grad_normed, values, inverse, gain):
        unit = values * inverse
        gain_grad = jnp.sum(grad_normed * unit, axis=0)
        scaled = grad_normed * gain
        back = inverse * (scaled - unit * jnp.mean(scaled * unit, axis=-1, keepdims=True))
        return back, gain_grad

    def backward(layer, dy, x_own, inverse, normed_all, normed_own, kept):
        q, k, v, u, lse, attended, hidden, inverse_two, normed_two, upward, active, pre_vec, post_vec = kept
        gain_a, gain_b = gains_a[layer].astype(f32), gains_b[layer].astype(f32)
        joint_w = joints[layer]
        dy_low = dy.astype(bf16)
        down_sum = reduce_scatter(blocks_of(chip_product(active, dy_low)))
        dactive = dense_nt(dy_low, downs[layer])
        _, pull = jax.vjp(lambda t: jax.nn.gelu(t, approximate=True), upward)
        dup = pull(dactive)[0].astype(bf16)
        up_sum = reduce_scatter(blocks_of(chip_product(normed_two, dup)))
        dnormed_two, gain_b_grad = rms_back(dense_nt(dup, ups[layer]), hidden, inverse_two, gain_b)
        dhidden = dy + dnormed_two
        dhidden_low = dhidden.astype(bf16)
        mixer_sum = reduce_scatter(blocks_of(chip_product(attended, dhidden_low)))
        datt = dense_nt(dhidden_low, mixers[layer]).astype(bf16)
        dq, dk, dv, pre_rows, post_rows = attention_backward(
            q, datt, u, lse, k, k.T, v, pre_vec, post_vec, place, bq, bk
        )
        got = swap_section(jnp.where(s == 0, dv, dk))
        dkv = (jnp.where(s == 0, dk, dv).astype(f32) + got.astype(f32)).astype(bf16)
        kv_w = lax.dynamic_slice_in_dim(joint_w, width * (1 + s), width, 1)
        dnormed = scatter_row(dense_nt(dkv, kv_w)) + dense_nt(dq, joint_w[:, :width])
        joint_sum = reduce_scatter(
            blocks_of(jnp.concatenate([chip_product(normed_own, dq), dense_tn(normed_all, dkv).astype(bf16)], axis=1))
        )
        dfront, gain_a_grad = rms_back(dnormed, x_own, inverse, gain_a)
        pre_grad = jnp.sum(pre_rows.reshape(HEADS, HEADS, HEAD), axis=-1).T * 0.125
        post_grad = jnp.sum(post_rows.reshape(HEADS, HEADS, HEAD), axis=-1)
        small = jnp.concatenate([gain_a_grad, gain_b_grad, pre_grad.reshape(-1), post_grad.reshape(-1)])
        return dhidden + dfront, (joint_sum, mixer_sum, up_sum, down_sum), small

    x0 = x_all.astype(f32)
    _, normed_all0 = rms_parts(x0, gains_a[0].astype(f32))
    x0_own = own_rows(x_all).astype(f32)
    inverse0, normed_own0 = rms_parts(x0_own, gains_a[0].astype(f32))
    out0, kept0 = forward(0, x0_own, normed_all0, normed_own0)
    x1_own = out0.astype(bf16).astype(f32)
    inverse1, normed_own1 = rms_parts(x1_own, gains_a[1].astype(f32))
    normed_all1 = gather_row(normed_own1)
    out1, kept1 = forward(1, x1_own, normed_all1, normed_own1)

    low_chip = ctx < chips
    there = [(i, chips + i) for i in range(chips)] + [(n - 1 - i, i) for i in range(chips)]
    here = [(n - 1 - i, chips + i) for i in range(chips)] + [(i, i) for i in range(chips)]
    one = lax.ppermute(jnp.where(low_chip, pick(cotangent[1], s), pick(cotangent[0], 1 - s)), "ctx", there)
    two = lax.ppermute(jnp.where(low_chip, pick(cotangent[0], s), pick(cotangent[1], 1 - s)), "ctx", here)
    dy1 = jnp.concatenate([jnp.where(m == 0, two, one), jnp.where(m == 0, one, two)]).astype(f32)

    def send_home(x):
        x = x.reshape(2, blk, width)
        one = lax.ppermute(jnp.where(m == 0, x[1], x[0]), "ctx", [(b, a) for a, b in there])
        two = lax.ppermute(jnp.where(m == 0, x[0], x[1]), "ctx", [(b, a) for a, b in here])
        return jnp.where(low_chip, jnp.stack([two, one]), jnp.stack([one, two]))

    y_home = send_home(out1.astype(bf16))
    dx1, sums1, small1 = backward(1, dy1, x1_own, inverse1, normed_all1, normed_own1, kept1)
    dy0 = dx1.astype(bf16).astype(f32)
    dx0, sums0, small0 = backward(0, dy0, x0_own, inverse0, normed_all0, normed_own0, kept0)
    dx_home = send_home(dx0.astype(bf16))

    got = swap_section(jnp.where(s == 0, y_home, dx_home))
    held = jnp.where(s == 0, dx_home, y_home)
    is_first = jnp.where(low_chip, s, 1 - s) == 0
    ends = jnp.stack([jnp.where(is_first, held, got), jnp.where(is_first, got, held)], axis=1)
    ends = ends.reshape(1, micro_count, row_count, local_len, width)

    small_got = swap_section(jnp.where(s == 0, small1, small0))
    small = all_sum(jnp.where(s == 0, small0, small1) + small_got)
    shard = width // (dp_count * n)
    at = (lax.axis_index("dp") * n + ctx) * shard
    gain_a_out = lax.dynamic_slice_in_dim(small[:width], at, shard, 0)
    gain_b_out = lax.dynamic_slice_in_dim(small[width : 2 * width], at, shard, 0)
    pre_out = small[2 * width : 2 * width + HEADS * HEADS].reshape(1, HEADS, HEADS)
    post_out = small[2 * width + HEADS * HEADS :].reshape(1, HEADS, HEADS)

    outs = []
    for at_zero, at_one in zip(sums0, sums1):
        other = swap_section(jnp.where(s == 0, at_one, at_zero))
        own = jnp.where(s == 0, at_zero, at_one)
        outs.append((jnp.where(s == 0, own, other), jnp.where(s == 0, other, own)))
    (joint_a, joint_b), mixer_halves, up_halves, down_halves = outs
    q_half = width // 2
    joint_out = jnp.concatenate([joint_a[:, :q_half], joint_b[:, :q_half], joint_a[:, q_half:], joint_b[:, q_half:]], axis=1)
    mixer_out, up_out, down_out = (jnp.concatenate(pair, axis=1) for pair in (mixer_halves, up_halves, down_halves))
    return (
        ends,
        gain_a_out[None],
        joint_out[None],
        pre_out,
        post_out,
        mixer_out[None],
        gain_b_out[None],
        up_out[None],
        down_out[None],
    )


def solution(mesh):
    in_specs = (
        P(None, "dp", "ctx", None),
        P(None, "dp"),
        P(None, "dp", "ctx", None),
        P("section", None),
        P("section", None, None),
        P("section", None, None),
        P("section", None, None),
        P("section", None, None),
        P("section", None),
        P("section", None, None),
        P("section", None, None),
    )
    out_specs = (
        P("section", None, "dp", "ctx", None),
        P("section", ("dp", "ctx")),
        P("section", ("dp", "ctx"), None),
        P("section", None, None),
        P("section", None, None),
        P("section", ("dp", "ctx"), None),
        P("section", ("dp", "ctx")),
        P("section", ("dp", "ctx"), None),
        P("section", ("dp", "ctx"), None),
    )
    return jax.shard_map(local, mesh=mesh, in_specs=in_specs, out_specs=out_specs, check_vma=False)
```

time: 2360 us -> 603 us (0.26)
  matrix products: 1160 us -> 92.6 us
  waiting for transfers between devices: 806 us -> 196 us
  other arithmetic: 195 us -> 43.2 us
  starting transfers between devices: 9.65 us -> 133 us
  blocking collectives: 76.3 us -> 0 us
  Pallas kernels: 0 us -> 64 us
    dot_general x66 -> x12, matrix products: 1070 us -> 39.8 us  [dense(): return jnp.dot(left_side, right_side, preferred_element_type=f32)]
    reduce_scatter x7 -> x0, waiting for transfers between devices: 563 us -> none  [the longest x4 563 us: local(): lax.psum_scatter(grad_sums, ('dp', 'ctx'), scatter_dimension=0, tiled=True)]
    all_gather x6 -> x0, waiting for transfers between devices: 237 us -> none  [the longest x3 120 us: forward_tick(): kv_all = lax.all_gather(kv_local, 'ctx', axis=1, tiled=True)]
    ppermute x6 -> x108, waiting for transfers between devices: 3.92 us -> 196 us  [the longest x66 181 us: xor_permute(): lax.ppermute(x, axis, [(i, i ^ by) for i in range(lax.axis_size(axis))])]
    ppermute x6 -> x108, starting transfers between devices: 9.09 us -> 133 us  [the longest x66 105 us: xor_permute(): lax.ppermute(x, axis, [(i, i ^ by) for i in range(lax.axis_size(axis))])]
    dot_general x6 -> x0, other arithmetic: 110 us -> none  [the longest x3 55.8 us: backward_tick(): jnp.einsum('rgcs,rhcs->gh', attention, grad_mixed, precision=HIGHEST)]
    unnamed x1 -> x0, blocking collectives: 76.3 us -> none
    pallas_call x0 -> x4, Pallas kernels: none -> 64 us  [the longest x2 39.7 us: attention_backward(): pl.pallas_call(functools.partial(backward_kernel, bq=bq, bk=bk), grid_spe...]
  transfers between devices with their start and end apart: 19 -> 108, of which waited for: 13 -> 47; matrix products, arithmetic and copies ran while one was open for 13% -> 31% of each run, Pallas kernels for 0% -> 11%
where the time goes in v1:
time: 603 us; the launch traced here: 596 us
  waiting for transfers between devices  196 us (33%)
  starting transfers between devices  133 us (22%)
  matrix products  92.6 us (15%)
  Pallas kernels  64 us (11%)
  local copies, waits for them, and re-layouts  63.6 us (11%)
  other arithmetic  43.2 us (7%)
    ppermute x66, waiting for transfers between devices, xor_permute(): lax.ppermute(x, axis, [(i, i ^ by) for i in range(lax.axis_size(axis))])  181 us
    ppermute x66, starting transfers between devices, xor_permute(): lax.ppermute(x, axis, [(i, i ^ by) for i in range(lax.axis_size(axis))])  105 us
    dot_general x12, matrix products, dense(): return jnp.dot(left_side, right_side, preferred_element_type=f32)  39.8 us
    pallas_call x2, Pallas kernels, attention_backward(): pl.pallas_call(functools.partial(backward_kernel, bq=bq, bk=bk), grid_spe...  39.7 us
    dot_general x10, matrix products, dense_nt(): lax.dot_general(left_side, right_side, (((1,), (1,)), ((), ())), preferre...  32.5 us
    pallas_call x2, Pallas kernels, attention_forward(): pl.pallas_call(functools.partial(forward_kernel, bq=bq, bk=bk), grid_spec...  24.4 us
    dot_general x10, matrix products, dense_tn(): lax.dot_general(left_side, right_side, (((0,), (0,)), ((), ())), preferre...  20.3 us
    unnamed x255, local copies, waits for them, and re-layouts  13.6 us
  transfers between devices with their start and end apart: 108, of which 47 were waited for; matrix products, arithmetic and copies ran while one was open for 31% of the time, Pallas kernels for 11%

profile of v1, /device:TPU:0, one launch (start us, length us, event | category | flops | bytes accessed | tf_op | source)
XLA Modules:
  0.0 595.8 jit_solution(7212102346172754619)
XLA Ops:
  40.7 12.3 %shard_map.178 = (bf16[256,768]{1,0:T(8,128)(2,1)}, bf16[3072,768]{1,0:T(8,128)(2,1)}, f32[4,1,768]{2,1,0:T(1,128)}) custom-call(s32[5]{0:T(128)} %stack.120.place, bf16[256,768]{1,0:T(8,128)(2,1)} %convolution_convert_fusion.19.q_ref, bf16[1024,768]{1,0:T(8,128)(2,1)} %copy.68.k_ref, bf16[1024,768]{1,0:T(8,128)(2,1)} %convolution_convert_fusion.8.v_ref, ...), custom_call_target="tpu_custom_call" | custom-call | flops 6039797760 | bytes 7864320 | tf_op jit(solution)/shard_map/pallas_call | solution.py:83
  55.2 7.0 %multiply_convert_fusion.1 = (bf16[256,3072]{1,0:T(8,128)(2,1)}, f32[256,3072]{1,0:T(8,128)}) fusion(bf16[256,768]{1,0:T(8,128)(2,1)S(1)} %multiply_convert_fusion.5, bf16[1,768,3072]{2,1,0:T(8,128)(2,1)} %param.20, bf16[1,768,3072]{2,1,0:T(8,128)(2,1)} %collective-permute-done.12, pred[]{:T(512)S(6)} %eq.41), kind=kOutput, calls=%fused_computation.53 | convolution fusion | flops 1217396736 | bytes 14548993 | tf_op jit(solution)/shard_map/dot_general | solution.py:20
  70.2 9.5 %collective-permute-start.1 = (bf16[128,768]{1,0:T(8,128)(2,1)}, bf16[128,768]{1,0:T(8,128)(2,1)}, u32[]{:S(2)}, u32[]{:S(2)}) collective-permute-start(bf16[128,768]{1,0:T(8,128)(2,1)} %get-tuple-element.122), channel_id=1, source_target_pairs={{0,2},{1,3},{3,0},{2,1},{4,6},{5,7},{7,4},{6,5},{8,10},{9,11},{11,... | collective-permute-start | bytes 589832 | tf_op jit(solution)/shard_map/ppermute | solution.py:450
  83.1 10.9 %collective-permute-done.1 = bf16[128,768]{1,0:T(8,128)(2,1)} collective-permute-done((bf16[128,768]{1,0:T(8,128)(2,1)}, bf16[128,768]{1,0:T(8,128)(2,1)}, u32[]{:S(2)}, u32[]{:S(2)}) %collective-permute-start.1) | collective-permute-done | bytes 196640 | tf_op jit(solution)/shard_map/ppermute | solution.py:450
  110.8 12.1 %shard_map.179 = (bf16[256,768]{1,0:T(8,128)(2,1)}, bf16[3072,768]{1,0:T(8,128)(2,1)}, f32[4,1,768]{2,1,0:T(1,128)}) custom-call(s32[5]{0:T(128)} %stack.120.place, bf16[256,768]{1,0:T(8,128)(2,1)} %convolution_convert_fusion.18.q_ref, bf16[1024,768]{1,0:T(8,128)(2,1)} %copy.72.k_ref, bf16[1024,768]{1,0:T(8,128)(2,1)} %convolution_convert_fusion.6.v_ref, ...), custom_call_target="tpu_custom_call" | custom-call | flops 6039797760 | bytes 7864320 | tf_op jit(solution)/shard_map/pallas_call | solution.py:83
  125.4 5.9 multiply_convert_fusion
  136.6 5.6 fusion.29
  151.5 19.9 %shard_map.180 = (bf16[256,768]{1,0:T(8,128)(2,1)}, bf16[1024,768]{1,0:T(8,128)(2,1)}, bf16[1024,768]{1,0:T(8,128)(2,1)}, f32[12,768]{1,0:T(8,128)}, f32[12,768]{1,0:T(8,128)}) custom-call(s32[5]{0:T(128)} %stack.120.place, bf16[256,768]{1,0:T(8,128)(2,1)} %convolution_convert_fusion.18.q_ref, bf16[256,768]{1,0:T(8,128)(2,1)} %convolution_convert_fusion.17.datt_ref, ...), custom_call_target="tpu_custom_call" | custom-call | flops 15099494400 | bytes 12582912 | tf_op jit(solution)/shard_map/pallas_call | solution.py:188
  186.5 16.6 %collective-permute-start.64 = (bf16[4,2,48,128]{3,2,0,1:T(8,128)(2,1)S(1)}, bf16[4,2,48,128]{3,2,0,1:T(8,128)(2,1)S(1)}, u32[]{:S(2)}, u32[]{:S(2)}) collective-permute-start(bf16[4,2,48,128]{3,2,0,1:T(8,128)(2,1)S(1)} %dynamic-slice_bitcast_fusion.24), channel_id=1, source_target_pairs={{0,2},{1,3},{2,0},{3,1},{4,6},{5,7},{6,4},{7,5},{8,10},{9,11},{10,... | collective-permute-start | bytes 294920 | tf_op jit(solution)/shard_map/ppermute | solution.py:241
  231.4 5.3 collective-permute-done.83
  263.3 7.4 %collective-permute-done.45 = bf16[4,2,48,512]{3,2,0,1:T(8,128)(2,1)S(1)} collective-permute-done((bf16[4,2,48,512]{3,2,0,1:T(8,128)(2,1)S(1)}, bf16[4,2,48,512]{3,2,0,1:T(8,128)(2,1)S(1)}, u32[]{:S(2)}, u32[]{:S(2)}) %collective-permute-start.45) | collective-permute-done | bytes 393248 | tf_op jit(solution)/shard_map/ppermute | solution.py:241
  271.6 7.2 %collective-permute-done.102 = bf16[4,2,192,128]{3,2,0,1:T(8,128)(2,1)S(1)} collective-permute-done((bf16[4,2,192,128]{3,2,0,1:T(8,128)(2,1)S(1)}, bf16[4,2,192,128]{3,2,0,1:T(8,128)(2,1)S(1)}, u32[]{:S(2)}, u32[]{:S(2)}) %collective-permute-start.102) | collective-permute-done | bytes 393248 | tf_op jit(solution)/shard_map/ppermute | solution.py:241
  279.6 5.3 collective-permute-done.43
  298.6 17.2 %collective-permute-done.100 = bf16[4,2,192,256]{3,2,0,1:T(8,128)(2,1)S(1)} collective-permute-done((bf16[4,2,192,256]{3,2,0,1:T(8,128)(2,1)S(1)}, bf16[4,2,192,256]{3,2,0,1:T(8,128)(2,1)S(1)}, u32[]{:S(2)}, u32[]{:S(2)}) %collective-permute-start.100) | collective-permute-done | bytes 786464 | tf_op jit(solution)/shard_map/ppermute | solution.py:241
  333.2 19.8 %shard_map.181 = (bf16[256,768]{1,0:T(8,128)(2,1)}, bf16[1024,768]{1,0:T(8,128)(2,1)}, bf16[1024,768]{1,0:T(8,128)(2,1)}, f32[12,768]{1,0:T(8,128)}, f32[12,768]{1,0:T(8,128)}) custom-call(s32[5]{0:T(128)} %stack.120.place, bf16[256,768]{1,0:T(8,128)(2,1)} %convolution_convert_fusion.19.q_ref, bf16[256,768]{1,0:T(8,128)(2,1)} %convolution_convert_fusion.16.datt_ref, ...), custom_call_target="tpu_custom_call" | custom-call | flops 15099494400 | bytes 12582912 | tf_op jit(solution)/shard_map/pallas_call | solution.py:188
  365.2 10.0 %collective-permute-start.68 = (bf16[48,384]{1,0:T(8,128)(2,1)S(1)}, bf16[48,384]{1,0:T(8,128)(2,1)S(1)}, u32[]{:S(2)}, u32[]{:S(2)}) collective-permute-start(bf16[48,384]{1,0:T(8,128)(2,1)S(1)} %copy-done.84), channel_id=1, source_target_pairs={{0,12},{4,8},{8,4},{12,0},{1,13},{5,9},{9,5},{13,1},{2,14},{6,10},... | collective-permute-start | bytes 110600 | tf_op jit(solution)/shard_map/ppermute | solution.py:241
  392.0 6.2 %collective-permute-done.53 = bf16[4,2,48,256]{3,2,1,0:T(8,128)(2,1)S(1)} collective-permute-done((bf16[4,2,48,256]{3,2,1,0:T(8,128)(2,1)S(1)}, bf16[4,2,48,256]{3,2,1,0:T(8,128)(2,1)S(1)}, u32[]{:S(2)}, u32[]{:S(2)}) %collective-permute-start.53) | collective-permute-done | bytes 196640 | tf_op jit(solution)/shard_map/ppermute | solution.py:241
  425.7 15.4 %collective-permute-done.91 = bf16[4,2,192,256]{3,2,1,0:T(8,128)(2,1)S(1)} collective-permute-done((bf16[4,2,192,256]{3,2,1,0:T(8,128)(2,1)S(1)}, bf16[4,2,192,256]{3,2,1,0:T(8,128)(2,1)S(1)}, u32[]{:S(2)}, u32[]{:S(2)}) %collective-permute-start.91) | collective-permute-done | bytes 786464 | tf_op jit(solution)/shard_map/ppermute | solution.py:241
  445.1 5.9 collective-permute-done.92
  451.5 7.6 %collective-permute-done.72 = bf16[4,2,48,768]{3,2,1,0:T(8,128)(2,1)S(1)} collective-permute-done((bf16[4,2,48,768]{3,2,1,0:T(8,128)(2,1)S(1)}, bf16[4,2,48,768]{3,2,1,0:T(8,128)(2,1)S(1)}, u32[]{:S(2)}, u32[]{:S(2)}) %collective-permute-start.72) | collective-permute-done | bytes 589856 | tf_op jit(solution)/shard_map/ppermute | solution.py:241
  472.3 8.2 %collective-permute-start.86 = (bf16[48,1536]{1,0:T(8,128)(2,1)}, bf16[48,1536]{1,0:T(8,128)(2,1)}, u32[]{:S(2)}, u32[]{:S(2)}) collective-permute-start(bf16[48,1536]{1,0:T(8,128)(2,1)} %get-tuple-element.137), channel_id=1, source_target_pairs={{0,8},{4,12},{8,0},{12,4},{1,9},{5,13},{9,1},{13,5},{2,10},{6,14},... | collective-permute-start | bytes 442376 | tf_op jit(solution)/shard_map/ppermute | solution.py:241
  509.9 10.6 %collective-permute-done.77 = bf16[48,1536]{1,0:T(8,128)(2,1)S(1)} collective-permute-done((bf16[48,1536]{1,0:T(8,128)(2,1)S(1)}, bf16[48,1536]{1,0:T(8,128)(2,1)S(1)}, u32[]{:S(2)}, u32[]{:S(2)}) %collective-permute-start.77) | collective-permute-done | bytes 147488 | tf_op jit(solution)/shard_map/ppermute | solution.py:241
  525.4 6.7 %collective-permute-done.36 = bf16[4,2,48,512]{3,2,0,1:T(8,128)(2,1)S(1)} collective-permute-done((bf16[4,2,48,512]{3,2,0,1:T(8,128)(2,1)S(1)}, bf16[4,2,48,512]{3,2,0,1:T(8,128)(2,1)S(1)}, u32[]{:S(2)}, u32[]{:S(2)}) %collective-permute-start.36) | collective-permute-done | bytes 393248 | tf_op jit(solution)/shard_map/ppermute | solution.py:241
  557.1 9.4 %collective-permute-done.21 = bf16[2,128,768]{2,1,0:T(8,128)(2,1)S(1)} collective-permute-done((bf16[2,128,768]{2,1,0:T(8,128)(2,1)S(1)}, bf16[2,128,768]{2,1,0:T(8,128)(2,1)S(1)}, u32[]{:S(2)}, u32[]{:S(2)}) %collective-permute-start.21) | collective-permute-done | bytes 393248 | tf_op jit(solution)/shard_map/ppermute | solution.py:241
  (718 shorter events, 350.2 us)
Async XLA Ops:
  19.0 34.0 %collective-permute-start.10 = (bf16[1,768,768]{2,1,0:T(8,128)(2,1)}, bf16[1,768,768]{2,1,0:T(8,128)(2,1)}, u32[]{:S(2)}, u32[]{:S(2)}) collective-permute-start(bf16[1,768,768]{2,1,0:T(8,128)(2,1)} %param.18), channel_id=1, source_target_pairs={{0,16},{16,0},{1,17},{17,1},{2,18},{18,2},{3,19},{19,3},{4,20},{20... | collective-permute-start | bytes 3538952 | tf_op jit(solution)/shard_map/ppermute | solution.py:237
  21.8 33.4 %collective-permute-start.12 = (bf16[1,768,3072]{2,1,0:T(8,128)(2,1)}, bf16[1,768,3072]{2,1,0:T(8,128)(2,1)}, u32[]{:S(2)}, u32[]{:S(2)}) collective-permute-start(bf16[1,768,3072]{2,1,0:T(8,128)(2,1)} %param.20), channel_id=1, source_target_pairs={{0,16},{16,0},{1,17},{17,1},{2,18},{18,2},{3,19},{19,3},{4,20},{20... | collective-permute-start | bytes 14155784 | tf_op jit(solution)/shard_map/ppermute | solution.py:237
  21.9 40.3 %collective-permute-start.13 = (bf16[1,3072,768]{2,1,0:T(8,128)(2,1)}, bf16[1,3072,768]{2,1,0:T(8,128)(2,1)}, u32[]{:S(2)}, u32[]{:S(2)}) collective-permute-start(bf16[1,3072,768]{2,1,0:T(8,128)(2,1)} %param.21), channel_id=1, source_target_pairs={{0,16},{16,0},{1,17},{17,1},{2,18},{18,2},{3,19},{19,3},{4,20},{20... | collective-permute-start | bytes 14155784 | tf_op jit(solution)/shard_map/ppermute | solution.py:237
  95.8 156.3 %collective-permute-start.99 = (bf16[256,384]{1,0:T(8,128)(2,1)}, bf16[256,384]{1,0:T(8,128)(2,1)}, u32[]{:S(2)}, u32[]{:S(2)}) collective-permute-start(bf16[256,384]{1,0:T(8,128)(2,1)} %get-tuple-element.149), channel_id=1, source_target_pairs={{0,16},{16,0},{1,17},{17,1},{2,18},{18,2},{3,19},{19,3},{4,20},{20... | collective-permute-start | bytes 589832 | tf_op jit(solution)/shard_map/ppermute | solution.py:237
  96.2 313.2 %collective-permute-start.32 = (bf16[256,768]{1,0:T(8,128)(2,1)}, bf16[256,768]{1,0:T(8,128)(2,1)}, u32[]{:S(2)}, u32[]{:S(2)}) collective-permute-start(bf16[256,768]{1,0:T(8,128)(2,1)} %fusion.91), channel_id=1, source_target_pairs={{0,16},{16,0},{1,17},{17,1},{2,18},{18,2},{3,19},{19,3},{4,20},{20... | collective-permute-start | bytes 1179656 | tf_op jit(solution)/shard_map/ppermute | solution.py:237
  96.4 89.7 %collective-permute-start.41 = (bf16[256,768]{1,0:T(8,128)(2,1)}, bf16[256,768]{1,0:T(8,128)(2,1)}, u32[]{:S(2)}, u32[]{:S(2)}) collective-permute-start(bf16[256,768]{1,0:T(8,128)(2,1)} %multiply_convert_fusion.4), channel_id=1, source_target_pairs={{0,16},{16,0},{1,17},{17,1},{2,18},{18,2},{3,19},{19,3},{4,20},{20... | collective-permute-start | bytes 1179656 | tf_op jit(solution)/shard_map/ppermute | solution.py:237
  122.9 61.0 %collective-permute-start.60 = (bf16[256,768]{1,0:T(8,128)(2,1)}, bf16[256,768]{1,0:T(8,128)(2,1)}, u32[]{:S(2)}, u32[]{:S(2)}) collective-permute-start(bf16[256,768]{1,0:T(8,128)(2,1)} %get-tuple-element.26), channel_id=1, source_target_pairs={{0,16},{16,0},{1,17},{17,1},{2,18},{18,2},{3,19},{19,3},{4,20},{20... | collective-permute-start | bytes 1179656 | tf_op jit(solution)/shard_map/ppermute | solution.py:237
  148.9 34.5 %collective-permute-start.61 = (bf16[256,384]{1,0:T(8,128)(2,1)}, bf16[256,384]{1,0:T(8,128)(2,1)}, u32[]{:S(2)}, u32[]{:S(2)}) collective-permute-start(bf16[256,384]{1,0:T(8,128)(2,1)} %get-tuple-element.155), channel_id=1, source_target_pairs={{0,16},{16,0},{1,17},{17,1},{2,18},{18,2},{3,19},{19,3},{4,20},{20... | collective-permute-start | bytes 589832 | tf_op jit(solution)/shard_map/ppermute | solution.py:237
  230.4 134.8 %collective-permute-start.51 = (bf16[256,768]{1,0:T(8,128)(2,1)}, bf16[256,768]{1,0:T(8,128)(2,1)}, u32[]{:S(2)}, u32[]{:S(2)}) collective-permute-start(bf16[256,768]{1,0:T(8,128)(2,1)} %get-tuple-element.25), channel_id=1, source_target_pairs={{0,16},{16,0},{1,17},{17,1},{2,18},{18,2},{3,19},{19,3},{4,20},{20... | collective-permute-start | bytes 1179656 | tf_op jit(solution)/shard_map/ppermute | solution.py:237
  254.3 42.6 %collective-permute-start.17 = (bf16[2,2,128,768]{3,2,1,0:T(8,128)(2,1)S(1)}, bf16[2,2,128,768]{3,2,1,0:T(8,128)(2,1)S(1)}, u32[]{:S(2)}, u32[]{:S(2)}) collective-permute-start(bf16[2,2,128,768]{3,2,1,0:T(8,128)(2,1)S(1)} %copy-done.56), channel_id=1, source_target_pairs={{0,16},{16,0},{1,17},{17,1},{2,18},{18,2},{3,19},{19,3},{4,20},{20... | collective-permute-start | bytes 2359304 | tf_op jit(solution)/shard_map/ppermute | solution.py:237
  291.6 90.0 %collective-permute-start.89 = (bf16[256,3072]{1,0:T(8,128)(2,1)}, bf16[256,3072]{1,0:T(8,128)(2,1)}, u32[]{:S(2)}, u32[]{:S(2)}) collective-permute-start(bf16[256,3072]{1,0:T(8,128)(2,1)} %get-tuple-element.186), channel_id=1, source_target_pairs={{0,16},{16,0},{1,17},{17,1},{2,18},{18,2},{3,19},{19,3},{4,20},{20... | collective-permute-start | bytes 4718600 | tf_op jit(solution)/shard_map/ppermute | solution.py:237
  316.8 46.1 %collective-permute-start.101 = (bf16[4,192,256]{2,1,0:T(8,128)(2,1)}, bf16[4,192,256]{2,1,0:T(8,128)(2,1)}, u32[]{:S(2)}, u32[]{:S(2)}) collective-permute-start(bf16[4,192,256]{2,1,0:T(8,128)(2,1)} %dynamic-slice_bitcast_fusion.8), channel_id=1, source_target_pairs={{0,2},{1,3},{2,0},{3,1},{4,6},{5,7},{6,4},{7,5},{8,10},{9,11},{10,... | collective-permute-start | bytes 1179656 | tf_op jit(solution)/shard_map/ppermute | solution.py:241
  365.2 44.3 %collective-permute-start.68 = (bf16[48,384]{1,0:T(8,128)(2,1)S(1)}, bf16[48,384]{1,0:T(8,128)(2,1)S(1)}, u32[]{:S(2)}, u32[]{:S(2)}) collective-permute-start(bf16[48,384]{1,0:T(8,128)(2,1)S(1)} %copy-done.84), channel_id=1, source_target_pairs={{0,12},{4,8},{8,4},{12,0},{1,13},{5,9},{9,5},{13,1},{2,14},{6,10},... | collective-permute-start | bytes 110600 | tf_op jit(solution)/shard_map/ppermute | solution.py:241
  375.3 35.7 %collective-permute-start.67 = (bf16[48,384]{1,0:T(8,128)(2,1)S(1)}, bf16[48,384]{1,0:T(8,128)(2,1)S(1)}, u32[]{:S(2)}, u32[]{:S(2)}) collective-permute-start(bf16[48,384]{1,0:T(8,128)(2,1)S(1)} %copy-done.83), channel_id=1, source_target_pairs={{0,8},{4,12},{8,0},{12,4},{1,9},{5,13},{9,1},{13,5},{2,10},{6,14},... | collective-permute-start | bytes 110600 | tf_op jit(solution)/shard_map/ppermute | solution.py:241
  381.7 31.3 %collective-permute-start.33 = (bf16[256,384]{1,0:T(8,128)(2,1)S(1)}, bf16[256,384]{1,0:T(8,128)(2,1)S(1)}, u32[]{:S(2)}, u32[]{:S(2)}) collective-permute-start(bf16[256,384]{1,0:T(8,128)(2,1)S(1)} %get-tuple-element.161), channel_id=1, source_target_pairs={{0,16},{16,0},{1,17},{17,1},{2,18},{18,2},{3,19},{19,3},{4,20},{20... | collective-permute-start | bytes 589832 | tf_op jit(solution)/shard_map/ppermute | solution.py:237
  415.6 68.9 %collective-permute-start.19 = (bf16[1024,768]{1,0:T(8,128)(2,1)S(1)}, bf16[1024,768]{1,0:T(8,128)(2,1)S(1)}, u32[]{:S(2)}, u32[]{:S(2)}) collective-permute-start(bf16[1024,768]{1,0:T(8,128)(2,1)S(1)} %broadcast_select_fusion.14), channel_id=1, source_target_pairs={{0,16},{16,0},{1,17},{17,1},{2,18},{18,2},{3,19},{19,3},{4,20},{20... | collective-permute-start | bytes 4718600 | tf_op jit(solution)/shard_map/ppermute | solution.py:237
  416.9 48.5 %collective-permute-start.106 = (bf16[192,384]{1,0:T(8,128)(2,1)S(1)}, bf16[192,384]{1,0:T(8,128)(2,1)S(1)}, u32[]{:S(2)}, u32[]{:S(2)}) collective-permute-start(bf16[192,384]{1,0:T(8,128)(2,1)S(1)} %get-tuple-element.132), channel_id=1, source_target_pairs={{0,12},{4,8},{8,4},{12,0},{1,13},{5,9},{9,5},{13,1},{2,14},{6,10},... | collective-permute-start | bytes 442376 | tf_op jit(solution)/shard_map/ppermute | solution.py:241
  422.0 44.6 %collective-permute-start.105 = (bf16[192,384]{1,0:T(8,128)(2,1)S(1)}, bf16[192,384]{1,0:T(8,128)(2,1)S(1)}, u32[]{:S(2)}, u32[]{:S(2)}) collective-permute-start(bf16[192,384]{1,0:T(8,128)(2,1)S(1)} %get-tuple-element.131), channel_id=1, source_target_pairs={{0,8},{4,12},{8,0},{12,4},{1,9},{5,13},{9,1},{13,5},{2,10},{6,14},... | collective-permute-start | bytes 442376 | tf_op jit(solution)/shard_map/ppermute | solution.py:241
  470.0 34.8 %collective-permute-start.87 = (bf16[48,1536]{1,0:T(8,128)(2,1)}, bf16[48,1536]{1,0:T(8,128)(2,1)}, u32[]{:S(2)}, u32[]{:S(2)}) collective-permute-start(bf16[48,1536]{1,0:T(8,128)(2,1)} %get-tuple-element.138), channel_id=1, source_target_pairs={{0,12},{4,8},{8,4},{12,0},{1,13},{5,9},{9,5},{13,1},{2,14},{6,10},... | collective-permute-start | bytes 442376 | tf_op jit(solution)/shard_map/ppermute | solution.py:241
  472.3 34.8 %collective-permute-start.86 = (bf16[48,1536]{1,0:T(8,128)(2,1)}, bf16[48,1536]{1,0:T(8,128)(2,1)}, u32[]{:S(2)}, u32[]{:S(2)}) collective-permute-start(bf16[48,1536]{1,0:T(8,128)(2,1)} %get-tuple-element.137), channel_id=1, source_target_pairs={{0,8},{4,12},{8,0},{12,4},{1,9},{5,13},{9,1},{13,5},{2,10},{6,14},... | collective-permute-start | bytes 442376 | tf_op jit(solution)/shard_map/ppermute | solution.py:241
  507.2 41.7 %collective-permute-start.49 = (bf16[48,1152]{1,0:T(8,128)(2,1)S(1)}, bf16[48,1152]{1,0:T(8,128)(2,1)S(1)}, u32[]{:S(2)}, u32[]{:S(2)}) collective-permute-start(bf16[48,1152]{1,0:T(8,128)(2,1)S(1)} %copy-done.79), channel_id=1, source_target_pairs={{0,12},{4,8},{8,4},{12,0},{1,13},{5,9},{9,5},{13,1},{2,14},{6,10},... | collective-permute-start | bytes 331784 | tf_op jit(solution)/shard_map/ppermute | solution.py:241
  509.0 42.1 %collective-permute-start.48 = (bf16[48,1152]{1,0:T(8,128)(2,1)S(1)}, bf16[48,1152]{1,0:T(8,128)(2,1)S(1)}, u32[]{:S(2)}, u32[]{:S(2)}) collective-permute-start(bf16[48,1152]{1,0:T(8,128)(2,1)S(1)} %copy-done.78), channel_id=1, source_target_pairs={{0,8},{4,12},{8,0},{12,4},{1,9},{5,13},{9,1},{13,5},{2,10},{6,14},... | collective-permute-start | bytes 331784 | tf_op jit(solution)/shard_map/ppermute | solution.py:241
  551.1 39.4 %collective-permute-start.24 = (bf16[128,768]{1,0:T(8,128)(2,1)}, bf16[128,768]{1,0:T(8,128)(2,1)S(1)}, u32[]{:S(2)}, u32[]{:S(2)}) collective-permute-start(bf16[128,768]{1,0:T(8,128)(2,1)} %get-tuple-element.167), channel_id=1, source_target_pairs={{2,3},{3,2},{0,0},{1,1},{6,7},{7,6},{4,4},{5,5},{10,11},{11,10},{8... | collective-permute-start | bytes 589832 | tf_op jit(solution)/shard_map/ppermute | solution.py:457
  552.7 37.8 %collective-permute-start.25 = (bf16[128,768]{1,0:T(8,128)(2,1)}, bf16[128,768]{1,0:T(8,128)(2,1)S(1)}, u32[]{:S(2)}, u32[]{:S(2)}) collective-permute-start(bf16[128,768]{1,0:T(8,128)(2,1)} %get-tuple-element.166), channel_id=1, source_target_pairs={{2,0},{3,1},{0,3},{1,2},{6,4},{7,5},{4,7},{5,6},{10,8},{11,9},{8,1... | collective-permute-start | bytes 589832 | tf_op jit(solution)/shard_map/ppermute | solution.py:456
  (200 other events, 2225.1 us)

commit v2 on v1

v2 whole, which is shorter than its diff:
```python
import functools

import jax
import jax.numpy as jnp
from jax import lax
from jax.experimental import pallas as pl
from jax.experimental.pallas import tpu as pltpu
from jax.sharding import PartitionSpec as P

HEADS = 12
HEAD = 64
eps = 1e-06
MASKED = -1e30
f32 = jnp.float32
bf16 = jnp.bfloat16
VMEM_BYTES = 58 * 1024 * 1024


def dense(left_side, right_side):
    return jnp.dot(left_side, right_side, preferred_element_type=f32)


def dense_tn(left_side, right_side):
    return lax.dot_general(
        left_side, right_side, (((0,), (0,)), ((), ())), preferred_element_type=f32
    )


def dense_nt(left_side, right_side):
    return lax.dot_general(
        left_side, right_side, (((1,), (1,)), ((), ())), preferred_element_type=f32
    )


GAIN_A, GAIN_B, PRE, POST = 0, 1, 8, 24
SMALL_ROWS = 40


def small_of(own, got, which):
    return lambda at, size: jnp.where(which == 0, own[at : at + size, :], got[at : at + size, :])


def rms_inverse(values):
    return lax.rsqrt(jnp.mean(values * values, axis=-1, keepdims=True) + eps)


def lane_parts(x):
    return [x[:, i : i + 128] for i in range(0, x.shape[1], 128)]


def bias_of(q_start, k_start, length, bq, bk):
    rows = q_start + lax.broadcasted_iota(jnp.int32, (bq, bk), 0)
    cols = k_start + lax.broadcasted_iota(jnp.int32, (bq, bk), 1)
    return jnp.where((cols <= rows) & (cols < length), 0.0, MASKED).astype(f32)


def attend_kernel(
    place, x_ref, small_own, small_got, joint_own, joint_got, *rest, bk, extra
):
    (
        att_ref, q_ref, own_ref, token_ref, normed_hbm, k_hbm, v_hbm, u_hbm, lse_hbm,
        joint, normed, k, v, u, lse, qp, logit, total, top, norm, sems,
    ) = rest[extra:]
    token_ref[0] = 0
    length, which = place[0], place[1]
    fetch((joint_own, joint_got), which, joint, sems.at[0])
    seq, width = x_ref.shape
    count = att_ref.shape[0]
    bq = count // 2
    small = small_of(small_own, small_got, which)
    gain, pre, post = small(GAIN_A, 1), small(PRE, HEADS), small(POST, HEADS)
    step_rows = min(256, seq)

    def normalise(i, carry):
        span = pl.ds(pl.multiple_of(i * step_rows, step_rows), step_rows)
        x = x_ref[span, :].astype(f32)
        normed[span, :] = (x * rms_inverse(x) * gain).astype(bf16)
        return carry

    lax.fori_loop(0, seq // step_rows, normalise, 0)
    for i in range(2):
        own_ref[i * bq : (i + 1) * bq, :] = normed[pl.ds(pl.multiple_of(place[2 + i], bq), bq), :]
    fetched((joint_own, joint_got), joint, sems.at[0])
    cut = width // 3
    for i in range(3):
        cols = slice(width + i * cut, width + (i + 1) * cut)
        k[:, i * cut : (i + 1) * cut] = dense(normed[...], joint[:, cols]).astype(bf16)
    for i in range(3):
        cols = slice(2 * width + i * cut, 2 * width + (i + 1) * cut)
        v[:, i * cut : (i + 1) * cut] = dense(normed[...], joint[:, cols]).astype(bf16)
    q_ref[...] = dense(own_ref[...], joint[:, :width]).astype(bf16)
    outs = [
        pltpu.make_async_copy(a, b, sems.at[1 + i])
        for i, (a, b) in enumerate(((normed, normed_hbm), (k, k_hbm), (v, v_hbm)))
    ]
    for out in outs:
        out.start()

    def rows_step(step, carry):
        q_start = place[2 + step]
        mine = pl.ds(pl.multiple_of(step * bq, bq), bq)
        q32 = q_ref[mine, :].astype(f32)
        for h in range(HEADS):
            qp[h * bq : (h + 1) * bq, :] = (q32 * pre[h : h + 1, :]).astype(bf16)
        blocks = (jnp.minimum(q_start + bq, length) + bk - 1) // bk
        top[...] = jnp.full_like(top, MASKED)
        total[...] = jnp.zeros_like(total)
        norm[...] = jnp.zeros_like(norm)

        def score(kb, c):
            bias = bias_of(q_start, kb * bk, length, bq, bk)
            tile = dense_nt(qp[...], k[pl.ds(pl.multiple_of(kb * bk, bk), bk), :])
            tile = (tile.reshape(HEADS, bq, bk) + bias[None]).reshape(HEADS * bq, bk)
            logit[kb] = tile
            top[...] = functools.reduce(jnp.maximum, lane_parts(tile), top[...])
            return c

        lax.fori_loop(0, blocks, score, 0)
        highest = jnp.max(top[...], axis=-1, keepdims=True)
        top[...] = jnp.broadcast_to(highest, top.shape)

        def apply(kb, c):
            high = top[...]
            parts = [jnp.exp(x - high) for x in lane_parts(logit[kb])]
            norm[...] = functools.reduce(jnp.add, parts, norm[...])
            e = jnp.concatenate([x.astype(bf16) for x in parts], axis=1)
            total[...] += dense(e, v[pl.ds(pl.multiple_of(kb * bk, bk), bk), :])
            return c

        lax.fori_loop(0, blocks, apply, 0)
        sums = jnp.sum(norm[...], axis=-1, keepdims=True)
        scale = 1.0 / sums
        rows = pl.ds(pl.multiple_of(step * HEADS * bq, HEADS * bq), HEADS * bq)
        lse[rows, :] = jnp.broadcast_to(highest + jnp.log(sums), top.shape)
        att = jnp.zeros((bq, width), f32)
        for g in range(HEADS):
            part = total[g * bq : (g + 1) * bq, :] * scale[g * bq : (g + 1) * bq]
            u[pl.ds(pl.multiple_of(step * HEADS * bq + g * bq, bq), bq), :] = part.astype(bf16)
            att = att + part * post[g : g + 1, :]
        att_ref[mine, :] = att.astype(bf16)
        return carry

    lax.fori_loop(0, 2, rows_step, 0)
    outs += [pltpu.make_async_copy(u, u_hbm, sems.at[4]), pltpu.make_async_copy(lse, lse_hbm, sems.at[5])]
    for out in outs[3:]:
        out.start()
    for out in outs:
        out.wait()


VMEM_SPEC = pl.BlockSpec(memory_space=pltpu.VMEM)
HBM_SPEC = pl.BlockSpec(memory_space=pl.ANY)
SMEM_SPEC = pl.BlockSpec(memory_space=pltpu.SMEM)
TOKEN = jax.ShapeDtypeStruct((1,), jnp.int32)


def attend(place, x_all, count, smalls, joints, bk, extras):
    seq, width = x_all.shape
    bq = count // 2
    shape = jax.ShapeDtypeStruct
    return pl.pallas_call(
        functools.partial(attend_kernel, bk=bk, extra=len(extras)),
        in_specs=[SMEM_SPEC] + [VMEM_SPEC] * 3 + [HBM_SPEC] * (2 + len(extras)),
        out_specs=[VMEM_SPEC] * 3 + [SMEM_SPEC] + [HBM_SPEC] * 5,
        out_shape=[shape((count, width), bf16)] * 3
        + [TOKEN]
        + [shape((seq, width), bf16)] * 3
        + [shape((HEADS * count, width), bf16), shape((HEADS * count, 128), f32)],
        scratch_shapes=[
            pltpu.VMEM((width, 3 * width), bf16),
            pltpu.VMEM((seq, width), bf16),
            pltpu.VMEM((seq, width), bf16),
            pltpu.VMEM((seq, width), bf16),
            pltpu.VMEM((HEADS * count, width), bf16),
            pltpu.VMEM((HEADS * count, 128), f32),
            pltpu.VMEM((HEADS * bq, width), bf16),
            pltpu.VMEM((seq // bk, HEADS * bq, bk), f32),
            pltpu.VMEM((HEADS * bq, width), f32),
            pltpu.VMEM((HEADS * bq, 128), f32),
            pltpu.VMEM((HEADS * bq, 128), f32),
            pltpu.SemaphoreType.DMA((6,)),
        ],
        compiler_params=pltpu.CompilerParams(vmem_limit_bytes=VMEM_BYTES),
        cost_estimate=pl.CostEstimate(
            flops=4 * HEADS * count * seq * width, bytes_accessed=30 * seq * width, transcendentals=HEADS * count * seq
        ),
    )(place, x_all, *smalls, *joints, *extras)


def feed_kernel(
    which, x_ref, att_ref, small_own, small_got,
    mixer_own, mixer_got, up_own, up_got, down_own, down_got, *rest, tile, extra,
):
    (
        out_ref, hidden_ref, two_ref, upward_hbm, active_hbm, token_ref,
        mixer, up, down, upward, active, sems,
    ) = rest[extra:]
    token_ref[0] = 0
    pairs = ((mixer_own, mixer_got), (up_own, up_got), (down_own, down_got))
    buffers = (mixer, up, down)
    for i in range(3):
        fetch(pairs[i], which[0], buffers[i], sems.at[i])
    gain = small_of(small_own, small_got, which[0])(GAIN_B, 1)
    fetched(pairs[0], mixer, sems.at[0])
    hidden = x_ref[...].astype(f32) + dense(att_ref[...], mixer[...])
    hidden_ref[...] = hidden
    two = (hidden * rms_inverse(hidden) * gain).astype(bf16)
    two_ref[...] = two
    fetched(pairs[1], up, sems.at[1])
    result, outs = hidden, []
    for j in range(down.shape[0] // tile):
        span = slice(j * tile, (j + 1) * tile)
        u = dense(two, up[:, span])
        upward[:, span] = u
        act = (0.5 * u * (1.0 + jnp.tanh(0.7978845608 * (u + 0.044715 * (u * u * u))))).astype(bf16)
        active[:, span] = act
        if j == 0:
            fetched(pairs[2], down, sems.at[2])
        result = result + dense(act, down[span, :])
    outs = [pltpu.make_async_copy(upward, upward_hbm, sems.at[3]), pltpu.make_async_copy(active, active_hbm, sems.at[4])]
    for out in outs:
        out.start()
    out_ref[...] = result.astype(bf16)
    for out in outs:
        out.wait()


def feed(which, x, attended, smalls, weights, ff, extras):
    count, width = x.shape
    shape = jax.ShapeDtypeStruct
    return pl.pallas_call(
        functools.partial(feed_kernel, tile=width, extra=len(extras)),
        in_specs=[SMEM_SPEC] + [VMEM_SPEC] * 4 + [HBM_SPEC] * (6 + len(extras)),
        out_specs=[VMEM_SPEC] * 3 + [HBM_SPEC] * 2 + [SMEM_SPEC],
        out_shape=[
            shape((count, width), bf16),
            shape((count, width), f32),
            shape((count, width), bf16),
            shape((count, ff), f32),
            shape((count, ff), bf16),
            TOKEN,
        ],
        scratch_shapes=[
            pltpu.VMEM((width, width), bf16),
            pltpu.VMEM((width, ff), bf16),
            pltpu.VMEM((ff, width), bf16),
            pltpu.VMEM((count, ff), f32),
            pltpu.VMEM((count, ff), bf16),
            pltpu.SemaphoreType.DMA((5,)),
        ],
        compiler_params=pltpu.CompilerParams(vmem_limit_bytes=VMEM_BYTES),
        cost_estimate=pl.CostEstimate(
            flops=2 * count * width * (2 * ff + width), bytes_accessed=4 * width * ff, transcendentals=count * ff
        ),
    )(which, x, attended, *smalls, *weights, *extras)


def fetch(pair, which, buffer, semaphore):
    for i, ref in enumerate(pair):

        @pl.when(which == i)
        def _(ref=ref):
            pltpu.make_async_copy(ref.at[0], buffer, semaphore).start()


def fetched(pair, buffer, semaphore):
    pltpu.make_async_copy(pair[0].at[0], buffer, semaphore).wait()


def gelu_slope(u):
    inner = 0.7978845608 * (u + 0.044715 * (u * u * u))
    t = jnp.tanh(inner)
    return 0.5 * (1.0 + t) + 0.5 * u * (1.0 - t * t) * (0.7978845608 + 0.1070322243 * (u * u))


def feed_back_kernel(
    which, dy_ref, upward_ref, hidden_ref, small_own, small_got,
    mixer_own, mixer_got, up_own, up_got, down_own, down_got, *rest, tile, extra,
):
    (
        dup_ref, dhidden_ref, low_ref, datt_ref, gain_grad_ref, token_ref,
        mixer, up, down, sems,
    ) = rest[extra:]
    token_ref[0] = 0
    pairs = ((down_own, down_got), (up_own, up_got), (mixer_own, mixer_got))
    for i, (pair, buffer) in enumerate(zip(pairs, (down, up, mixer))):
        fetch(pair, which[0], buffer, sems.at[i])
    gain = small_of(small_own, small_got, which[0])(GAIN_B, 1)
    dy = dy_ref[...]
    fetched(pairs[0], down, sems.at[0])
    grad = jnp.zeros(hidden_ref.shape, f32)
    for j in range(down.shape[0] // tile):
        span = slice(j * tile, (j + 1) * tile)
        dactive = dense_nt(dy, down[span, :])
        dup = (dactive * gelu_slope(upward_ref[:, span])).astype(bf16)
        dup_ref[:, span] = dup
        if j == 0:
            fetched(pairs[1], up, sems.at[1])
        grad = grad + dense_nt(dup, up[:, span])
    hidden = hidden_ref[...]
    inverse = rms_inverse(hidden)
    unit = hidden * inverse
    gain_grad_ref[...] = jnp.sum(grad * unit, axis=0, keepdims=True)
    scaled = grad * gain
    dhidden = dy.astype(f32) + inverse * (scaled - unit * jnp.mean(scaled * unit, axis=-1, keepdims=True))
    dhidden_ref[...] = dhidden
    low = dhidden.astype(bf16)
    low_ref[...] = low
    fetched(pairs[2], mixer, sems.at[2])
    datt_ref[...] = dense_nt(low, mixer[...]).astype(bf16)


def feed_back(which, dy, upward, hidden, smalls, weights, extras):
    count, width = dy.shape
    ff = upward.shape[1]
    shape = jax.ShapeDtypeStruct
    return pl.pallas_call(
        functools.partial(feed_back_kernel, tile=width, extra=len(extras)),
        in_specs=[SMEM_SPEC] + [VMEM_SPEC] * 5 + [HBM_SPEC] * (6 + len(extras)),
        out_specs=[VMEM_SPEC] * 5 + [SMEM_SPEC],
        out_shape=[
            shape((count, ff), bf16),
            shape((count, width), f32),
            shape((count, width), bf16),
            shape((count, width), bf16),
            shape((1, width), f32),
            TOKEN,
        ],
        scratch_shapes=[
            pltpu.VMEM((width, width), bf16),
            pltpu.VMEM((width, ff), bf16),
            pltpu.VMEM((ff, width), bf16),
            pltpu.SemaphoreType.DMA((3,)),
        ],
        compiler_params=pltpu.CompilerParams(vmem_limit_bytes=VMEM_BYTES),
        cost_estimate=pl.CostEstimate(
            flops=2 * count * width * (2 * ff + width), bytes_accessed=4 * width * ff, transcendentals=count * ff
        ),
    )(which, dy, upward, hidden, *smalls, *weights, *extras)


def attend_back_kernel(
    place, q_ref, datt_ref, u_ref, lse_ref, k_ref, v_ref, small_own, small_got, *rest, bq, bk, extra
):
    (
        dq_ref, keep_ref, send_ref, pre_grad_ref, post_grad_ref, token_ref,
        qp, dp, dk, dv, w, delta,
    ) = rest[extra:]
    token_ref[0] = 0
    step = pl.program_id(0)
    length, which, q_start = place[0], place[1], place[2 + step]
    small = small_of(small_own, small_got, which)
    pre, post = small(PRE, HEADS), small(POST, HEADS)

    @pl.when(step == 0)
    def _():
        dk[...] = jnp.zeros_like(dk)
        dv[...] = jnp.zeros_like(dv)
        pre_grad_ref[...] = jnp.zeros_like(pre_grad_ref)
        post_grad_ref[...] = jnp.zeros_like(post_grad_ref)

    q32 = q_ref[...].astype(f32)
    datt = datt_ref[...].astype(f32)
    for h in range(HEADS):
        part = slice(h * bq, (h + 1) * bq)
        qp[part, :] = (q32 * pre[h : h + 1, :]).astype(bf16)
        scaled = datt * post[h : h + 1, :]
        dp[part, :] = scaled.astype(bf16)
        u = u_ref[part, :].astype(f32)
        delta[part, :] = jnp.broadcast_to(jnp.sum(scaled * u, axis=-1, keepdims=True), (bq, 128))
        post_grad_ref[h : h + 1, :] += jnp.sum(datt * u, axis=0, keepdims=True)
    w[...] = jnp.zeros_like(w)
    blocks = (jnp.minimum(q_start + bq, length) + bk - 1) // bk

    def block(kb, c):
        span = pl.ds(pl.multiple_of(kb * bk, bk), bk)
        bias = bias_of(q_start, kb * bk, length, bq, bk)
        k_blk, v_blk = k_ref[span, :], v_ref[span, :]
        logits = dense_nt(qp[...], k_blk)
        logits = (logits.reshape(HEADS, bq, bk) + bias[None]).reshape(HEADS * bq, bk)
        grad = dense_nt(dp[...], v_blk)
        lse, spread = lse_ref[...], delta[...]
        attention, dlog = [], []
        for x, g in zip(lane_parts(logits), lane_parts(grad)):
            a = jnp.exp(x - lse)
            attention.append(a.astype(bf16))
            dlog.append((a * (g - spread)).astype(bf16))
        attention, dlog = jnp.concatenate(attention, axis=1), jnp.concatenate(dlog, axis=1)
        dv[span, :] += dense_tn(attention, dp[...])
        dk[span, :] += dense_tn(dlog, qp[...])
        w[...] += dense(dlog, k_blk)
        return c

    lax.fori_loop(0, blocks, block, 0)
    dq = jnp.zeros_like(q32)
    for h in range(HEADS):
        part = w[h * bq : (h + 1) * bq, :]
        dq = dq + part * pre[h : h + 1, :]
        pre_grad_ref[h : h + 1, :] += jnp.sum(part * q32, axis=0, keepdims=True)
    dq_ref[...] = dq.astype(bf16)

    for section, (kept, sent) in enumerate(((dk, dv), (dv, dk))):

        @pl.when((step == pl.num_programs(0) - 1) & (place[4] == section))
        def _(kept=kept, sent=sent):
            keep_ref[...] = kept[...].astype(bf16)
            send_ref[...] = sent[...].astype(bf16)


def attend_back(place, q, datt, u, lse, k, v, smalls, bk, extras):
    count, width = q.shape
    seq = k.shape[0]
    bq = count // 2
    full = lambda i, place: (0, 0)
    row = lambda i, place: (i, 0)
    shape = jax.ShapeDtypeStruct
    return pl.pallas_call(
        functools.partial(attend_back_kernel, bq=bq, bk=bk, extra=len(extras)),
        grid_spec=pltpu.PrefetchScalarGridSpec(
            num_scalar_prefetch=1,
            grid=(2,),
            in_specs=[
                pl.BlockSpec((bq, width), row),
                pl.BlockSpec((bq, width), row),
                pl.BlockSpec((HEADS * bq, width), row),
                pl.BlockSpec((HEADS * bq, 128), row),
                pl.BlockSpec((seq, width), full),
                pl.BlockSpec((seq, width), full),
                pl.BlockSpec((SMALL_ROWS, width), full),
                pl.BlockSpec((SMALL_ROWS, width), full),
            ]
            + [HBM_SPEC] * len(extras),
            out_specs=[
                pl.BlockSpec((bq, width), row),
                pl.BlockSpec((seq, width), full),
                pl.BlockSpec((seq, width), full),
                pl.BlockSpec((HEADS, width), full),
                pl.BlockSpec((HEADS, width), full),
                SMEM_SPEC,
            ],
            scratch_shapes=[
                pltpu.VMEM((HEADS * bq, width), bf16),
                pltpu.VMEM((HEADS * bq, width), bf16),
                pltpu.VMEM((seq, width), f32),
                pltpu.VMEM((seq, width), f32),
                pltpu.VMEM((HEADS * bq, width), f32),
                pltpu.VMEM((HEADS * bq, 128), f32),
            ],
        ),
        out_shape=[
            shape((count, width), bf16),
            shape((seq, width), bf16),
            shape((seq, width), bf16),
            shape((HEADS, width), f32),
            shape((HEADS, width), f32),
            TOKEN,
        ],
        compiler_params=pltpu.CompilerParams(vmem_limit_bytes=VMEM_BYTES),
        cost_estimate=pl.CostEstimate(
            flops=10 * HEADS * count * seq * width * 5 // 8,
            bytes_accessed=10 * seq * width + 2 * HEADS * count * width,
            transcendentals=HEADS * count * seq * 5 // 8,
        ),
    )(place, q, datt, u, lse, k, v, *smalls, *extras)


def swap_section(x):
    return lax.ppermute(x, "section", [(0, 1), (1, 0)])


def xor_permute(x, axis, by):
    return lax.ppermute(x, axis, [(i, i ^ by) for i in range(lax.axis_size(axis))])


def from_xor_order(x, index):
    places = range(x.shape[0])
    return jnp.concatenate([lax.dynamic_index_in_dim(x, index ^ i, 0) for i in places])


def token_kernel(*refs):
    refs[-1][0] = 0


def token_after(*arrays):
    return pl.pallas_call(
        token_kernel,
        in_specs=[HBM_SPEC] * len(arrays),
        out_specs=SMEM_SPEC,
        out_shape=TOKEN,
    )(*arrays)[0]


class Summer:
    def __init__(self, blocks, backwards):
        self.dp_count, ctx_count = blocks[0].shape[:2]
        bits = [1 << i for i in range(ctx_count.bit_length() - 1)]
        self.left = bits[::-1]
        self.order = bits[::-1] if backwards else bits
        self.parts = [x.reshape((self.dp_count,) + (2,) * len(bits) + x.shape[2:]) for x in blocks]

    def send(self, token=0):
        bit, self.order = self.order[0], self.order[1:]
        self.axis = 1 + self.left.index(bit)
        self.left = [b for b in self.left if b != bit]
        self.mine = (lax.axis_index("ctx") // bit) % 2
        at = 1 - self.mine + token
        sent = [lax.dynamic_index_in_dim(x, at, self.axis, keepdims=False) for x in self.parts]
        sent = sent[0] if len(sent) == 1 else jnp.concatenate(sent, axis=-1)
        self.got = xor_permute(sent, "ctx", bit)
        return [sent]

    def add(self, token):
        at, parts = 0, []
        for x in self.parts:
            kept = lax.dynamic_index_in_dim(x, self.mine + token, self.axis, keepdims=False)
            got = self.got[..., at : at + x.shape[-1]]
            at += x.shape[-1]
            parts.append((kept.astype(f32) + got.astype(f32)).astype(bf16))
        self.parts = parts

    def rest(self, token):
        self.add(token)
        while self.order:
            self.send()
            self.add(0)


class LastSum:
    def __init__(self, summers, rows):
        pieces = []
        for x in [x for one in summers for x in one.parts]:
            pieces += [x[:, i : i + rows] for i in range(0, x.shape[1], rows)]
        self.part = jnp.concatenate(pieces, axis=-1)

    def send(self):
        dp = lax.axis_index("dp")
        sent = [
            lax.dynamic_index_in_dim(self.part, dp ^ by, 0, keepdims=False)
            for by in range(1, self.part.shape[0])
        ]
        self.got = [xor_permute(x, "dp", by) for by, x in enumerate(sent, 1)]
        return sent

    def finish(self, token):
        total = lax.dynamic_index_in_dim(self.part, lax.axis_index("dp") + token, 0, keepdims=False)
        total = total.astype(f32)
        for got in self.got:
            total = total + got.astype(f32)
        return total


def all_sum(vector):
    for axis in ("ctx", "dp"):
        parts = [xor_permute(vector, axis, by) for by in range(1, lax.axis_size(axis))]
        for part in parts:
            vector = vector + part
    return vector


def local(
    inputs, lengths, cotangent, first_gain, joint_weight, pre_mix, post_mix,
    mixer_weight, second_gain, up_weight, down_weight,
):
    s = lax.axis_index("section")
    ctx = lax.axis_index("ctx")
    n = lax.axis_size("ctx")
    dp_count = lax.axis_size("dp")
    chips = n // 2
    micro_count, row_count, local_len, width = inputs.shape
    ff = up_weight.shape[2]
    seq = local_len * n
    blk = local_len // 2
    m = ctx // chips
    xi = ctx % chips
    core = xi * 2 + s
    zero = jnp.zeros((), jnp.int32)
    inputs = inputs.reshape(micro_count, 2, blk, width)
    cotangent = cotangent.reshape(micro_count, 2, blk, width)
    pick = lambda arr, i: lax.dynamic_index_in_dim(arr, i, 0, keepdims=False)

    spread = lambda mix: jnp.dot(mix, jnp.repeat(jnp.eye(HEADS, dtype=f32), HEAD, axis=1), precision=lax.Precision.HIGHEST)
    lines = lambda x, size: jnp.pad(x, ((0, size - x.shape[0]), (0, 0)))
    gains = jnp.concatenate([first_gain, second_gain]).astype(f32)
    small_own = jnp.concatenate(
        [lines(gains, PRE), lines(0.125 * spread(pre_mix[0].T), POST - PRE), lines(spread(post_mix[0]), SMALL_ROWS - POST)]
    )
    smalls = (small_own, swap_section(small_own))
    joints, mixers, ups, downs = (
        (w, swap_section(w)) for w in (joint_weight, mixer_weight, up_weight, down_weight)
    )

    mine = pick(inputs, m)
    pieces = []
    for d in range(1, n):
        target = m ^ (1 if d >= chips else 0)
        pieces.append(xor_permute(pick(pick(inputs, target), s), "ctx", d))
    other_pieces = [swap_section(x) for x in pieces]
    own_half = jnp.stack([pick(mine, s)] + pieces)
    other_half = jnp.stack([pick(mine, 1 - s)] + other_pieces)
    first, second = jnp.where(s == 0, own_half, other_half), jnp.where(s == 0, other_half, own_half)
    x_all = from_xor_order(jnp.stack([first, second], axis=1), ctx).reshape(seq, width)

    length = pick(lengths.reshape(-1), m)
    low_start = core * blk
    high_start = (2 * n - 1 - core) * blk
    bk = min(256, seq)
    places = [
        jnp.stack([length, (s != layer).astype(jnp.int32), low_start, high_start, s]).astype(jnp.int32)
        for layer in range(2)
    ]

    def own_rows(x):
        return jnp.concatenate(
            [
                lax.dynamic_slice_in_dim(x, low_start, blk, 0),
                lax.dynamic_slice_in_dim(x, high_start, blk, 0),
            ]
        )

    def gather_row(x):
        got = [xor_permute(x, "ctx", d) for d in range(1, chips)]
        own = jnp.stack([x] + got)
        other = jnp.stack([swap_section(y) for y in [x] + got])
        first, second = jnp.where(s == 0, own, other), jnp.where(s == 0, other, own)
        cores = from_xor_order(jnp.stack([first, second], axis=1), xi).reshape(n, 2, blk, width)
        return jnp.concatenate([cores[i, 0] for i in range(n)] + [cores[n - 1 - i, 1] for i in range(n)])

    def scatter_row(x, token):
        parts = x.astype(bf16).reshape(2 * n, blk, width)
        cores = jnp.stack([parts[i if h == 0 else 2 * n - 1 - i] for i in range(n) for h in range(2)])
        cores = cores.reshape(chips, 2, 2, blk, width)
        kept = lax.dynamic_index_in_dim(cores, s, 1, keepdims=False)
        got = swap_section(lax.dynamic_index_in_dim(cores, 1 - s, 1, keepdims=False))
        low = (kept.astype(f32) + got.astype(f32)).astype(bf16)
        total = pick(low, xi).astype(f32)
        for d in range(1, chips):
            total = total + xor_permute(pick(low, xi ^ d), "ctx", d).astype(f32)
        return total.reshape(2 * blk, width), low

    def forward(layer, x_all, x_own, extras):
        attended, q, normed_own, token, normed_all, k, v, u, lse = attend(
            places[layer], x_all, 2 * blk, smalls, joints, bk, extras[0]
        )
        weights = [x for pair in (mixers, ups, downs) for x in pair]
        out, hidden, normed_two, upward, active, token = feed(
            places[layer][1:2], x_own, attended, smalls, weights, ff, extras[1]
        )
        rows = [(x, swap_section(x)) for x in (active, normed_two, attended, normed_own)]
        return out, (q, k, v, u, lse, hidden, upward, rows, normed_all)

    def half(x, which):
        return lax.dynamic_slice_in_dim(x, which * (x.shape[1] // 2), x.shape[1] // 2, 1)

    def chip_half(x, token):
        return half(x, s + token), swap_section(half(x, 1 - s - token))

    def product(left, right):
        return (dense_tn(left[0], right[0]) + dense_tn(left[1], right[1])).astype(bf16)

    def blocks_of(grad):
        return grad.reshape(dp_count, n, grad.shape[0] // (dp_count * n), grad.shape[1])

    shard = width // (dp_count * n)

    def backward(layer, dy, x_own, kept, earlier):
        q, k, v, u, lse, hidden, upward, rows, normed_all = kept
        rows_active, rows_two, rows_attended, rows_normed = rows
        here = s == layer
        joint_w = jnp.where(here, joints[0][0], joints[1][0])
        q_w = joint_w[:, :width]
        kv_w = lax.dynamic_slice_in_dim(joint_w, width * (1 + s), width, 1)
        gain_a = jnp.where(here, smalls[0][GAIN_A], smalls[1][GAIN_A])
        down_sum = Summer([blocks_of(product(rows_active, chip_half(dy, zero)))], False)
        extras = down_sum.send() + earlier[0]()
        weights = [x for pair in (mixers, ups, downs) for x in pair]
        dup, dhidden, dhidden_low, datt, gain_b_grad, token = feed_back(
            places[layer][1:2], dy, upward, hidden, smalls, weights, extras
        )
        dup_half = chip_half(dup, zero)
        dhidden_half = chip_half(dhidden_low, zero)
        extras = earlier[1](token)
        up_sum = Summer(
            [blocks_of(product(rows_two, dup_half)), blocks_of(product(rows_attended, dhidden_half))], True
        )
        extras = extras + up_sum.send()
        dq, dkv_keep, dkv_send, pre_rows, post_rows, token = attend_back(
            places[layer], q, datt, u, lse, k, v, smalls, bk, extras
        )
        token = token_after(token, dkv_send, down_sum.got, up_sum.got, *earlier[2]())
        got = swap_section(dkv_send)
        dq_half = chip_half(dq, token)
        for one in (down_sum, up_sum):
            one.add(token)
        earlier[3](token, (down_sum, up_sum))
        dkv = (dkv_keep.astype(f32) + got.astype(f32)).astype(bf16)
        scattered, travels = scatter_row(dense_nt(dkv, kv_w), token)
        cut = 2 * width // 3
        kv_part = dense_tn(normed_all, dkv).astype(bf16)
        q_part = product(rows_normed, dq_half)
        kv_sum = Summer([blocks_of(kv_part)[..., :cut]], False)
        q_sum = Summer([blocks_of(kv_part)[..., cut:], blocks_of(q_part)], True)
        dnormed = scattered + dense_nt(dq, q_w)
        values = x_own.astype(f32)
        inverse = rms_inverse(values)
        unit = values * inverse
        gain_a_grad = jnp.sum(dnormed * unit, axis=0)
        scaled = dnormed * gain_a
        dfront = inverse * (scaled - unit * jnp.mean(scaled * unit, axis=-1, keepdims=True))
        small = (gain_a_grad, gain_b_grad.reshape(-1), pre_rows, post_rows)
        sums = (down_sum, up_sum, kv_sum, q_sum)
        return dhidden + dfront, sums, small, (scattered, travels, kv_part, q_part)

    x0_own = own_rows(x_all)
    x1_own, kept0 = forward(0, x_all, x0_own, ((), ()))
    x1_all = gather_row(x1_own)

    low_chip = ctx < chips
    there = [(i, chips + i) for i in range(chips)] + [(n - 1 - i, i) for i in range(chips)]
    here = [(n - 1 - i, chips + i) for i in range(chips)] + [(i, i) for i in range(chips)]
    first = jnp.where(low_chip, s, 1 - s) + token_after(x1_all)
    halves = lax.dynamic_index_in_dim(cotangent, first, 1, keepdims=False)
    ones, twos = jnp.where(low_chip, halves[1], halves[0]), jnp.where(low_chip, halves[0], halves[1])
    one, two = lax.ppermute(ones, "ctx", there), lax.ppermute(twos, "ctx", here)
    dy1 = jnp.concatenate([jnp.where(m == 0, two, one), jnp.where(m == 0, one, two)])
    y, kept1 = forward(1, x1_all, x1_own, ((ones, twos), (dy1,)))

    def send_home(x):
        x = x.reshape(2, blk, width)
        one = lax.ppermute(jnp.where(m == 0, x[1], x[0]), "ctx", [(b, a) for a, b in there])
        two = lax.ppermute(jnp.where(m == 0, x[0], x[1]), "ctx", [(b, a) for a, b in here])
        return jnp.where(low_chip, jnp.stack([two, one]), jnp.stack([one, two]))

    nothing = lambda *_: []
    dx1, (down1, up1, kv1, q1), small1, (arrived, *_) = backward(
        1, dy1, x1_own, kept1, (nothing, nothing, nothing, nothing)
    )
    dy0 = dx1.astype(bf16)
    arrived = token_after(arrived)
    state = {}

    def at_first():
        return down1.send(arrived) + up1.send(arrived) + kv1.send(arrived) + q1.send(arrived)

    def after_feed(token):
        token = token_after(token, down1.got, up1.got)
        for one in (down1, up1):
            one.rest(token)
        state["last1"] = LastSum([down1, up1], shard)
        return state["last1"].send()

    def after_attention():
        return [kv1.got, q1.got] + state["last1"].got

    def at_last(token, sums):
        for one in (kv1, q1):
            one.add(token)
            one.send()
        for one in sums:
            one.send()

    dx0, (down0, up0, kv0, q0), small0, (scattered, travels, kv_part, q_part) = backward(
        0, dy0, x0_own, kept0, (at_first, after_feed, after_attention, at_last)
    )
    for one in (kv0, q0):
        one.send()
    token = token_after(travels, kv_part, q_part)
    for one in (down0, up0, kv1, q1):
        one.rest(token)
    big = LastSum([down0, up0, kv1, q1], shard)
    sent = big.send()
    token = token_after(*sent)
    for one in (kv0, q0):
        one.add(token)
        one.send()
    dx_home = send_home(dx0.astype(bf16))
    y_home = send_home(y + token.astype(bf16))

    heads_of = jnp.repeat(jnp.eye(HEADS, dtype=f32), HEAD, axis=0)

    def small_sums(gain_a_grad, gain_b_grad, pre_rows, post_rows):
        per_head = lambda rows: jnp.dot(rows, heads_of, precision=lax.Precision.HIGHEST)
        pre, post = 0.125 * per_head(pre_rows).T, per_head(post_rows)
        return jnp.concatenate([gain_a_grad, gain_b_grad, pre.reshape(-1), post.reshape(-1)])

    small0, small1 = small_sums(*small0), small_sums(*small1)
    small_got = swap_section(jnp.where(s == 0, small1, small0))
    small = all_sum(jnp.where(s == 0, small0, small1) + small_got)
    for one in (kv0, q0):
        one.rest(zero)
    joint0 = LastSum([kv0, q0], shard)
    joint0.send()

    got = swap_section(jnp.where(s == 0, y_home, dx_home))
    held = jnp.where(s == 0, dx_home, y_home)
    is_first = jnp.where(low_chip, s, 1 - s) == 0
    ends = jnp.stack([jnp.where(is_first, held, got), jnp.where(is_first, got, held)], axis=1)
    ends = ends.reshape(1, micro_count, row_count, local_len, width)

    at = (lax.axis_index("dp") * n + ctx) * shard
    gain_a_out = lax.dynamic_slice_in_dim(small[:width], at, shard, 0)
    gain_b_out = lax.dynamic_slice_in_dim(small[width : 2 * width], at, shard, 0)
    pre_out = small[2 * width : 2 * width + HEADS * HEADS].reshape(1, HEADS, HEADS)
    post_out = small[2 * width + HEADS * HEADS :].reshape(1, HEADS, HEADS)

    big0_columns = state["last1"].part.shape[-1]
    big = big.finish(zero)
    big0, joint1 = big[:, :big0_columns], big[:, big0_columns:]
    pairs = ((big0, state["last1"].finish(zero)), (joint0.finish(zero), joint1))
    outs = []
    for at_zero, at_one in pairs:
        other = swap_section(jnp.where(s == 0, at_one, at_zero))
        own = jnp.where(s == 0, at_zero, at_one)
        outs.append((jnp.where(s == 0, own, other), jnp.where(s == 0, other, own)))
    (big_a, big_b), (joint_a, joint_b) = outs
    half_d, half_ff, times = width // 2, ff // 2, ff // width
    side = lambda *cuts: jnp.concatenate([x[:, at : at + size] for x, at, size in cuts], axis=1)
    down_out = jnp.concatenate([side((big_a, i * half_d, half_d), (big_b, i * half_d, half_d)) for i in range(times)])
    at = times * half_d
    up_out = side((big_a, at, half_ff), (big_b, at, half_ff))
    mixer_out = side((big_a, at + half_ff, half_d), (big_b, at + half_ff, half_d))
    joint_out = side((joint_a, width, half_d), (joint_b, width, half_d), (joint_a, 0, width), (joint_b, 0, width))
    return (
        ends,
        gain_a_out[None],
        joint_out[None],
        pre_out,
        post_out,
        mixer_out[None],
        gain_b_out[None],
        up_out[None],
        down_out[None],
    )


def solution(mesh):
    in_specs = (
        P(None, "dp", "ctx", None),
        P(None, "dp"),
        P(None, "dp", "ctx", None),
        P("section", None),
        P("section", None, None),
        P("section", None, None),
        P("section", None, None),
        P("section", None, None),
        P("section", None),
        P("section", None, None),
        P("section", None, None),
    )
    out_specs = (
        P("section", None, "dp", "ctx", None),
        P("section", ("dp", "ctx")),
        P("section", ("dp", "ctx"), None),
        P("section", None, None),
        P("section", None, None),
        P("section", ("dp", "ctx"), None),
        P("section", ("dp", "ctx")),
        P("section", ("dp", "ctx"), None),
        P("section", ("dp", "ctx"), None),
    )
    return jax.shard_map(local, mesh=mesh, in_specs=in_specs, out_specs=out_specs, check_vma=False)
```

time: 603 us -> 541 us (0.90)
  waiting for transfers between devices: 196 us -> 93.3 us
  Pallas kernels: 64 us -> 141 us
  matrix products: 92.6 us -> 45.9 us
  starting transfers between devices: 133 us -> 88.9 us
  other arithmetic: 43.2 us -> 67.1 us
  local copies, waits for them, and re-layouts: 63.6 us -> 80.8 us
  between operations: 3.57 us -> 14.7 us
    ppermute x66 -> x37, waiting for transfers between devices: 181 us -> 91.7 us  [xor_permute(): lax.ppermute(x, axis, [(i, i ^ by) for i in range(lax.axis_size(axis))])]
    pallas_call x4 -> x15, Pallas kernels: 64 us -> 141 us  [the longest x2 50 us: attend_back(): pl.pallas_call(functools.partial(attend_back_kernel, bq=bq, bk=bk, extra=...]
    ppermute x66 -> x37, starting transfers between devices: 105 us -> 58.7 us  [xor_permute(): lax.ppermute(x, axis, [(i, i ^ by) for i in range(lax.axis_size(axis))])]
    dot_general x12 -> x6, matrix products: 39.8 us -> 5.75 us  [the longest x4 5.33 us: small_sums(): jnp.dot(rows, heads_of, precision=lax.Precision.HIGHEST)]
    dot_general x10 -> x4, matrix products: 32.5 us -> 11.3 us  [dense_nt(): lax.dot_general(left_side, right_side, (((1,), (1,)), ((), ())), preferre...]
    ppermute x0 -> x6, local copies, waits for them, and re-layouts: none -> 12.7 us  [xor_permute(): lax.ppermute(x, axis, [(i, i ^ by) for i in range(lax.axis_size(axis))])]
    squeeze x27 -> x28, local copies, waits for them, and re-layouts: 4.5 us -> 16.4 us  [the longest x25 11.7 us: send(): lax.dynamic_index_in_dim(x, at, self.axis, keepdims=False)]
    unnamed x255 -> x211, local copies, waits for them, and re-layouts: 13.6 us -> 24.9 us
  transfers between devices with their start and end apart: 108 -> 77, of which waited for: 47 -> 22; matrix products, arithmetic and copies ran while one was open for 31% -> 31% of each run, Pallas kernels for 11% -> 22%
where the time goes in v2:
time: 541 us; the launch traced here: 532 us
  Pallas kernels  141 us (26%)
  waiting for transfers between devices  93.3 us (17%)
  starting transfers between devices  88.9 us (16%)
  local copies, waits for them, and re-layouts  80.8 us (15%)
  other arithmetic  67.1 us (12%)
  matrix products  45.9 us (8%)
  between operations  14.7 us (3%)
    ppermute x37, waiting for transfers between devices, xor_permute(): lax.ppermute(x, axis, [(i, i ^ by) for i in range(lax.axis_size(axis))])  91.7 us
    ppermute x37, starting transfers between devices, xor_permute(): lax.ppermute(x, axis, [(i, i ^ by) for i in range(lax.axis_size(axis))])  58.7 us
    pallas_call x2, Pallas kernels, attend_back(): pl.pallas_call(functools.partial(attend_back_kernel, bq=bq, bk=bk, extra=...  50 us
    pallas_call x2, Pallas kernels, attend(): pl.pallas_call(functools.partial(attend_kernel, bk=bk, extra=len(extras))...  41.1 us
    dot_general x18, matrix products, dense_tn(): lax.dot_general(left_side, right_side, (((0,), (0,)), ((), ())), preferre...  28.8 us
    unnamed x211, local copies, waits for them, and re-layouts  24.9 us
    pallas_call x2, Pallas kernels, feed_back(): pl.pallas_call(functools.partial(feed_back_kernel, tile=width, extra=len(...  22.2 us
    pallas_call x2, Pallas kernels, feed(): pl.pallas_call(functools.partial(feed_kernel, tile=width, extra=len(extra...  21.9 us
  transfers between devices with their start and end apart: 77, of which 22 were waited for; matrix products, arithmetic and copies ran while one was open for 31% of the time, Pallas kernels for 22%

profile of v2, /device:TPU:0, one launch (start us, length us, event | category | flops | bytes accessed | tf_op | source)
XLA Modules:
  0.0 531.5 jit_solution(3053224278833478053)
XLA Ops:
  9.3 5.9 %collective-permute-done.1 = bf16[128,768]{1,0:T(8,128)(2,1)S(1)} collective-permute-done((bf16[128,768]{1,0:T(8,128)(2,1)S(1)}, bf16[128,768]{1,0:T(8,128)(2,1)S(1)}, u32[]{:S(2)}, u32[]{:S(2)}) %collective-permute-start.1) | collective-permute-done | bytes 196640 | tf_op jit(solution)/shard_map/ppermute | solution.py:472
  17.3 4.7 collective-permute-done
  26.1 20.5 %shard_map.178 = (bf16[256,768]{1,0:T(8,128)(2,1)}, bf16[256,768]{1,0:T(8,128)(2,1)}, bf16[256,768]{1,0:T(8,128)(2,1)}, s32[1]{0:T(128)}, bf16[1024,768]{1,0:T(8...) custom-call(s32[5]{0:T(128)} %stack.143.place, ...), custom_call_target="tpu_custom_call" | custom-call | flops 9663676416 | bytes 23592960 | tf_op jit(solution)/shard_map/pallas_call | solution.py:161
  47.7 10.8 %shard_map.179 = (bf16[256,768]{1,0:T(8,128)(2,1)}, f32[256,768]{1,0:T(8,128)}, bf16[256,768]{1,0:T(8,128)(2,1)}, f32[256,3072]{1,0:T(8,128)}, bf16[256,3072]{1,0:T(8,128)(2,1)}, /*index=5*/s32[1]{0:T(128)}) custom-call(s32[1]{0:T(128)} %bitcast.which, bf16[256,768]{1,0:T(8,128)(2,1)} %pad_maximum_fusion.15.x_ref, ...), custom_call_target="tpu_custom_call" | custom-call | flops 2717908992 | bytes 9437184 | tf_op jit(solution)/shard_map/pallas_call | solution.py:231
  61.8 9.8 %collective-permute-done.11 = bf16[256,768]{1,0:T(8,128)(2,1)S(1)} collective-permute-done((bf16[256,768]{1,0:T(8,128)(2,1)}, bf16[256,768]{1,0:T(8,128)(2,1)S(1)}, u32[]{:S(2)}, u32[]{:S(2)}) %collective-permute-start.11) | collective-permute-done | bytes 393248 | tf_op jit(solution)/shard_map/ppermute | solution.py:472
  78.1 16.9 %collective-permute-start.15 = (bf16[128,768]{1,0:T(8,128)(2,1)S(1)}, bf16[128,768]{1,0:T(8,128)(2,1)S(1)}, u32[]{:S(2)}, u32[]{:S(2)}) collective-permute-start(bf16[128,768]{1,0:T(8,128)(2,1)S(1)} %get-tuple-element.153.rest_0_), channel_id=1, source_target_pairs={{0,2},{1,3},{3,0},{2,1},{4,6},{5,7},{7,4},{6,5},{8,10},{9,11},{11,... | collective-permute-start | bytes 589832 | tf_op jit(solution)/shard_map/ppermute | solution.py:723
  95.0 20.6 %shard_map.181 = (bf16[256,768]{1,0:T(8,128)(2,1)}, bf16[256,768]{1,0:T(8,128)(2,1)}, bf16[256,768]{1,0:T(8,128)(2,1)}, s32[1]{0:T(128)}, bf16[1024,768]{1,0:T(8...) custom-call(s32[5]{0:T(128)} %stack.151.place, ...), custom_call_target="tpu_custom_call" | custom-call | flops 9663676416 | bytes 23592960 | tf_op jit(solution)/shard_map/pallas_call | solution.py:161
  116.4 11.1 %shard_map.182 = (bf16[256,768]{1,0:T(8,128)(2,1)}, f32[256,768]{1,0:T(8,128)}, bf16[256,768]{1,0:T(8,128)(2,1)}, f32[256,3072]{1,0:T(8,128)}, bf16[256,3072]{1,0:T(8,128)(2,1)}, /*index=5*/s32[1]{0:T(128)}) custom-call(s32[1]{0:T(128)} %bitcast.1.which, bf16[256,768]{1,0:T(8,128)(2,1)} %get-tuple-element.59.x_ref, ...), custom_call_target="tpu_custom_call" | custom-call | flops 2717908992 | bytes 9437184 | tf_op jit(solution)/shard_map/pallas_call | solution.py:231
  129.8 5.4 %broadcast_select_fusion = (bf16[1,768,2304]{2,1,0:T(8,128)(2,1)}, bf16[1,768,2304]{2,1,0:T(8,128)(2,1)}) fusion(bf16[1,768,2304]{2,1,0:T(8,128)(2,1)S(1)} %copy-done.17, bf16[1,768,2304]{2,1,0:T(8,128)(2,1)} %collective-permute-done.7.joint_got, pred[]{:T(512)S(6)} %eq.67, pred[]{:T(512)S(6)} %eq.70), kind=kLoop, calls=%fused_computation.4 | loop fusion | flops 3538944 | bytes 14155778 | tf_op jit(solution)/shard_map/jit(_where)/select_n | solution.py:669
  138.9 10.9 %shard_map.183 = (bf16[256,3072]{1,0:T(8,128)(2,1)}, f32[256,768]{1,0:T(8,128)}, bf16[256,768]{1,0:T(8,128)(2,1)}, bf16[256,768]{1,0:T(8,128)(2,1)}, f32[1,768]{1,0:T(1,128)}, /*index=5*/s32[1]{0:T(128)}) custom-call(s32[1]{0:T(128)} %bitcast.1.which, bf16[256,768]{1,0:T(8,128)(2,1)} %pad_maximum_fusion.11.rest_0_.dy_ref, ...), custom_call_target="tpu_custom_call" | custom-call | flops 2717908992 | bytes 9437184 | tf_op jit(solution)/shard_map/pallas_call | solution.py:317
  165.8 25.1 %shard_map.184 = (bf16[256,768]{1,0:T(8,128)(2,1)}, bf16[1024,768]{1,0:T(8,128)(2,1)}, bf16[1024,768]{1,0:T(8,128)(2,1)}, f32[12,768]{1,0:T(8,128)}, f32[12,768]{1,0:T(8,128)}, /*index=5*/s32[1]{0:T(128)}) custom-call(s32[5]{0:T(128)} %stack.151.place, bf16[256,768]{1,0:T(8,128)(2,1)} %get-tuple-element.65.q_ref, ...), custom_call_target="tpu_custom_call" | custom-call | flops 15099494400 | bytes 12582912 | tf_op jit(solution)/shard_map/pallas_call | solution.py:417
  226.5 4.0 collective-permute-start.24
  233.4 6.5 %collective-permute-done.24 = bf16[2,128,768]{2,1,0:T(8,128)(2,1)S(1)} collective-permute-done((bf16[2,128,768]{2,1,0:T(8,128)(2,1)S(1)}, bf16[2,128,768]{2,1,0:T(8,128)(2,1)S(1)}, u32[]{:S(2)}, u32[]{:S(2)}) %collective-permute-start.24) | collective-permute-done | bytes 393248 | tf_op jit(solution)/shard_map/ppermute | solution.py:472
  260.1 11.3 %shard_map.187 = (bf16[256,3072]{1,0:T(8,128)(2,1)}, f32[256,768]{1,0:T(8,128)}, bf16[256,768]{1,0:T(8,128)(2,1)}, bf16[256,768]{1,0:T(8,128)(2,1)}, f32[1,768]{1,0:T(1,128)}, /*index=5*/s32[1]{0:T(128)}) custom-call(s32[1]{0:T(128)} %bitcast.which, bf16[256,768]{1,0:T(8,128)(2,1)} %copy-done.16, f32[256,3072]{1,0:T(8,128)} %get-tuple-element.77.upward_ref, ...), custom_call_target="tpu_custom_call" | custom-call | flops 2717908992 | bytes 9437184 | tf_op jit(solution)/shard_map/pallas_call | solution.py:317
  285.2 18.2 %collective-permute-done.45 = bf16[4,2,48,640]{3,2,0,1:T(8,128)(2,1)S(1)} collective-permute-done((bf16[4,2,48,640]{3,2,0,1:T(8,128)(2,1)}, bf16[4,2,48,640]{3,2,0,1:T(8,128)(2,1)S(1)}, u32[]{:S(2)}, u32[]{:S(2)}) %collective-permute-start.45) | collective-permute-done | bytes 491552 | tf_op jit(solution)/shard_map/ppermute | solution.py:472
  319.0 4.2 collective-permute-start.47
  333.2 24.9 %shard_map.189 = (bf16[256,768]{1,0:T(8,128)(2,1)}, bf16[1024,768]{1,0:T(8,128)(2,1)}, bf16[1024,768]{1,0:T(8,128)(2,1)}, f32[12,768]{1,0:T(8,128)}, f32[12,768]{1,0:T(8,128)}, /*index=5*/s32[1]{0:T(128)}) custom-call(s32[5]{0:T(128)} %stack.143.place, bf16[256,768]{1,0:T(8,128)(2,1)} %get-tuple-element.84.q_ref, ...), custom_call_target="tpu_custom_call" | custom-call | flops 15099494400 | bytes 12582912 | tf_op jit(solution)/shard_map/pallas_call | solution.py:417
  376.5 4.7 collective-permute-start.54
  408.7 10.3 %collective-permute-done.51 = bf16[4,192,384]{2,1,0:T(8,128)(2,1)} collective-permute-done((bf16[4,192,384]{2,1,0:T(8,128)(2,1)}, bf16[4,192,384]{2,1,0:T(8,128)(2,1)}, u32[]{:S(2)}, u32[]{:S(2)}) %collective-permute-start.51) | collective-permute-done | bytes 589856 | tf_op jit(solution)/shard_map/ppermute | solution.py:472
  438.6 4.0 collective-permute-start.73
  452.6 12.8 %collective-permute-done.39 = bf16[2,128,768]{2,1,0:T(8,128)(2,1)} collective-permute-done((bf16[2,128,768]{2,1,0:T(8,128)(2,1)}, bf16[2,128,768]{2,1,0:T(8,128)(2,1)}, u32[]{:S(2)}, u32[]{:S(2)}) %collective-permute-start.39) | collective-permute-done | bytes 393248 | tf_op jit(solution)/shard_map/ppermute | solution.py:472
  491.6 4.0 collective-permute-done.74
  507.5 7.1 %collective-permute-start.69 = (bf16[48,1152]{1,0:T(8,128)(2,1)S(1)}, bf16[48,1152]{1,0:T(8,128)(2,1)S(1)}, u32[]{:S(2)}, u32[]{:S(2)}) collective-permute-start(bf16[48,1152]{1,0:T(8,128)(2,1)S(1)} %get-tuple-element.169), channel_id=1, source_target_pairs={{0,4},{4,0},{8,12},{12,8},{1,5},{5,1},{9,13},{13,9},{2,6},{6,2},{1... | collective-permute-start | bytes 331784 | tf_op jit(solution)/shard_map/ppermute | solution.py:472
  518.3 7.8 %collective-permute-done.70 = bf16[48,1152]{1,0:T(8,128)(2,1)S(1)} collective-permute-done((bf16[48,1152]{1,0:T(8,128)(2,1)S(1)}, bf16[48,1152]{1,0:T(8,128)(2,1)S(1)}, u32[]{:S(2)}, u32[]{:S(2)}) %collective-permute-start.70) | collective-permute-done | bytes 110624 | tf_op jit(solution)/shard_map/ppermute | solution.py:472
  (555 shorter events, 255.3 us)
Async XLA Ops:
  0.7 46.0 %collective-permute-start.10 = (bf16[1,3072,768]{2,1,0:T(8,128)(2,1)}, bf16[1,3072,768]{2,1,0:T(8,128)(2,1)}, u32[]{:S(2)}, u32[]{:S(2)}) collective-permute-start(bf16[1,3072,768]{2,1,0:T(8,128)(2,1)} %down_own.7), channel_id=1, source_target_pairs={{0,16},{16,0},{1,17},{17,1},{2,18},{18,2},{3,19},{19,3},{4,20},{20... | collective-permute-start | bytes 14155784 | tf_op jit(solution)/shard_map/ppermute | solution.py:468
  1.2 45.5 %collective-permute-start.9 = (bf16[1,768,3072]{2,1,0:T(8,128)(2,1)}, bf16[1,768,3072]{2,1,0:T(8,128)(2,1)}, u32[]{:S(2)}, u32[]{:S(2)}) collective-permute-start(bf16[1,768,3072]{2,1,0:T(8,128)(2,1)} %up_own.7), channel_id=1, source_target_pairs={{0,16},{16,0},{1,17},{17,1},{2,18},{18,2},{3,19},{19,3},{4,20},{20... | collective-permute-start | bytes 14155784 | tf_op jit(solution)/shard_map/ppermute | solution.py:468
  77.4 38.2 %collective-permute-start.14 = (bf16[128,768]{1,0:T(8,128)(2,1)S(1)}, bf16[128,768]{1,0:T(8,128)(2,1)S(1)}, u32[]{:S(2)}, u32[]{:S(2)}) collective-permute-start(bf16[128,768]{1,0:T(8,128)(2,1)S(1)} %get-tuple-element.152.rest_1_), channel_id=1, source_target_pairs={{3,2},{2,3},{0,0},{1,1},{7,6},{6,7},{4,4},{5,5},{11,10},{10,11},{8... | collective-permute-start | bytes 589832 | tf_op jit(solution)/shard_map/ppermute | solution.py:723
  78.1 37.5 %collective-permute-start.15 = (bf16[128,768]{1,0:T(8,128)(2,1)S(1)}, bf16[128,768]{1,0:T(8,128)(2,1)S(1)}, u32[]{:S(2)}, u32[]{:S(2)}) collective-permute-start(bf16[128,768]{1,0:T(8,128)(2,1)S(1)} %get-tuple-element.153.rest_0_), channel_id=1, source_target_pairs={{0,2},{1,3},{3,0},{2,1},{4,6},{5,7},{7,4},{6,5},{8,10},{9,11},{11,... | collective-permute-start | bytes 589832 | tf_op jit(solution)/shard_map/ppermute | solution.py:723
  129.2 147.3 %collective-permute-start.35 = (bf16[256,768]{1,0:T(8,128)(2,1)}, bf16[256,768]{1,0:T(8,128)(2,1)}, u32[]{:S(2)}, u32[]{:S(2)}) collective-permute-start(bf16[256,768]{1,0:T(8,128)(2,1)} %get-tuple-element.58.att_ref), channel_id=1, source_target_pairs={{0,16},{16,0},{1,17},{17,1},{2,18},{18,2},{3,19},{19,3},{4,20},{20... | collective-permute-start | bytes 1179656 | tf_op jit(solution)/shard_map/ppermute | solution.py:468
  135.1 118.6 %collective-permute-start.25 = (bf16[256,3072]{1,0:T(8,128)(2,1)}, bf16[256,3072]{1,0:T(8,128)(2,1)}, u32[]{:S(2)}, u32[]{:S(2)}) collective-permute-start(bf16[256,3072]{1,0:T(8,128)(2,1)} %get-tuple-element.79), channel_id=1, source_target_pairs={{0,16},{16,0},{1,17},{17,1},{2,18},{18,2},{3,19},{19,3},{4,20},{20... | collective-permute-start | bytes 4718600 | tf_op jit(solution)/shard_map/ppermute | solution.py:468
  154.3 42.1 %collective-permute-start.27 = (bf16[4,2,192,384]{3,2,0,1:T(8,128)(2,1)}, bf16[4,2,192,384]{3,2,0,1:T(8,128)(2,1)}, u32[]{:S(2)}, u32[]{:S(2)}) collective-permute-start(bf16[4,2,192,384]{3,2,0,1:T(8,128)(2,1)} %copy_bitcast_fusion.7), channel_id=1, source_target_pairs={{0,1},{1,0},{2,3},{3,2},{4,5},{5,4},{6,7},{7,6},{8,9},{9,8},{10,11... | collective-permute-start | bytes 3538952 | tf_op jit(solution)/shard_map/ppermute | solution.py:472
  165.8 34.3 %collective-permute-start.28 = (bf16[4,2,48,1920]{3,2,0,1:T(8,128)(2,1)}, bf16[4,2,48,1920]{3,2,0,1:T(8,128)(2,1)}, u32[]{:S(2)}, u32[]{:S(2)}) collective-permute-start(bf16[4,2,48,1920]{3,2,0,1:T(8,128)(2,1)} %pad_maximum_fusion.2), channel_id=1, source_target_pairs={{0,2},{1,3},{2,0},{3,1},{4,6},{5,7},{6,4},{7,5},{8,10},{9,11},{10,... | collective-permute-start | bytes 4423688 | tf_op jit(solution)/shard_map/ppermute | solution.py:472
  196.4 126.7 %collective-permute-start.33 = (bf16[256,768]{1,0:T(8,128)(2,1)}, bf16[256,768]{1,0:T(8,128)(2,1)}, u32[]{:S(2)}, u32[]{:S(2)}) collective-permute-start(bf16[256,768]{1,0:T(8,128)(2,1)} %get-tuple-element.91), channel_id=1, source_target_pairs={{0,16},{16,0},{1,17},{17,1},{2,18},{18,2},{3,19},{19,3},{4,20},{20... | collective-permute-start | bytes 1179656 | tf_op jit(solution)/shard_map/ppermute | solution.py:468
  243.5 36.8 %collective-permute-start.44 = (bf16[4,2,48,512]{3,2,0,1:T(8,128)(2,1)}, bf16[4,2,48,512]{3,2,0,1:T(8,128)(2,1)}, u32[]{:S(2)}, u32[]{:S(2)}) collective-permute-start(bf16[4,2,48,512]{3,2,0,1:T(8,128)(2,1)} %copy_bitcast_fusion.11), channel_id=1, source_target_pairs={{0,1},{1,0},{2,3},{3,2},{4,5},{5,4},{6,7},{7,6},{8,9},{9,8},{10,11... | collective-permute-start | bytes 1179656 | tf_op jit(solution)/shard_map/ppermute | solution.py:472
  253.7 51.7 %collective-permute-start.32 = (bf16[4,48,1920]{2,1,0:T(8,128)(2,1)}, bf16[4,48,1920]{2,1,0:T(8,128)(2,1)}, u32[]{:S(2)}, u32[]{:S(2)}) collective-permute-start(bf16[4,48,1920]{2,1,0:T(8,128)(2,1)} %pad_maximum_fusion.9.rest_2_), channel_id=1, source_target_pairs={{0,1},{1,0},{2,3},{3,2},{4,5},{5,4},{6,7},{7,6},{8,9},{9,8},{10,11... | collective-permute-start | bytes 2211848 | tf_op jit(solution)/shard_map/ppermute | solution.py:472
  276.5 29.0 %collective-permute-start.31 = (bf16[4,192,384]{2,1,0:T(8,128)(2,1)}, bf16[4,192,384]{2,1,0:T(8,128)(2,1)S(1)}, u32[]{:S(2)}, u32[]{:S(2)}) collective-permute-start(bf16[4,192,384]{2,1,0:T(8,128)(2,1)} %dynamic-slice_bitcast_fusion.5.rest_1_), channel_id=1, source_target_pairs={{0,2},{1,3},{2,0},{3,1},{4,6},{5,7},{6,4},{7,5},{8,10},{9,11},{10,... | collective-permute-start | bytes 1769480 | tf_op jit(solution)/shard_map/ppermute | solution.py:472
  280.3 43.0 %collective-permute-start.34 = (bf16[256,1536]{1,0:T(8,128)(2,1)}, bf16[256,1536]{1,0:T(8,128)(2,1)}, u32[]{:S(2)}, u32[]{:S(2)}) collective-permute-start(bf16[256,1536]{1,0:T(8,128)(2,1)} %constant_dynamic-slice_fusion.13), channel_id=1, source_target_pairs={{0,16},{16,0},{1,17},{17,1},{2,18},{18,2},{3,19},{19,3},{4,20},{20... | collective-permute-start | bytes 2359304 | tf_op jit(solution)/shard_map/ppermute | solution.py:468
  303.4 58.8 %collective-permute-start.42 = (bf16[4,2,192,384]{3,2,0,1:T(8,128)(2,1)}, bf16[4,2,192,384]{3,2,0,1:T(8,128)(2,1)}, u32[]{:S(2)}, u32[]{:S(2)}) collective-permute-start(bf16[4,2,192,384]{3,2,0,1:T(8,128)(2,1)} %copy_bitcast_fusion.5), channel_id=1, source_target_pairs={{0,1},{1,0},{2,3},{3,2},{4,5},{5,4},{6,7},{7,6},{8,9},{9,8},{10,11... | collective-permute-start | bytes 3538952 | tf_op jit(solution)/shard_map/ppermute | solution.py:472
  319.0 49.0 %collective-permute-start.46 = (bf16[48,3456]{1,0:T(8,128)(2,1)}, bf16[48,3456]{1,0:T(8,128)(2,1)S(1)}, u32[]{:S(2)}, u32[]{:S(2)}) collective-permute-start(bf16[48,3456]{1,0:T(8,128)(2,1)} %get-tuple-element.149.rest_0_), channel_id=1, source_target_pairs={{0,4},{4,0},{8,12},{12,8},{1,5},{5,1},{9,13},{13,9},{2,6},{6,2},{1... | collective-permute-start | bytes 995336 | tf_op jit(solution)/shard_map/ppermute | solution.py:472
  319.0 49.0 %collective-permute-start.47 = (bf16[48,3456]{1,0:T(8,128)(2,1)}, bf16[48,3456]{1,0:T(8,128)(2,1)S(1)}, u32[]{:S(2)}, u32[]{:S(2)}) collective-permute-start(bf16[48,3456]{1,0:T(8,128)(2,1)} %get-tuple-element.148.rest_1_), channel_id=1, source_target_pairs={{0,8},{4,12},{8,0},{12,4},{1,9},{5,13},{9,1},{13,5},{2,10},{6,14},... | collective-permute-start | bytes 995336 | tf_op jit(solution)/shard_map/ppermute | solution.py:472
  323.1 44.9 %collective-permute-start.48 = (bf16[48,3456]{1,0:T(8,128)(2,1)}, bf16[48,3456]{1,0:T(8,128)(2,1)}, u32[]{:S(2)}, u32[]{:S(2)}) collective-permute-start(bf16[48,3456]{1,0:T(8,128)(2,1)} %get-tuple-element.147.rest_2_), channel_id=1, source_target_pairs={{0,12},{4,8},{8,4},{12,0},{1,13},{5,9},{9,5},{13,1},{2,14},{6,10},... | collective-permute-start | bytes 995336 | tf_op jit(solution)/shard_map/ppermute | solution.py:472
  332.4 33.0 %collective-permute-start.43 = (bf16[4,2,48,1920]{3,2,0,1:T(8,128)(2,1)}, bf16[4,2,48,1920]{3,2,0,1:T(8,128)(2,1)}, u32[]{:S(2)}, u32[]{:S(2)}) collective-permute-start(bf16[4,2,48,1920]{3,2,0,1:T(8,128)(2,1)} %pad_maximum_fusion.3), channel_id=1, source_target_pairs={{0,2},{1,3},{2,0},{3,1},{4,6},{5,7},{6,4},{7,5},{8,10},{9,11},{10,... | collective-permute-start | bytes 4423688 | tf_op jit(solution)/shard_map/ppermute | solution.py:472
  362.1 39.9 %collective-permute-start.49 = (bf16[256,768]{1,0:T(8,128)(2,1)}, bf16[256,768]{1,0:T(8,128)(2,1)}, u32[]{:S(2)}, u32[]{:S(2)}) collective-permute-start(bf16[256,768]{1,0:T(8,128)(2,1)} %get-tuple-element.100), channel_id=1, source_target_pairs={{0,16},{16,0},{1,17},{17,1},{2,18},{18,2},{3,19},{19,3},{4,20},{20... | collective-permute-start | bytes 1179656 | tf_op jit(solution)/shard_map/ppermute | solution.py:468
  365.4 26.6 %collective-permute-start.37 = (bf16[1024,768]{1,0:T(8,128)(2,1)}, bf16[1024,768]{1,0:T(8,128)(2,1)}, u32[]{:S(2)}, u32[]{:S(2)}) collective-permute-start(bf16[1024,768]{1,0:T(8,128)(2,1)} %get-tuple-element.95.refs_1_), channel_id=1, source_target_pairs={{0,16},{16,0},{1,17},{17,1},{2,18},{18,2},{3,19},{19,3},{4,20},{20... | collective-permute-start | bytes 4718600 | tf_op jit(solution)/shard_map/ppermute | solution.py:468
  376.5 56.4 %collective-permute-start.54 = (bf16[4,48,640]{2,1,0:T(8,128)(2,1)}, bf16[4,48,640]{2,1,0:T(8,128)(2,1)}, u32[]{:S(2)}, u32[]{:S(2)}) collective-permute-start(bf16[4,48,640]{2,1,0:T(8,128)(2,1)} %pad_maximum_fusion.16), channel_id=1, source_target_pairs={{0,1},{1,0},{2,3},{3,2},{4,5},{5,4},{6,7},{7,6},{8,9},{9,8},{10,11... | collective-permute-start | bytes 737288 | tf_op jit(solution)/shard_map/ppermute | solution.py:472
  383.8 47.4 %collective-permute-start.53 = (bf16[4,48,512]{2,1,0:T(8,128)(2,1)}, bf16[4,48,512]{2,1,0:T(8,128)(2,1)}, u32[]{:S(2)}, u32[]{:S(2)}) collective-permute-start(bf16[4,48,512]{2,1,0:T(8,128)(2,1)} %dynamic-slice_bitcast_fusion.16), channel_id=1, source_target_pairs={{0,2},{1,3},{2,0},{3,1},{4,6},{5,7},{6,4},{7,5},{8,10},{9,11},{10,... | collective-permute-start | bytes 589832 | tf_op jit(solution)/shard_map/ppermute | solution.py:472
  438.6 50.7 %collective-permute-start.72 = (bf16[48,4608]{1,0:T(8,128)(2,1)}, bf16[48,4608]{1,0:T(8,128)(2,1)}, u32[]{:S(2)}, u32[]{:S(2)}) collective-permute-start(bf16[48,4608]{1,0:T(8,128)(2,1)} %get-tuple-element.132.refs_0_), channel_id=1, source_target_pairs={{0,4},{4,0},{8,12},{12,8},{1,5},{5,1},{9,13},{13,9},{2,6},{6,2},{1... | collective-permute-start | bytes 1327112 | tf_op jit(solution)/shard_map/ppermute | solution.py:472
  438.6 53.0 %collective-permute-start.73 = (bf16[48,4608]{1,0:T(8,128)(2,1)}, bf16[48,4608]{1,0:T(8,128)(2,1)}, u32[]{:S(2)}, u32[]{:S(2)}) collective-permute-start(bf16[48,4608]{1,0:T(8,128)(2,1)} %get-tuple-element.131.refs_1_), channel_id=1, source_target_pairs={{0,8},{4,12},{8,0},{12,4},{1,9},{5,13},{9,1},{13,5},{2,10},{6,14},... | collective-permute-start | bytes 1327112 | tf_op jit(solution)/shard_map/ppermute | solution.py:472
  (144 other events, 1371.5 us)

commit v3 on v2

--- a/solution.py
+++ b/solution.py
@@ -1,4 +1,6 @@
 import functools
+import math
+import types
 
 import jax
 import jax.numpy as jnp
@@ -13,7 +15,9 @@
 MASKED = -1e30
 f32 = jnp.float32
 bf16 = jnp.bfloat16
-VMEM_BYTES = 58 * 1024 * 1024
+MIB = 1024 * 1024
+SMALL_VMEM = 36 * MIB
+BIG_VMEM = 60 * MIB
 
 
 def dense(left_side, right_side):
@@ -54,32 +58,32 @@
     return jnp.where((cols <= rows) & (cols < length), 0.0, MASKED).astype(f32)
 
 
-def attend_kernel(
-    place, x_ref, small_own, small_got, joint_own, joint_got, *rest, bk, extra
-):
+def attend_kernel(place, small_own, small_got, joint_own, joint_got, *rest, bk, count_in):
     (
-        att_ref, q_ref, own_ref, token_ref, normed_hbm, k_hbm, v_hbm, u_hbm, lse_hbm,
-        joint, normed, k, v, u, lse, qp, logit, total, top, norm, sems,
-    ) = rest[extra:]
+        att_ref, q_ref, own_ref, x_ref, token_ref, normed_hbm, k_hbm, v_hbm, u_hbm, lse_hbm,
+        joint, raw, normed, k, v, u, lse, qp, logit, total, top, norm, sems,
+    ) = rest[count_in:]
     token_ref[0] = 0
     length, which = place[0], place[1]
     fetch((joint_own, joint_got), which, joint, sems.at[0])
-    seq, width = x_ref.shape
+    seq, width = normed.shape
     count = att_ref.shape[0]
     bq = count // 2
     small = small_of(small_own, small_got, which)
     gain, pre, post = small(GAIN_A, 1), small(PRE, HEADS), small(POST, HEADS)
-    step_rows = min(256, seq)
-
-    def normalise(i, carry):
-        span = pl.ds(pl.multiple_of(i * step_rows, step_rows), step_rows)
-        x = x_ref[span, :].astype(f32)
-        normed[span, :] = (x * rms_inverse(x) * gain).astype(bf16)
-        return carry
-
-    lax.fori_loop(0, seq // step_rows, normalise, 0)
+    at = 5
+    for piece in rest[:count_in]:
+        for j in range(piece.shape[0] // bq):
+            x = piece[j * bq : (j + 1) * bq, :]
+            span = pl.ds(pl.multiple_of(place[at] * bq, bq), bq)
+            raw[span, :] = x
+            x = x.astype(f32)
+            normed[span, :] = (x * rms_inverse(x) * gain).astype(bf16)
+            at += 1
     for i in range(2):
-        own_ref[i * bq : (i + 1) * bq, :] = normed[pl.ds(pl.multiple_of(place[2 + i], bq), bq), :]
+        span = pl.ds(pl.multiple_of(place[2 + i], bq), bq)
+        own_ref[i * bq : (i + 1) * bq, :] = normed[span, :]
+        x_ref[i * bq : (i + 1) * bq, :] = raw[span, :]
     fetched((joint_own, joint_got), joint, sems.at[0])
     cut = width // 3
     for i in range(3):
@@ -149,25 +153,64 @@
 
 
 VMEM_SPEC = pl.BlockSpec(memory_space=pltpu.VMEM)
-HBM_SPEC = pl.BlockSpec(memory_space=pl.ANY)
+ANY_SPEC = pl.BlockSpec(memory_space=pl.ANY)
+HBM_SPEC = pl.BlockSpec(memory_space=pltpu.HBM)
 SMEM_SPEC = pl.BlockSpec(memory_space=pltpu.SMEM)
 TOKEN = jax.ShapeDtypeStruct((1,), jnp.int32)
 
-
-def attend(place, x_all, count, smalls, joints, bk, extras):
-    seq, width = x_all.shape
+LARGE = 64 * 1024
+SMALL_COST = pl.CostEstimate(flops=0, bytes_accessed=0, transcendentals=0)
+
+
+def in_hbm(spec, x):
+    return spec in (VMEM_SPEC, HBM_SPEC) and math.prod(x.shape) >= LARGE
+
+
+def from_hbm(spec, x):
+    return pltpu.with_memory_space_constraint(x, pltpu.HBM) if in_hbm(spec, x) else x
+
+
+def result_in_hbm(spec, x):
+    return pltpu.HBM(x.shape, x.dtype) if in_hbm(spec, x) else x
+
+
+def one_step(kernel, *, in_specs, out_specs, out_shape, **rest):
+    def whole(spec, x):
+        if spec is not VMEM_SPEC:
+            return spec
+        zeros = (0,) * len(x.shape)
+        return pl.BlockSpec(x.shape, lambda i: zeros, pipeline_mode=pl.Buffered(1))
+
+    def run(*args):
+        return pl.pallas_call(
+            kernel,
+            cost_estimate=SMALL_COST,
+            grid=(1,),
+            in_specs=[whole(*x) for x in zip(in_specs, args, strict=True)],
+            out_specs=[whole(*x) for x in zip(out_specs, out_shape, strict=True)],
+            out_shape=[result_in_hbm(*x) for x in zip(out_specs, out_shape)],
+            **rest,
+        )(*[from_hbm(*x) for x in zip(in_specs, args)])
+
+    return run
+
+
+def attend(place, pieces, count, smalls, joints, bk):
+    width = pieces[0].shape[1]
+    seq = sum(x.shape[0] for x in pieces)
     bq = count // 2
     shape = jax.ShapeDtypeStruct
-    return pl.pallas_call(
-        functools.partial(attend_kernel, bk=bk, extra=len(extras)),
-        in_specs=[SMEM_SPEC] + [VMEM_SPEC] * 3 + [HBM_SPEC] * (2 + len(extras)),
-        out_specs=[VMEM_SPEC] * 3 + [SMEM_SPEC] + [HBM_SPEC] * 5,
-        out_shape=[shape((count, width), bf16)] * 3
+    return one_step(
+        functools.partial(attend_kernel, bk=bk, count_in=len(pieces)),
+        in_specs=[SMEM_SPEC] + [VMEM_SPEC] * 2 + [HBM_SPEC] * 2 + [VMEM_SPEC] * len(pieces),
+        out_specs=[VMEM_SPEC] * 4 + [SMEM_SPEC] + [HBM_SPEC] * 5,
+        out_shape=[shape((count, width), bf16)] * 4
         + [TOKEN]
         + [shape((seq, width), bf16)] * 3
         + [shape((HEADS * count, width), bf16), shape((HEADS * count, 128), f32)],
         scratch_shapes=[
             pltpu.VMEM((width, 3 * width), bf16),
+            pltpu.VMEM((seq, width), bf16),
             pltpu.VMEM((seq, width), bf16),
             pltpu.VMEM((seq, width), bf16),
             pltpu.VMEM((seq, width), bf16),
@@ -180,11 +223,8 @@
             pltpu.VMEM((HEADS * bq, 128), f32),
             pltpu.SemaphoreType.DMA((6,)),
         ],
-        compiler_params=pltpu.CompilerParams(vmem_limit_bytes=VMEM_BYTES),
-        cost_estimate=pl.CostEstimate(
-            flops=4 * HEADS * count * seq * width, bytes_accessed=30 * seq * width, transcendentals=HEADS * count * seq
-        ),
-    )(place, x_all, *smalls, *joints, *extras)
+        compiler_params=pltpu.CompilerParams(vmem_limit_bytes=BIG_VMEM),
+    )(place, *smalls, *joints, *pieces)
 
 
 def feed_kernel(
@@ -228,7 +268,7 @@
 def feed(which, x, attended, smalls, weights, ff, extras):
     count, width = x.shape
     shape = jax.ShapeDtypeStruct
-    return pl.pallas_call(
+    return one_step(
         functools.partial(feed_kernel, tile=width, extra=len(extras)),
         in_specs=[SMEM_SPEC] + [VMEM_SPEC] * 4 + [HBM_SPEC] * (6 + len(extras)),
         out_specs=[VMEM_SPEC] * 3 + [HBM_SPEC] * 2 + [SMEM_SPEC],
@@ -248,10 +288,7 @@
             pltpu.VMEM((count, ff), bf16),
             pltpu.SemaphoreType.DMA((5,)),
         ],
-        compiler_params=pltpu.CompilerParams(vmem_limit_bytes=VMEM_BYTES),
-        cost_estimate=pl.CostEstimate(
-            flops=2 * count * width * (2 * ff + width), bytes_accessed=4 * width * ff, transcendentals=count * ff
-        ),
+        compiler_params=pltpu.CompilerParams(vmem_limit_bytes=SMALL_VMEM),
     )(which, x, attended, *smalls, *weights, *extras)
 
 
@@ -278,10 +315,20 @@
     mixer_own, mixer_got, up_own, up_got, down_own, down_got, *rest, tile, extra,
 ):
     (
-        dup_ref, dhidden_ref, low_ref, datt_ref, gain_grad_ref, token_ref,
+        keep_ref, send_ref, dhidden_ref, datt_ref, gain_grad_ref, token_ref,
         mixer, up, down, sems,
     ) = rest[extra:]
     token_ref[0] = 0
+    width = dy_ref.shape[1]
+    half_ff, half = down.shape[0] // 2, width // 2
+
+    def put(value, number, at):
+        for ref, equal in ((keep_ref, True), (send_ref, False)):
+
+            @pl.when((which[1] == number) == equal)
+            def _(ref=ref):
+                ref[:, at : at + value.shape[1]] = value
+
     pairs = ((down_own, down_got), (up_own, up_got), (mixer_own, mixer_got))
     for i, (pair, buffer) in enumerate(zip(pairs, (down, up, mixer))):
         fetch(pair, which[0], buffer, sems.at[i])
@@ -293,7 +340,7 @@
         span = slice(j * tile, (j + 1) * tile)
         dactive = dense_nt(dy, down[span, :])
         dup = (dactive * gelu_slope(upward_ref[:, span])).astype(bf16)
-        dup_ref[:, span] = dup
+        put(dup, j * tile // half_ff, j * tile % half_ff)
         if j == 0:
             fetched(pairs[1], up, sems.at[1])
         grad = grad + dense_nt(dup, up[:, span])
@@ -305,7 +352,8 @@
     dhidden = dy.astype(f32) + inverse * (scaled - unit * jnp.mean(scaled * unit, axis=-1, keepdims=True))
     dhidden_ref[...] = dhidden
     low = dhidden.astype(bf16)
-    low_ref[...] = low
+    for i in range(2):
+        put(low[:, i * half : (i + 1) * half], i, half_ff)
     fetched(pairs[2], mixer, sems.at[2])
     datt_ref[...] = dense_nt(low, mixer[...]).astype(bf16)
 
@@ -314,14 +362,14 @@
     count, width = dy.shape
     ff = upward.shape[1]
     shape = jax.ShapeDtypeStruct
-    return pl.pallas_call(
+    return one_step(
         functools.partial(feed_back_kernel, tile=width, extra=len(extras)),
         in_specs=[SMEM_SPEC] + [VMEM_SPEC] * 5 + [HBM_SPEC] * (6 + len(extras)),
         out_specs=[VMEM_SPEC] * 5 + [SMEM_SPEC],
         out_shape=[
-            shape((count, ff), bf16),
+            shape((count, (ff + width) // 2), bf16),
+            shape((count, (ff + width) // 2), bf16),
             shape((count, width), f32),
-            shape((count, width), bf16),
             shape((count, width), bf16),
             shape((1, width), f32),
             TOKEN,
@@ -332,10 +380,7 @@
             pltpu.VMEM((ff, width), bf16),
             pltpu.SemaphoreType.DMA((3,)),
         ],
-        compiler_params=pltpu.CompilerParams(vmem_limit_bytes=VMEM_BYTES),
-        cost_estimate=pl.CostEstimate(
-            flops=2 * count * width * (2 * ff + width), bytes_accessed=4 * width * ff, transcendentals=count * ff
-        ),
+        compiler_params=pltpu.CompilerParams(vmem_limit_bytes=SMALL_VMEM),
     )(which, dy, upward, hidden, *smalls, *weights, *extras)
 
 
@@ -415,7 +460,8 @@
     row = lambda i, place: (i, 0)
     shape = jax.ShapeDtypeStruct
     return pl.pallas_call(
-        functools.partial(attend_back_kernel, bq=bq, bk=bk, extra=len(extras)),
+        cost_estimate=SMALL_COST,
+        kernel=functools.partial(attend_back_kernel, bq=bq, bk=bk, extra=len(extras)),
         grid_spec=pltpu.PrefetchScalarGridSpec(
             num_scalar_prefetch=1,
             grid=(2,),
@@ -455,12 +501,7 @@
             shape((HEADS, width), f32),
             TOKEN,
         ],
-        compiler_params=pltpu.CompilerParams(vmem_limit_bytes=VMEM_BYTES),
-        cost_estimate=pl.CostEstimate(
-            flops=10 * HEADS * count * seq * width * 5 // 8,
-            bytes_accessed=10 * seq * width + 2 * HEADS * count * width,
-            transcendentals=HEADS * count * seq * 5 // 8,
-        ),
+        compiler_params=pltpu.CompilerParams(vmem_limit_bytes=BIG_VMEM),
     )(place, q, datt, u, lse, k, v, *smalls, *extras)
 
 
@@ -482,12 +523,390 @@
 
 
 def token_after(*arrays):
+    arrays = [x if x.ndim == 1 else x[(0,) * (x.ndim - 2)][:16, :128] for x in arrays]
     return pl.pallas_call(
         token_kernel,
-        in_specs=[HBM_SPEC] * len(arrays),
+        cost_estimate=SMALL_COST,
+        in_specs=[SMEM_SPEC if x.ndim == 1 else VMEM_SPEC for x in arrays],
         out_specs=SMEM_SPEC,
         out_shape=TOKEN,
     )(*arrays)[0]
+
+
+def half_columns(ref, which, size):
+    return ref[:, pl.ds(pl.multiple_of(which * size, size), size)]
+
+
+def split_blocks(blocks, kept, sent, mine):
+    for i in range(kept.shape[0]):
+        kept[i] = blocks[2 * i + mine]
+        sent[i] = blocks[2 * i + 1 - mine]
+
+
+def split_blocks_first(blocks, kept, sent, mine):
+    for i in range(kept.shape[0]):
+        at = 4 * (i // 2) + i % 2
+        kept[i] = blocks[at + 2 * mine]
+        sent[i] = blocks[at + 2 * (1 - mine)]
+
+
+def down_kernel(seat, active, active_other, dy, dy_other, kept, sent, token_ref, blocks):
+    token_ref[0] = 0
+    rows, size = blocks.shape[1:]
+    right, right_other = (half_columns(x, seat[0], size) for x in (dy, dy_other))
+    tile = dy.shape[1]
+    for j in range(active.shape[1] // tile):
+        cols = slice(j * tile, (j + 1) * tile)
+        grad = dense_tn(active[:, cols], right) + dense_tn(active_other[:, cols], right_other)
+        each = tile // rows
+        blocks[j * each : (j + 1) * each] = grad.astype(bf16).reshape(each, rows, size)
+    split_blocks(blocks, kept, sent, seat[1] % 2)
+
+
+def up_kernel(seat, two, two_other, att, att_other, right, right_other, kept, sent, token_ref, blocks):
+    token_ref[0] = 0
+    rows, size = blocks.shape[1:]
+    cut = size - att.shape[1] // 2
+    tile = cut // 2
+    for j in range(2):
+        cols = slice(j * tile, (j + 1) * tile)
+        grad = dense_tn(two[...], right[:, cols]) + dense_tn(two_other[...], right_other[:, cols])
+        blocks[:, :, cols] = grad.astype(bf16).reshape(-1, rows, tile)
+    grad = dense_tn(att[...], right[:, cut:]) + dense_tn(att_other[...], right_other[:, cut:])
+    blocks[:, :, cut:] = grad.astype(bf16).reshape(-1, rows, size - cut)
+    split_blocks_first(blocks, kept, sent, seat[1] // 2)
+
+
+def halves_of(kernel, seat, arrays, count, rows, size, flops):
+    shape = jax.ShapeDtypeStruct((count // 2, rows, size), bf16)
+    return one_step(
+        kernel,
+        in_specs=[SMEM_SPEC] + [VMEM_SPEC] * len(arrays),
+        out_specs=[VMEM_SPEC, VMEM_SPEC, SMEM_SPEC],
+        out_shape=[shape, shape, TOKEN],
+        scratch_shapes=[pltpu.VMEM((count, rows, size), bf16)],
+        compiler_params=pltpu.CompilerParams(vmem_limit_bytes=SMALL_VMEM),
+    )(seat, *arrays)
+
+
+def second_kernel(seat, token_in, *refs, bits, passing, closing):
+    count = len(bits)
+    refs = refs[passing:]
+    parts, refs = refs[2 * count : 2 * count + closing], refs[: 2 * count] + refs[2 * count + closing :]
+    refs[4 * count][0] = token_in[0]
+    if closing:
+        refs[4 * count + 1][...] = functools.reduce(jnp.add, [x[...].astype(f32) for x in parts])
+    for i, bit in enumerate(bits):
+        kept, got = refs[2 * i], refs[2 * i + 1]
+        kept_out, sent_out = refs[2 * count + 2 * i], refs[2 * count + 2 * i + 1]
+        mine = (seat[1] // bit) % 2
+        for j in range(kept_out.shape[0]):
+            for out, at in ((kept_out, 2 * j + mine), (sent_out, 2 * j + 1 - mine)):
+                out[j] = (kept[at].astype(f32) + got[at].astype(f32)).astype(bf16)
+
+
+def last_kernel(seat, token_in, *refs, count, rows, dp_count, passing):
+    refs = refs[passing:]
+    total, outs, token_ref = refs[2 * count], refs[2 * count + 1 : 2 * count + dp_count], refs[2 * count + dp_count]
+    token_ref[0] = token_in[0]
+    at = 0
+    for i in range(count):
+        kept, got = refs[2 * i], refs[2 * i + 1]
+        size = kept.shape[2]
+        for j in range(kept.shape[1] // rows):
+            part = slice(j * rows, (j + 1) * rows)
+            for by in range(len(outs) + 1):
+                z = seat[2] ^ by
+                value = kept[z, part, :].astype(f32) + got[z, part, :].astype(f32)
+                if by == 0:
+                    total[:, at : at + size] = value
+                else:
+                    outs[by - 1][:, at : at + size] = value.astype(bf16)
+            at += size
+
+
+def halved_kernel(seat, token_in, *refs, count, rows, passing):
+    refs = refs[passing:]
+    kept_out, sent_out, token_ref = refs[2 * count : 2 * count + 3]
+    token_ref[0] = token_in[0]
+    mine = seat[2] % 2
+    at = 0
+    for i in range(count):
+        kept, got = refs[2 * i], refs[2 * i + 1]
+        size = kept.shape[2]
+        for j in range(kept.shape[1] // rows):
+            part = slice(j * rows, (j + 1) * rows)
+            for b in range(2):
+                for out, z in ((kept_out, 2 * b + mine), (sent_out, 2 * b + 1 - mine)):
+                    value = kept[z, part, :].astype(f32) + got[z, part, :].astype(f32)
+                    out[b, :, at : at + size] = value.astype(bf16)
+            at += size
+
+
+def middle_kernel(seat, token_in, *refs, passing):
+    kept, got, total, sent, token_ref = refs[passing : passing + 5]
+    token_ref[0] = token_in[0]
+    mine = seat[2] // 2
+    total[...] = kept[mine].astype(f32) + got[mine].astype(f32)
+    sent[...] = (kept[1 - mine].astype(f32) + got[1 - mine].astype(f32)).astype(bf16)
+
+
+class Halved:
+    def __init__(self, kept, sent):
+        self.kept, self.got = kept, xor_permute(sent, "dp", 1)
+
+
+def halved_step(seat, token, sums, rows, passing):
+    specs_in, specs_out, shapes, aliases = handed_on(passing, 2, 3)
+    size = sum(x.kept.shape[1] // rows * x.kept.shape[2] for x in sums)
+    shape = jax.ShapeDtypeStruct((2, rows, size), bf16)
+    kept, sent, token, *passing = one_step(
+        functools.partial(halved_kernel, count=len(sums), rows=rows, passing=len(passing)),
+        in_specs=[SMEM_SPEC] * 2 + specs_in + [VMEM_SPEC] * (2 * len(sums)),
+        out_specs=[VMEM_SPEC] * 2 + [SMEM_SPEC] + specs_out,
+        out_shape=[shape, shape, TOKEN] + shapes,
+        input_output_aliases=aliases,
+        compiler_params=pltpu.CompilerParams(vmem_limit_bytes=SMALL_VMEM),
+    )(seat, token, *passing, *[y for x in sums for y in (x.kept, x.got)])
+    return Halved(kept, sent), token, tuple(passing)
+
+
+def middle_step(seat, token, halved, passing):
+    specs_in, specs_out, shapes, aliases = handed_on(passing, 2, 3)
+    shape = jax.ShapeDtypeStruct
+    total, sent, token, *passing = one_step(
+        functools.partial(middle_kernel, passing=len(passing)),
+        in_specs=[SMEM_SPEC] * 2 + specs_in + [VMEM_SPEC] * 2,
+        out_specs=[VMEM_SPEC] * 2 + [SMEM_SPEC] + specs_out,
+        out_shape=[shape(halved.kept.shape[1:], f32), shape(halved.kept.shape[1:], bf16), TOKEN] + shapes,
+        input_output_aliases=aliases,
+        compiler_params=pltpu.CompilerParams(vmem_limit_bytes=SMALL_VMEM),
+    )(seat, token, *passing, halved.kept, halved.got)
+    halved.parts = (total, xor_permute(sent, "dp", 2))
+    return token, tuple(passing)
+
+
+class FastSum:
+    def __init__(self, kept, sent, bits, token=None):
+        self.kept, self.bits, self.token = kept, bits, token
+        self.got = xor_permute(sent, "ctx", bits[0])
+
+    def start(self):
+        self.got = xor_permute(self.sent, "ctx", self.bits[1])
+
+
+def handed_on(passing, before, after):
+    specs = [ANY_SPEC] * len(passing)
+    shapes = [jax.ShapeDtypeStruct(x.shape, x.dtype) for x in passing]
+    return specs, specs, shapes, {before + i: after + i for i in range(len(passing))}
+
+
+def hand_on_kernel(token_in, *refs, meanwhile, passing):
+    refs[meanwhile + passing][0] = token_in[0]
+
+
+def hand_on(token, meanwhile, passing):
+    specs_in, specs_out, shapes, aliases = handed_on(passing, 1 + len(meanwhile), 1)
+    outs = one_step(
+        functools.partial(hand_on_kernel, meanwhile=len(meanwhile), passing=len(passing)),
+        in_specs=[SMEM_SPEC] + [VMEM_SPEC] * len(meanwhile) + specs_in,
+        out_specs=[SMEM_SPEC] + specs_out,
+        out_shape=[TOKEN] + shapes,
+        input_output_aliases=aliases,
+    )(token, *meanwhile, *passing)
+    return outs[0], outs[1:]
+
+
+def second_step(seat, token, sums, passing, closing):
+    closed = [jax.ShapeDtypeStruct(x.shape, f32) for x in closing[:1]]
+    specs_in, specs_out, shapes, aliases = handed_on(passing, 2, 2 * len(sums) + 1 + len(closed))
+    shape = lambda x: jax.ShapeDtypeStruct((x.shape[0] // 2,) + x.shape[1:], bf16)
+    outs = one_step(
+        functools.partial(second_kernel, bits=[x.bits[1] for x in sums], passing=len(passing), closing=len(closing)),
+        in_specs=[SMEM_SPEC] * 2 + specs_in + [VMEM_SPEC] * (2 * len(sums) + len(closing)),
+        out_specs=[VMEM_SPEC] * (2 * len(sums)) + [SMEM_SPEC] + [VMEM_SPEC] * len(closed) + specs_out,
+        out_shape=[shape(x.kept) for x in sums for _ in range(2)] + [TOKEN] + closed + shapes,
+        input_output_aliases=aliases,
+        compiler_params=pltpu.CompilerParams(vmem_limit_bytes=SMALL_VMEM),
+    )(seat, token, *passing, *[y for x in sums for y in (x.kept, x.got)], *closing)
+    for i, x in enumerate(sums):
+        x.kept, x.sent = outs[2 * i], outs[2 * i + 1]
+    outs = outs[2 * len(sums) :]
+    return outs[0], outs[1 + len(closed) :], outs[1] if closed else None
+
+
+def last_step(seat, token, sums, rows, passing):
+    dp_count = sums[0].kept.shape[0]
+    specs_in, specs_out, shapes, aliases = handed_on(passing, 2, dp_count + 1)
+    size = sum(x.kept.shape[1] // rows * x.kept.shape[2] for x in sums)
+    shape = jax.ShapeDtypeStruct((rows, size), bf16)
+    outs = one_step(
+        functools.partial(last_kernel, count=len(sums), rows=rows, dp_count=dp_count, passing=len(passing)),
+        in_specs=[SMEM_SPEC] * 2 + specs_in + [VMEM_SPEC] * (2 * len(sums)),
+        out_specs=[VMEM_SPEC] * dp_count + [SMEM_SPEC] + specs_out,
+        out_shape=[jax.ShapeDtypeStruct((rows, size), f32)] + [shape] * (dp_count - 1) + [TOKEN] + shapes,
+        input_output_aliases=aliases,
+        compiler_params=pltpu.CompilerParams(vmem_limit_bytes=SMALL_VMEM),
+    )(seat, token, *passing, *[y for x in sums for y in (x.kept, x.got)])
+    gots = [xor_permute(x, "dp", by) for by, x in enumerate(outs[1:dp_count], 1)]
+    return outs[0], gots, outs[dp_count], outs[dp_count + 1 :]
+
+
+def final_parts_kernel(seat, *refs, counts):
+    *refs, keep, send = refs
+    sums, at = [], 0
+    for count in counts:
+        sums.append(functools.reduce(jnp.add, [x[...].astype(f32) for x in refs[at : at + count]]))
+        at += count
+    cut = sums[0].shape[1]
+    for section in range(2):
+
+        @pl.when(seat[0] == section)
+        def _(section=section):
+            for out, layer in ((keep, section), (send, 1 - section)):
+                out[:, :cut] = sums[2 * layer]
+                out[:, cut:] = sums[2 * layer + 1]
+
+
+def final_parts(seat, groups):
+    parts = [x for group in groups for x in group]
+    rows = parts[0].shape[0]
+    out = jax.ShapeDtypeStruct((rows, groups[0][0].shape[1] + groups[1][0].shape[1]), f32)
+    return one_step(
+        functools.partial(final_parts_kernel, counts=[len(x) for x in groups]),
+        in_specs=[SMEM_SPEC] + [VMEM_SPEC] * len(parts),
+        out_specs=[VMEM_SPEC] * 2,
+        out_shape=[out, out],
+        compiler_params=pltpu.CompilerParams(vmem_limit_bytes=SMALL_VMEM),
+    )(seat, *parts)
+
+
+def final_outs_kernel(seat, keep, got, joint, mixer, up, down):
+    half, half_up, rows = mixer.shape[1] // 2, up.shape[1] // 2, mixer.shape[0]
+    width = 2 * half
+    for section in range(2):
+
+        @pl.when(seat[0] == section)
+        def _(section=section):
+            for i, ref in enumerate((keep, got) if section == 0 else (got, keep)):
+                times = down.shape[0] // rows
+                for j in range(times):
+                    down[j * rows : (j + 1) * rows, i * half : (i + 1) * half] = ref[:, j * half : (j + 1) * half]
+                at = times * half
+                up[:, i * half_up : (i + 1) * half_up] = ref[:, at : at + half_up]
+                at += half_up
+                mixer[:, i * half : (i + 1) * half] = ref[:, at : at + half]
+                at += half
+                joint[:, (1 + i) * width : (2 + i) * width] = ref[:, at : at + width]
+                joint[:, i * half : (i + 1) * half] = ref[:, at + width : at + width + half]
+
+
+def final_outs(seat, keep, got, width, ff):
+    rows = keep.shape[0]
+    shape = lambda *x: jax.ShapeDtypeStruct(x, f32)
+    return one_step(
+        final_outs_kernel,
+        in_specs=[SMEM_SPEC] + [VMEM_SPEC] * 2,
+        out_specs=[VMEM_SPEC] * 4,
+        out_shape=[shape(rows, 3 * width), shape(rows, width), shape(rows, ff), shape(rows * (ff // width), width)],
+        compiler_params=pltpu.CompilerParams(vmem_limit_bytes=SMALL_VMEM),
+    )(seat, keep, got)
+
+
+def mix_grads_kernel(small, pre, post):
+    rows = lax.broadcasted_iota(jnp.int32, (HEADS, small.shape[1]), 0)
+    cols = lax.broadcasted_iota(jnp.int32, (HEADS, small.shape[1]), 1)
+    heads = jnp.where(cols // HEAD == rows, 1.0, 0.0).astype(f32)
+    dot = lambda a, b: lax.dot_general(
+        a, b, (((1,), (1,)), ((), ())), precision=lax.Precision.HIGHEST, preferred_element_type=f32
+    )
+    pre[...] = 0.125 * dot(heads, small[2 : 2 + HEADS, :])
+    post[...] = dot(small[2 + HEADS : 2 + 2 * HEADS, :], heads)
+
+
+def mix_grads(small):
+    out = jax.ShapeDtypeStruct((HEADS, HEADS), f32)
+    return one_step(mix_grads_kernel, in_specs=[VMEM_SPEC], out_specs=[VMEM_SPEC] * 2, out_shape=[out, out])(small)
+
+
+def total_of(part, gots):
+    for got in gots:
+        part = part + got.astype(f32)
+    return part
+
+
+def join_kernel(
+    seat, token_in, keep_ref, got_ref, normed_ref, own, own_other, dq, dq_other, joint_own, joint_got,
+    small_own, small_got, dn_kept, dn_sent, dnq_ref, a_kept, a_sent, b_kept, b_sent, gain_grad_ref, token_ref,
+    kv_w, q_w, dkv, dn, a_blocks, b_blocks, sems,
+):
+    token_ref[0] = token_in[0]
+    width = dkv.shape[1]
+    section, which = seat[0], seat[3]
+    for i, ref in enumerate((joint_own, joint_got)):
+
+        @pl.when(which == i)
+        def _(ref=ref):
+            cols = pl.ds(pl.multiple_of((1 + section) * width, width), width)
+            pltpu.make_async_copy(ref.at[0, :, cols], kv_w, sems.at[0]).start()
+            pltpu.make_async_copy(ref.at[0, :, pl.ds(0, width)], q_w, sems.at[1]).start()
+
+    dkv[...] = (keep_ref[...].astype(f32) + got_ref[...].astype(f32)).astype(bf16)
+    rows, size_a, size_b = a_blocks.shape[1], a_blocks.shape[2], b_blocks.shape[2]
+    grad = dense_tn(normed_ref[...], dkv[:, :size_a])
+    a_blocks[...] = grad.astype(bf16).reshape(-1, rows, size_a)
+    grad = dense_tn(normed_ref[...], dkv[:, size_a:])
+    b_blocks[:, :, : width - size_a] = grad.astype(bf16).reshape(-1, rows, width - size_a)
+    half = width // 2
+    grad = dense_tn(own[...], half_columns(dq, section, half)) + dense_tn(
+        own_other[...], half_columns(dq_other, section, half)
+    )
+    b_blocks[:, :, width - size_a :] = grad.astype(bf16).reshape(-1, rows, half)
+    split_blocks(a_blocks, a_kept, a_sent, seat[1] % 2)
+    split_blocks_first(b_blocks, b_kept, b_sent, seat[1] // 2)
+    for i in range(2):
+        pltpu.make_async_copy(joint_own.at[0, :, pl.ds(0, width)], (kv_w, q_w)[i], sems.at[i]).wait()
+    back = dense_nt(dkv[...], kv_w[...])
+    dn[...] = back.astype(bf16)
+    back_q = dense_nt(dq[...], q_w[...])
+    dnq_ref[...] = back_q
+    gain_grad = jnp.sum(back * normed_ref[...].astype(f32), axis=0, keepdims=True)
+    gain_grad = gain_grad + jnp.sum(back_q * own[...].astype(f32), axis=0, keepdims=True)
+    gain_grad_ref[...] = gain_grad / small_of(small_own, small_got, which)(GAIN_A, 1)
+    blk = own.shape[0] // 2
+    last = dn.shape[0] // blk - 1
+    for i in range(dn_kept.shape[0] // blk):
+        for out, side in ((dn_kept, section), (dn_sent, 1 - section)):
+            core = (i // 2) * 2 + side
+            at = core if i % 2 == 0 else last - core
+            out[i * blk : (i + 1) * blk, :] = dn[pl.ds(pl.multiple_of(at * blk, blk), blk), :]
+
+
+def join(seat, token, arrays, joints, smalls, count, rows):
+    seq, width = arrays[0].shape
+    own_count = arrays[3].shape[0]
+    size_a = 2 * width // 3
+    size_b = width - size_a + width // 2
+    shape = jax.ShapeDtypeStruct
+    a_shape, b_shape = (shape((count // 2, rows, size), bf16) for size in (size_a, size_b))
+    half_rows = shape((seq // 2, width), bf16)
+    return one_step(
+        join_kernel,
+        in_specs=[SMEM_SPEC] * 2 + [VMEM_SPEC] * 7 + [HBM_SPEC] * 2 + [VMEM_SPEC] * 2,
+        out_specs=[VMEM_SPEC] * 8 + [SMEM_SPEC],
+        out_shape=[half_rows, half_rows, shape((own_count, width), f32)]
+        + [a_shape, a_shape, b_shape, b_shape, shape((1, width), f32), TOKEN],
+        scratch_shapes=[
+            pltpu.VMEM((width, width), bf16),
+            pltpu.VMEM((width, width), bf16),
+            pltpu.VMEM((seq, width), bf16),
+            pltpu.VMEM((seq, width), bf16),
+            pltpu.VMEM((count, rows, size_a), bf16),
+            pltpu.VMEM((count, rows, size_b), bf16),
+            pltpu.SemaphoreType.DMA((2,)),
+        ],
+        compiler_params=pltpu.CompilerParams(vmem_limit_bytes=SMALL_VMEM),
+    )(seat, token, *arrays, *joints, *smalls)
 
 
 class Summer:
@@ -541,20 +960,17 @@
         self.got = [xor_permute(x, "dp", by) for by, x in enumerate(sent, 1)]
         return sent
 
-    def finish(self, token):
-        total = lax.dynamic_index_in_dim(self.part, lax.axis_index("dp") + token, 0, keepdims=False)
-        total = total.astype(f32)
-        for got in self.got:
-            total = total + got.astype(f32)
-        return total
-
-
-def all_sum(vector):
-    for axis in ("ctx", "dp"):
-        parts = [xor_permute(vector, axis, by) for by in range(1, lax.axis_size(axis))]
-        for part in parts:
-            vector = vector + part
-    return vector
+    @property
+    def total(self):
+        return lax.dynamic_index_in_dim(self.part, lax.axis_index("dp"), 0, keepdims=False).astype(f32)
+
+
+def all_sum(x, tokens):
+    steps = [(axis, 1 << i) for axis in ("ctx", "dp") for i in range(lax.axis_size(axis).bit_length() - 1)]
+    for i, (axis, bit) in enumerate(steps):
+        got = xor_permute(x, axis, bit)
+        x = x + tokens[min(i, len(tokens) - 1)].astype(f32) + got
+    return x
 
 
 def local(
@@ -594,11 +1010,10 @@
     for d in range(1, n):
         target = m ^ (1 if d >= chips else 0)
         pieces.append(xor_permute(pick(pick(inputs, target), s), "ctx", d))
-    other_pieces = [swap_section(x) for x in pieces]
-    own_half = jnp.stack([pick(mine, s)] + pieces)
-    other_half = jnp.stack([pick(mine, 1 - s)] + other_pieces)
-    first, second = jnp.where(s == 0, own_half, other_half), jnp.where(s == 0, other_half, own_half)
-    x_all = from_xor_order(jnp.stack([first, second], axis=1), ctx).reshape(seq, width)
+    other_pieces = [swap_section(jnp.concatenate(pieces))]
+    chip_of = [ctx ^ d for d in range(1, n)]
+    blocks0 = [2 * ctx, 2 * ctx + 1] + [2 * c + s for c in chip_of] + [2 * c + 1 - s for c in chip_of]
+    pieces0 = [mine.reshape(2 * blk, width)] + pieces + other_pieces
 
     length = pick(lengths.reshape(-1), m)
     low_start = core * blk
@@ -609,51 +1024,26 @@
         for layer in range(2)
     ]
 
-    def own_rows(x):
-        return jnp.concatenate(
-            [
-                lax.dynamic_slice_in_dim(x, low_start, blk, 0),
-                lax.dynamic_slice_in_dim(x, high_start, blk, 0),
-            ]
-        )
-
     def gather_row(x):
-        got = [xor_permute(x, "ctx", d) for d in range(1, chips)]
-        own = jnp.stack([x] + got)
-        other = jnp.stack([swap_section(y) for y in [x] + got])
-        first, second = jnp.where(s == 0, own, other), jnp.where(s == 0, other, own)
-        cores = from_xor_order(jnp.stack([first, second], axis=1), xi).reshape(n, 2, blk, width)
-        return jnp.concatenate([cores[i, 0] for i in range(n)] + [cores[n - 1 - i, 1] for i in range(n)])
-
-    def scatter_row(x, token):
-        parts = x.astype(bf16).reshape(2 * n, blk, width)
-        cores = jnp.stack([parts[i if h == 0 else 2 * n - 1 - i] for i in range(n) for h in range(2)])
-        cores = cores.reshape(chips, 2, 2, blk, width)
-        kept = lax.dynamic_index_in_dim(cores, s, 1, keepdims=False)
-        got = swap_section(lax.dynamic_index_in_dim(cores, 1 - s, 1, keepdims=False))
-        low = (kept.astype(f32) + got.astype(f32)).astype(bf16)
-        total = pick(low, xi).astype(f32)
-        for d in range(1, chips):
-            total = total + xor_permute(pick(low, xi ^ d), "ctx", d).astype(f32)
-        return total.reshape(2 * blk, width), low
-
-    def forward(layer, x_all, x_own, extras):
-        attended, q, normed_own, token, normed_all, k, v, u, lse = attend(
-            places[layer], x_all, 2 * blk, smalls, joints, bk, extras[0]
+        got = [x] + [xor_permute(x, "ctx", d) for d in range(1, chips)]
+        cores = [(xi ^ d) * 2 + side for side in (s, 1 - s) for d in range(chips)]
+        return got + [swap_section(y) for y in got], [b for c in cores for b in (c, 2 * n - 1 - c)]
+
+    def forward(layer, pieces, blocks, meanwhile):
+        place = jnp.concatenate([places[layer], jnp.stack(blocks).astype(jnp.int32)])
+        attended, q, normed_own, x_own, token, normed_all, k, v, u, lse = attend(
+            place, pieces, 2 * blk, smalls, joints, bk
         )
         weights = [x for pair in (mixers, ups, downs) for x in pair]
         out, hidden, normed_two, upward, active, token = feed(
-            places[layer][1:2], x_own, attended, smalls, weights, ff, extras[1]
+            places[layer][1:2], x_own, attended, smalls, weights, ff, meanwhile
         )
         rows = [(x, swap_section(x)) for x in (active, normed_two, attended, normed_own)]
-        return out, (q, k, v, u, lse, hidden, upward, rows, normed_all)
+        return out, (x_own, q, k, v, u, lse, hidden, upward, rows, normed_all)
 
     def half(x, which):
         return lax.dynamic_slice_in_dim(x, which * (x.shape[1] // 2), x.shape[1] // 2, 1)
 
-    def chip_half(x, token):
-        return half(x, s + token), swap_section(half(x, 1 - s - token))
-
     def product(left, right):
         return (dense_tn(left[0], right[0]) + dense_tn(left[1], right[1])).astype(bf16)
 
@@ -662,133 +1052,216 @@
 
     shard = width // (dp_count * n)
 
-    def backward(layer, dy, x_own, kept, earlier):
-        q, k, v, u, lse, hidden, upward, rows, normed_all = kept
+    fast = n == 4 and dp_count == 4 and shard % 16 == 0
+    count = dp_count * n
+    seats = [jnp.stack([s, ctx, lax.axis_index("dp"), s != layer]).astype(jnp.int32) for layer in range(2)]
+
+    class Slow:
+        def first(left, right, backwards):
+            one = Summer([blocks_of(product(a, b)) for a, b in zip(left, right)], backwards)
+            one.token = token_after(*one.send()).reshape(1)
+            return one
+
+        def second(token, sums, passing=(), closing=()):
+            for one in sums:
+                one.add(token[0])
+            return token, passing, total_of(closing[0], closing[1:]) if closing else None
+
+        def last(token, sums, passing=()):
+            for one in sums:
+                one.rest(token[0])
+            one = LastSum(sums, shard)
+            one.send()
+            one.parts = (one.total, *one.got)
+            return one, token, passing
+
+        halved = last
+
+        def middle(token, one, passing=()):
+            return token, passing
+
+    class Fast:
+        def first(left, right, backwards):
+            flat = [x for pair in left for x in pair]
+            if backwards:
+                arrays, size, rows = flat + list(right), (ff + width) // 2, shard
+            else:
+                arrays, size, rows = flat + list(right), width // 2, ff // count
+            flops = 4 * flat[0].shape[0] * rows * count * size
+            kernel = up_kernel if backwards else down_kernel
+            kept, sent, token = halves_of(kernel, seats[0], arrays, count, rows, size, flops)
+            return FastSum(kept, sent, (2, 1) if backwards else (1, 2), token)
+
+        def second(token, sums, passing=(), closing=()):
+            return second_step(seats[0], token, sums, passing, closing)
+
+        def last(token, sums, passing=()):
+            part, gots, token, passing = last_step(seats[0], token, sums, shard, passing)
+            one = types.SimpleNamespace(parts=(part, *gots))
+            return one, token, passing
+
+        def halved(token, sums, passing=()):
+            return halved_step(seats[0], token, sums, shard, passing)
+
+        def middle(token, one, passing=()):
+            return middle_step(seats[0], token, one, passing)
+
+    steps = Fast if fast else Slow
+
+    def backward(layer, dy, kept, earlier):
+        x_own, q, k, v, u, lse, hidden, upward, rows, normed_all = kept
         rows_active, rows_two, rows_attended, rows_normed = rows
         here = s == layer
-        joint_w = jnp.where(here, joints[0][0], joints[1][0])
-        q_w = joint_w[:, :width]
-        kv_w = lax.dynamic_slice_in_dim(joint_w, width * (1 + s), width, 1)
         gain_a = jnp.where(here, smalls[0][GAIN_A], smalls[1][GAIN_A])
-        down_sum = Summer([blocks_of(product(rows_active, chip_half(dy, zero)))], False)
-        extras = down_sum.send() + earlier[0]()
+        dy_other = swap_section(dy)
+        if fast:
+            down_sum = steps.first([rows_active], (dy, dy_other), False)
+        else:
+            down_sum = steps.first([rows_active], [(half(dy, s), half(dy_other, s))], False)
+        earlier[0]()
         weights = [x for pair in (mixers, ups, downs) for x in pair]
-        dup, dhidden, dhidden_low, datt, gain_b_grad, token = feed_back(
-            places[layer][1:2], dy, upward, hidden, smalls, weights, extras
+        keep, send, dhidden, datt, gain_b_grad, token = feed_back(
+            jnp.stack([s != layer, s]).astype(jnp.int32), dy, upward, hidden, smalls, weights, (down_sum.token,)
         )
-        dup_half = chip_half(dup, zero)
-        dhidden_half = chip_half(dhidden_low, zero)
-        extras = earlier[1](token)
-        up_sum = Summer(
-            [blocks_of(product(rows_two, dup_half)), blocks_of(product(rows_attended, dhidden_half))], True
+        token, (send,) = earlier[1](token, (send,))
+        other = swap_section(send)
+        if fast:
+            up_sum = steps.first([rows_two, rows_attended], (keep, other), True)
+        else:
+            cut = ff // 2
+            pairs = [(keep[:, :cut], other[:, :cut]), (keep[:, cut:], other[:, cut:])]
+            up_sum = steps.first([rows_two, rows_attended], pairs, True)
+        dq, dkv_keep, dkv_send, pre_rows, post_rows, token = attend_back(
+            places[layer], q, datt, u, lse, k, v, smalls, bk, (token, up_sum.token)
         )
-        extras = extras + up_sum.send()
-        dq, dkv_keep, dkv_send, pre_rows, post_rows, token = attend_back(
-            places[layer], q, datt, u, lse, k, v, smalls, bk, extras
-        )
-        token = token_after(token, dkv_send, down_sum.got, up_sum.got, *earlier[2]())
-        got = swap_section(dkv_send)
-        dq_half = chip_half(dq, token)
-        for one in (down_sum, up_sum):
-            one.add(token)
-        earlier[3](token, (down_sum, up_sum))
-        dkv = (dkv_keep.astype(f32) + got.astype(f32)).astype(bf16)
-        scattered, travels = scatter_row(dense_nt(dkv, kv_w), token)
-        cut = 2 * width // 3
-        kv_part = dense_tn(normed_all, dkv).astype(bf16)
-        q_part = product(rows_normed, dq_half)
-        kv_sum = Summer([blocks_of(kv_part)[..., :cut]], False)
-        q_sum = Summer([blocks_of(kv_part)[..., cut:], blocks_of(q_part)], True)
-        dnormed = scattered + dense_nt(dq, q_w)
+        token, (dkv_send, dq) = earlier[2](token, (down_sum, up_sum), (dkv_send, dq))
+        got, dq_other = swap_section(dkv_send), swap_section(dq)
+        if fast:
+            dn_kept, dn_sent, dnq, a_kept, a_sent, b_kept, b_sent, gain_a_grad, token = join(
+                seats[layer], token, (dkv_keep, got, normed_all, *rows_normed, dq, dq_other), joints, smalls, count, shard
+            )
+            kv_sum, q_sum = FastSum(a_kept, a_sent, (1, 2)), FastSum(b_kept, b_sent, (2, 1))
+            dn_kept, dn_sent = (x.reshape(chips, 2, blk, width) for x in (dn_kept, dn_sent))
+        else:
+            joint_w = jnp.where(here, joints[0][0], joints[1][0])
+            kv_w = lax.dynamic_slice_in_dim(joint_w, width * (1 + s), width, 1)
+            dkv = (dkv_keep.astype(f32) + got.astype(f32)).astype(bf16)
+            dn = dense_nt(dkv, kv_w)
+            gain_a_grad = jnp.sum(dn * normed_all.astype(f32), axis=0)
+            dn = dn.astype(bf16).reshape(2 * n, blk, width)
+            dn = jnp.stack([dn[i if h == 0 else 2 * n - 1 - i] for i in range(n) for h in range(2)])
+            dn = dn.reshape(chips, 2, 2, blk, width)
+            dn_kept = lax.dynamic_index_in_dim(dn, s, 1, keepdims=False)
+            dn_sent = lax.dynamic_index_in_dim(dn, 1 - s, 1, keepdims=False)
+            dnq = dense_nt(dq, joint_w[:, :width])
+            gain_a_grad = (gain_a_grad + jnp.sum(dnq * rows_normed[0].astype(f32), axis=0)) / gain_a
+            kv_part = blocks_of(dense_tn(normed_all, dkv).astype(bf16))
+            q_part = blocks_of(product(rows_normed, (half(dq, s), half(dq_other, s))))
+            cut = 2 * width // 3
+            kv_sum = Summer([kv_part[..., :cut]], False)
+            q_sum = Summer([kv_part[..., cut:], q_part], True)
+            kv_sum.send()
+            q_sum.send()
+        token, (dn_sent,) = earlier[3](token, (dn_sent,), (down_sum, up_sum))
+        low = (dn_kept.astype(f32) + swap_section(dn_sent).astype(f32)).astype(bf16)
+        gots = [xor_permute(pick(low, xi ^ d), "ctx", d) for d in range(1, chips)]
+        sums = (down_sum, up_sum, kv_sum, q_sum)
+        token = earlier[4](token, low, sums)
+        scattered = pick(low, xi + token[0]).astype(f32)
+        for x in gots:
+            scattered = scattered + x.astype(f32)
+        scaled = (scattered.reshape(2 * blk, width) + dnq) * gain_a
         values = x_own.astype(f32)
         inverse = rms_inverse(values)
         unit = values * inverse
-        gain_a_grad = jnp.sum(dnormed * unit, axis=0)
-        scaled = dnormed * gain_a
         dfront = inverse * (scaled - unit * jnp.mean(scaled * unit, axis=-1, keepdims=True))
-        small = (gain_a_grad, gain_b_grad.reshape(-1), pre_rows, post_rows)
-        sums = (down_sum, up_sum, kv_sum, q_sum)
-        return dhidden + dfront, sums, small, (scattered, travels, kv_part, q_part)
-
-    x0_own = own_rows(x_all)
-    x1_own, kept0 = forward(0, x_all, x0_own, ((), ()))
-    x1_all = gather_row(x1_own)
+        small = jnp.concatenate([gain_a_grad.reshape(1, -1), gain_b_grad.reshape(1, -1), pre_rows, post_rows])
+        return dhidden + dfront, sums, small, token
 
     low_chip = ctx < chips
     there = [(i, chips + i) for i in range(chips)] + [(n - 1 - i, i) for i in range(chips)]
     here = [(n - 1 - i, chips + i) for i in range(chips)] + [(i, i) for i in range(chips)]
-    first = jnp.where(low_chip, s, 1 - s) + token_after(x1_all)
+    first = jnp.where(low_chip, s, 1 - s)
     halves = lax.dynamic_index_in_dim(cotangent, first, 1, keepdims=False)
     ones, twos = jnp.where(low_chip, halves[1], halves[0]), jnp.where(low_chip, halves[0], halves[1])
     one, two = lax.ppermute(ones, "ctx", there), lax.ppermute(twos, "ctx", here)
     dy1 = jnp.concatenate([jnp.where(m == 0, two, one), jnp.where(m == 0, one, two)])
-    y, kept1 = forward(1, x1_all, x1_own, ((ones, twos), (dy1,)))
+    x1, kept0 = forward(0, pieces0, blocks0, (one, two))
+    y, kept1 = forward(1, *gather_row(x1), ())
 
     def send_home(x):
         x = x.reshape(2, blk, width)
         one = lax.ppermute(jnp.where(m == 0, x[1], x[0]), "ctx", [(b, a) for a, b in there])
         two = lax.ppermute(jnp.where(m == 0, x[0], x[1]), "ctx", [(b, a) for a, b in here])
+        return one, two
+
+    def at_home(one, two):
         return jnp.where(low_chip, jnp.stack([two, one]), jnp.stack([one, two]))
 
-    nothing = lambda *_: []
-    dx1, (down1, up1, kv1, q1), small1, (arrived, *_) = backward(
-        1, dy1, x1_own, kept1, (nothing, nothing, nothing, nothing)
+    def start(sums):
+        for one in sums:
+            one.start() if fast else one.send()
+
+    def no_step():
+        return None
+
+    state = {}
+
+    def after_attention(token, sums, passing):
+        token, passing, _ = steps.second(token, sums, passing)
+        start(sums)
+        return token, passing
+
+    def after_join(token, passing, sums):
+        state["big"], token, passing = steps.halved(token, sums, passing)
+        return token, passing
+
+    def after_low(token, low, sums):
+        token = token_after(token, low).reshape(1)
+        token, _, _ = steps.second(token, sums[2:])
+        start(sums[2:])
+        return token
+
+    first_steps = (no_step, lambda token, passing: (token, passing), after_attention, after_join, after_low)
+    dx1, (_, _, kv1, q1), small1, _ = backward(1, dy1, kept1, first_steps)
+    dy0 = dx1.astype(bf16)
+    y_sent = send_home(y)
+
+    def after_feed(token, passing):
+        state["joint1"], token, passing = steps.halved(token, [kv1, q1], (*passing, *y_sent))
+        token, (passing, *state["y"]) = steps.middle(token, state["big"], passing)
+        return token, (passing,)
+
+    def after_attention(token, sums, passing):
+        token, passing, state["big1"] = steps.second(token, sums, passing, state["big"].parts)
+        start(sums)
+        token, passing = steps.middle(token, state["joint1"], passing)
+        return token, passing
+
+    def after_join(token, passing, sums):
+        state["big0"], token, passing = steps.halved(token, sums, passing)
+        state["token"] = token
+        return token, passing
+
+    def after_low(token, low, sums):
+        token = token_after(token, low).reshape(1)
+        token, _, _ = steps.second(token, sums[2:])
+        start(sums[2:])
+        return steps.middle(token, state["big0"])[0]
+
+    dx0, (down0, up0, kv0, q0), small0, token = backward(
+        0, dy0, kept0, (no_step, after_feed, after_attention, after_join, after_low)
     )
-    dy0 = dx1.astype(bf16)
-    arrived = token_after(arrived)
-    state = {}
-
-    def at_first():
-        return down1.send(arrived) + up1.send(arrived) + kv1.send(arrived) + q1.send(arrived)
-
-    def after_feed(token):
-        token = token_after(token, down1.got, up1.got)
-        for one in (down1, up1):
-            one.rest(token)
-        state["last1"] = LastSum([down1, up1], shard)
-        return state["last1"].send()
-
-    def after_attention():
-        return [kv1.got, q1.got] + state["last1"].got
-
-    def at_last(token, sums):
-        for one in (kv1, q1):
-            one.add(token)
-            one.send()
-        for one in sums:
-            one.send()
-
-    dx0, (down0, up0, kv0, q0), small0, (scattered, travels, kv_part, q_part) = backward(
-        0, dy0, x0_own, kept0, (at_first, after_feed, after_attention, at_last)
-    )
-    for one in (kv0, q0):
-        one.send()
-    token = token_after(travels, kv_part, q_part)
-    for one in (down0, up0, kv1, q1):
-        one.rest(token)
-    big = LastSum([down0, up0, kv1, q1], shard)
-    sent = big.send()
-    token = token_after(*sent)
-    for one in (kv0, q0):
-        one.add(token)
-        one.send()
-    dx_home = send_home(dx0.astype(bf16))
-    y_home = send_home(y + token.astype(bf16))
-
-    heads_of = jnp.repeat(jnp.eye(HEADS, dtype=f32), HEAD, axis=0)
-
-    def small_sums(gain_a_grad, gain_b_grad, pre_rows, post_rows):
-        per_head = lambda rows: jnp.dot(rows, heads_of, precision=lax.Precision.HIGHEST)
-        pre, post = 0.125 * per_head(pre_rows).T, per_head(post_rows)
-        return jnp.concatenate([gain_a_grad, gain_b_grad, pre.reshape(-1), post.reshape(-1)])
-
-    small0, small1 = small_sums(*small0), small_sums(*small1)
+    early = token
+    dx0 = dx0.astype(bf16)
+    dx_home = at_home(*send_home(dx0))
+    y_home = at_home(*state["y"])
+    token = token_after(dx0).reshape(1)
+
     small_got = swap_section(jnp.where(s == 0, small1, small0))
-    small = all_sum(jnp.where(s == 0, small0, small1) + small_got)
-    for one in (kv0, q0):
-        one.rest(zero)
-    joint0 = LastSum([kv0, q0], shard)
-    joint0.send()
+    small = jnp.where(s == 0, small0, small1) + small_got
+    joint0, last_token, _ = steps.last(token, [kv0, q0])
+    small = all_sum(small, (state["token"][0], early[0], token[0], last_token[0]))
 
     got = swap_section(jnp.where(s == 0, y_home, dx_home))
     held = jnp.where(s == 0, dx_home, y_home)
@@ -797,34 +1270,36 @@
     ends = ends.reshape(1, micro_count, row_count, local_len, width)
 
     at = (lax.axis_index("dp") * n + ctx) * shard
-    gain_a_out = lax.dynamic_slice_in_dim(small[:width], at, shard, 0)
-    gain_b_out = lax.dynamic_slice_in_dim(small[width : 2 * width], at, shard, 0)
-    pre_out = small[2 * width : 2 * width + HEADS * HEADS].reshape(1, HEADS, HEADS)
-    post_out = small[2 * width + HEADS * HEADS :].reshape(1, HEADS, HEADS)
-
-    big0_columns = state["last1"].part.shape[-1]
-    big = big.finish(zero)
-    big0, joint1 = big[:, :big0_columns], big[:, big0_columns:]
-    pairs = ((big0, state["last1"].finish(zero)), (joint0.finish(zero), joint1))
-    outs = []
-    for at_zero, at_one in pairs:
-        other = swap_section(jnp.where(s == 0, at_one, at_zero))
-        own = jnp.where(s == 0, at_zero, at_one)
-        outs.append((jnp.where(s == 0, own, other), jnp.where(s == 0, other, own)))
-    (big_a, big_b), (joint_a, joint_b) = outs
+    gain_a_out, gain_b_out = (lax.dynamic_slice_in_dim(small[i], at, shard, 0) for i in range(2))
+    pre_out, post_out = mix_grads(small)
     half_d, half_ff, times = width // 2, ff // 2, ff // width
-    side = lambda *cuts: jnp.concatenate([x[:, at : at + size] for x, at, size in cuts], axis=1)
-    down_out = jnp.concatenate([side((big_a, i * half_d, half_d), (big_b, i * half_d, half_d)) for i in range(times)])
-    at = times * half_d
-    up_out = side((big_a, at, half_ff), (big_b, at, half_ff))
-    mixer_out = side((big_a, at + half_ff, half_d), (big_b, at + half_ff, half_d))
-    joint_out = side((joint_a, width, half_d), (joint_b, width, half_d), (joint_a, 0, width), (joint_b, 0, width))
+    if fast:
+        groups = (state["big0"].parts, joint0.parts, (state["big1"],), state["joint1"].parts)
+        keep, send = final_parts(seats[0], groups)
+        joint_out, mixer_out, up_out, down_out = final_outs(seats[0], keep, swap_section(send), width, ff)
+    else:
+        big0, joint0, joint1 = (total_of(x.parts[0], x.parts[1:]) for x in (state["big0"], joint0, state["joint1"]))
+        pairs = ((big0, state["big1"]), (joint0, joint1))
+        outs = []
+        for at_zero, at_one in pairs:
+            other = swap_section(jnp.where(s == 0, at_one, at_zero))
+            own = jnp.where(s == 0, at_zero, at_one)
+            outs.append((jnp.where(s == 0, own, other), jnp.where(s == 0, other, own)))
+        (big_a, big_b), (joint_a, joint_b) = outs
+        side = lambda *cuts: jnp.concatenate([x[:, at : at + size] for x, at, size in cuts], axis=1)
+        down_out = jnp.concatenate(
+            [side((big_a, i * half_d, half_d), (big_b, i * half_d, half_d)) for i in range(times)]
+        )
+        at = times * half_d
+        up_out = side((big_a, at, half_ff), (big_b, at, half_ff))
+        mixer_out = side((big_a, at + half_ff, half_d), (big_b, at + half_ff, half_d))
+        joint_out = side((joint_a, width, half_d), (joint_b, width, half_d), (joint_a, 0, width), (joint_b, 0, width))
     return (
         ends,
         gain_a_out[None],
         joint_out[None],
-        pre_out,
-        post_out,
+        pre_out[None],
+        post_out[None],
         mixer_out[None],
         gain_b_out[None],
         up_out[None],

time: 541 us -> 439 us (0.81)
  Pallas kernels: 141 us -> 216 us
  other arithmetic: 67.1 us -> 9.86 us
  matrix products: 45.9 us -> 1.81 us
  local copies, waits for them, and re-layouts: 80.8 us -> 40.6 us
  waiting for transfers between devices: 93.3 us -> 78.4 us
  starting transfers between devices: 88.9 us -> 79.9 us
  between operations: 14.7 us -> 6.08 us
    pallas_call x15 -> x31, Pallas kernels: 141 us -> 216 us  [the longest x26 172 us: run(): pl.pallas_call(kernel, cost_estimate=SMALL_COST, grid=(1,), in_specs=[who...]
    dot_general x26 -> x0, matrix products: 45.4 us -> none  [the longest x18 28.8 us: dense_tn(): lax.dot_general(left_side, right_side, (((0,), (0,)), ((), ())), preferre...]
    ppermute x37 -> x35, waiting for transfers between devices: 91.7 us -> 61.7 us  [xor_permute(): lax.ppermute(x, axis, [(i, i ^ by) for i in range(lax.axis_size(axis))])]
    convert_element_type x20 -> x3, other arithmetic: 23.5 us -> 0.64 us  [the longest x2 0.37 us: backward(): low = (dn_kept.astype(f32) + swap_section(dn_sent).astype(f32)).astype(bf16)]
    squeeze x30 -> x2, local copies, waits for them, and re-layouts: 17.3 us -> 0.03 us  [token_after(): x[(0,) * (x.ndim - 2)][:16, :128]]
    ppermute x34 -> x29, waiting for transfers between devices: 1.62 us -> 16.6 us  [swap_section(): return lax.ppermute(x, 'section', [(0, 1), (1, 0)])]
    ppermute x6 -> x0, local copies, waits for them, and re-layouts: 12.7 us -> none  [xor_permute(): lax.ppermute(x, axis, [(i, i ^ by) for i in range(lax.axis_size(axis))])]
    ppermute x1, starting transfers between devices: 16.9 us -> 4.77 us  [local(): lax.ppermute(ones, 'ctx', there)]
  transfers between devices with their start and end apart: 77 -> 70, of which waited for: 22 -> 29; matrix products, arithmetic and copies ran while one was open for 31% -> 6% of each run, Pallas kernels for 22% -> 29%
where the time goes in v3:
time: 439 us; the launch traced here: 432 us
  Pallas kernels  216 us (49%)
  starting transfers between devices  79.9 us (18%)
  waiting for transfers between devices  78.4 us (18%)
  local copies, waits for them, and re-layouts  40.6 us (9%)
  other arithmetic  9.86 us (2%)
  between operations  6.08 us (1%)
    pallas_call x26, Pallas kernels, run(): pl.pallas_call(kernel, cost_estimate=SMALL_COST, grid=(1,), in_specs=[who...  172 us
    ppermute x35, waiting for transfers between devices, xor_permute(): lax.ppermute(x, axis, [(i, i ^ by) for i in range(lax.axis_size(axis))])  61.7 us
    ppermute x35, starting transfers between devices, xor_permute(): lax.ppermute(x, axis, [(i, i ^ by) for i in range(lax.axis_size(axis))])  59.4 us
    pallas_call x2, Pallas kernels, attend_back(): pl.pallas_call(cost_estimate=SMALL_COST, kernel=functools.partial(attend_...  39.3 us
    unnamed x162, local copies, waits for them, and re-layouts  27.2 us
    ppermute x29, waiting for transfers between devices, swap_section(): return lax.ppermute(x, 'section', [(0, 1), (1, 0)])  16.6 us
  transfers between devices with their start and end apart: 70, of which 29 were waited for; matrix products, arithmetic and copies ran while one was open for 6% of the time, Pallas kernels for 29%

profile of v3, /device:TPU:0, one launch (start us, length us, event | category | flops | bytes accessed | tf_op | source)
XLA Modules:
  0.0 432.3 jit_solution(14613206708676112246)
XLA Ops:
  15.4 4.8 %collective-permute-done.6.rest_3_ = bf16[128,768]{1,0:T(8,128)(2,1)S(1)} collective-permute-done((bf16[128,768]{1,0:T(8,128)(2,1)S(1)}, bf16[128,768]{1,0:T(8,128)(2,1)S(1)}, u32[]{:S(2)}, u32[]{:S(2)}) %collective-permute-start.6) | collective-permute-done | bytes 196640 | tf_op jit(solution)/shard_map/ppermute | solution.py:513
  33.8 17.9 %shard_map.178 = (bf16[256,768]{1,0:T(8,128)(2,1)}, bf16[256,768]{1,0:T(8,128)(2,1)}, bf16[256,768]{1,0:T(8,128)(2,1)}, bf16[256,768]{1,0:T(8,128)(2,1)}, s32[1]...) custom-call(s32[13]{0:T(128)} %concatenate.30.place, ...), custom_call_target="tpu_custom_call" | custom-call | tf_op jit(solution)/shard_map/pallas_call | solution.py:185
  54.7 10.8 %shard_map.179 = (bf16[256,768]{1,0:T(8,128)(2,1)}, f32[256,768]{1,0:T(8,128)}, bf16[256,768]{1,0:T(8,128)(2,1)}, f32[256,3072]{1,0:T(8,128)}, bf16[256,3072]{1,0:T(8,128)(2,1)}, /*index=5*/s32[1]{0:T(128)}) custom-call(s32[1]{0:T(128)} %bitcast.which, bf16[256,768]{1,0:T(8,128)(2,1)} %get-tuple-element.157.x_ref, ...), custom_call_target="tpu_custom_call" | custom-call | tf_op jit(solution)/shard_map/pallas_call | solution.py:185
  66.1 10.3 %collective-permute-done.11.rest_1_ = bf16[256,768]{1,0:T(8,128)(2,1)S(1)} collective-permute-done((bf16[256,768]{1,0:T(8,128)(2,1)}, bf16[256,768]{1,0:T(8,128)(2,1)S(1)}, u32[]{:S(2)}, u32[]{:S(2)}) %collective-permute-start.11) | collective-permute-done | bytes 393248 | tf_op jit(solution)/shard_map/ppermute | solution.py:513
  79.2 17.8 %shard_map.180 = (bf16[256,768]{1,0:T(8,128)(2,1)}, bf16[256,768]{1,0:T(8,128)(2,1)}, bf16[256,768]{1,0:T(8,128)(2,1)}, bf16[256,768]{1,0:T(8,128)(2,1)}, s32[1]...) custom-call(s32[13]{0:T(128)} %concatenate.27.place, ...), custom_call_target="tpu_custom_call" | custom-call | tf_op jit(solution)/shard_map/pallas_call | solution.py:185
  97.0 10.8 %shard_map.181 = (bf16[256,768]{1,0:T(8,128)(2,1)}, f32[256,768]{1,0:T(8,128)}, bf16[256,768]{1,0:T(8,128)(2,1)}, f32[256,3072]{1,0:T(8,128)}, bf16[256,3072]{1,0:T(8,128)(2,1)}, /*index=5*/s32[1]{0:T(128)}) custom-call(s32[1]{0:T(128)} %bitcast.2.which, bf16[256,768]{1,0:T(8,128)(2,1)} %get-tuple-element.160.x_ref, ...), custom_call_target="tpu_custom_call" | custom-call | tf_op jit(solution)/shard_map/pallas_call | solution.py:185
  113.9 6.3 %shard_map.182 = (bf16[8,192,384]{2,1,0:T(8,128)(2,1)}, bf16[8,192,384]{2,1,0:T(8,128)(2,1)}, s32[1]{0:T(128)}) custom-call(s32[4]{0:T(128)S(1)} %pad_add_fusion.2.seat, bf16[256,3072]{1,0:T(8,128)(2,1)} %get-tuple-element.164.active, bf16[256,3072]{1,0:T(8,128)(2,1)} %copy-done.24, bf16[256,768]{1,0:T(8,128)(2,1)} %copy-done.20, bf16[256,768]{1,0:T(8,128)(2,1)} %copy-done.60), custom_call_target="tpu_custom_call" | custom-call | tf_op jit(solution)/shard_map/pallas_call | solution.py:185
  120.2 12.7 %shard_map.183 = (bf16[256,1920]{1,0:T(8,128)(2,1)}, bf16[256,1920]{1,0:T(8,128)(2,1)}, f32[256,768]{1,0:T(8,128)}, bf16[256,768]{1,0:T(8,128)(2,1)}, f32[1,768]{1,0:T(1,128)S(1)}, /*index=5*/s32[1]{0:T(128)}) custom-call(s32[2]{0:T(128)S(1)} %pad_add_fusion.1.which, bf16[256,768]{1,0:T(8,128)(2,1)} %copy-done.20, ...), custom_call_target="tpu_custom_call" | custom-call | tf_op jit(solution)/shard_map/pallas_call | solution.py:185
  137.7 5.6 %shard_map.184 = (bf16[8,48,1920]{2,1,0:T(8,128)(2,1)}, bf16[8,48,1920]{2,1,0:T(8,128)(2,1)}, s32[1]{0:T(128)}) custom-call(s32[4]{0:T(128)S(1)} %pad_add_fusion.2.seat, bf16[256,768]{1,0:T(8,128)(2,1)} %get-tuple-element.174.two, bf16[256,768]{1,0:T(8,128)(2,1)} %copy-done.66, bf16[256,768]{1,0:T(8,128)(2,1)} %get-tuple-element.161.att_ref.att, ...), custom_call_target="tpu_custom_call" | custom-call | tf_op jit(solution)/shard_map/pallas_call | solution.py:185
  143.3 10.4 %collective-permute-start.20 = (bf16[8,48,1920]{2,1,0:T(8,128)(2,1)}, bf16[8,48,1920]{2,1,0:T(8,128)(2,1)S(1)}, u32[]{:S(2)}, u32[]{:S(2)}) collective-permute-start(bf16[8,48,1920]{2,1,0:T(8,128)(2,1)} %get-tuple-element.184), channel_id=1, source_target_pairs={{0,2},{1,3},{2,0},{3,1},{4,6},{5,7},{6,4},{7,5},{8,10},{9,11},{10,... | collective-permute-start | bytes 4423688 | tf_op jit(solution)/shard_map/ppermute | solution.py:513
  155.5 19.6 %shard_map.185 = (bf16[256,768]{1,0:T(8,128)(2,1)}, bf16[1024,768]{1,0:T(8,128)(2,1)}, bf16[1024,768]{1,0:T(8,128)(2,1)}, f32[12,768]{1,0:T(8,128)}, f32[12,768]{1,0:T(8,128)}, /*index=5*/s32[1]{0:T(128)}) custom-call(s32[5]{0:T(128)} %stack.172.place, bf16[256,768]{1,0:T(8,128)(2,1)} %get-tuple-element.167.q_ref, ...), custom_call_target="tpu_custom_call" | custom-call | tf_op jit(solution)/shard_map/pallas_call | solution.py:462
  175.1 6.8 %collective-permute-done.19.refs_3_ = bf16[8,192,384]{2,1,0:T(8,128)(2,1)S(1)} collective-permute-done((bf16[8,192,384]{2,1,0:T(8,128)(2,1)}, bf16[8,192,384]{2,1,0:T(8,128)(2,1)S(1)}, u32[]{:S(2)}, u32[]{:S(2)}) %collective-permute-start.19) | collective-permute-done | bytes 1179680 | tf_op jit(solution)/shard_map/ppermute | solution.py:513
  181.9 4.9 %collective-permute-done.20.refs_5_ = bf16[8,48,1920]{2,1,0:T(8,128)(2,1)S(1)} collective-permute-done((bf16[8,48,1920]{2,1,0:T(8,128)(2,1)}, bf16[8,48,1920]{2,1,0:T(8,128)(2,1)S(1)}, u32[]{:S(2)}, u32[]{:S(2)}) %collective-permute-start.20) | collective-permute-done | bytes 1474592 | tf_op jit(solution)/shard_map/ppermute | solution.py:513
  190.3 5.1 %shard_map.186 = (bf16[4,192,384]{2,1,0:T(8,128)(2,1)}, bf16[4,192,384]{2,1,0:T(8,128)(2,1)}, bf16[4,48,1920]{2,1,0:T(8,128)(2,1)}, bf16[4,48,1920]{2,1,0:T(8,12...) custom-call(s32[4]{0:T(128)S(1)} %pad_add_fusion.2.seat, ...), custom_call_target="tpu_custom_call", output_to_operand_aliasing={{5}: (2, {}), {6}: (3, {})} | custom-call | tf_op jit(solution)/shard_map/pallas_call | solution.py:185
  201.4 10.1 %shard_map.187 = (bf16[512,768]{1,0:T(8,128)(2,1)}, bf16[512,768]{1,0:T(8,128)(2,1)}, f32[256,768]{1,0:T(8,128)}, bf16[8,48,512]{2,1,0:T(8,128)(2,1)}, bf16[8,48...) custom-call(s32[4]{0:T(128)S(1)} %get-tuple-element.325.seat, ...), custom_call_target="tpu_custom_call" | custom-call | tf_op jit(solution)/shard_map/pallas_call | solution.py:185
  228.9 5.3 %collective-permute-done.27.refs_1_ = bf16[8,48,512]{2,1,0:T(8,128)(2,1)} collective-permute-done((bf16[8,48,512]{2,1,0:T(8,128)(2,1)}, bf16[8,48,512]{2,1,0:T(8,128)(2,1)}, u32[]{:S(2)}, u32[]{:S(2)}) %collective-permute-start.27) | collective-permute-done | bytes 393248 | tf_op jit(solution)/shard_map/ppermute | solution.py:513
  248.9 6.3 %shard_map.191 = (bf16[8,192,384]{2,1,0:T(8,128)(2,1)}, bf16[8,192,384]{2,1,0:T(8,128)(2,1)}, s32[1]{0:T(128)}) custom-call(s32[4]{0:T(128)S(1)} %pad_add_fusion.2.seat, bf16[256,3072]{1,0:T(8,128)(2,1)} %get-tuple-element.208.active, bf16[256,3072]{1,0:T(8,128)(2,1)} %collective-permute-done.30.active_other, bf16[256,768]{1,0:T(8,128)(2,1)} %copy-done.21, ...), custom_call_target="tpu_custom_call" | custom-call | tf_op jit(solution)/shard_map/pallas_call | solution.py:185
  255.2 12.4 %shard_map.192 = (bf16[256,1920]{1,0:T(8,128)(2,1)}, bf16[256,1920]{1,0:T(8,128)(2,1)}, f32[256,768]{1,0:T(8,128)}, bf16[256,768]{1,0:T(8,128)(2,1)}, f32[1,768]{1,0:T(1,128)S(1)}, /*index=5*/s32[1]{0:T(128)}) custom-call(s32[2]{0:T(128)S(1)} %pad_add_fusion.which, bf16[256,768]{1,0:T(8,128)(2,1)} %copy-done.21, f32[256,3072]{1,0:T(8,128)} %get-tuple-element.206.upward_ref, ...), custom_call_target="tpu_custom_call" | custom-call | tf_op jit(solution)/shard_map/pallas_call | solution.py:185
  281.3 5.6 %shard_map.195 = (bf16[8,48,1920]{2,1,0:T(8,128)(2,1)}, bf16[8,48,1920]{2,1,0:T(8,128)(2,1)}, s32[1]{0:T(128)}) custom-call(s32[4]{0:T(128)S(1)} %pad_add_fusion.2.seat, bf16[256,768]{1,0:T(8,128)(2,1)} %get-tuple-element.231.two, bf16[256,768]{1,0:T(8,128)(2,1)} %copy-done.68, bf16[256,768]{1,0:T(8,128)(2,1)} %get-tuple-element.158.att_ref.att, ...), custom_call_target="tpu_custom_call" | custom-call | tf_op jit(solution)/shard_map/pallas_call | solution.py:185
  293.5 19.7 %shard_map.196 = (bf16[256,768]{1,0:T(8,128)(2,1)}, bf16[1024,768]{1,0:T(8,128)(2,1)}, bf16[1024,768]{1,0:T(8,128)(2,1)}, f32[12,768]{1,0:T(8,128)}, f32[12,768]{1,0:T(8,128)}, /*index=5*/s32[1]{0:T(128)}) custom-call(s32[5]{0:T(128)} %stack.173.place, bf16[256,768]{1,0:T(8,128)(2,1)} %get-tuple-element.211.q_ref, ...), custom_call_target="tpu_custom_call" | custom-call | tf_op jit(solution)/shard_map/pallas_call | solution.py:462
  315.5 6.0 %collective-permute-done.41.refs_5_ = bf16[8,48,1920]{2,1,0:T(8,128)(2,1)S(1)} collective-permute-done((bf16[8,48,1920]{2,1,0:T(8,128)(2,1)}, bf16[8,48,1920]{2,1,0:T(8,128)(2,1)S(1)}, u32[]{:S(2)}, u32[]{:S(2)}) %collective-permute-start.41) | collective-permute-done | bytes 1474592 | tf_op jit(solution)/shard_map/ppermute | solution.py:513
  322.6 5.4 %shard_map.197 = (bf16[4,192,384]{2,1,0:T(8,128)(2,1)}, bf16[4,192,384]{2,1,0:T(8,128)(2,1)}, bf16[4,48,1920]{2,1,0:T(8,128)(2,1)}, bf16[4,48,1920]{2,1,0:T(8,12...) custom-call(s32[4]{0:T(128)S(1)} %pad_add_fusion.2.seat, ...), custom_call_target="tpu_custom_call", output_to_operand_aliasing={{6}: (2, {}), {7}: (3, {})} | custom-call | tf_op jit(solution)/shard_map/pallas_call | solution.py:185
  339.8 10.1 %shard_map.199 = (bf16[512,768]{1,0:T(8,128)(2,1)}, bf16[512,768]{1,0:T(8,128)(2,1)}, f32[256,768]{1,0:T(8,128)}, bf16[8,48,512]{2,1,0:T(8,128)(2,1)}, bf16[8,48...) custom-call(s32[4]{0:T(128)S(1)} %pad_add_fusion.2.seat, ...), custom_call_target="tpu_custom_call" | custom-call | tf_op jit(solution)/shard_map/pallas_call | solution.py:185
  411.9 5.1 %collective-permute-done.63 = f32[26,768]{1,0:T(8,128)S(1)} collective-permute-done((f32[26,768]{1,0:T(8,128)S(1)}, f32[26,768]{1,0:T(8,128)S(1)}, u32[]{:S(2)}, u32[]{:S(2)}) %collective-permute-start.63) | collective-permute-done | bytes 79904 | tf_op jit(solution)/shard_map/ppermute | solution.py:513
  (368 shorter events, 196.5 us)
Async XLA Ops:
  0.7 51.1 %collective-permute-start.10 = (bf16[1,3072,768]{2,1,0:T(8,128)(2,1)}, bf16[1,3072,768]{2,1,0:T(8,128)(2,1)}, u32[]{:S(2)}, u32[]{:S(2)}) collective-permute-start(bf16[1,3072,768]{2,1,0:T(8,128)(2,1)} %down_own.7), channel_id=1, source_target_pairs={{0,16},{16,0},{1,17},{17,1},{2,18},{18,2},{3,19},{19,3},{4,20},{20... | collective-permute-start | bytes 14155784 | tf_op jit(solution)/shard_map/ppermute | solution.py:509
  1.2 50.6 %collective-permute-start.9 = (bf16[1,768,3072]{2,1,0:T(8,128)(2,1)}, bf16[1,768,3072]{2,1,0:T(8,128)(2,1)}, u32[]{:S(2)}, u32[]{:S(2)}) collective-permute-start(bf16[1,768,3072]{2,1,0:T(8,128)(2,1)} %up_own.7), channel_id=1, source_target_pairs={{0,16},{16,0},{1,17},{17,1},{2,18},{18,2},{3,19},{19,3},{4,20},{20... | collective-permute-start | bytes 14155784 | tf_op jit(solution)/shard_map/ppermute | solution.py:509
  1.3 25.1 %collective-permute-start.3 = (bf16[1,768,2304]{2,1,0:T(8,128)(2,1)}, bf16[1,768,2304]{2,1,0:T(8,128)(2,1)}, u32[]{:S(2)}, u32[]{:S(2)}) collective-permute-start(bf16[1,768,2304]{2,1,0:T(8,128)(2,1)} %joint_own.7), channel_id=1, source_target_pairs={{0,16},{16,0},{1,17},{17,1},{2,18},{18,2},{3,19},{19,3},{4,20},{20... | collective-permute-start | bytes 10616840 | tf_op jit(solution)/shard_map/ppermute | solution.py:509
  10.9 40.9 %collective-permute-start.8 = (bf16[1,768,768]{2,1,0:T(8,128)(2,1)}, bf16[1,768,768]{2,1,0:T(8,128)(2,1)S(1)}, u32[]{:S(2)}, u32[]{:S(2)}) collective-permute-start(bf16[1,768,768]{2,1,0:T(8,128)(2,1)} %mixer_own.7), channel_id=1, source_target_pairs={{0,16},{16,0},{1,17},{17,1},{2,18},{18,2},{3,19},{19,3},{4,20},{20... | collective-permute-start | bytes 3538952 | tf_op jit(solution)/shard_map/ppermute | solution.py:509
  24.7 27.0 %collective-permute-start = (bf16[128,768]{1,0:T(8,128)(2,1)}, bf16[128,768]{1,0:T(8,128)(2,1)S(1)}, u32[]{:S(2)}, u32[]{:S(2)}) collective-permute-start(bf16[128,768]{1,0:T(8,128)(2,1)} %get-tuple-element.329), channel_id=1, source_target_pairs={{3,2},{2,3},{0,0},{1,1},{7,6},{6,7},{4,4},{5,5},{11,10},{10,11},{8... | collective-permute-start | bytes 589832 | tf_op jit(solution)/shard_map/ppermute | solution.py:1187
  26.3 25.4 %collective-permute-start.1 = (bf16[128,768]{1,0:T(8,128)(2,1)S(1)}, bf16[128,768]{1,0:T(8,128)(2,1)S(1)}, u32[]{:S(2)}, u32[]{:S(2)}) collective-permute-start(bf16[128,768]{1,0:T(8,128)(2,1)S(1)} %get-tuple-element.330), channel_id=1, source_target_pairs={{0,2},{1,3},{3,0},{2,1},{4,6},{5,7},{7,4},{6,5},{8,10},{9,11},{11,... | collective-permute-start | bytes 589832 | tf_op jit(solution)/shard_map/ppermute | solution.py:1187
  143.3 43.4 %collective-permute-start.20 = (bf16[8,48,1920]{2,1,0:T(8,128)(2,1)}, bf16[8,48,1920]{2,1,0:T(8,128)(2,1)S(1)}, u32[]{:S(2)}, u32[]{:S(2)}) collective-permute-start(bf16[8,48,1920]{2,1,0:T(8,128)(2,1)} %get-tuple-element.184), channel_id=1, source_target_pairs={{0,2},{1,3},{2,0},{3,1},{4,6},{5,7},{6,4},{7,5},{8,10},{9,11},{10,... | collective-permute-start | bytes 4423688 | tf_op jit(solution)/shard_map/ppermute | solution.py:513
  153.7 28.2 %collective-permute-start.19 = (bf16[8,192,384]{2,1,0:T(8,128)(2,1)}, bf16[8,192,384]{2,1,0:T(8,128)(2,1)S(1)}, u32[]{:S(2)}, u32[]{:S(2)}) collective-permute-start(bf16[8,192,384]{2,1,0:T(8,128)(2,1)} %get-tuple-element.182), channel_id=1, source_target_pairs={{0,1},{1,0},{2,3},{3,2},{4,5},{5,4},{6,7},{7,6},{8,9},{9,8},{10,11... | collective-permute-start | bytes 3538952 | tf_op jit(solution)/shard_map/ppermute | solution.py:513
  219.4 25.2 %collective-permute-start.30 = (bf16[256,3072]{1,0:T(8,128)(2,1)}, bf16[256,3072]{1,0:T(8,128)(2,1)}, u32[]{:S(2)}, u32[]{:S(2)}) collective-permute-start(bf16[256,3072]{1,0:T(8,128)(2,1)} %get-tuple-element.208.active), channel_id=1, source_target_pairs={{0,16},{16,0},{1,17},{17,1},{2,18},{18,2},{3,19},{19,3},{4,20},{20... | collective-permute-start | bytes 4718600 | tf_op jit(solution)/shard_map/ppermute | solution.py:509
  224.9 47.6 %collective-permute-start.36 = (bf16[2,48,3456]{2,1,0:T(8,128)(2,1)}, bf16[2,48,3456]{2,1,0:T(8,128)(2,1)S(1)}, u32[]{:S(2)}, u32[]{:S(2)}) collective-permute-start(bf16[2,48,3456]{2,1,0:T(8,128)(2,1)} %get-tuple-element.229), channel_id=1, source_target_pairs={{0,4},{4,0},{8,12},{12,8},{1,5},{5,1},{9,13},{13,9},{2,6},{6,2},{1... | collective-permute-start | bytes 1990664 | tf_op jit(solution)/shard_map/ppermute | solution.py:513
  242.7 25.0 %collective-permute-start.35 = (bf16[4,48,640]{2,1,0:T(8,128)(2,1)S(1)}, bf16[4,48,640]{2,1,0:T(8,128)(2,1)S(1)}, u32[]{:S(2)}, u32[]{:S(2)}) collective-permute-start(bf16[4,48,640]{2,1,0:T(8,128)(2,1)S(1)} %copy-done.78), channel_id=1, source_target_pairs={{0,1},{1,0},{2,3},{3,2},{4,5},{5,4},{6,7},{7,6},{8,9},{9,8},{10,11... | collective-permute-start | bytes 737288 | tf_op jit(solution)/shard_map/ppermute | solution.py:513
  243.2 24.4 %collective-permute-start.32 = (bf16[128,768]{1,0:T(8,128)(2,1)S(1)}, bf16[128,768]{1,0:T(8,128)(2,1)S(1)}, u32[]{:S(2)}, u32[]{:S(2)}) collective-permute-start(bf16[128,768]{1,0:T(8,128)(2,1)S(1)} %get-tuple-element.334), channel_id=1, source_target_pairs={{2,0},{3,1},{0,3},{1,2},{6,4},{7,5},{4,7},{5,6},{10,8},{11,9},{8,1... | collective-permute-start | bytes 589832 | tf_op jit(solution)/shard_map/ppermute | solution.py:1194
  244.6 23.1 %collective-permute-start.33 = (bf16[128,768]{1,0:T(8,128)(2,1)S(1)}, bf16[128,768]{1,0:T(8,128)(2,1)S(1)}, u32[]{:S(2)}, u32[]{:S(2)}) collective-permute-start(bf16[128,768]{1,0:T(8,128)(2,1)S(1)} %get-tuple-element.333), channel_id=1, source_target_pairs={{2,3},{3,2},{0,0},{1,1},{6,7},{7,6},{4,4},{5,5},{10,11},{11,10},{8... | collective-permute-start | bytes 589832 | tf_op jit(solution)/shard_map/ppermute | solution.py:1195
  245.3 22.4 %collective-permute-start.34 = (bf16[4,48,512]{2,1,0:T(8,128)(2,1)S(1)}, bf16[4,48,512]{2,1,0:T(8,128)(2,1)S(1)}, u32[]{:S(2)}, u32[]{:S(2)}) collective-permute-start(bf16[4,48,512]{2,1,0:T(8,128)(2,1)S(1)} %copy-done.79), channel_id=1, source_target_pairs={{0,2},{1,3},{2,0},{3,1},{4,6},{5,7},{6,4},{7,5},{8,10},{9,11},{10,... | collective-permute-start | bytes 589832 | tf_op jit(solution)/shard_map/ppermute | solution.py:513
  286.9 34.6 %collective-permute-start.41 = (bf16[8,48,1920]{2,1,0:T(8,128)(2,1)}, bf16[8,48,1920]{2,1,0:T(8,128)(2,1)S(1)}, u32[]{:S(2)}, u32[]{:S(2)}) collective-permute-start(bf16[8,48,1920]{2,1,0:T(8,128)(2,1)} %get-tuple-element.241), channel_id=1, source_target_pairs={{0,2},{1,3},{2,0},{3,1},{4,6},{5,7},{6,4},{7,5},{8,10},{9,11},{10,... | collective-permute-start | bytes 4423688 | tf_op jit(solution)/shard_map/ppermute | solution.py:513
  287.5 27.9 %collective-permute-start.40 = (bf16[8,192,384]{2,1,0:T(8,128)(2,1)}, bf16[8,192,384]{2,1,0:T(8,128)(2,1)S(1)}, u32[]{:S(2)}, u32[]{:S(2)}) collective-permute-start(bf16[8,192,384]{2,1,0:T(8,128)(2,1)} %get-tuple-element.239), channel_id=1, source_target_pairs={{0,1},{1,0},{2,3},{3,2},{4,5},{5,4},{6,7},{7,6},{8,9},{9,8},{10,11... | collective-permute-start | bytes 3538952 | tf_op jit(solution)/shard_map/ppermute | solution.py:513
  288.1 25.2 %collective-permute-start.42 = (bf16[48,3456]{1,0:T(8,128)(2,1)}, bf16[48,3456]{1,0:T(8,128)(2,1)}, u32[]{:S(2)}, u32[]{:S(2)}) collective-permute-start(bf16[48,3456]{1,0:T(8,128)(2,1)} %get-tuple-element.243), channel_id=1, source_target_pairs={{0,8},{4,12},{8,0},{12,4},{1,9},{5,13},{9,1},{13,5},{2,10},{6,14},... | collective-permute-start | bytes 995336 | tf_op jit(solution)/shard_map/ppermute | solution.py:513
  290.7 37.4 %collective-permute-start.43 = (bf16[2,48,1152]{2,1,0:T(8,128)(2,1)}, bf16[2,48,1152]{2,1,0:T(8,128)(2,1)S(1)}, u32[]{:S(2)}, u32[]{:S(2)}) collective-permute-start(bf16[2,48,1152]{2,1,0:T(8,128)(2,1)} %get-tuple-element.248), channel_id=1, source_target_pairs={{0,4},{4,0},{8,12},{12,8},{1,5},{5,1},{9,13},{13,9},{2,6},{6,2},{1... | collective-permute-start | bytes 663560 | tf_op jit(solution)/shard_map/ppermute | solution.py:513
  331.0 19.2 %collective-permute-start.48 = (bf16[4,48,1920]{2,1,0:T(8,128)(2,1)}, bf16[4,48,1920]{2,1,0:T(8,128)(2,1)}, u32[]{:S(2)}, u32[]{:S(2)}) collective-permute-start(bf16[4,48,1920]{2,1,0:T(8,128)(2,1)} %get-tuple-element.261), channel_id=1, source_target_pairs={{0,1},{1,0},{2,3},{3,2},{4,5},{5,4},{6,7},{7,6},{8,9},{9,8},{10,11... | collective-permute-start | bytes 2211848 | tf_op jit(solution)/shard_map/ppermute | solution.py:513
  363.9 24.8 %collective-permute-start.59 = (f32[26,768]{1,0:T(8,128)S(1)}, f32[26,768]{1,0:T(8,128)}, u32[]{:S(2)}, u32[]{:S(2)}) collective-permute-start(f32[26,768]{1,0:T(8,128)S(1)} %add_add_fusion.3), channel_id=1, source_target_pairs={{0,2},{1,3},{2,0},{3,1},{4,6},{5,7},{6,4},{7,5},{8,10},{9,11},{10,... | collective-permute-start | bytes 239624 | tf_op jit(solution)/shard_map/ppermute | solution.py:513
  367.8 21.8 %collective-permute-start.53 = (bf16[2,128,768]{2,1,0:T(8,128)(2,1)}, bf16[2,128,768]{2,1,0:T(8,128)(2,1)}, u32[]{:S(2)}, u32[]{:S(2)}) collective-permute-start(bf16[2,128,768]{2,1,0:T(8,128)(2,1)} %dynamic-slice_bitcast_fusion), channel_id=1, source_target_pairs={{0,1},{1,0},{2,3},{3,2},{4,5},{5,4},{6,7},{7,6},{8,9},{9,8},{10,11... | collective-permute-start | bytes 1179656 | tf_op jit(solution)/shard_map/ppermute | solution.py:513
  375.0 36.5 %collective-permute-start.68 = (bf16[48,1152]{1,0:T(8,128)(2,1)S(1)}, bf16[48,1152]{1,0:T(8,128)(2,1)S(1)}, u32[]{:S(2)}, u32[]{:S(2)}) collective-permute-start(bf16[48,1152]{1,0:T(8,128)(2,1)S(1)} %get-tuple-element.296), channel_id=1, source_target_pairs={{0,8},{4,12},{8,0},{12,4},{1,9},{5,13},{9,1},{13,5},{2,10},{6,14},... | collective-permute-start | bytes 331784 | tf_op jit(solution)/shard_map/ppermute | solution.py:513
  388.7 33.3 %collective-permute-start.64 = (bf16[48,3456]{1,0:T(8,128)(2,1)}, bf16[48,3456]{1,0:T(8,128)(2,1)}, u32[]{:S(2)}, u32[]{:S(2)}) collective-permute-start(bf16[48,3456]{1,0:T(8,128)(2,1)} %get-tuple-element.289), channel_id=1, source_target_pairs={{0,8},{4,12},{8,0},{12,4},{1,9},{5,13},{9,1},{13,5},{2,10},{6,14},... | collective-permute-start | bytes 995336 | tf_op jit(solution)/shard_map/ppermute | solution.py:513
  398.9 23.1 %collective-permute-start.65 = (bf16[48,1152]{1,0:T(8,128)(2,1)S(1)}, bf16[48,1152]{1,0:T(8,128)(2,1)S(1)}, u32[]{:S(2)}, u32[]{:S(2)}) collective-permute-start(bf16[48,1152]{1,0:T(8,128)(2,1)S(1)} %get-tuple-element.291), channel_id=1, source_target_pairs={{0,4},{4,0},{8,12},{12,8},{1,5},{5,1},{9,13},{13,9},{2,6},{6,2},{1... | collective-permute-start | bytes 331784 | tf_op jit(solution)/shard_map/ppermute | solution.py:513
  (126 other events, 799.5 us)

commit v4 on v3

--- a/solution.py
+++ b/solution.py
@@ -37,6 +37,7 @@
 
 
 GAIN_A, GAIN_B, PRE, POST = 0, 1, 8, 24
+SECTION, CTX, DP, LENGTH, STARTS, WHICH, BLOCKS = 0, 1, 2, 3, 4, 6, 8
 SMALL_ROWS = 40
 
 
@@ -58,30 +59,30 @@
     return jnp.where((cols <= rows) & (cols < length), 0.0, MASKED).astype(f32)
 
 
-def attend_kernel(place, small_own, small_got, joint_own, joint_got, *rest, bk, count_in):
+def attend_kernel(info, small_own, small_got, joint_own, joint_got, *rest, bk, count_in, layer):
     (
         att_ref, q_ref, own_ref, x_ref, token_ref, normed_hbm, k_hbm, v_hbm, u_hbm, lse_hbm,
         joint, raw, normed, k, v, u, lse, qp, logit, total, top, norm, sems,
     ) = rest[count_in:]
     token_ref[0] = 0
-    length, which = place[0], place[1]
+    length, which = info[LENGTH], info[WHICH + layer]
     fetch((joint_own, joint_got), which, joint, sems.at[0])
     seq, width = normed.shape
     count = att_ref.shape[0]
     bq = count // 2
     small = small_of(small_own, small_got, which)
     gain, pre, post = small(GAIN_A, 1), small(PRE, HEADS), small(POST, HEADS)
-    at = 5
+    at = BLOCKS + layer * (seq // bq)
     for piece in rest[:count_in]:
         for j in range(piece.shape[0] // bq):
             x = piece[j * bq : (j + 1) * bq, :]
-            span = pl.ds(pl.multiple_of(place[at] * bq, bq), bq)
+            span = pl.ds(pl.multiple_of(info[at] * bq, bq), bq)
             raw[span, :] = x
             x = x.astype(f32)
             normed[span, :] = (x * rms_inverse(x) * gain).astype(bf16)
             at += 1
     for i in range(2):
-        span = pl.ds(pl.multiple_of(place[2 + i], bq), bq)
+        span = pl.ds(pl.multiple_of(info[STARTS + i], bq), bq)
         own_ref[i * bq : (i + 1) * bq, :] = normed[span, :]
         x_ref[i * bq : (i + 1) * bq, :] = raw[span, :]
     fetched((joint_own, joint_got), joint, sems.at[0])
@@ -101,7 +102,7 @@
         out.start()
 
     def rows_step(step, carry):
-        q_start = place[2 + step]
+        q_start = info[STARTS + step]
         mine = pl.ds(pl.multiple_of(step * bq, bq), bq)
         q32 = q_ref[mine, :].astype(f32)
         for h in range(HEADS):
@@ -153,6 +154,7 @@
 
 
 VMEM_SPEC = pl.BlockSpec(memory_space=pltpu.VMEM)
+FAR_SPEC = pl.BlockSpec(memory_space=pltpu.VMEM)
 ANY_SPEC = pl.BlockSpec(memory_space=pl.ANY)
 HBM_SPEC = pl.BlockSpec(memory_space=pltpu.HBM)
 SMEM_SPEC = pl.BlockSpec(memory_space=pltpu.SMEM)
@@ -163,7 +165,7 @@
 
 
 def in_hbm(spec, x):
-    return spec in (VMEM_SPEC, HBM_SPEC) and math.prod(x.shape) >= LARGE
+    return (spec is FAR_SPEC or spec is HBM_SPEC) and math.prod(x.shape) >= LARGE
 
 
 def from_hbm(spec, x):
@@ -176,7 +178,7 @@
 
 def one_step(kernel, *, in_specs, out_specs, out_shape, **rest):
     def whole(spec, x):
-        if spec is not VMEM_SPEC:
+        if spec is not VMEM_SPEC and spec is not FAR_SPEC:
             return spec
         zeros = (0,) * len(x.shape)
         return pl.BlockSpec(x.shape, lambda i: zeros, pipeline_mode=pl.Buffered(1))
@@ -195,15 +197,15 @@
     return run
 
 
-def attend(place, pieces, count, smalls, joints, bk):
+def attend(info, layer, pieces, count, smalls, joints, bk):
     width = pieces[0].shape[1]
     seq = sum(x.shape[0] for x in pieces)
     bq = count // 2
     shape = jax.ShapeDtypeStruct
     return one_step(
-        functools.partial(attend_kernel, bk=bk, count_in=len(pieces)),
+        functools.partial(attend_kernel, bk=bk, count_in=len(pieces), layer=layer),
         in_specs=[SMEM_SPEC] + [VMEM_SPEC] * 2 + [HBM_SPEC] * 2 + [VMEM_SPEC] * len(pieces),
-        out_specs=[VMEM_SPEC] * 4 + [SMEM_SPEC] + [HBM_SPEC] * 5,
+        out_specs=[VMEM_SPEC, FAR_SPEC, FAR_SPEC, VMEM_SPEC, SMEM_SPEC] + [HBM_SPEC] * 5,
         out_shape=[shape((count, width), bf16)] * 4
         + [TOKEN]
         + [shape((seq, width), bf16)] * 3
@@ -224,23 +226,24 @@
             pltpu.SemaphoreType.DMA((6,)),
         ],
         compiler_params=pltpu.CompilerParams(vmem_limit_bytes=BIG_VMEM),
-    )(place, *smalls, *joints, *pieces)
+    )(info, *smalls, *joints, *pieces)
 
 
 def feed_kernel(
-    which, x_ref, att_ref, small_own, small_got,
-    mixer_own, mixer_got, up_own, up_got, down_own, down_got, *rest, tile, extra,
+    info, x_ref, att_ref, small_own, small_got,
+    mixer_own, mixer_got, up_own, up_got, down_own, down_got, *rest, tile, extra, layer,
 ):
     (
         out_ref, hidden_ref, two_ref, upward_hbm, active_hbm, token_ref,
         mixer, up, down, upward, active, sems,
     ) = rest[extra:]
     token_ref[0] = 0
+    which = info[WHICH + layer]
     pairs = ((mixer_own, mixer_got), (up_own, up_got), (down_own, down_got))
     buffers = (mixer, up, down)
     for i in range(3):
-        fetch(pairs[i], which[0], buffers[i], sems.at[i])
-    gain = small_of(small_own, small_got, which[0])(GAIN_B, 1)
+        fetch(pairs[i], which, buffers[i], sems.at[i])
+    gain = small_of(small_own, small_got, which)(GAIN_B, 1)
     fetched(pairs[0], mixer, sems.at[0])
     hidden = x_ref[...].astype(f32) + dense(att_ref[...], mixer[...])
     hidden_ref[...] = hidden
@@ -265,13 +268,13 @@
         out.wait()
 
 
-def feed(which, x, attended, smalls, weights, ff, extras):
+def feed(info, layer, x, attended, smalls, weights, ff, extras):
     count, width = x.shape
     shape = jax.ShapeDtypeStruct
     return one_step(
-        functools.partial(feed_kernel, tile=width, extra=len(extras)),
+        functools.partial(feed_kernel, tile=width, extra=len(extras), layer=layer),
         in_specs=[SMEM_SPEC] + [VMEM_SPEC] * 4 + [HBM_SPEC] * (6 + len(extras)),
-        out_specs=[VMEM_SPEC] * 3 + [HBM_SPEC] * 2 + [SMEM_SPEC],
+        out_specs=[VMEM_SPEC, FAR_SPEC, FAR_SPEC] + [HBM_SPEC] * 2 + [SMEM_SPEC],
         out_shape=[
             shape((count, width), bf16),
             shape((count, width), f32),
@@ -289,7 +292,7 @@
             pltpu.SemaphoreType.DMA((5,)),
         ],
         compiler_params=pltpu.CompilerParams(vmem_limit_bytes=SMALL_VMEM),
-    )(which, x, attended, *smalls, *weights, *extras)
+    )(info, x, attended, *smalls, *weights, *extras)
 
 
 def fetch(pair, which, buffer, semaphore):
@@ -311,39 +314,48 @@
 
 
 def feed_back_kernel(
-    which, dy_ref, upward_ref, hidden_ref, small_own, small_got,
-    mixer_own, mixer_got, up_own, up_got, down_own, down_got, *rest, tile, extra,
+    info, dy_ref, upward_hbm, hidden_hbm, small_own, small_got,
+    mixer_own, mixer_got, up_own, up_got, down_own, down_got, *rest, tile, extra, layer,
 ):
     (
         keep_ref, send_ref, dhidden_ref, datt_ref, gain_grad_ref, token_ref,
-        mixer, up, down, sems,
+        mixer, up, down, upward_ref, hidden_ref, sems,
     ) = rest[extra:]
     token_ref[0] = 0
+    which = info[WHICH + layer]
     width = dy_ref.shape[1]
     half_ff, half = down.shape[0] // 2, width // 2
 
     def put(value, number, at):
         for ref, equal in ((keep_ref, True), (send_ref, False)):
 
-            @pl.when((which[1] == number) == equal)
+            @pl.when((info[SECTION] == number) == equal)
             def _(ref=ref):
                 ref[:, at : at + value.shape[1]] = value
 
     pairs = ((down_own, down_got), (up_own, up_got), (mixer_own, mixer_got))
     for i, (pair, buffer) in enumerate(zip(pairs, (down, up, mixer))):
-        fetch(pair, which[0], buffer, sems.at[i])
-    gain = small_of(small_own, small_got, which[0])(GAIN_B, 1)
+        fetch(pair, which, buffer, sems.at[i])
+        if i == 0:
+            upward_copy = pltpu.make_async_copy(upward_hbm, upward_ref, sems.at[3])
+            hidden_copy = pltpu.make_async_copy(hidden_hbm, hidden_ref, sems.at[4])
+            upward_copy.start()
+            hidden_copy.start()
+    gain = small_of(small_own, small_got, which)(GAIN_B, 1)
     dy = dy_ref[...]
     fetched(pairs[0], down, sems.at[0])
     grad = jnp.zeros(hidden_ref.shape, f32)
     for j in range(down.shape[0] // tile):
         span = slice(j * tile, (j + 1) * tile)
         dactive = dense_nt(dy, down[span, :])
+        if j == 0:
+            upward_copy.wait()
         dup = (dactive * gelu_slope(upward_ref[:, span])).astype(bf16)
         put(dup, j * tile // half_ff, j * tile % half_ff)
         if j == 0:
             fetched(pairs[1], up, sems.at[1])
         grad = grad + dense_nt(dup, up[:, span])
+    hidden_copy.wait()
     hidden = hidden_ref[...]
     inverse = rms_inverse(hidden)
     unit = hidden * inverse
@@ -354,21 +366,22 @@
     low = dhidden.astype(bf16)
     for i in range(2):
         put(low[:, i * half : (i + 1) * half], i, half_ff)
+        put(dy[:, i * half : (i + 1) * half], i, half_ff + half)
     fetched(pairs[2], mixer, sems.at[2])
     datt_ref[...] = dense_nt(low, mixer[...]).astype(bf16)
 
 
-def feed_back(which, dy, upward, hidden, smalls, weights, extras):
+def feed_back(info, layer, dy, upward, hidden, smalls, weights, extras):
     count, width = dy.shape
     ff = upward.shape[1]
     shape = jax.ShapeDtypeStruct
     return one_step(
-        functools.partial(feed_back_kernel, tile=width, extra=len(extras)),
-        in_specs=[SMEM_SPEC] + [VMEM_SPEC] * 5 + [HBM_SPEC] * (6 + len(extras)),
-        out_specs=[VMEM_SPEC] * 5 + [SMEM_SPEC],
+        functools.partial(feed_back_kernel, tile=width, extra=len(extras), layer=layer),
+        in_specs=[SMEM_SPEC, VMEM_SPEC, HBM_SPEC, HBM_SPEC, VMEM_SPEC, VMEM_SPEC] + [HBM_SPEC] * (6 + len(extras)),
+        out_specs=[VMEM_SPEC, VMEM_SPEC, FAR_SPEC, VMEM_SPEC, VMEM_SPEC, SMEM_SPEC],
         out_shape=[
-            shape((count, (ff + width) // 2), bf16),
-            shape((count, (ff + width) // 2), bf16),
+            shape((count, ff // 2 + width), bf16),
+            shape((count, ff // 2 + width), bf16),
             shape((count, width), f32),
             shape((count, width), bf16),
             shape((1, width), f32),
@@ -378,22 +391,31 @@
             pltpu.VMEM((width, width), bf16),
             pltpu.VMEM((width, ff), bf16),
             pltpu.VMEM((ff, width), bf16),
-            pltpu.SemaphoreType.DMA((3,)),
+            pltpu.VMEM((count, ff), f32),
+            pltpu.VMEM((count, width), f32),
+            pltpu.SemaphoreType.DMA((5,)),
         ],
         compiler_params=pltpu.CompilerParams(vmem_limit_bytes=SMALL_VMEM),
-    )(which, dy, upward, hidden, *smalls, *weights, *extras)
+    )(info, dy, upward, hidden, *smalls, *weights, *extras)
 
 
 def attend_back_kernel(
-    place, q_ref, datt_ref, u_ref, lse_ref, k_ref, v_ref, small_own, small_got, *rest, bq, bk, extra
+    info, q_ref, datt_ref, u_ref, lse_ref, k_hbm, v_hbm, small_own, small_got, *rest, bq, bk, extra, layer
 ):
     (
         dq_ref, keep_ref, send_ref, pre_grad_ref, post_grad_ref, token_ref,
-        qp, dp, dk, dv, w, delta,
+        qp, dp, dk, dv, w, delta, k_ref, v_ref, sems,
     ) = rest[extra:]
     token_ref[0] = 0
     step = pl.program_id(0)
-    length, which, q_start = place[0], place[1], place[2 + step]
+    copies = [pltpu.make_async_copy(x, y, sems.at[i]) for i, (x, y) in enumerate(((k_hbm, k_ref), (v_hbm, v_ref)))]
+
+    @pl.when(step == 0)
+    def _():
+        for copy in copies:
+            copy.start()
+
+    length, which, q_start = info[LENGTH], info[WHICH + layer], info[STARTS + step]
     small = small_of(small_own, small_got, which)
     pre, post = small(PRE, HEADS), small(POST, HEADS)
 
@@ -416,6 +438,11 @@
         post_grad_ref[h : h + 1, :] += jnp.sum(datt * u, axis=0, keepdims=True)
     w[...] = jnp.zeros_like(w)
     blocks = (jnp.minimum(q_start + bq, length) + bk - 1) // bk
+
+    @pl.when(step == 0)
+    def _():
+        for copy in copies:
+            copy.wait()
 
     def block(kb, c):
         span = pl.ds(pl.multiple_of(kb * bk, bk), bk)
@@ -446,13 +473,13 @@
 
     for section, (kept, sent) in enumerate(((dk, dv), (dv, dk))):
 
-        @pl.when((step == pl.num_programs(0) - 1) & (place[4] == section))
+        @pl.when((step == pl.num_programs(0) - 1) & (info[SECTION] == section))
         def _(kept=kept, sent=sent):
             keep_ref[...] = kept[...].astype(bf16)
             send_ref[...] = sent[...].astype(bf16)
 
 
-def attend_back(place, q, datt, u, lse, k, v, smalls, bk, extras):
+def attend_back(info, layer, q, datt, u, lse, k, v, smalls, bk, extras):
     count, width = q.shape
     seq = k.shape[0]
     bq = count // 2
@@ -461,7 +488,7 @@
     shape = jax.ShapeDtypeStruct
     return pl.pallas_call(
         cost_estimate=SMALL_COST,
-        kernel=functools.partial(attend_back_kernel, bq=bq, bk=bk, extra=len(extras)),
+        kernel=functools.partial(attend_back_kernel, bq=bq, bk=bk, extra=len(extras), layer=layer),
         grid_spec=pltpu.PrefetchScalarGridSpec(
             num_scalar_prefetch=1,
             grid=(2,),
@@ -470,8 +497,8 @@
                 pl.BlockSpec((bq, width), row),
                 pl.BlockSpec((HEADS * bq, width), row),
                 pl.BlockSpec((HEADS * bq, 128), row),
-                pl.BlockSpec((seq, width), full),
-                pl.BlockSpec((seq, width), full),
+                HBM_SPEC,
+                HBM_SPEC,
                 pl.BlockSpec((SMALL_ROWS, width), full),
                 pl.BlockSpec((SMALL_ROWS, width), full),
             ]
@@ -491,6 +518,9 @@
                 pltpu.VMEM((seq, width), f32),
                 pltpu.VMEM((HEADS * bq, width), f32),
                 pltpu.VMEM((HEADS * bq, 128), f32),
+                pltpu.VMEM((seq, width), bf16),
+                pltpu.VMEM((seq, width), bf16),
+                pltpu.SemaphoreType.DMA((2,)),
             ],
         ),
         out_shape=[
@@ -502,7 +532,7 @@
             TOKEN,
         ],
         compiler_params=pltpu.CompilerParams(vmem_limit_bytes=BIG_VMEM),
-    )(place, q, datt, u, lse, k, v, *smalls, *extras)
+    )(info, q, datt, u, lse, k, v, *smalls, *extras)
 
 
 def swap_section(x):
@@ -550,48 +580,49 @@
         sent[i] = blocks[at + 2 * (1 - mine)]
 
 
-def down_kernel(seat, active, active_other, dy, dy_other, kept, sent, token_ref, blocks):
+def products_kernel(
+    seat, active, active_other, two, two_other, att, att_other, right, right_other,
+    down_kept, down_sent, up_kept, up_sent, token_ref, down_blocks, up_blocks,
+):
     token_ref[0] = 0
-    rows, size = blocks.shape[1:]
-    right, right_other = (half_columns(x, seat[0], size) for x in (dy, dy_other))
-    tile = dy.shape[1]
-    for j in range(active.shape[1] // tile):
-        cols = slice(j * tile, (j + 1) * tile)
-        grad = dense_tn(active[:, cols], right) + dense_tn(active_other[:, cols], right_other)
-        each = tile // rows
-        blocks[j * each : (j + 1) * each] = grad.astype(bf16).reshape(each, rows, size)
-    split_blocks(blocks, kept, sent, seat[1] % 2)
-
-
-def up_kernel(seat, two, two_other, att, att_other, right, right_other, kept, sent, token_ref, blocks):
-    token_ref[0] = 0
-    rows, size = blocks.shape[1:]
-    cut = size - att.shape[1] // 2
-    tile = cut // 2
+    width = att.shape[1]
+    half, half_ff = width // 2, active.shape[1] // 2
+    both = lambda left, left_other, cols: dense_tn(left, right[:, cols]) + dense_tn(left_other, right_other[:, cols])
+    rows = down_blocks.shape[1]
+    each = width // rows
+    for j in range(active.shape[1] // width):
+        cols = slice(j * width, (j + 1) * width)
+        grad = both(active[:, cols], active_other[:, cols], slice(half_ff + half, half_ff + width))
+        down_blocks[j * each : (j + 1) * each] = grad.astype(bf16).reshape(each, rows, half)
+    split_blocks(down_blocks, down_kept, down_sent, seat[CTX] % 2)
+    rows = up_blocks.shape[1]
+    tile = half_ff // 2
     for j in range(2):
         cols = slice(j * tile, (j + 1) * tile)
-        grad = dense_tn(two[...], right[:, cols]) + dense_tn(two_other[...], right_other[:, cols])
-        blocks[:, :, cols] = grad.astype(bf16).reshape(-1, rows, tile)
-    grad = dense_tn(att[...], right[:, cut:]) + dense_tn(att_other[...], right_other[:, cut:])
-    blocks[:, :, cut:] = grad.astype(bf16).reshape(-1, rows, size - cut)
-    split_blocks_first(blocks, kept, sent, seat[1] // 2)
-
-
-def halves_of(kernel, seat, arrays, count, rows, size, flops):
-    shape = jax.ShapeDtypeStruct((count // 2, rows, size), bf16)
-    return one_step(
-        kernel,
-        in_specs=[SMEM_SPEC] + [VMEM_SPEC] * len(arrays),
-        out_specs=[VMEM_SPEC, VMEM_SPEC, SMEM_SPEC],
-        out_shape=[shape, shape, TOKEN],
-        scratch_shapes=[pltpu.VMEM((count, rows, size), bf16)],
+        up_blocks[:, :, cols] = both(two[...], two_other[...], cols).astype(bf16).reshape(-1, rows, tile)
+    cols = slice(half_ff, half_ff + half)
+    up_blocks[:, :, cols] = both(att[...], att_other[...], cols).astype(bf16).reshape(-1, rows, half)
+    split_blocks_first(up_blocks, up_kept, up_sent, seat[CTX] // 2)
+
+
+def products(seat, arrays, count, rows):
+    ff, width = arrays[0].shape[1], arrays[4].shape[1]
+    down, up = (ff // count, width // 2), (rows, (ff + width) // 2)
+    shape = lambda x: jax.ShapeDtypeStruct((count // 2, *x), bf16)
+    outs = one_step(
+        products_kernel,
+        in_specs=[SMEM_SPEC] + [FAR_SPEC] * 6 + [VMEM_SPEC] * 2,
+        out_specs=[FAR_SPEC] * 4 + [SMEM_SPEC],
+        out_shape=[shape(down)] * 2 + [shape(up)] * 2 + [TOKEN],
+        scratch_shapes=[pltpu.VMEM((count, *down), bf16), pltpu.VMEM((count, *up), bf16)],
         compiler_params=pltpu.CompilerParams(vmem_limit_bytes=SMALL_VMEM),
     )(seat, *arrays)
-
-
-def second_kernel(seat, token_in, *refs, bits, passing, closing):
+    return FastSum(*outs[:2], (1, 2)), FastSum(*outs[2:4], (2, 1)), outs[4]
+
+
+def second_kernel(seat, token_in, *refs, bits, passing, closing, behind):
     count = len(bits)
-    refs = refs[passing:]
+    refs = refs[behind + passing :]
     parts, refs = refs[2 * count : 2 * count + closing], refs[: 2 * count] + refs[2 * count + closing :]
     refs[4 * count][0] = token_in[0]
     if closing:
@@ -625,9 +656,12 @@
             at += size
 
 
-def halved_kernel(seat, token_in, *refs, count, rows, passing):
+def halved_kernel(seat, token_in, *refs, count, rows, passing, closing):
     refs = refs[passing:]
+    parts, refs = refs[2 * count : 2 * count + closing], refs[: 2 * count] + refs[2 * count + closing :]
     kept_out, sent_out, token_ref = refs[2 * count : 2 * count + 3]
+    if closing:
+        refs[2 * count + 3][...] = functools.reduce(jnp.add, [x[...].astype(f32) for x in parts])
     token_ref[0] = token_in[0]
     mine = seat[2] % 2
     at = 0
@@ -656,28 +690,29 @@
         self.kept, self.got = kept, xor_permute(sent, "dp", 1)
 
 
-def halved_step(seat, token, sums, rows, passing):
-    specs_in, specs_out, shapes, aliases = handed_on(passing, 2, 3)
+def halved_step(seat, token, sums, rows, passing, closing, spec):
+    closed = [jax.ShapeDtypeStruct(x.shape, f32) for x in closing[:1]]
+    specs_in, specs_out, shapes, aliases = handed_on(passing, 2, 3 + len(closed))
     size = sum(x.kept.shape[1] // rows * x.kept.shape[2] for x in sums)
     shape = jax.ShapeDtypeStruct((2, rows, size), bf16)
-    kept, sent, token, *passing = one_step(
-        functools.partial(halved_kernel, count=len(sums), rows=rows, passing=len(passing)),
-        in_specs=[SMEM_SPEC] * 2 + specs_in + [VMEM_SPEC] * (2 * len(sums)),
-        out_specs=[VMEM_SPEC] * 2 + [SMEM_SPEC] + specs_out,
-        out_shape=[shape, shape, TOKEN] + shapes,
+    kept, sent, token, *rest = one_step(
+        functools.partial(halved_kernel, count=len(sums), rows=rows, passing=len(passing), closing=len(closing)),
+        in_specs=[SMEM_SPEC] * 2 + specs_in + [spec] * (2 * len(sums) + len(closing)),
+        out_specs=[spec, VMEM_SPEC, SMEM_SPEC] + [FAR_SPEC] * len(closed) + specs_out,
+        out_shape=[shape, shape, TOKEN] + closed + shapes,
         input_output_aliases=aliases,
         compiler_params=pltpu.CompilerParams(vmem_limit_bytes=SMALL_VMEM),
-    )(seat, token, *passing, *[y for x in sums for y in (x.kept, x.got)])
-    return Halved(kept, sent), token, tuple(passing)
-
-
-def middle_step(seat, token, halved, passing):
+    )(seat, token, *passing, *[y for x in sums for y in (x.kept, x.got)], *closing)
+    return Halved(kept, sent), token, tuple(rest[len(closed) :]), rest[0] if closed else None
+
+
+def middle_step(seat, token, halved, passing, spec):
     specs_in, specs_out, shapes, aliases = handed_on(passing, 2, 3)
     shape = jax.ShapeDtypeStruct
     total, sent, token, *passing = one_step(
         functools.partial(middle_kernel, passing=len(passing)),
-        in_specs=[SMEM_SPEC] * 2 + specs_in + [VMEM_SPEC] * 2,
-        out_specs=[VMEM_SPEC] * 2 + [SMEM_SPEC] + specs_out,
+        in_specs=[SMEM_SPEC] * 2 + specs_in + [spec] * 2,
+        out_specs=[FAR_SPEC, VMEM_SPEC, SMEM_SPEC] + specs_out,
         out_shape=[shape(halved.kept.shape[1:], f32), shape(halved.kept.shape[1:], bf16), TOKEN] + shapes,
         input_output_aliases=aliases,
         compiler_params=pltpu.CompilerParams(vmem_limit_bytes=SMALL_VMEM),
@@ -687,8 +722,8 @@
 
 
 class FastSum:
-    def __init__(self, kept, sent, bits, token=None):
-        self.kept, self.bits, self.token = kept, bits, token
+    def __init__(self, kept, sent, bits):
+        self.kept, self.bits = kept, bits
         self.got = xor_permute(sent, "ctx", bits[0])
 
     def start(self):
@@ -717,18 +752,18 @@
     return outs[0], outs[1:]
 
 
-def second_step(seat, token, sums, passing, closing):
+def second_step(seat, token, sums, passing, closing, behind, spec):
     closed = [jax.ShapeDtypeStruct(x.shape, f32) for x in closing[:1]]
-    specs_in, specs_out, shapes, aliases = handed_on(passing, 2, 2 * len(sums) + 1 + len(closed))
+    specs_in, specs_out, shapes, aliases = handed_on(passing, 2 + len(behind), 2 * len(sums) + 1 + len(closed))
     shape = lambda x: jax.ShapeDtypeStruct((x.shape[0] // 2,) + x.shape[1:], bf16)
     outs = one_step(
-        functools.partial(second_kernel, bits=[x.bits[1] for x in sums], passing=len(passing), closing=len(closing)),
-        in_specs=[SMEM_SPEC] * 2 + specs_in + [VMEM_SPEC] * (2 * len(sums) + len(closing)),
-        out_specs=[VMEM_SPEC] * (2 * len(sums)) + [SMEM_SPEC] + [VMEM_SPEC] * len(closed) + specs_out,
+        functools.partial(second_kernel, bits=[x.bits[1] for x in sums], passing=len(passing), closing=len(closing), behind=len(behind)),
+        in_specs=[SMEM_SPEC] * 2 + [ANY_SPEC] * len(behind) + specs_in + [spec] * (2 * len(sums) + len(closing)),
+        out_specs=[VMEM_SPEC] * (2 * len(sums)) + [SMEM_SPEC] + [FAR_SPEC] * len(closed) + specs_out,
         out_shape=[shape(x.kept) for x in sums for _ in range(2)] + [TOKEN] + closed + shapes,
         input_output_aliases=aliases,
         compiler_params=pltpu.CompilerParams(vmem_limit_bytes=SMALL_VMEM),
-    )(seat, token, *passing, *[y for x in sums for y in (x.kept, x.got)], *closing)
+    )(seat, token, *behind, *passing, *[y for x in sums for y in (x.kept, x.got)], *closing)
     for i, x in enumerate(sums):
         x.kept, x.sent = outs[2 * i], outs[2 * i + 1]
     outs = outs[2 * len(sums) :]
@@ -813,20 +848,22 @@
     )(seat, keep, got)
 
 
-def mix_grads_kernel(small, pre, post):
+def mix_grads_kernel(small, _, pre, post):
     rows = lax.broadcasted_iota(jnp.int32, (HEADS, small.shape[1]), 0)
     cols = lax.broadcasted_iota(jnp.int32, (HEADS, small.shape[1]), 1)
     heads = jnp.where(cols // HEAD == rows, 1.0, 0.0).astype(f32)
     dot = lambda a, b: lax.dot_general(
         a, b, (((1,), (1,)), ((), ())), precision=lax.Precision.HIGHEST, preferred_element_type=f32
     )
-    pre[...] = 0.125 * dot(heads, small[2 : 2 + HEADS, :])
-    post[...] = dot(small[2 + HEADS : 2 + 2 * HEADS, :], heads)
-
-
-def mix_grads(small):
-    out = jax.ShapeDtypeStruct((HEADS, HEADS), f32)
-    return one_step(mix_grads_kernel, in_specs=[VMEM_SPEC], out_specs=[VMEM_SPEC] * 2, out_shape=[out, out])(small)
+    pre[:, 0, :] = 0.125 * dot(heads, small[2 : 2 + HEADS, :])
+    post[:, 0, :] = dot(small[2 + HEADS : 2 + 2 * HEADS, :], heads)
+
+
+def mix_grads(small, behind):
+    out = jax.ShapeDtypeStruct((HEADS, 1, HEADS), f32)
+    return one_step(
+        mix_grads_kernel, in_specs=[VMEM_SPEC, ANY_SPEC], out_specs=[VMEM_SPEC] * 2, out_shape=[out, out]
+    )(small, behind)
 
 
 def total_of(part, gots):
@@ -838,11 +875,11 @@
 def join_kernel(
     seat, token_in, keep_ref, got_ref, normed_ref, own, own_other, dq, dq_other, joint_own, joint_got,
     small_own, small_got, dn_kept, dn_sent, dnq_ref, a_kept, a_sent, b_kept, b_sent, gain_grad_ref, token_ref,
-    kv_w, q_w, dkv, dn, a_blocks, b_blocks, sems,
+    kv_w, q_w, dkv, dn, a_blocks, b_blocks, sems, *, layer,
 ):
     token_ref[0] = token_in[0]
     width = dkv.shape[1]
-    section, which = seat[0], seat[3]
+    section, which = seat[SECTION], seat[WHICH + layer]
     for i, ref in enumerate((joint_own, joint_got)):
 
         @pl.when(which == i)
@@ -882,7 +919,7 @@
             out[i * blk : (i + 1) * blk, :] = dn[pl.ds(pl.multiple_of(at * blk, blk), blk), :]
 
 
-def join(seat, token, arrays, joints, smalls, count, rows):
+def join(seat, layer, token, arrays, joints, smalls, count, rows):
     seq, width = arrays[0].shape
     own_count = arrays[3].shape[0]
     size_a = 2 * width // 3
@@ -891,8 +928,13 @@
     a_shape, b_shape = (shape((count // 2, rows, size), bf16) for size in (size_a, size_b))
     half_rows = shape((seq // 2, width), bf16)
     return one_step(
-        join_kernel,
-        in_specs=[SMEM_SPEC] * 2 + [VMEM_SPEC] * 7 + [HBM_SPEC] * 2 + [VMEM_SPEC] * 2,
+        functools.partial(join_kernel, layer=layer),
+        in_specs=[SMEM_SPEC] * 2
+        + [VMEM_SPEC] * 2
+        + [FAR_SPEC] * 3
+        + [VMEM_SPEC] * 2
+        + [HBM_SPEC] * 2
+        + [VMEM_SPEC] * 2,
         out_specs=[VMEM_SPEC] * 8 + [SMEM_SPEC],
         out_shape=[half_rows, half_rows, shape((own_count, width), f32)]
         + [a_shape, a_shape, b_shape, b_shape, shape((1, width), f32), TOKEN],
@@ -1019,24 +1061,22 @@
     low_start = core * blk
     high_start = (2 * n - 1 - core) * blk
     bk = min(256, seq)
-    places = [
-        jnp.stack([length, (s != layer).astype(jnp.int32), low_start, high_start, s]).astype(jnp.int32)
-        for layer in range(2)
-    ]
+    cores1 = [(xi ^ d) * 2 + side for side in (s, 1 - s) for d in range(chips)]
+    blocks1 = [b for c in cores1 for b in (c, 2 * n - 1 - c)]
+    info = [s, ctx, lax.axis_index("dp"), length, low_start, high_start, s != 0, s != 1, *blocks0, *blocks1]
+    info = jnp.stack([jnp.asarray(x, jnp.int32) for x in info])
 
     def gather_row(x):
         got = [x] + [xor_permute(x, "ctx", d) for d in range(1, chips)]
-        cores = [(xi ^ d) * 2 + side for side in (s, 1 - s) for d in range(chips)]
-        return got + [swap_section(y) for y in got], [b for c in cores for b in (c, 2 * n - 1 - c)]
-
-    def forward(layer, pieces, blocks, meanwhile):
-        place = jnp.concatenate([places[layer], jnp.stack(blocks).astype(jnp.int32)])
+        return got + [swap_section(y) for y in got]
+
+    def forward(layer, pieces, meanwhile):
         attended, q, normed_own, x_own, token, normed_all, k, v, u, lse = attend(
-            place, pieces, 2 * blk, smalls, joints, bk
+            info, layer, pieces, 2 * blk, smalls, joints, bk
         )
         weights = [x for pair in (mixers, ups, downs) for x in pair]
         out, hidden, normed_two, upward, active, token = feed(
-            places[layer][1:2], x_own, attended, smalls, weights, ff, meanwhile
+            info, layer, x_own, attended, smalls, weights, ff, meanwhile
         )
         rows = [(x, swap_section(x)) for x in (active, normed_two, attended, normed_own)]
         return out, (x_own, q, k, v, u, lse, hidden, upward, rows, normed_all)
@@ -1054,15 +1094,17 @@
 
     fast = n == 4 and dp_count == 4 and shard % 16 == 0
     count = dp_count * n
-    seats = [jnp.stack([s, ctx, lax.axis_index("dp"), s != layer]).astype(jnp.int32) for layer in range(2)]
 
     class Slow:
-        def first(left, right, backwards):
-            one = Summer([blocks_of(product(a, b)) for a, b in zip(left, right)], backwards)
-            one.token = token_after(*one.send()).reshape(1)
-            return one
-
-        def second(token, sums, passing=(), closing=()):
+        def first(rows, keep, other):
+            active, two, att, _ = rows
+            cut, end = ff // 2, (ff + width) // 2
+            of = lambda *cols: (keep[:, slice(*cols)], other[:, slice(*cols)])
+            down_sum = Summer([blocks_of(product(active, of(end, None)))], False)
+            up_sum = Summer([blocks_of(product(two, of(0, cut))), blocks_of(product(att, of(cut, end)))], True)
+            return down_sum, up_sum, token_after(*down_sum.send(), *up_sum.send()).reshape(1)
+
+        def second(token, sums, passing=(), closing=(), behind=()):
             for one in sums:
                 one.add(token[0])
             return token, passing, total_of(closing[0], closing[1:]) if closing else None
@@ -1075,70 +1117,52 @@
             one.parts = (one.total, *one.got)
             return one, token, passing
 
-        halved = last
+        def halved(token, sums, passing=(), closing=()):
+            return *Slow.last(token, sums, passing), total_of(closing[0], closing[1:]) if closing else None
 
         def middle(token, one, passing=()):
             return token, passing
 
     class Fast:
-        def first(left, right, backwards):
-            flat = [x for pair in left for x in pair]
-            if backwards:
-                arrays, size, rows = flat + list(right), (ff + width) // 2, shard
-            else:
-                arrays, size, rows = flat + list(right), width // 2, ff // count
-            flops = 4 * flat[0].shape[0] * rows * count * size
-            kernel = up_kernel if backwards else down_kernel
-            kept, sent, token = halves_of(kernel, seats[0], arrays, count, rows, size, flops)
-            return FastSum(kept, sent, (2, 1) if backwards else (1, 2), token)
-
-        def second(token, sums, passing=(), closing=()):
-            return second_step(seats[0], token, sums, passing, closing)
+        def first(rows, keep, other):
+            return products(info, (*rows[0], *rows[1], *rows[2], keep, other), count, shard)
+
+        def second(token, sums, passing=(), closing=(), behind=()):
+            return second_step(info, token, sums, passing, closing, behind, VMEM_SPEC if behind else FAR_SPEC)
 
         def last(token, sums, passing=()):
-            part, gots, token, passing = last_step(seats[0], token, sums, shard, passing)
+            part, gots, token, passing = last_step(info, token, sums, shard, passing)
             one = types.SimpleNamespace(parts=(part, *gots))
             return one, token, passing
 
-        def halved(token, sums, passing=()):
-            return halved_step(seats[0], token, sums, shard, passing)
+        def halved(token, sums, passing=(), closing=()):
+            return halved_step(info, token, sums, shard, passing, closing, VMEM_SPEC if closing else FAR_SPEC)
 
         def middle(token, one, passing=()):
-            return middle_step(seats[0], token, one, passing)
+            return middle_step(info, token, one, passing, FAR_SPEC if passing else VMEM_SPEC)
 
     steps = Fast if fast else Slow
 
     def backward(layer, dy, kept, earlier):
         x_own, q, k, v, u, lse, hidden, upward, rows, normed_all = kept
-        rows_active, rows_two, rows_attended, rows_normed = rows
+        rows_normed = rows[3]
         here = s == layer
         gain_a = jnp.where(here, smalls[0][GAIN_A], smalls[1][GAIN_A])
-        dy_other = swap_section(dy)
-        if fast:
-            down_sum = steps.first([rows_active], (dy, dy_other), False)
-        else:
-            down_sum = steps.first([rows_active], [(half(dy, s), half(dy_other, s))], False)
         earlier[0]()
         weights = [x for pair in (mixers, ups, downs) for x in pair]
         keep, send, dhidden, datt, gain_b_grad, token = feed_back(
-            jnp.stack([s != layer, s]).astype(jnp.int32), dy, upward, hidden, smalls, weights, (down_sum.token,)
+            info, layer, dy, upward, hidden, smalls, weights, ()
         )
         token, (send,) = earlier[1](token, (send,))
-        other = swap_section(send)
-        if fast:
-            up_sum = steps.first([rows_two, rows_attended], (keep, other), True)
-        else:
-            cut = ff // 2
-            pairs = [(keep[:, :cut], other[:, :cut]), (keep[:, cut:], other[:, cut:])]
-            up_sum = steps.first([rows_two, rows_attended], pairs, True)
+        down_sum, up_sum, first_token = steps.first(rows, keep, swap_section(send))
         dq, dkv_keep, dkv_send, pre_rows, post_rows, token = attend_back(
-            places[layer], q, datt, u, lse, k, v, smalls, bk, (token, up_sum.token)
+            info, layer, q, datt, u, lse, k, v, smalls, bk, (token, first_token)
         )
         token, (dkv_send, dq) = earlier[2](token, (down_sum, up_sum), (dkv_send, dq))
         got, dq_other = swap_section(dkv_send), swap_section(dq)
         if fast:
             dn_kept, dn_sent, dnq, a_kept, a_sent, b_kept, b_sent, gain_a_grad, token = join(
-                seats[layer], token, (dkv_keep, got, normed_all, *rows_normed, dq, dq_other), joints, smalls, count, shard
+                info, layer, token, (dkv_keep, got, normed_all, *rows_normed, dq, dq_other), joints, smalls, count, shard
             )
             kv_sum, q_sum = FastSum(a_kept, a_sent, (1, 2)), FastSum(b_kept, b_sent, (2, 1))
             dn_kept, dn_sent = (x.reshape(chips, 2, blk, width) for x in (dn_kept, dn_sent))
@@ -1186,8 +1210,8 @@
     ones, twos = jnp.where(low_chip, halves[1], halves[0]), jnp.where(low_chip, halves[0], halves[1])
     one, two = lax.ppermute(ones, "ctx", there), lax.ppermute(twos, "ctx", here)
     dy1 = jnp.concatenate([jnp.where(m == 0, two, one), jnp.where(m == 0, one, two)])
-    x1, kept0 = forward(0, pieces0, blocks0, (one, two))
-    y, kept1 = forward(1, *gather_row(x1), ())
+    x1, kept0 = forward(0, pieces0, (one, two))
+    y, kept1 = forward(1, gather_row(x1), ())
 
     def send_home(x):
         x = x.reshape(2, blk, width)
@@ -1213,12 +1237,11 @@
         return token, passing
 
     def after_join(token, passing, sums):
-        state["big"], token, passing = steps.halved(token, sums, passing)
+        state["big"], token, passing, _ = steps.halved(token, sums, passing)
         return token, passing
 
     def after_low(token, low, sums):
-        token = token_after(token, low).reshape(1)
-        token, _, _ = steps.second(token, sums[2:])
+        token, _, _ = steps.second(token, sums[2:], behind=(low,))
         start(sums[2:])
         return token
 
@@ -1228,7 +1251,7 @@
     y_sent = send_home(y)
 
     def after_feed(token, passing):
-        state["joint1"], token, passing = steps.halved(token, [kv1, q1], (*passing, *y_sent))
+        state["joint1"], token, passing, _ = steps.halved(token, [kv1, q1], (*passing, *y_sent))
         token, (passing, *state["y"]) = steps.middle(token, state["big"], passing)
         return token, (passing,)
 
@@ -1239,13 +1262,12 @@
         return token, passing
 
     def after_join(token, passing, sums):
-        state["big0"], token, passing = steps.halved(token, sums, passing)
+        state["big0"], token, passing, state["joint1"] = steps.halved(token, sums, passing, state["joint1"].parts)
         state["token"] = token
         return token, passing
 
     def after_low(token, low, sums):
-        token = token_after(token, low).reshape(1)
-        token, _, _ = steps.second(token, sums[2:])
+        token, _, _ = steps.second(token, sums[2:], behind=(low,))
         start(sums[2:])
         return steps.middle(token, state["big0"])[0]
 
@@ -1256,11 +1278,10 @@
     dx0 = dx0.astype(bf16)
     dx_home = at_home(*send_home(dx0))
     y_home = at_home(*state["y"])
-    token = token_after(dx0).reshape(1)
 
     small_got = swap_section(jnp.where(s == 0, small1, small0))
     small = jnp.where(s == 0, small0, small1) + small_got
-    joint0, last_token, _ = steps.last(token, [kv0, q0])
+    joint0, last_token, _ = steps.last(token, [kv0, q0], (dx0,))
     small = all_sum(small, (state["token"][0], early[0], token[0], last_token[0]))
 
     got = swap_section(jnp.where(s == 0, y_home, dx_home))
@@ -1271,15 +1292,16 @@
 
     at = (lax.axis_index("dp") * n + ctx) * shard
     gain_a_out, gain_b_out = (lax.dynamic_slice_in_dim(small[i], at, shard, 0) for i in range(2))
-    pre_out, post_out = mix_grads(small)
     half_d, half_ff, times = width // 2, ff // 2, ff // width
     if fast:
-        groups = (state["big0"].parts, joint0.parts, (state["big1"],), state["joint1"].parts)
-        keep, send = final_parts(seats[0], groups)
-        joint_out, mixer_out, up_out, down_out = final_outs(seats[0], keep, swap_section(send), width, ff)
+        groups = (state["big0"].parts, joint0.parts, (state["big1"],), (state["joint1"],))
+        keep, send = final_parts(info, groups)
+        behind = keep
+        joint_out, mixer_out, up_out, down_out = final_outs(info, keep, swap_section(send), width, ff)
     else:
-        big0, joint0, joint1 = (total_of(x.parts[0], x.parts[1:]) for x in (state["big0"], joint0, state["joint1"]))
-        pairs = ((big0, state["big1"]), (joint0, joint1))
+        behind = small
+        big0, joint0 = (total_of(x.parts[0], x.parts[1:]) for x in (state["big0"], joint0))
+        pairs = ((big0, state["big1"]), (joint0, state["joint1"]))
         outs = []
         for at_zero, at_one in pairs:
             other = swap_section(jnp.where(s == 0, at_one, at_zero))
@@ -1294,12 +1316,13 @@
         up_out = side((big_a, at, half_ff), (big_b, at, half_ff))
         mixer_out = side((big_a, at + half_ff, half_d), (big_b, at + half_ff, half_d))
         joint_out = side((joint_a, width, half_d), (joint_b, width, half_d), (joint_a, 0, width), (joint_b, 0, width))
+    pre_out, post_out = (x.transpose(1, 0, 2) for x in mix_grads(small, behind))
     return (
         ends,
         gain_a_out[None],
         joint_out[None],
-        pre_out[None],
-        post_out[None],
+        pre_out,
+        post_out,
         mixer_out[None],
         gain_b_out[None],
         up_out[None],

time: 439 us -> 415 us (0.945)
  starting transfers between devices: 79.9 us -> 60.1 us
  other arithmetic: 9.86 us -> 17.6 us
  waiting for transfers between devices: 78.4 us -> 73.8 us
    pallas_call x2, Pallas kernels: 39.3 us -> 57.5 us  [attend_back(): pl.pallas_call(cost_estimate=SMALL_COST, kernel=functools.partial(attend_...]
    ppermute x35, starting transfers between devices: 59.4 us -> 43.3 us  [xor_permute(): lax.ppermute(x, axis, [(i, i ^ by) for i in range(lax.axis_size(axis))])]
    pallas_call x26 -> x24, Pallas kernels: 172 us -> 156 us  [run(): pl.pallas_call(kernel, cost_estimate=SMALL_COST, grid=(1,), in_specs=[who...]
    ppermute x35, waiting for transfers between devices: 61.7 us -> 56.2 us  [xor_permute(): lax.ppermute(x, axis, [(i, i ^ by) for i in range(lax.axis_size(axis))])]
    pallas_call x3 -> x0, Pallas kernels: 4.88 us -> none  [token_after(): pl.pallas_call(token_kernel, cost_estimate=SMALL_COST, in_specs=[SMEM_SPE...]
    unnamed x162 -> x218, local copies, waits for them, and re-layouts: 27.2 us -> 30.2 us
    ppermute x29 -> x27, waiting for transfers between devices: 16.6 us -> 17.2 us  [swap_section(): return lax.ppermute(x, 'section', [(0, 1), (1, 0)])]
  transfers between devices with their start and end apart: 70 -> 68, of which waited for: 29 -> 33; matrix products, arithmetic and copies ran while one was open for 6% -> 6% of each run, Pallas kernels for 29% -> 34%
where the time goes in v4:
time: 415 us; the launch traced here: 409 us
  Pallas kernels  214 us (52%)
  waiting for transfers between devices  73.8 us (18%)
  starting transfers between devices  60.1 us (14%)
  local copies, waits for them, and re-layouts  37.1 us (9%)
  other arithmetic  17.6 us (4%)
  between operations  5.57 us (1%)
    pallas_call x24, Pallas kernels, run(): pl.pallas_call(kernel, cost_estimate=SMALL_COST, grid=(1,), in_specs=[who...  156 us
    pallas_call x2, Pallas kernels, attend_back(): pl.pallas_call(cost_estimate=SMALL_COST, kernel=functools.partial(attend_...  57.5 us
    ppermute x35, waiting for transfers between devices, xor_permute(): lax.ppermute(x, axis, [(i, i ^ by) for i in range(lax.axis_size(axis))])  56.2 us
    ppermute x35, starting transfers between devices, xor_permute(): lax.ppermute(x, axis, [(i, i ^ by) for i in range(lax.axis_size(axis))])  43.3 us
    unnamed x218, local copies, waits for them, and re-layouts  30.2 us
    ppermute x27, waiting for transfers between devices, swap_section(): return lax.ppermute(x, 'section', [(0, 1), (1, 0)])  17.2 us
  transfers between devices with their start and end apart: 68, of which 33 were waited for; matrix products, arithmetic and copies ran while one was open for 6% of the time, Pallas kernels for 34%

profile of v4, /device:TPU:0, one launch (start us, length us, event | category | flops | bytes accessed | tf_op | source)
XLA Modules:
  0.0 409.5 jit_solution(12737289416823966606)
XLA Ops:
  15.4 4.8 %collective-permute-done.6.rest_3_ = bf16[128,768]{1,0:T(8,128)(2,1)S(1)} collective-permute-done((bf16[128,768]{1,0:T(8,128)(2,1)S(1)}, bf16[128,768]{1,0:T(8,128)(2,1)S(1)}, u32[]{:S(2)}, u32[]{:S(2)}) %collective-permute-start.6) | collective-permute-done | bytes 196640 | tf_op jit(solution)/shard_map/ppermute | solution.py:543
  26.3 4.8 %collective-permute-start.1 = (bf16[128,768]{1,0:T(8,128)(2,1)S(1)}, bf16[128,768]{1,0:T(8,128)(2,1)S(1)}, u32[]{:S(2)}, u32[]{:S(2)}) collective-permute-start(bf16[128,768]{1,0:T(8,128)(2,1)S(1)} %get-tuple-element.317), channel_id=1, source_target_pairs={{0,2},{1,3},{3,0},{2,1},{4,6},{5,7},{7,4},{6,5},{8,10},{9,11},{11,... | collective-permute-start | bytes 589832 | tf_op jit(solution)/shard_map/ppermute | solution.py:1211
  33.7 23.3 %shard_map.178 = (bf16[256,768]{1,0:T(8,128)(2,1)}, bf16[256,768]{1,0:T(8,128)(2,1)}, bf16[256,768]{1,0:T(8,128)(2,1)}, bf16[256,768]{1,0:T(8,128)(2,1)}, s32[1]...) custom-call(s32[24]{0:T(128)} %stack.141.info.seat, ...), custom_call_target="tpu_custom_call" | custom-call | tf_op jit(solution)/shard_map/pallas_call | solution.py:187
  62.0 10.0 %shard_map.179 = (bf16[256,768]{1,0:T(8,128)(2,1)S(1)}, f32[256,768]{1,0:T(8,128)}, bf16[256,768]{1,0:T(8,128)(2,1)}, f32[256,3072]{1,0:T(8,128)}, bf16[256,3072]{1,0:T(8,128)(2,1)}, /*index=5*/s32[1]{0:T(128)}) custom-call(s32[24]{0:T(128)S(1)} %copy-done.46, bf16[256,768]{1,0:T(8,128)(2,1)S(1)} %copy-done.13, bf16[256,768]{1,0:T(8,128)(2,1)S(1)} %copy-done.20, ...), custom_call_target="tpu_custom_call" | custom-call | tf_op jit(solution)/shard_map/pallas_call | solution.py:187
  72.7 10.1 %collective-permute-done.11.rest_1_ = bf16[256,768]{1,0:T(8,128)(2,1)S(1)} collective-permute-done((bf16[256,768]{1,0:T(8,128)(2,1)S(1)}, bf16[256,768]{1,0:T(8,128)(2,1)S(1)}, u32[]{:S(2)}, u32[]{:S(2)}) %collective-permute-start.11) | collective-permute-done | bytes 393248 | tf_op jit(solution)/shard_map/ppermute | solution.py:543
  85.2 23.1 %shard_map.180 = (bf16[256,768]{1,0:T(8,128)(2,1)}, bf16[256,768]{1,0:T(8,128)(2,1)}, bf16[256,768]{1,0:T(8,128)(2,1)}, bf16[256,768]{1,0:T(8,128)(2,1)}, s32[1]...) custom-call(s32[24]{0:T(128)} %stack.141.info.seat, ...), custom_call_target="tpu_custom_call" | custom-call | tf_op jit(solution)/shard_map/pallas_call | solution.py:187
  110.3 10.0 %shard_map.181 = (bf16[256,768]{1,0:T(8,128)(2,1)S(1)}, f32[256,768]{1,0:T(8,128)}, bf16[256,768]{1,0:T(8,128)(2,1)}, f32[256,3072]{1,0:T(8,128)}, bf16[256,3072]{1,0:T(8,128)(2,1)}, /*index=5*/s32[1]{0:T(128)}) custom-call(s32[24]{0:T(128)S(1)} %copy-done.47, bf16[256,768]{1,0:T(8,128)(2,1)S(1)} %copy-done.15, bf16[256,768]{1,0:T(8,128)(2,1)S(1)} %copy-done.22, ...), custom_call_target="tpu_custom_call" | custom-call | tf_op jit(solution)/shard_map/pallas_call | solution.py:187
  121.3 11.1 %shard_map.182 = (bf16[256,2304]{1,0:T(8,128)(2,1)S(1)}, bf16[256,2304]{1,0:T(8,128)(2,1)S(1)}, f32[256,768]{1,0:T(8,128)}, bf16[256,768]{1,0:T(8,128)(2,1)S(1)}, f32[1,768]{1,0:T(1,128)S(1)}, /*index=5*/s32[1]{0:T(128)}) custom-call(s32[24]{0:T(128)S(1)} %copy-done.47, bf16[256,768]{1,0:T(8,128)(2,1)S(1)} %pad_maximum_fusion.2.dy_ref, ...), custom_call_target="tpu_custom_call" | custom-call | tf_op jit(solution)/shard_map/pallas_call | solution.py:187
  138.4 8.7 %shard_map.183 = (bf16[8,192,384]{2,1,0:T(8,128)(2,1)}, bf16[8,192,384]{2,1,0:T(8,128)(2,1)}, bf16[8,48,1920]{2,1,0:T(8,128)(2,1)}, bf16[8,48,1920]{2,1,0:T(8,128)(2,1)}, s32[1]{0:T(128)}) custom-call(s32[24]{0:T(128)S(1)} %copy-done.47, bf16[256,3072]{1,0:T(8,128)(2,1)} %get-tuple-element.171.active, bf16[256,3072]{1,0:T(8,128)(2,1)} %copy-done.69, ...), custom_call_target="tpu_custom_call" | custom-call | tf_op jit(solution)/shard_map/pallas_call | solution.py:187
  147.8 28.7 %shard_map.184 = (bf16[256,768]{1,0:T(8,128)(2,1)}, bf16[1024,768]{1,0:T(8,128)(2,1)}, bf16[1024,768]{1,0:T(8,128)(2,1)}, f32[12,768]{1,0:T(8,128)}, f32[12,768]{1,0:T(8,128)}, /*index=5*/s32[1]{0:T(128)}) custom-call(s32[24]{0:T(128)} %stack.141.info.seat, bf16[256,768]{1,0:T(8,128)(2,1)} %get-tuple-element.164.q_ref, bf16[256,768]{1,0:T(8,128)(2,1)} %copy-done.40, ...), custom_call_target="tpu_custom_call" | custom-call | tf_op jit(solution)/shard_map/pallas_call | solution.py:489
  176.5 5.4 %collective-permute-done.19.refs_5_ = bf16[8,48,1920]{2,1,0:T(8,128)(2,1)S(1)} collective-permute-done((bf16[8,48,1920]{2,1,0:T(8,128)(2,1)}, bf16[8,48,1920]{2,1,0:T(8,128)(2,1)S(1)}, u32[]{:S(2)}, u32[]{:S(2)}) %collective-permute-start.19) | collective-permute-done | bytes 1474592 | tf_op jit(solution)/shard_map/ppermute | solution.py:543
  185.5 4.3 %shard_map.185 = (bf16[4,192,384]{2,1,0:T(8,128)(2,1)S(1)}, bf16[4,192,384]{2,1,0:T(8,128)(2,1)S(1)}, bf16[4,48,1920]{2,1,0:T(8,128)(2,1)S(1)}, bf16[4,48,1920]{...) custom-call(s32[24]{0:T(128)S(1)} %copy-done.48, ...), custom_call_target="tpu_custom_call", output_to_operand_aliasing={{5}: (2, {}), {6}: (3, {})} | custom-call | tf_op jit(solution)/shard_map/pallas_call | solution.py:187
  196.4 8.4 %shard_map.186 = (bf16[512,768]{1,0:T(8,128)(2,1)S(1)}, bf16[512,768]{1,0:T(8,128)(2,1)S(1)}, f32[256,768]{1,0:T(8,128)S(1)}, bf16[8,48,512]{2,1,0:T(8,128)(2,1)...) custom-call(s32[24]{0:T(128)S(1)} %copy-done.48, ...), custom_call_target="tpu_custom_call" | custom-call | tf_op jit(solution)/shard_map/pallas_call | solution.py:187
  211.5 3.4 shard_map.187
  224.1 5.3 %collective-permute-done.26.refs_2_ = bf16[8,48,512]{2,1,0:T(8,128)(2,1)S(1)} collective-permute-done((bf16[8,48,512]{2,1,0:T(8,128)(2,1)}, bf16[8,48,512]{2,1,0:T(8,128)(2,1)S(1)}, u32[]{:S(2)}, u32[]{:S(2)}) %collective-permute-start.26) | collective-permute-done | bytes 393248 | tf_op jit(solution)/shard_map/ppermute | solution.py:543
  240.3 3.3 collective-permute-start.31
  243.9 10.9 %shard_map.189 = (bf16[256,2304]{1,0:T(8,128)(2,1)S(1)}, bf16[256,2304]{1,0:T(8,128)(2,1)S(1)}, f32[256,768]{1,0:T(8,128)}, bf16[256,768]{1,0:T(8,128)(2,1)S(1)}, f32[1,768]{1,0:T(1,128)S(1)}, /*index=5*/s32[1]{0:T(128)}) custom-call(s32[24]{0:T(128)S(1)} %copy-done.48, bf16[256,768]{1,0:T(8,128)(2,1)S(1)} %fusion.16.dy_ref, ...), custom_call_target="tpu_custom_call" | custom-call | tf_op jit(solution)/shard_map/pallas_call | solution.py:187
  266.1 8.6 %shard_map.192 = (bf16[8,192,384]{2,1,0:T(8,128)(2,1)}, bf16[8,192,384]{2,1,0:T(8,128)(2,1)}, bf16[8,48,1920]{2,1,0:T(8,128)(2,1)}, bf16[8,48,1920]{2,1,0:T(8,128)(2,1)}, s32[1]{0:T(128)}) custom-call(s32[24]{0:T(128)S(1)} %copy-done.48, bf16[256,3072]{1,0:T(8,128)(2,1)} %get-tuple-element.227.active, ...), custom_call_target="tpu_custom_call" | custom-call | tf_op jit(solution)/shard_map/pallas_call | solution.py:187
  279.6 28.8 %shard_map.193 = (bf16[256,768]{1,0:T(8,128)(2,1)}, bf16[1024,768]{1,0:T(8,128)(2,1)}, bf16[1024,768]{1,0:T(8,128)(2,1)}, f32[12,768]{1,0:T(8,128)}, f32[12,768]{1,0:T(8,128)}, /*index=5*/s32[1]{0:T(128)}) custom-call(s32[24]{0:T(128)} %stack.141.info.seat, bf16[256,768]{1,0:T(8,128)(2,1)} %get-tuple-element.207.q_ref, bf16[256,768]{1,0:T(8,128)(2,1)} %copy-done.39, ...), custom_call_target="tpu_custom_call" | custom-call | tf_op jit(solution)/shard_map/pallas_call | solution.py:489
  313.0 4.9 %shard_map.194 = (bf16[4,192,384]{2,1,0:T(8,128)(2,1)S(1)}, bf16[4,192,384]{2,1,0:T(8,128)(2,1)S(1)}, bf16[4,48,1920]{2,1,0:T(8,128)(2,1)S(1)}, bf16[4,48,1920]{...) custom-call(s32[24]{0:T(128)S(1)} %copy-done.49, ...), custom_call_target="tpu_custom_call", output_to_operand_aliasing={{6}: (2, {}), {7}: (3, {})} | custom-call | tf_op jit(solution)/shard_map/pallas_call | solution.py:187
  326.9 7.6 %shard_map.196 = (bf16[512,768]{1,0:T(8,128)(2,1)S(1)}, bf16[512,768]{1,0:T(8,128)(2,1)S(1)}, f32[256,768]{1,0:T(8,128)S(1)}, bf16[8,48,512]{2,1,0:T(8,128)(2,1)...) custom-call(s32[24]{0:T(128)S(1)} %copy-done.49, ...), custom_call_target="tpu_custom_call" | custom-call | tf_op jit(solution)/shard_map/pallas_call | solution.py:187
  356.8 3.6 collective-permute-done.49.refs_2_
  388.7 3.0 collective-permute-start.65
  396.8 3.5 collective-permute-done.65.refs_4_
  (403 shorter events, 168.4 us)
Async XLA Ops:
  0.7 56.5 %collective-permute-start.10 = (bf16[1,3072,768]{2,1,0:T(8,128)(2,1)}, bf16[1,3072,768]{2,1,0:T(8,128)(2,1)}, u32[]{:S(2)}, u32[]{:S(2)}) collective-permute-start(bf16[1,3072,768]{2,1,0:T(8,128)(2,1)} %down_own.7), channel_id=1, source_target_pairs={{0,16},{16,0},{1,17},{17,1},{2,18},{18,2},{3,19},{19,3},{4,20},{20... | collective-permute-start | bytes 14155784 | tf_op jit(solution)/shard_map/ppermute | solution.py:539
  1.2 56.0 %collective-permute-start.9 = (bf16[1,768,3072]{2,1,0:T(8,128)(2,1)}, bf16[1,768,3072]{2,1,0:T(8,128)(2,1)}, u32[]{:S(2)}, u32[]{:S(2)}) collective-permute-start(bf16[1,768,3072]{2,1,0:T(8,128)(2,1)} %up_own.7), channel_id=1, source_target_pairs={{0,16},{16,0},{1,17},{17,1},{2,18},{18,2},{3,19},{19,3},{4,20},{20... | collective-permute-start | bytes 14155784 | tf_op jit(solution)/shard_map/ppermute | solution.py:539
  1.3 25.1 %collective-permute-start.3 = (bf16[1,768,2304]{2,1,0:T(8,128)(2,1)}, bf16[1,768,2304]{2,1,0:T(8,128)(2,1)}, u32[]{:S(2)}, u32[]{:S(2)}) collective-permute-start(bf16[1,768,2304]{2,1,0:T(8,128)(2,1)} %joint_own.7), channel_id=1, source_target_pairs={{0,16},{16,0},{1,17},{17,1},{2,18},{18,2},{3,19},{19,3},{4,20},{20... | collective-permute-start | bytes 10616840 | tf_op jit(solution)/shard_map/ppermute | solution.py:539
  10.9 46.2 %collective-permute-start.8 = (bf16[1,768,768]{2,1,0:T(8,128)(2,1)}, bf16[1,768,768]{2,1,0:T(8,128)(2,1)S(1)}, u32[]{:S(2)}, u32[]{:S(2)}) collective-permute-start(bf16[1,768,768]{2,1,0:T(8,128)(2,1)} %mixer_own.7), channel_id=1, source_target_pairs={{0,16},{16,0},{1,17},{17,1},{2,18},{18,2},{3,19},{19,3},{4,20},{20... | collective-permute-start | bytes 3538952 | tf_op jit(solution)/shard_map/ppermute | solution.py:539
  24.7 32.3 %collective-permute-start = (bf16[128,768]{1,0:T(8,128)(2,1)}, bf16[128,768]{1,0:T(8,128)(2,1)S(1)}, u32[]{:S(2)}, u32[]{:S(2)}) collective-permute-start(bf16[128,768]{1,0:T(8,128)(2,1)} %get-tuple-element.316), channel_id=1, source_target_pairs={{3,2},{2,3},{0,0},{1,1},{7,6},{6,7},{4,4},{5,5},{11,10},{10,11},{8... | collective-permute-start | bytes 589832 | tf_op jit(solution)/shard_map/ppermute | solution.py:1211
  26.3 30.8 %collective-permute-start.1 = (bf16[128,768]{1,0:T(8,128)(2,1)S(1)}, bf16[128,768]{1,0:T(8,128)(2,1)S(1)}, u32[]{:S(2)}, u32[]{:S(2)}) collective-permute-start(bf16[128,768]{1,0:T(8,128)(2,1)S(1)} %get-tuple-element.317), channel_id=1, source_target_pairs={{0,2},{1,3},{3,0},{2,1},{4,6},{5,7},{7,4},{6,5},{8,10},{9,11},{11,... | collective-permute-start | bytes 589832 | tf_op jit(solution)/shard_map/ppermute | solution.py:1211
  147.1 34.8 %collective-permute-start.19 = (bf16[8,48,1920]{2,1,0:T(8,128)(2,1)}, bf16[8,48,1920]{2,1,0:T(8,128)(2,1)S(1)}, u32[]{:S(2)}, u32[]{:S(2)}) collective-permute-start(bf16[8,48,1920]{2,1,0:T(8,128)(2,1)} %get-tuple-element.182), channel_id=1, source_target_pairs={{0,2},{1,3},{2,0},{3,1},{4,6},{5,7},{6,4},{7,5},{8,10},{9,11},{10,... | collective-permute-start | bytes 4423688 | tf_op jit(solution)/shard_map/ppermute | solution.py:543
  147.1 29.3 %collective-permute-start.18 = (bf16[8,192,384]{2,1,0:T(8,128)(2,1)}, bf16[8,192,384]{2,1,0:T(8,128)(2,1)S(1)}, u32[]{:S(2)}, u32[]{:S(2)}) collective-permute-start(bf16[8,192,384]{2,1,0:T(8,128)(2,1)} %get-tuple-element.180), channel_id=1, source_target_pairs={{0,1},{1,0},{2,3},{3,2},{4,5},{5,4},{6,7},{7,6},{8,9},{9,8},{10,11... | collective-permute-start | bytes 3538952 | tf_op jit(solution)/shard_map/ppermute | solution.py:543
  191.7 18.9 %collective-permute-start.24 = (bf16[4,48,1920]{2,1,0:T(8,128)(2,1)S(1)}, bf16[4,48,1920]{2,1,0:T(8,128)(2,1)S(1)}, u32[]{:S(2)}, u32[]{:S(2)}) collective-permute-start(bf16[4,48,1920]{2,1,0:T(8,128)(2,1)S(1)} %get-tuple-element.195), channel_id=1, source_target_pairs={{0,1},{1,0},{2,3},{3,2},{4,5},{5,4},{6,7},{7,6},{8,9},{9,8},{10,11... | collective-permute-start | bytes 2211848 | tf_op jit(solution)/shard_map/ppermute | solution.py:543
  216.4 48.9 %collective-permute-start.34 = (bf16[256,3072]{1,0:T(8,128)(2,1)}, bf16[256,3072]{1,0:T(8,128)(2,1)}, u32[]{:S(2)}, u32[]{:S(2)}) collective-permute-start(bf16[256,3072]{1,0:T(8,128)(2,1)} %get-tuple-element.227.active), channel_id=1, source_target_pairs={{0,16},{16,0},{1,17},{17,1},{2,18},{18,2},{3,19},{19,3},{4,20},{20... | collective-permute-start | bytes 4718600 | tf_op jit(solution)/shard_map/ppermute | solution.py:539
  220.4 17.5 %collective-permute-start.28 = (bf16[2,128,768]{2,1,0:T(8,128)(2,1)}, bf16[2,128,768]{2,1,0:T(8,128)(2,1)}, u32[]{:S(2)}, u32[]{:S(2)}) collective-permute-start(bf16[2,128,768]{2,1,0:T(8,128)(2,1)} %dynamic-slice_bitcast_fusion.1), channel_id=1, source_target_pairs={{0,1},{1,0},{2,3},{3,2},{4,5},{5,4},{6,7},{7,6},{8,9},{9,8},{10,11... | collective-permute-start | bytes 1179656 | tf_op jit(solution)/shard_map/ppermute | solution.py:543
  222.3 18.0 %collective-permute-start.29 = (bf16[128,768]{1,0:T(8,128)(2,1)}, bf16[128,768]{1,0:T(8,128)(2,1)S(1)}, u32[]{:S(2)}, u32[]{:S(2)}) collective-permute-start(bf16[128,768]{1,0:T(8,128)(2,1)} %get-tuple-element.321), channel_id=1, source_target_pairs={{2,0},{3,1},{0,3},{1,2},{6,4},{7,5},{4,7},{5,6},{10,8},{11,9},{8,1... | collective-permute-start | bytes 589832 | tf_op jit(solution)/shard_map/ppermute | solution.py:1218
  229.5 25.3 %collective-permute-start.30 = (bf16[128,768]{1,0:T(8,128)(2,1)}, bf16[128,768]{1,0:T(8,128)(2,1)S(1)}, u32[]{:S(2)}, u32[]{:S(2)}) collective-permute-start(bf16[128,768]{1,0:T(8,128)(2,1)} %get-tuple-element.320), channel_id=1, source_target_pairs={{2,3},{3,2},{0,0},{1,1},{6,7},{7,6},{4,4},{5,5},{10,11},{11,10},{8... | collective-permute-start | bytes 589832 | tf_op jit(solution)/shard_map/ppermute | solution.py:1219
  231.2 27.1 %collective-permute-start.33 = (bf16[2,48,3456]{2,1,0:T(8,128)(2,1)S(1)}, bf16[2,48,3456]{2,1,0:T(8,128)(2,1)}, u32[]{:S(2)}, u32[]{:S(2)}) collective-permute-start(bf16[2,48,3456]{2,1,0:T(8,128)(2,1)S(1)} %copy-done.58), channel_id=1, source_target_pairs={{0,4},{4,0},{8,12},{12,8},{1,5},{5,1},{9,13},{13,9},{2,6},{6,2},{1... | collective-permute-start | bytes 1990664 | tf_op jit(solution)/shard_map/ppermute | solution.py:543
  238.0 16.8 %collective-permute-start.32 = (bf16[4,48,640]{2,1,0:T(8,128)(2,1)S(1)}, bf16[4,48,640]{2,1,0:T(8,128)(2,1)S(1)}, u32[]{:S(2)}, u32[]{:S(2)}) collective-permute-start(bf16[4,48,640]{2,1,0:T(8,128)(2,1)S(1)} %get-tuple-element.219), channel_id=1, source_target_pairs={{0,1},{1,0},{2,3},{3,2},{4,5},{5,4},{6,7},{7,6},{8,9},{9,8},{10,11... | collective-permute-start | bytes 737288 | tf_op jit(solution)/shard_map/ppermute | solution.py:543
  274.8 34.6 %collective-permute-start.39 = (bf16[8,48,1920]{2,1,0:T(8,128)(2,1)}, bf16[8,48,1920]{2,1,0:T(8,128)(2,1)S(1)}, u32[]{:S(2)}, u32[]{:S(2)}) collective-permute-start(bf16[8,48,1920]{2,1,0:T(8,128)(2,1)} %get-tuple-element.238), channel_id=1, source_target_pairs={{0,2},{1,3},{2,0},{3,1},{4,6},{5,7},{6,4},{7,5},{8,10},{9,11},{10,... | collective-permute-start | bytes 4423688 | tf_op jit(solution)/shard_map/ppermute | solution.py:543
  274.8 33.6 %collective-permute-start.38 = (bf16[8,192,384]{2,1,0:T(8,128)(2,1)}, bf16[8,192,384]{2,1,0:T(8,128)(2,1)S(1)}, u32[]{:S(2)}, u32[]{:S(2)}) collective-permute-start(bf16[8,192,384]{2,1,0:T(8,128)(2,1)} %get-tuple-element.236), channel_id=1, source_target_pairs={{0,1},{1,0},{2,3},{3,2},{4,5},{5,4},{6,7},{7,6},{8,9},{9,8},{10,11... | collective-permute-start | bytes 3538952 | tf_op jit(solution)/shard_map/ppermute | solution.py:543
  275.4 33.0 %collective-permute-start.40 = (bf16[48,3456]{1,0:T(8,128)(2,1)S(1)}, bf16[48,3456]{1,0:T(8,128)(2,1)S(1)}, u32[]{:S(2)}, u32[]{:S(2)}) collective-permute-start(bf16[48,3456]{1,0:T(8,128)(2,1)S(1)} %get-tuple-element.240), channel_id=1, source_target_pairs={{0,8},{4,12},{8,0},{12,4},{1,9},{5,13},{9,1},{13,5},{2,10},{6,14},... | collective-permute-start | bytes 995336 | tf_op jit(solution)/shard_map/ppermute | solution.py:543
  278.0 39.8 %collective-permute-start.41 = (bf16[2,48,1152]{2,1,0:T(8,128)(2,1)S(1)}, bf16[2,48,1152]{2,1,0:T(8,128)(2,1)}, u32[]{:S(2)}, u32[]{:S(2)}) collective-permute-start(bf16[2,48,1152]{2,1,0:T(8,128)(2,1)S(1)} %get-tuple-element.245), channel_id=1, source_target_pairs={{0,4},{4,0},{8,12},{12,8},{1,5},{5,1},{9,13},{13,9},{2,6},{6,2},{1... | collective-permute-start | bytes 663560 | tf_op jit(solution)/shard_map/ppermute | solution.py:543
  320.3 18.9 %collective-permute-start.46 = (bf16[4,48,1920]{2,1,0:T(8,128)(2,1)S(1)}, bf16[4,48,1920]{2,1,0:T(8,128)(2,1)S(1)}, u32[]{:S(2)}, u32[]{:S(2)}) collective-permute-start(bf16[4,48,1920]{2,1,0:T(8,128)(2,1)S(1)} %get-tuple-element.258), channel_id=1, source_target_pairs={{0,1},{1,0},{2,3},{3,2},{4,5},{5,4},{6,7},{7,6},{8,9},{9,8},{10,11... | collective-permute-start | bytes 2211848 | tf_op jit(solution)/shard_map/ppermute | solution.py:543
  348.9 16.4 %collective-permute-start.51 = (bf16[2,48,3456]{2,1,0:T(8,128)(2,1)}, bf16[2,48,3456]{2,1,0:T(8,128)(2,1)S(1)}, u32[]{:S(2)}, u32[]{:S(2)}) collective-permute-start(bf16[2,48,3456]{2,1,0:T(8,128)(2,1)} %copy-done.59), channel_id=1, source_target_pairs={{0,4},{4,0},{8,12},{12,8},{1,5},{5,1},{9,13},{13,9},{2,6},{6,2},{1... | collective-permute-start | bytes 1990664 | tf_op jit(solution)/shard_map/ppermute | solution.py:543
  352.6 21.7 %collective-permute-start.58 = (f32[26,768]{1,0:T(8,128)}, f32[26,768]{1,0:T(8,128)}, u32[]{:S(2)}, u32[]{:S(2)}) collective-permute-start(f32[26,768]{1,0:T(8,128)} %add_add_fusion.3), channel_id=1, source_target_pairs={{0,2},{1,3},{2,0},{3,1},{4,6},{5,7},{6,4},{7,5},{8,10},{9,11},{10,... | collective-permute-start | bytes 239624 | tf_op jit(solution)/shard_map/ppermute | solution.py:543
  355.7 21.2 %collective-permute-start.52 = (bf16[2,128,768]{2,1,0:T(8,128)(2,1)}, bf16[2,128,768]{2,1,0:T(8,128)(2,1)}, u32[]{:S(2)}, u32[]{:S(2)}) collective-permute-start(bf16[2,128,768]{2,1,0:T(8,128)(2,1)} %dynamic-slice_bitcast_fusion), channel_id=1, source_target_pairs={{0,1},{1,0},{2,3},{3,2},{4,5},{5,4},{6,7},{7,6},{8,9},{9,8},{10,11... | collective-permute-start | bytes 1179656 | tf_op jit(solution)/shard_map/ppermute | solution.py:543
  372.3 24.4 %collective-permute-start.63 = (bf16[48,3456]{1,0:T(8,128)(2,1)}, bf16[48,3456]{1,0:T(8,128)(2,1)S(1)}, u32[]{:S(2)}, u32[]{:S(2)}) collective-permute-start(bf16[48,3456]{1,0:T(8,128)(2,1)} %copy-done.63), channel_id=1, source_target_pairs={{0,8},{4,12},{8,0},{12,4},{1,9},{5,13},{9,1},{13,5},{2,10},{6,14},... | collective-permute-start | bytes 995336 | tf_op jit(solution)/shard_map/ppermute | solution.py:543
  (153 other events, 1170.1 us)

commit v5 on v4

--- a/solution.py
+++ b/solution.py
@@ -240,29 +240,31 @@
     token_ref[0] = 0
     which = info[WHICH + layer]
     pairs = ((mixer_own, mixer_got), (up_own, up_got), (down_own, down_got))
-    buffers = (mixer, up, down)
-    for i in range(3):
-        fetch(pairs[i], which, buffers[i], sems.at[i])
+    fetch(pairs[0], which, mixer, sems.at[0])
+    tiles = down.shape[0] // tile
+    for j in range(tiles):
+        fetch(pairs[1], which, up, sems.at[1 + j], column_part(j, tile))
+        fetch(pairs[2], which, down, sems.at[1 + tiles + j], row_part(j, tile))
     gain = small_of(small_own, small_got, which)(GAIN_B, 1)
     fetched(pairs[0], mixer, sems.at[0])
     hidden = x_ref[...].astype(f32) + dense(att_ref[...], mixer[...])
     hidden_ref[...] = hidden
     two = (hidden * rms_inverse(hidden) * gain).astype(bf16)
     two_ref[...] = two
-    fetched(pairs[1], up, sems.at[1])
     result, outs = hidden, []
-    for j in range(down.shape[0] // tile):
+    for j in range(tiles):
         span = slice(j * tile, (j + 1) * tile)
+        fetched(pairs[1], up, sems.at[1 + j], column_part(j, tile))
         u = dense(two, up[:, span])
         upward[:, span] = u
         act = (0.5 * u * (1.0 + jnp.tanh(0.7978845608 * (u + 0.044715 * (u * u * u))))).astype(bf16)
         active[:, span] = act
-        if j == 0:
-            fetched(pairs[2], down, sems.at[2])
+        part = column_part(j, tile)
+        for i, (x, y) in enumerate(((upward, upward_hbm), (active, active_hbm))):
+            outs.append(pltpu.make_async_copy(x.at[part], y.at[part], sems.at[1 + (2 + i) * tiles + j]))
+            outs[-1].start()
+        fetched(pairs[2], down, sems.at[1 + tiles + j], row_part(j, tile))
         result = result + dense(act, down[span, :])
-    outs = [pltpu.make_async_copy(upward, upward_hbm, sems.at[3]), pltpu.make_async_copy(active, active_hbm, sems.at[4])]
-    for out in outs:
-        out.start()
     out_ref[...] = result.astype(bf16)
     for out in outs:
         out.wait()
@@ -289,22 +291,30 @@
             pltpu.VMEM((ff, width), bf16),
             pltpu.VMEM((count, ff), f32),
             pltpu.VMEM((count, ff), bf16),
-            pltpu.SemaphoreType.DMA((5,)),
+            pltpu.SemaphoreType.DMA((1 + 4 * (ff // width),)),
         ],
         compiler_params=pltpu.CompilerParams(vmem_limit_bytes=SMALL_VMEM),
     )(info, x, attended, *smalls, *weights, *extras)
 
 
-def fetch(pair, which, buffer, semaphore):
+def fetch(pair, which, buffer, semaphore, at=()):
     for i, ref in enumerate(pair):
 
         @pl.when(which == i)
         def _(ref=ref):
-            pltpu.make_async_copy(ref.at[0], buffer, semaphore).start()
-
-
-def fetched(pair, buffer, semaphore):
-    pltpu.make_async_copy(pair[0].at[0], buffer, semaphore).wait()
+            pltpu.make_async_copy(ref.at[(0, *at)], buffer.at[at] if at else buffer, semaphore).start()
+
+
+def fetched(pair, buffer, semaphore, at=()):
+    pltpu.make_async_copy(pair[0].at[(0, *at)], buffer.at[at] if at else buffer, semaphore).wait()
+
+
+def row_part(i, size):
+    return pl.ds(i * size, size), slice(None)
+
+
+def column_part(i, size):
+    return slice(None), pl.ds(i * size, size)
 
 
 def gelu_slope(u):
@@ -334,26 +344,28 @@
                 ref[:, at : at + value.shape[1]] = value
 
     pairs = ((down_own, down_got), (up_own, up_got), (mixer_own, mixer_got))
-    for i, (pair, buffer) in enumerate(zip(pairs, (down, up, mixer))):
-        fetch(pair, which, buffer, sems.at[i])
-        if i == 0:
-            upward_copy = pltpu.make_async_copy(upward_hbm, upward_ref, sems.at[3])
-            hidden_copy = pltpu.make_async_copy(hidden_hbm, hidden_ref, sems.at[4])
+    tiles = down.shape[0] // tile
+    for j in range(tiles):
+        fetch(pairs[0], which, down, sems.at[j], row_part(j, tile))
+        if j == 0:
+            upward_copy = pltpu.make_async_copy(upward_hbm, upward_ref, sems.at[2 * tiles])
             upward_copy.start()
-            hidden_copy.start()
+        fetch(pairs[1], which, up, sems.at[tiles + j], column_part(j, tile))
+    hidden_copy = pltpu.make_async_copy(hidden_hbm, hidden_ref, sems.at[2 * tiles + 1])
+    hidden_copy.start()
+    fetch(pairs[2], which, mixer, sems.at[2 * tiles + 2])
     gain = small_of(small_own, small_got, which)(GAIN_B, 1)
     dy = dy_ref[...]
-    fetched(pairs[0], down, sems.at[0])
     grad = jnp.zeros(hidden_ref.shape, f32)
-    for j in range(down.shape[0] // tile):
+    for j in range(tiles):
         span = slice(j * tile, (j + 1) * tile)
+        fetched(pairs[0], down, sems.at[j], row_part(j, tile))
         dactive = dense_nt(dy, down[span, :])
         if j == 0:
             upward_copy.wait()
         dup = (dactive * gelu_slope(upward_ref[:, span])).astype(bf16)
         put(dup, j * tile // half_ff, j * tile % half_ff)
-        if j == 0:
-            fetched(pairs[1], up, sems.at[1])
+        fetched(pairs[1], up, sems.at[tiles + j], column_part(j, tile))
         grad = grad + dense_nt(dup, up[:, span])
     hidden_copy.wait()
     hidden = hidden_ref[...]
@@ -367,7 +379,7 @@
     for i in range(2):
         put(low[:, i * half : (i + 1) * half], i, half_ff)
         put(dy[:, i * half : (i + 1) * half], i, half_ff + half)
-    fetched(pairs[2], mixer, sems.at[2])
+    fetched(pairs[2], mixer, sems.at[2 * tiles + 2])
     datt_ref[...] = dense_nt(low, mixer[...]).astype(bf16)
 
 
@@ -393,7 +405,7 @@
             pltpu.VMEM((ff, width), bf16),
             pltpu.VMEM((count, ff), f32),
             pltpu.VMEM((count, width), f32),
-            pltpu.SemaphoreType.DMA((5,)),
+            pltpu.SemaphoreType.DMA((2 * (ff // width) + 3,)),
         ],
         compiler_params=pltpu.CompilerParams(vmem_limit_bytes=SMALL_VMEM),
     )(info, dy, upward, hidden, *smalls, *weights, *extras)

time: 415 us -> 410 us (0.988)
  Pallas kernels: 214 us -> 179 us
  starting transfers between devices: 60.1 us -> 75.4 us
  waiting for transfers between devices: 73.8 us -> 88.5 us
    pallas_call x2, Pallas kernels: 57.5 us -> 37.8 us  [attend_back(): pl.pallas_call(cost_estimate=SMALL_COST, kernel=functools.partial(attend_...]
    ppermute x35, waiting for transfers between devices: 56.2 us -> 73.8 us  [xor_permute(): lax.ppermute(x, axis, [(i, i ^ by) for i in range(lax.axis_size(axis))])]
    ppermute x35, starting transfers between devices: 43.3 us -> 59.5 us  [xor_permute(): lax.ppermute(x, axis, [(i, i ^ by) for i in range(lax.axis_size(axis))])]
    pallas_call x24, Pallas kernels: 156 us -> 141 us  [run(): pl.pallas_call(kernel, cost_estimate=SMALL_COST, grid=(1,), in_specs=[who...]
  transfers between devices with their start and end apart: 68 -> 68, of which waited for: 33 -> 32; matrix products, arithmetic and copies ran while one was open for 6% -> 7% of each run, Pallas kernels for 34% -> 28%
where the time goes in v5:
time: 410 us; the launch traced here: 404 us
  Pallas kernels  179 us (44%)
  waiting for transfers between devices  88.5 us (22%)
  starting transfers between devices  75.4 us (18%)
  local copies, waits for them, and re-layouts  37.1 us (9%)
  other arithmetic  17.6 us (4%)
  between operations  5.32 us (1%)
    pallas_call x24, Pallas kernels, run(): pl.pallas_call(kernel, cost_estimate=SMALL_COST, grid=(1,), in_specs=[who...  141 us
    ppermute x35, waiting for transfers between devices, xor_permute(): lax.ppermute(x, axis, [(i, i ^ by) for i in range(lax.axis_size(axis))])  73.8 us
    ppermute x35, starting transfers between devices, xor_permute(): lax.ppermute(x, axis, [(i, i ^ by) for i in range(lax.axis_size(axis))])  59.5 us
    pallas_call x2, Pallas kernels, attend_back(): pl.pallas_call(cost_estimate=SMALL_COST, kernel=functools.partial(attend_...  37.8 us
    unnamed x218, local copies, waits for them, and re-layouts  30.2 us
    ppermute x27, waiting for transfers between devices, swap_section(): return lax.ppermute(x, 'section', [(0, 1), (1, 0)])  14.3 us
  transfers between devices with their start and end apart: 68, of which 32 were waited for; matrix products, arithmetic and copies ran while one was open for 7% of the time, Pallas kernels for 28%

profile of v5, /device:TPU:0, one launch (start us, length us, event | category | flops | bytes accessed | tf_op | source)
XLA Modules:
  0.0 404.1 jit_solution(9448713782423511969)
XLA Ops:
  15.4 4.8 %collective-permute-done.6.rest_3_ = bf16[128,768]{1,0:T(8,128)(2,1)S(1)} collective-permute-done((bf16[128,768]{1,0:T(8,128)(2,1)S(1)}, bf16[128,768]{1,0:T(8,128)(2,1)S(1)}, u32[]{:S(2)}, u32[]{:S(2)}) %collective-permute-start.6) | collective-permute-done | bytes 196640 | tf_op jit(solution)/shard_map/ppermute | solution.py:555
  26.3 4.8 %collective-permute-start.1 = (bf16[128,768]{1,0:T(8,128)(2,1)S(1)}, bf16[128,768]{1,0:T(8,128)(2,1)S(1)}, u32[]{:S(2)}, u32[]{:S(2)}) collective-permute-start(bf16[128,768]{1,0:T(8,128)(2,1)S(1)} %get-tuple-element.317), channel_id=1, source_target_pairs={{0,2},{1,3},{3,0},{2,1},{4,6},{5,7},{7,4},{6,5},{8,10},{9,11},{11,... | collective-permute-start | bytes 589832 | tf_op jit(solution)/shard_map/ppermute | solution.py:1223
  33.7 18.2 %shard_map.178 = (bf16[256,768]{1,0:T(8,128)(2,1)}, bf16[256,768]{1,0:T(8,128)(2,1)}, bf16[256,768]{1,0:T(8,128)(2,1)}, bf16[256,768]{1,0:T(8,128)(2,1)}, s32[1]...) custom-call(s32[24]{0:T(128)} %stack.141.info.seat, ...), custom_call_target="tpu_custom_call" | custom-call | tf_op jit(solution)/shard_map/pallas_call | solution.py:187
  56.9 8.5 %shard_map.179 = (bf16[256,768]{1,0:T(8,128)(2,1)S(1)}, f32[256,768]{1,0:T(8,128)}, bf16[256,768]{1,0:T(8,128)(2,1)}, f32[256,3072]{1,0:T(8,128)}, bf16[256,3072]{1,0:T(8,128)(2,1)}, /*index=5*/s32[1]{0:T(128)}) custom-call(s32[24]{0:T(128)S(1)} %copy-done.46, bf16[256,768]{1,0:T(8,128)(2,1)S(1)} %copy-done.13, bf16[256,768]{1,0:T(8,128)(2,1)S(1)} %copy-done.20, ...), custom_call_target="tpu_custom_call" | custom-call | tf_op jit(solution)/shard_map/pallas_call | solution.py:187
  66.1 10.1 %collective-permute-done.11.rest_1_ = bf16[256,768]{1,0:T(8,128)(2,1)S(1)} collective-permute-done((bf16[256,768]{1,0:T(8,128)(2,1)S(1)}, bf16[256,768]{1,0:T(8,128)(2,1)S(1)}, u32[]{:S(2)}, u32[]{:S(2)}) %collective-permute-start.11) | collective-permute-done | bytes 393248 | tf_op jit(solution)/shard_map/ppermute | solution.py:555
  78.6 18.1 %shard_map.180 = (bf16[256,768]{1,0:T(8,128)(2,1)}, bf16[256,768]{1,0:T(8,128)(2,1)}, bf16[256,768]{1,0:T(8,128)(2,1)}, bf16[256,768]{1,0:T(8,128)(2,1)}, s32[1]...) custom-call(s32[24]{0:T(128)} %stack.141.info.seat, ...), custom_call_target="tpu_custom_call" | custom-call | tf_op jit(solution)/shard_map/pallas_call | solution.py:187
  98.7 8.6 %shard_map.181 = (bf16[256,768]{1,0:T(8,128)(2,1)S(1)}, f32[256,768]{1,0:T(8,128)}, bf16[256,768]{1,0:T(8,128)(2,1)}, f32[256,3072]{1,0:T(8,128)}, bf16[256,3072]{1,0:T(8,128)(2,1)}, /*index=5*/s32[1]{0:T(128)}) custom-call(s32[24]{0:T(128)S(1)} %copy-done.47, bf16[256,768]{1,0:T(8,128)(2,1)S(1)} %copy-done.15, bf16[256,768]{1,0:T(8,128)(2,1)S(1)} %copy-done.22, ...), custom_call_target="tpu_custom_call" | custom-call | tf_op jit(solution)/shard_map/pallas_call | solution.py:187
  108.4 9.8 %shard_map.182 = (bf16[256,2304]{1,0:T(8,128)(2,1)S(1)}, bf16[256,2304]{1,0:T(8,128)(2,1)S(1)}, f32[256,768]{1,0:T(8,128)}, bf16[256,768]{1,0:T(8,128)(2,1)S(1)}, f32[1,768]{1,0:T(1,128)S(1)}, /*index=5*/s32[1]{0:T(128)}) custom-call(s32[24]{0:T(128)S(1)} %copy-done.47, bf16[256,768]{1,0:T(8,128)(2,1)S(1)} %pad_maximum_fusion.2.dy_ref, ...), custom_call_target="tpu_custom_call" | custom-call | tf_op jit(solution)/shard_map/pallas_call | solution.py:187
  124.2 8.6 %shard_map.183 = (bf16[8,192,384]{2,1,0:T(8,128)(2,1)}, bf16[8,192,384]{2,1,0:T(8,128)(2,1)}, bf16[8,48,1920]{2,1,0:T(8,128)(2,1)}, bf16[8,48,1920]{2,1,0:T(8,128)(2,1)}, s32[1]{0:T(128)}) custom-call(s32[24]{0:T(128)S(1)} %copy-done.47, bf16[256,3072]{1,0:T(8,128)(2,1)} %get-tuple-element.171.active, bf16[256,3072]{1,0:T(8,128)(2,1)} %copy-done.69, ...), custom_call_target="tpu_custom_call" | custom-call | tf_op jit(solution)/shard_map/pallas_call | solution.py:187
  132.8 10.7 %collective-permute-start.19 = (bf16[8,48,1920]{2,1,0:T(8,128)(2,1)}, bf16[8,48,1920]{2,1,0:T(8,128)(2,1)S(1)}, u32[]{:S(2)}, u32[]{:S(2)}) collective-permute-start(bf16[8,48,1920]{2,1,0:T(8,128)(2,1)} %get-tuple-element.182), channel_id=1, source_target_pairs={{0,2},{1,3},{2,0},{3,1},{4,6},{5,7},{6,4},{7,5},{8,10},{9,11},{10,... | collective-permute-start | bytes 4423688 | tf_op jit(solution)/shard_map/ppermute | solution.py:555
  144.1 19.0 %shard_map.184 = (bf16[256,768]{1,0:T(8,128)(2,1)}, bf16[1024,768]{1,0:T(8,128)(2,1)}, bf16[1024,768]{1,0:T(8,128)(2,1)}, f32[12,768]{1,0:T(8,128)}, f32[12,768]{1,0:T(8,128)}, /*index=5*/s32[1]{0:T(128)}) custom-call(s32[24]{0:T(128)} %stack.141.info.seat, bf16[256,768]{1,0:T(8,128)(2,1)} %get-tuple-element.164.q_ref, bf16[256,768]{1,0:T(8,128)(2,1)} %copy-done.40, ...), custom_call_target="tpu_custom_call" | custom-call | tf_op jit(solution)/shard_map/pallas_call | solution.py:501
  163.1 8.6 %collective-permute-done.18.refs_3_ = bf16[8,192,384]{2,1,0:T(8,128)(2,1)S(1)} collective-permute-done((bf16[8,192,384]{2,1,0:T(8,128)(2,1)}, bf16[8,192,384]{2,1,0:T(8,128)(2,1)S(1)}, u32[]{:S(2)}, u32[]{:S(2)}) %collective-permute-start.18) | collective-permute-done | bytes 1179680 | tf_op jit(solution)/shard_map/ppermute | solution.py:555
  171.7 4.9 %collective-permute-done.19.refs_5_ = bf16[8,48,1920]{2,1,0:T(8,128)(2,1)S(1)} collective-permute-done((bf16[8,48,1920]{2,1,0:T(8,128)(2,1)}, bf16[8,48,1920]{2,1,0:T(8,128)(2,1)S(1)}, u32[]{:S(2)}, u32[]{:S(2)}) %collective-permute-start.19) | collective-permute-done | bytes 1474592 | tf_op jit(solution)/shard_map/ppermute | solution.py:555
  180.1 4.3 %shard_map.185 = (bf16[4,192,384]{2,1,0:T(8,128)(2,1)S(1)}, bf16[4,192,384]{2,1,0:T(8,128)(2,1)S(1)}, bf16[4,48,1920]{2,1,0:T(8,128)(2,1)S(1)}, bf16[4,48,1920]{...) custom-call(s32[24]{0:T(128)S(1)} %copy-done.48, ...), custom_call_target="tpu_custom_call", output_to_operand_aliasing={{5}: (2, {}), {6}: (3, {})} | custom-call | tf_op jit(solution)/shard_map/pallas_call | solution.py:187
  191.1 8.4 %shard_map.186 = (bf16[512,768]{1,0:T(8,128)(2,1)S(1)}, bf16[512,768]{1,0:T(8,128)(2,1)S(1)}, f32[256,768]{1,0:T(8,128)S(1)}, bf16[8,48,512]{2,1,0:T(8,128)(2,1)...) custom-call(s32[24]{0:T(128)S(1)} %copy-done.48, ...), custom_call_target="tpu_custom_call" | custom-call | tf_op jit(solution)/shard_map/pallas_call | solution.py:187
  219.3 6.3 %collective-permute-done.26.refs_2_ = bf16[8,48,512]{2,1,0:T(8,128)(2,1)S(1)} collective-permute-done((bf16[8,48,512]{2,1,0:T(8,128)(2,1)}, bf16[8,48,512]{2,1,0:T(8,128)(2,1)S(1)}, u32[]{:S(2)}, u32[]{:S(2)}) %collective-permute-start.26) | collective-permute-done | bytes 393248 | tf_op jit(solution)/shard_map/ppermute | solution.py:555
  240.0 9.8 %shard_map.189 = (bf16[256,2304]{1,0:T(8,128)(2,1)S(1)}, bf16[256,2304]{1,0:T(8,128)(2,1)S(1)}, f32[256,768]{1,0:T(8,128)}, bf16[256,768]{1,0:T(8,128)(2,1)S(1)}, f32[1,768]{1,0:T(1,128)S(1)}, /*index=5*/s32[1]{0:T(128)}) custom-call(s32[24]{0:T(128)S(1)} %copy-done.48, bf16[256,768]{1,0:T(8,128)(2,1)S(1)} %fusion.16.dy_ref, ...), custom_call_target="tpu_custom_call" | custom-call | tf_op jit(solution)/shard_map/pallas_call | solution.py:187
  261.1 8.6 %shard_map.192 = (bf16[8,192,384]{2,1,0:T(8,128)(2,1)}, bf16[8,192,384]{2,1,0:T(8,128)(2,1)}, bf16[8,48,1920]{2,1,0:T(8,128)(2,1)}, bf16[8,48,1920]{2,1,0:T(8,128)(2,1)}, s32[1]{0:T(128)}) custom-call(s32[24]{0:T(128)S(1)} %copy-done.48, bf16[256,3072]{1,0:T(8,128)(2,1)} %get-tuple-element.227.active, ...), custom_call_target="tpu_custom_call" | custom-call | tf_op jit(solution)/shard_map/pallas_call | solution.py:187
  274.6 18.9 %shard_map.193 = (bf16[256,768]{1,0:T(8,128)(2,1)}, bf16[1024,768]{1,0:T(8,128)(2,1)}, bf16[1024,768]{1,0:T(8,128)(2,1)}, f32[12,768]{1,0:T(8,128)}, f32[12,768]{1,0:T(8,128)}, /*index=5*/s32[1]{0:T(128)}) custom-call(s32[24]{0:T(128)} %stack.141.info.seat, bf16[256,768]{1,0:T(8,128)(2,1)} %get-tuple-element.207.q_ref, bf16[256,768]{1,0:T(8,128)(2,1)} %copy-done.39, ...), custom_call_target="tpu_custom_call" | custom-call | tf_op jit(solution)/shard_map/pallas_call | solution.py:501
  293.5 4.6 %collective-permute-done.38.refs_3_ = bf16[8,192,384]{2,1,0:T(8,128)(2,1)S(1)} collective-permute-done((bf16[8,192,384]{2,1,0:T(8,128)(2,1)}, bf16[8,192,384]{2,1,0:T(8,128)(2,1)S(1)}, u32[]{:S(2)}, u32[]{:S(2)}) %collective-permute-start.38) | collective-permute-done | bytes 1179680 | tf_op jit(solution)/shard_map/ppermute | solution.py:555
  298.1 6.2 %collective-permute-done.39.refs_5_ = bf16[8,48,1920]{2,1,0:T(8,128)(2,1)S(1)} collective-permute-done((bf16[8,48,1920]{2,1,0:T(8,128)(2,1)}, bf16[8,48,1920]{2,1,0:T(8,128)(2,1)S(1)}, u32[]{:S(2)}, u32[]{:S(2)}) %collective-permute-start.39) | collective-permute-done | bytes 1474592 | tf_op jit(solution)/shard_map/ppermute | solution.py:555
  308.0 4.9 %shard_map.194 = (bf16[4,192,384]{2,1,0:T(8,128)(2,1)S(1)}, bf16[4,192,384]{2,1,0:T(8,128)(2,1)S(1)}, bf16[4,48,1920]{2,1,0:T(8,128)(2,1)S(1)}, bf16[4,48,1920]{...) custom-call(s32[24]{0:T(128)S(1)} %copy-done.49, ...), custom_call_target="tpu_custom_call", output_to_operand_aliasing={{6}: (2, {}), {7}: (3, {})} | custom-call | tf_op jit(solution)/shard_map/pallas_call | solution.py:187
  321.9 7.6 %shard_map.196 = (bf16[512,768]{1,0:T(8,128)(2,1)S(1)}, bf16[512,768]{1,0:T(8,128)(2,1)S(1)}, f32[256,768]{1,0:T(8,128)S(1)}, bf16[8,48,512]{2,1,0:T(8,128)(2,1)...) custom-call(s32[24]{0:T(128)S(1)} %copy-done.49, ...), custom_call_target="tpu_custom_call" | custom-call | tf_op jit(solution)/shard_map/pallas_call | solution.py:187
  391.6 3.5 collective-permute-done.65.refs_4_
  (403 shorter events, 181.0 us)
Async XLA Ops:
  0.7 51.3 %collective-permute-start.10 = (bf16[1,3072,768]{2,1,0:T(8,128)(2,1)}, bf16[1,3072,768]{2,1,0:T(8,128)(2,1)}, u32[]{:S(2)}, u32[]{:S(2)}) collective-permute-start(bf16[1,3072,768]{2,1,0:T(8,128)(2,1)} %down_own.7), channel_id=1, source_target_pairs={{0,16},{16,0},{1,17},{17,1},{2,18},{18,2},{3,19},{19,3},{4,20},{20... | collective-permute-start | bytes 14155784 | tf_op jit(solution)/shard_map/ppermute | solution.py:551
  1.2 50.8 %collective-permute-start.9 = (bf16[1,768,3072]{2,1,0:T(8,128)(2,1)}, bf16[1,768,3072]{2,1,0:T(8,128)(2,1)}, u32[]{:S(2)}, u32[]{:S(2)}) collective-permute-start(bf16[1,768,3072]{2,1,0:T(8,128)(2,1)} %up_own.7), channel_id=1, source_target_pairs={{0,16},{16,0},{1,17},{17,1},{2,18},{18,2},{3,19},{19,3},{4,20},{20... | collective-permute-start | bytes 14155784 | tf_op jit(solution)/shard_map/ppermute | solution.py:551
  1.3 25.1 %collective-permute-start.3 = (bf16[1,768,2304]{2,1,0:T(8,128)(2,1)}, bf16[1,768,2304]{2,1,0:T(8,128)(2,1)}, u32[]{:S(2)}, u32[]{:S(2)}) collective-permute-start(bf16[1,768,2304]{2,1,0:T(8,128)(2,1)} %joint_own.7), channel_id=1, source_target_pairs={{0,16},{16,0},{1,17},{17,1},{2,18},{18,2},{3,19},{19,3},{4,20},{20... | collective-permute-start | bytes 10616840 | tf_op jit(solution)/shard_map/ppermute | solution.py:551
  10.9 41.1 %collective-permute-start.8 = (bf16[1,768,768]{2,1,0:T(8,128)(2,1)}, bf16[1,768,768]{2,1,0:T(8,128)(2,1)S(1)}, u32[]{:S(2)}, u32[]{:S(2)}) collective-permute-start(bf16[1,768,768]{2,1,0:T(8,128)(2,1)} %mixer_own.7), channel_id=1, source_target_pairs={{0,16},{16,0},{1,17},{17,1},{2,18},{18,2},{3,19},{19,3},{4,20},{20... | collective-permute-start | bytes 3538952 | tf_op jit(solution)/shard_map/ppermute | solution.py:551
  24.7 27.2 %collective-permute-start = (bf16[128,768]{1,0:T(8,128)(2,1)}, bf16[128,768]{1,0:T(8,128)(2,1)S(1)}, u32[]{:S(2)}, u32[]{:S(2)}) collective-permute-start(bf16[128,768]{1,0:T(8,128)(2,1)} %get-tuple-element.316), channel_id=1, source_target_pairs={{3,2},{2,3},{0,0},{1,1},{7,6},{6,7},{4,4},{5,5},{11,10},{10,11},{8... | collective-permute-start | bytes 589832 | tf_op jit(solution)/shard_map/ppermute | solution.py:1223
  26.3 25.6 %collective-permute-start.1 = (bf16[128,768]{1,0:T(8,128)(2,1)S(1)}, bf16[128,768]{1,0:T(8,128)(2,1)S(1)}, u32[]{:S(2)}, u32[]{:S(2)}) collective-permute-start(bf16[128,768]{1,0:T(8,128)(2,1)S(1)} %get-tuple-element.317), channel_id=1, source_target_pairs={{0,2},{1,3},{3,0},{2,1},{4,6},{5,7},{7,4},{6,5},{8,10},{9,11},{11,... | collective-permute-start | bytes 589832 | tf_op jit(solution)/shard_map/ppermute | solution.py:1223
  132.8 43.7 %collective-permute-start.19 = (bf16[8,48,1920]{2,1,0:T(8,128)(2,1)}, bf16[8,48,1920]{2,1,0:T(8,128)(2,1)S(1)}, u32[]{:S(2)}, u32[]{:S(2)}) collective-permute-start(bf16[8,48,1920]{2,1,0:T(8,128)(2,1)} %get-tuple-element.182), channel_id=1, source_target_pairs={{0,2},{1,3},{2,0},{3,1},{4,6},{5,7},{6,4},{7,5},{8,10},{9,11},{10,... | collective-permute-start | bytes 4423688 | tf_op jit(solution)/shard_map/ppermute | solution.py:555
  143.6 28.1 %collective-permute-start.18 = (bf16[8,192,384]{2,1,0:T(8,128)(2,1)}, bf16[8,192,384]{2,1,0:T(8,128)(2,1)S(1)}, u32[]{:S(2)}, u32[]{:S(2)}) collective-permute-start(bf16[8,192,384]{2,1,0:T(8,128)(2,1)} %get-tuple-element.180), channel_id=1, source_target_pairs={{0,1},{1,0},{2,3},{3,2},{4,5},{5,4},{6,7},{7,6},{8,9},{9,8},{10,11... | collective-permute-start | bytes 3538952 | tf_op jit(solution)/shard_map/ppermute | solution.py:555
  186.4 18.9 %collective-permute-start.24 = (bf16[4,48,1920]{2,1,0:T(8,128)(2,1)S(1)}, bf16[4,48,1920]{2,1,0:T(8,128)(2,1)S(1)}, u32[]{:S(2)}, u32[]{:S(2)}) collective-permute-start(bf16[4,48,1920]{2,1,0:T(8,128)(2,1)S(1)} %get-tuple-element.195), channel_id=1, source_target_pairs={{0,1},{1,0},{2,3},{3,2},{4,5},{5,4},{6,7},{7,6},{8,9},{9,8},{10,11... | collective-permute-start | bytes 2211848 | tf_op jit(solution)/shard_map/ppermute | solution.py:555
  211.1 49.3 %collective-permute-start.34 = (bf16[256,3072]{1,0:T(8,128)(2,1)}, bf16[256,3072]{1,0:T(8,128)(2,1)}, u32[]{:S(2)}, u32[]{:S(2)}) collective-permute-start(bf16[256,3072]{1,0:T(8,128)(2,1)} %get-tuple-element.227.active), channel_id=1, source_target_pairs={{0,16},{16,0},{1,17},{17,1},{2,18},{18,2},{3,19},{19,3},{4,20},{20... | collective-permute-start | bytes 4718600 | tf_op jit(solution)/shard_map/ppermute | solution.py:551
  216.1 18.0 %collective-permute-start.28 = (bf16[2,128,768]{2,1,0:T(8,128)(2,1)}, bf16[2,128,768]{2,1,0:T(8,128)(2,1)}, u32[]{:S(2)}, u32[]{:S(2)}) collective-permute-start(bf16[2,128,768]{2,1,0:T(8,128)(2,1)} %dynamic-slice_bitcast_fusion.1), channel_id=1, source_target_pairs={{0,1},{1,0},{2,3},{3,2},{4,5},{5,4},{6,7},{7,6},{8,9},{9,8},{10,11... | collective-permute-start | bytes 1179656 | tf_op jit(solution)/shard_map/ppermute | solution.py:555
  218.4 18.0 %collective-permute-start.29 = (bf16[128,768]{1,0:T(8,128)(2,1)}, bf16[128,768]{1,0:T(8,128)(2,1)S(1)}, u32[]{:S(2)}, u32[]{:S(2)}) collective-permute-start(bf16[128,768]{1,0:T(8,128)(2,1)} %get-tuple-element.321), channel_id=1, source_target_pairs={{2,0},{3,1},{0,3},{1,2},{6,4},{7,5},{4,7},{5,6},{10,8},{11,9},{8,1... | collective-permute-start | bytes 589832 | tf_op jit(solution)/shard_map/ppermute | solution.py:1230
  225.6 24.2 %collective-permute-start.30 = (bf16[128,768]{1,0:T(8,128)(2,1)}, bf16[128,768]{1,0:T(8,128)(2,1)S(1)}, u32[]{:S(2)}, u32[]{:S(2)}) collective-permute-start(bf16[128,768]{1,0:T(8,128)(2,1)} %get-tuple-element.320), channel_id=1, source_target_pairs={{2,3},{3,2},{0,0},{1,1},{6,7},{7,6},{4,4},{5,5},{10,11},{11,10},{8... | collective-permute-start | bytes 589832 | tf_op jit(solution)/shard_map/ppermute | solution.py:1231
  227.2 26.2 %collective-permute-start.33 = (bf16[2,48,3456]{2,1,0:T(8,128)(2,1)S(1)}, bf16[2,48,3456]{2,1,0:T(8,128)(2,1)}, u32[]{:S(2)}, u32[]{:S(2)}) collective-permute-start(bf16[2,48,3456]{2,1,0:T(8,128)(2,1)S(1)} %copy-done.58), channel_id=1, source_target_pairs={{0,4},{4,0},{8,12},{12,8},{1,5},{5,1},{9,13},{13,9},{2,6},{6,2},{1... | collective-permute-start | bytes 1990664 | tf_op jit(solution)/shard_map/ppermute | solution.py:555
  269.8 34.6 %collective-permute-start.39 = (bf16[8,48,1920]{2,1,0:T(8,128)(2,1)}, bf16[8,48,1920]{2,1,0:T(8,128)(2,1)S(1)}, u32[]{:S(2)}, u32[]{:S(2)}) collective-permute-start(bf16[8,48,1920]{2,1,0:T(8,128)(2,1)} %get-tuple-element.238), channel_id=1, source_target_pairs={{0,2},{1,3},{2,0},{3,1},{4,6},{5,7},{6,4},{7,5},{8,10},{9,11},{10,... | collective-permute-start | bytes 4423688 | tf_op jit(solution)/shard_map/ppermute | solution.py:555
  269.8 28.3 %collective-permute-start.38 = (bf16[8,192,384]{2,1,0:T(8,128)(2,1)}, bf16[8,192,384]{2,1,0:T(8,128)(2,1)S(1)}, u32[]{:S(2)}, u32[]{:S(2)}) collective-permute-start(bf16[8,192,384]{2,1,0:T(8,128)(2,1)} %get-tuple-element.236), channel_id=1, source_target_pairs={{0,1},{1,0},{2,3},{3,2},{4,5},{5,4},{6,7},{7,6},{8,9},{9,8},{10,11... | collective-permute-start | bytes 3538952 | tf_op jit(solution)/shard_map/ppermute | solution.py:555
  270.4 23.1 %collective-permute-start.40 = (bf16[48,3456]{1,0:T(8,128)(2,1)S(1)}, bf16[48,3456]{1,0:T(8,128)(2,1)S(1)}, u32[]{:S(2)}, u32[]{:S(2)}) collective-permute-start(bf16[48,3456]{1,0:T(8,128)(2,1)S(1)} %get-tuple-element.240), channel_id=1, source_target_pairs={{0,8},{4,12},{8,0},{12,4},{1,9},{5,13},{9,1},{13,5},{2,10},{6,14},... | collective-permute-start | bytes 995336 | tf_op jit(solution)/shard_map/ppermute | solution.py:555
  273.0 39.9 %collective-permute-start.41 = (bf16[2,48,1152]{2,1,0:T(8,128)(2,1)S(1)}, bf16[2,48,1152]{2,1,0:T(8,128)(2,1)}, u32[]{:S(2)}, u32[]{:S(2)}) collective-permute-start(bf16[2,48,1152]{2,1,0:T(8,128)(2,1)S(1)} %get-tuple-element.245), channel_id=1, source_target_pairs={{0,4},{4,0},{8,12},{12,8},{1,5},{5,1},{9,13},{13,9},{2,6},{6,2},{1... | collective-permute-start | bytes 663560 | tf_op jit(solution)/shard_map/ppermute | solution.py:555
  315.3 18.9 %collective-permute-start.46 = (bf16[4,48,1920]{2,1,0:T(8,128)(2,1)S(1)}, bf16[4,48,1920]{2,1,0:T(8,128)(2,1)S(1)}, u32[]{:S(2)}, u32[]{:S(2)}) collective-permute-start(bf16[4,48,1920]{2,1,0:T(8,128)(2,1)S(1)} %get-tuple-element.258), channel_id=1, source_target_pairs={{0,1},{1,0},{2,3},{3,2},{4,5},{5,4},{6,7},{7,6},{8,9},{9,8},{10,11... | collective-permute-start | bytes 2211848 | tf_op jit(solution)/shard_map/ppermute | solution.py:555
  315.9 16.1 %collective-permute-start.45 = (bf16[4,192,384]{2,1,0:T(8,128)(2,1)S(1)}, bf16[4,192,384]{2,1,0:T(8,128)(2,1)S(1)}, u32[]{:S(2)}, u32[]{:S(2)}) collective-permute-start(bf16[4,192,384]{2,1,0:T(8,128)(2,1)S(1)} %get-tuple-element.256), channel_id=1, source_target_pairs={{0,2},{1,3},{2,0},{3,1},{4,6},{5,7},{6,4},{7,5},{8,10},{9,11},{10,... | collective-permute-start | bytes 1769480 | tf_op jit(solution)/shard_map/ppermute | solution.py:555
  345.1 16.3 %collective-permute-start.51 = (bf16[2,48,3456]{2,1,0:T(8,128)(2,1)}, bf16[2,48,3456]{2,1,0:T(8,128)(2,1)S(1)}, u32[]{:S(2)}, u32[]{:S(2)}) collective-permute-start(bf16[2,48,3456]{2,1,0:T(8,128)(2,1)} %copy-done.59), channel_id=1, source_target_pairs={{0,4},{4,0},{8,12},{12,8},{1,5},{5,1},{9,13},{13,9},{2,6},{6,2},{1... | collective-permute-start | bytes 1990664 | tf_op jit(solution)/shard_map/ppermute | solution.py:555
  346.9 22.4 %collective-permute-start.58 = (f32[26,768]{1,0:T(8,128)}, f32[26,768]{1,0:T(8,128)}, u32[]{:S(2)}, u32[]{:S(2)}) collective-permute-start(f32[26,768]{1,0:T(8,128)} %add_add_fusion.3), channel_id=1, source_target_pairs={{0,2},{1,3},{2,0},{3,1},{4,6},{5,7},{6,4},{7,5},{8,10},{9,11},{10,... | collective-permute-start | bytes 239624 | tf_op jit(solution)/shard_map/ppermute | solution.py:555
  350.9 21.0 %collective-permute-start.52 = (bf16[2,128,768]{2,1,0:T(8,128)(2,1)}, bf16[2,128,768]{2,1,0:T(8,128)(2,1)}, u32[]{:S(2)}, u32[]{:S(2)}) collective-permute-start(bf16[2,128,768]{2,1,0:T(8,128)(2,1)} %dynamic-slice_bitcast_fusion), channel_id=1, source_target_pairs={{0,1},{1,0},{2,3},{3,2},{4,5},{5,4},{6,7},{7,6},{8,9},{9,8},{10,11... | collective-permute-start | bytes 1179656 | tf_op jit(solution)/shard_map/ppermute | solution.py:555
  367.6 24.0 %collective-permute-start.63 = (bf16[48,3456]{1,0:T(8,128)(2,1)}, bf16[48,3456]{1,0:T(8,128)(2,1)S(1)}, u32[]{:S(2)}, u32[]{:S(2)}) collective-permute-start(bf16[48,3456]{1,0:T(8,128)(2,1)} %copy-done.63), channel_id=1, source_target_pairs={{0,8},{4,12},{8,0},{12,4},{1,9},{5,13},{9,1},{13,5},{2,10},{6,14},... | collective-permute-start | bytes 995336 | tf_op jit(solution)/shard_map/ppermute | solution.py:555
  (153 other events, 1151.0 us)

commit v6 on v5

--- a/solution.py
+++ b/solution.py
@@ -593,20 +593,19 @@
 
 
 def products_kernel(
-    seat, active, active_other, two, two_other, att, att_other, right, right_other,
-    down_kept, down_sent, up_kept, up_sent, token_ref, down_blocks, up_blocks,
+    seat, active_hbm, active_other_hbm, two, two_other, att, att_other, right, right_other,
+    down_kept, down_sent, up_kept, up_sent, token_ref, active, active_other, down_blocks, up_blocks, sems,
 ):
     token_ref[0] = 0
+    copies = [
+        pltpu.make_async_copy(x, y, sems.at[i])
+        for i, (x, y) in enumerate(((active_hbm, active), (active_other_hbm, active_other)))
+    ]
+    for copy in copies:
+        copy.start()
     width = att.shape[1]
     half, half_ff = width // 2, active.shape[1] // 2
     both = lambda left, left_other, cols: dense_tn(left, right[:, cols]) + dense_tn(left_other, right_other[:, cols])
-    rows = down_blocks.shape[1]
-    each = width // rows
-    for j in range(active.shape[1] // width):
-        cols = slice(j * width, (j + 1) * width)
-        grad = both(active[:, cols], active_other[:, cols], slice(half_ff + half, half_ff + width))
-        down_blocks[j * each : (j + 1) * each] = grad.astype(bf16).reshape(each, rows, half)
-    split_blocks(down_blocks, down_kept, down_sent, seat[CTX] % 2)
     rows = up_blocks.shape[1]
     tile = half_ff // 2
     for j in range(2):
@@ -615,6 +614,15 @@
     cols = slice(half_ff, half_ff + half)
     up_blocks[:, :, cols] = both(att[...], att_other[...], cols).astype(bf16).reshape(-1, rows, half)
     split_blocks_first(up_blocks, up_kept, up_sent, seat[CTX] // 2)
+    for copy in copies:
+        copy.wait()
+    rows = down_blocks.shape[1]
+    each = width // rows
+    for j in range(active.shape[1] // width):
+        cols = slice(j * width, (j + 1) * width)
+        grad = both(active[:, cols], active_other[:, cols], slice(half_ff + half, half_ff + width))
+        down_blocks[j * each : (j + 1) * each] = grad.astype(bf16).reshape(each, rows, half)
+    split_blocks(down_blocks, down_kept, down_sent, seat[CTX] % 2)
 
 
 def products(seat, arrays, count, rows):
@@ -623,10 +631,16 @@
     shape = lambda x: jax.ShapeDtypeStruct((count // 2, *x), bf16)
     outs = one_step(
         products_kernel,
-        in_specs=[SMEM_SPEC] + [FAR_SPEC] * 6 + [VMEM_SPEC] * 2,
+        in_specs=[SMEM_SPEC] + [HBM_SPEC] * 2 + [FAR_SPEC] * 4 + [VMEM_SPEC] * 2,
         out_specs=[FAR_SPEC] * 4 + [SMEM_SPEC],
         out_shape=[shape(down)] * 2 + [shape(up)] * 2 + [TOKEN],
-        scratch_shapes=[pltpu.VMEM((count, *down), bf16), pltpu.VMEM((count, *up), bf16)],
+        scratch_shapes=[
+            pltpu.VMEM(arrays[0].shape, bf16),
+            pltpu.VMEM(arrays[1].shape, bf16),
+            pltpu.VMEM((count, *down), bf16),
+            pltpu.VMEM((count, *up), bf16),
+            pltpu.SemaphoreType.DMA((2,)),
+        ],
         compiler_params=pltpu.CompilerParams(vmem_limit_bytes=SMALL_VMEM),
     )(seat, *arrays)
     return FastSum(*outs[:2], (1, 2)), FastSum(*outs[2:4], (2, 1)), outs[4]

time: 410 us -> 409 us (level)
  Pallas kernels: 179 us -> 188 us
  waiting for transfers between devices: 88.5 us -> 80.6 us
    ppermute x35, waiting for transfers between devices: 73.8 us -> 66 us  [xor_permute(): lax.ppermute(x, axis, [(i, i ^ by) for i in range(lax.axis_size(axis))])]
    pallas_call x2, Pallas kernels: 37.8 us -> 44.4 us  [attend_back(): pl.pallas_call(cost_estimate=SMALL_COST, kernel=functools.partial(attend_...]
  transfers between devices with their start and end apart: 68 -> 68, of which waited for: 32 -> 32; matrix products, arithmetic and copies ran while one was open for 7% -> 7% of each run, Pallas kernels for 28% -> 30%
where the time goes in v6:
time: 409 us; the launch traced here: 403 us
  Pallas kernels  188 us (46%)
  waiting for transfers between devices  80.6 us (20%)
  starting transfers between devices  73.2 us (18%)
  local copies, waits for them, and re-layouts  37.1 us (9%)
  other arithmetic  17.6 us (4%)
  between operations  5.32 us (1%)
    pallas_call x24, Pallas kernels, run(): pl.pallas_call(kernel, cost_estimate=SMALL_COST, grid=(1,), in_specs=[who...  143 us
    ppermute x35, waiting for transfers between devices, xor_permute(): lax.ppermute(x, axis, [(i, i ^ by) for i in range(lax.axis_size(axis))])  66 us
    ppermute x35, starting transfers between devices, xor_permute(): lax.ppermute(x, axis, [(i, i ^ by) for i in range(lax.axis_size(axis))])  57.3 us
    pallas_call x2, Pallas kernels, attend_back(): pl.pallas_call(cost_estimate=SMALL_COST, kernel=functools.partial(attend_...  44.4 us
    unnamed x218, local copies, waits for them, and re-layouts  30.2 us
    ppermute x27, waiting for transfers between devices, swap_section(): return lax.ppermute(x, 'section', [(0, 1), (1, 0)])  14.3 us
  transfers between devices with their start and end apart: 68, of which 32 were waited for; matrix products, arithmetic and copies ran while one was open for 7% of the time, Pallas kernels for 30%

profile of v6, /device:TPU:0, one launch (start us, length us, event | category | flops | bytes accessed | tf_op | source)
XLA Modules:
  0.0 403.1 jit_solution(14177906086544998007)
XLA Ops:
  15.4 4.8 %collective-permute-done.6.rest_3_ = bf16[128,768]{1,0:T(8,128)(2,1)S(1)} collective-permute-done((bf16[128,768]{1,0:T(8,128)(2,1)S(1)}, bf16[128,768]{1,0:T(8,128)(2,1)S(1)}, u32[]{:S(2)}, u32[]{:S(2)}) %collective-permute-start.6) | collective-permute-done | bytes 196640 | tf_op jit(solution)/shard_map/ppermute | solution.py:555
  26.3 4.8 %collective-permute-start.1 = (bf16[128,768]{1,0:T(8,128)(2,1)S(1)}, bf16[128,768]{1,0:T(8,128)(2,1)S(1)}, u32[]{:S(2)}, u32[]{:S(2)}) collective-permute-start(bf16[128,768]{1,0:T(8,128)(2,1)S(1)} %get-tuple-element.317), channel_id=1, source_target_pairs={{0,2},{1,3},{3,0},{2,1},{4,6},{5,7},{7,4},{6,5},{8,10},{9,11},{11,... | collective-permute-start | bytes 589832 | tf_op jit(solution)/shard_map/ppermute | solution.py:1237
  33.7 19.9 %shard_map.178 = (bf16[256,768]{1,0:T(8,128)(2,1)}, bf16[256,768]{1,0:T(8,128)(2,1)}, bf16[256,768]{1,0:T(8,128)(2,1)}, bf16[256,768]{1,0:T(8,128)(2,1)}, s32[1]...) custom-call(s32[24]{0:T(128)} %stack.141.info.seat, ...), custom_call_target="tpu_custom_call" | custom-call | tf_op jit(solution)/shard_map/pallas_call | solution.py:187
  58.6 8.5 %shard_map.179 = (bf16[256,768]{1,0:T(8,128)(2,1)S(1)}, f32[256,768]{1,0:T(8,128)}, bf16[256,768]{1,0:T(8,128)(2,1)}, f32[256,3072]{1,0:T(8,128)}, bf16[256,3072]{1,0:T(8,128)(2,1)}, /*index=5*/s32[1]{0:T(128)}) custom-call(s32[24]{0:T(128)S(1)} %copy-done.46, bf16[256,768]{1,0:T(8,128)(2,1)S(1)} %copy-done.13, bf16[256,768]{1,0:T(8,128)(2,1)S(1)} %copy-done.20, ...), custom_call_target="tpu_custom_call" | custom-call | tf_op jit(solution)/shard_map/pallas_call | solution.py:187
  69.5 8.9 %collective-permute-done.11.rest_1_ = bf16[256,768]{1,0:T(8,128)(2,1)S(1)} collective-permute-done((bf16[256,768]{1,0:T(8,128)(2,1)S(1)}, bf16[256,768]{1,0:T(8,128)(2,1)S(1)}, u32[]{:S(2)}, u32[]{:S(2)}) %collective-permute-start.11) | collective-permute-done | bytes 393248 | tf_op jit(solution)/shard_map/ppermute | solution.py:555
  80.8 19.8 %shard_map.180 = (bf16[256,768]{1,0:T(8,128)(2,1)}, bf16[256,768]{1,0:T(8,128)(2,1)}, bf16[256,768]{1,0:T(8,128)(2,1)}, bf16[256,768]{1,0:T(8,128)(2,1)}, s32[1]...) custom-call(s32[24]{0:T(128)} %stack.141.info.seat, ...), custom_call_target="tpu_custom_call" | custom-call | tf_op jit(solution)/shard_map/pallas_call | solution.py:187
  102.7 8.6 %shard_map.181 = (bf16[256,768]{1,0:T(8,128)(2,1)S(1)}, f32[256,768]{1,0:T(8,128)}, bf16[256,768]{1,0:T(8,128)(2,1)}, f32[256,3072]{1,0:T(8,128)}, bf16[256,3072]{1,0:T(8,128)(2,1)}, /*index=5*/s32[1]{0:T(128)}) custom-call(s32[24]{0:T(128)S(1)} %copy-done.47, bf16[256,768]{1,0:T(8,128)(2,1)S(1)} %copy-done.15, bf16[256,768]{1,0:T(8,128)(2,1)S(1)} %copy-done.22, ...), custom_call_target="tpu_custom_call" | custom-call | tf_op jit(solution)/shard_map/pallas_call | solution.py:187
  112.3 9.8 %shard_map.182 = (bf16[256,2304]{1,0:T(8,128)(2,1)S(1)}, bf16[256,2304]{1,0:T(8,128)(2,1)S(1)}, f32[256,768]{1,0:T(8,128)}, bf16[256,768]{1,0:T(8,128)(2,1)S(1)}, f32[1,768]{1,0:T(1,128)S(1)}, /*index=5*/s32[1]{0:T(128)}) custom-call(s32[24]{0:T(128)S(1)} %copy-done.47, bf16[256,768]{1,0:T(8,128)(2,1)S(1)} %pad_maximum_fusion.2.dy_ref, ...), custom_call_target="tpu_custom_call" | custom-call | tf_op jit(solution)/shard_map/pallas_call | solution.py:187
  128.1 8.1 %shard_map.183 = (bf16[8,192,384]{2,1,0:T(8,128)(2,1)}, bf16[8,192,384]{2,1,0:T(8,128)(2,1)}, bf16[8,48,1920]{2,1,0:T(8,128)(2,1)}, bf16[8,48,1920]{2,1,0:T(8,128)(2,1)}, s32[1]{0:T(128)}) custom-call(s32[24]{0:T(128)S(1)} %copy-done.47, bf16[256,3072]{1,0:T(8,128)(2,1)} %get-tuple-element.171.active_hbm, bf16[256,3072]{1,0:T(8,128)(2,1)} %copy-done.69, ...), custom_call_target="tpu_custom_call" | custom-call | tf_op jit(solution)/shard_map/pallas_call | solution.py:187
  136.2 6.8 %collective-permute-start.19 = (bf16[8,48,1920]{2,1,0:T(8,128)(2,1)}, bf16[8,48,1920]{2,1,0:T(8,128)(2,1)S(1)}, u32[]{:S(2)}, u32[]{:S(2)}) collective-permute-start(bf16[8,48,1920]{2,1,0:T(8,128)(2,1)} %get-tuple-element.182), channel_id=1, source_target_pairs={{0,2},{1,3},{2,0},{3,1},{4,6},{5,7},{6,4},{7,5},{8,10},{9,11},{10,... | collective-permute-start | bytes 4423688 | tf_op jit(solution)/shard_map/ppermute | solution.py:555
  143.5 22.3 %shard_map.184 = (bf16[256,768]{1,0:T(8,128)(2,1)}, bf16[1024,768]{1,0:T(8,128)(2,1)}, bf16[1024,768]{1,0:T(8,128)(2,1)}, f32[12,768]{1,0:T(8,128)}, f32[12,768]{1,0:T(8,128)}, /*index=5*/s32[1]{0:T(128)}) custom-call(s32[24]{0:T(128)} %stack.141.info.seat, bf16[256,768]{1,0:T(8,128)(2,1)} %get-tuple-element.164.q_ref, bf16[256,768]{1,0:T(8,128)(2,1)} %copy-done.40, ...), custom_call_target="tpu_custom_call" | custom-call | tf_op jit(solution)/shard_map/pallas_call | solution.py:501
  165.8 5.3 %collective-permute-done.18.refs_3_ = bf16[8,192,384]{2,1,0:T(8,128)(2,1)S(1)} collective-permute-done((bf16[8,192,384]{2,1,0:T(8,128)(2,1)}, bf16[8,192,384]{2,1,0:T(8,128)(2,1)S(1)}, u32[]{:S(2)}, u32[]{:S(2)}) %collective-permute-start.18) | collective-permute-done | bytes 1179680 | tf_op jit(solution)/shard_map/ppermute | solution.py:555
  171.2 4.9 %collective-permute-done.19.refs_5_ = bf16[8,48,1920]{2,1,0:T(8,128)(2,1)S(1)} collective-permute-done((bf16[8,48,1920]{2,1,0:T(8,128)(2,1)}, bf16[8,48,1920]{2,1,0:T(8,128)(2,1)S(1)}, u32[]{:S(2)}, u32[]{:S(2)}) %collective-permute-start.19) | collective-permute-done | bytes 1474592 | tf_op jit(solution)/shard_map/ppermute | solution.py:555
  179.6 4.3 %shard_map.185 = (bf16[4,192,384]{2,1,0:T(8,128)(2,1)S(1)}, bf16[4,192,384]{2,1,0:T(8,128)(2,1)S(1)}, bf16[4,48,1920]{2,1,0:T(8,128)(2,1)S(1)}, bf16[4,48,1920]{...) custom-call(s32[24]{0:T(128)S(1)} %copy-done.48, ...), custom_call_target="tpu_custom_call", output_to_operand_aliasing={{5}: (2, {}), {6}: (3, {})} | custom-call | tf_op jit(solution)/shard_map/pallas_call | solution.py:187
  190.6 8.4 %shard_map.186 = (bf16[512,768]{1,0:T(8,128)(2,1)S(1)}, bf16[512,768]{1,0:T(8,128)(2,1)S(1)}, f32[256,768]{1,0:T(8,128)S(1)}, bf16[8,48,512]{2,1,0:T(8,128)(2,1)...) custom-call(s32[24]{0:T(128)S(1)} %copy-done.48, ...), custom_call_target="tpu_custom_call" | custom-call | tf_op jit(solution)/shard_map/pallas_call | solution.py:187
  218.7 6.3 %collective-permute-done.26.refs_2_ = bf16[8,48,512]{2,1,0:T(8,128)(2,1)S(1)} collective-permute-done((bf16[8,48,512]{2,1,0:T(8,128)(2,1)}, bf16[8,48,512]{2,1,0:T(8,128)(2,1)S(1)}, u32[]{:S(2)}, u32[]{:S(2)}) %collective-permute-start.26) | collective-permute-done | bytes 393248 | tf_op jit(solution)/shard_map/ppermute | solution.py:555
  239.4 9.8 %shard_map.189 = (bf16[256,2304]{1,0:T(8,128)(2,1)S(1)}, bf16[256,2304]{1,0:T(8,128)(2,1)S(1)}, f32[256,768]{1,0:T(8,128)}, bf16[256,768]{1,0:T(8,128)(2,1)S(1)}, f32[1,768]{1,0:T(1,128)S(1)}, /*index=5*/s32[1]{0:T(128)}) custom-call(s32[24]{0:T(128)S(1)} %copy-done.48, bf16[256,768]{1,0:T(8,128)(2,1)S(1)} %fusion.16.dy_ref, ...), custom_call_target="tpu_custom_call" | custom-call | tf_op jit(solution)/shard_map/pallas_call | solution.py:187
  260.6 8.2 %shard_map.192 = (bf16[8,192,384]{2,1,0:T(8,128)(2,1)}, bf16[8,192,384]{2,1,0:T(8,128)(2,1)}, bf16[8,48,1920]{2,1,0:T(8,128)(2,1)}, bf16[8,48,1920]{2,1,0:T(8,128)(2,1)}, s32[1]{0:T(128)}) custom-call(s32[24]{0:T(128)S(1)} %copy-done.48, bf16[256,3072]{1,0:T(8,128)(2,1)} %get-tuple-element.227.active_hbm, ...), custom_call_target="tpu_custom_call" | custom-call | tf_op jit(solution)/shard_map/pallas_call | solution.py:187
  273.6 22.2 %shard_map.193 = (bf16[256,768]{1,0:T(8,128)(2,1)}, bf16[1024,768]{1,0:T(8,128)(2,1)}, bf16[1024,768]{1,0:T(8,128)(2,1)}, f32[12,768]{1,0:T(8,128)}, f32[12,768]{1,0:T(8,128)}, /*index=5*/s32[1]{0:T(128)}) custom-call(s32[24]{0:T(128)} %stack.141.info.seat, bf16[256,768]{1,0:T(8,128)(2,1)} %get-tuple-element.207.q_ref, bf16[256,768]{1,0:T(8,128)(2,1)} %copy-done.39, ...), custom_call_target="tpu_custom_call" | custom-call | tf_op jit(solution)/shard_map/pallas_call | solution.py:501
  297.1 6.2 %collective-permute-done.39.refs_5_ = bf16[8,48,1920]{2,1,0:T(8,128)(2,1)S(1)} collective-permute-done((bf16[8,48,1920]{2,1,0:T(8,128)(2,1)}, bf16[8,48,1920]{2,1,0:T(8,128)(2,1)S(1)}, u32[]{:S(2)}, u32[]{:S(2)}) %collective-permute-start.39) | collective-permute-done | bytes 1474592 | tf_op jit(solution)/shard_map/ppermute | solution.py:555
  307.0 4.9 %shard_map.194 = (bf16[4,192,384]{2,1,0:T(8,128)(2,1)S(1)}, bf16[4,192,384]{2,1,0:T(8,128)(2,1)S(1)}, bf16[4,48,1920]{2,1,0:T(8,128)(2,1)S(1)}, bf16[4,48,1920]{...) custom-call(s32[24]{0:T(128)S(1)} %copy-done.49, ...), custom_call_target="tpu_custom_call", output_to_operand_aliasing={{6}: (2, {}), {7}: (3, {})} | custom-call | tf_op jit(solution)/shard_map/pallas_call | solution.py:187
  320.9 7.6 %shard_map.196 = (bf16[512,768]{1,0:T(8,128)(2,1)S(1)}, bf16[512,768]{1,0:T(8,128)(2,1)S(1)}, f32[256,768]{1,0:T(8,128)S(1)}, bf16[8,48,512]{2,1,0:T(8,128)(2,1)...) custom-call(s32[24]{0:T(128)S(1)} %copy-done.49, ...), custom_call_target="tpu_custom_call" | custom-call | tf_op jit(solution)/shard_map/pallas_call | solution.py:187
  352.4 3.4 collective-permute-done.49.refs_2_
  390.6 3.5 collective-permute-done.65.refs_4_
  (403 shorter events, 180.6 us)
Async XLA Ops:
  0.7 53.1 %collective-permute-start.10 = (bf16[1,3072,768]{2,1,0:T(8,128)(2,1)}, bf16[1,3072,768]{2,1,0:T(8,128)(2,1)}, u32[]{:S(2)}, u32[]{:S(2)}) collective-permute-start(bf16[1,3072,768]{2,1,0:T(8,128)(2,1)} %down_own.7), channel_id=1, source_target_pairs={{0,16},{16,0},{1,17},{17,1},{2,18},{18,2},{3,19},{19,3},{4,20},{20... | collective-permute-start | bytes 14155784 | tf_op jit(solution)/shard_map/ppermute | solution.py:551
  1.2 52.6 %collective-permute-start.9 = (bf16[1,768,3072]{2,1,0:T(8,128)(2,1)}, bf16[1,768,3072]{2,1,0:T(8,128)(2,1)}, u32[]{:S(2)}, u32[]{:S(2)}) collective-permute-start(bf16[1,768,3072]{2,1,0:T(8,128)(2,1)} %up_own.7), channel_id=1, source_target_pairs={{0,16},{16,0},{1,17},{17,1},{2,18},{18,2},{3,19},{19,3},{4,20},{20... | collective-permute-start | bytes 14155784 | tf_op jit(solution)/shard_map/ppermute | solution.py:551
  1.3 25.1 %collective-permute-start.3 = (bf16[1,768,2304]{2,1,0:T(8,128)(2,1)}, bf16[1,768,2304]{2,1,0:T(8,128)(2,1)}, u32[]{:S(2)}, u32[]{:S(2)}) collective-permute-start(bf16[1,768,2304]{2,1,0:T(8,128)(2,1)} %joint_own.7), channel_id=1, source_target_pairs={{0,16},{16,0},{1,17},{17,1},{2,18},{18,2},{3,19},{19,3},{4,20},{20... | collective-permute-start | bytes 10616840 | tf_op jit(solution)/shard_map/ppermute | solution.py:551
  10.9 42.8 %collective-permute-start.8 = (bf16[1,768,768]{2,1,0:T(8,128)(2,1)}, bf16[1,768,768]{2,1,0:T(8,128)(2,1)S(1)}, u32[]{:S(2)}, u32[]{:S(2)}) collective-permute-start(bf16[1,768,768]{2,1,0:T(8,128)(2,1)} %mixer_own.7), channel_id=1, source_target_pairs={{0,16},{16,0},{1,17},{17,1},{2,18},{18,2},{3,19},{19,3},{4,20},{20... | collective-permute-start | bytes 3538952 | tf_op jit(solution)/shard_map/ppermute | solution.py:551
  24.7 28.9 %collective-permute-start = (bf16[128,768]{1,0:T(8,128)(2,1)}, bf16[128,768]{1,0:T(8,128)(2,1)S(1)}, u32[]{:S(2)}, u32[]{:S(2)}) collective-permute-start(bf16[128,768]{1,0:T(8,128)(2,1)} %get-tuple-element.316), channel_id=1, source_target_pairs={{3,2},{2,3},{0,0},{1,1},{7,6},{6,7},{4,4},{5,5},{11,10},{10,11},{8... | collective-permute-start | bytes 589832 | tf_op jit(solution)/shard_map/ppermute | solution.py:1237
  26.3 27.4 %collective-permute-start.1 = (bf16[128,768]{1,0:T(8,128)(2,1)S(1)}, bf16[128,768]{1,0:T(8,128)(2,1)S(1)}, u32[]{:S(2)}, u32[]{:S(2)}) collective-permute-start(bf16[128,768]{1,0:T(8,128)(2,1)S(1)} %get-tuple-element.317), channel_id=1, source_target_pairs={{0,2},{1,3},{3,0},{2,1},{4,6},{5,7},{7,4},{6,5},{8,10},{9,11},{11,... | collective-permute-start | bytes 589832 | tf_op jit(solution)/shard_map/ppermute | solution.py:1237
  136.2 39.8 %collective-permute-start.19 = (bf16[8,48,1920]{2,1,0:T(8,128)(2,1)}, bf16[8,48,1920]{2,1,0:T(8,128)(2,1)S(1)}, u32[]{:S(2)}, u32[]{:S(2)}) collective-permute-start(bf16[8,48,1920]{2,1,0:T(8,128)(2,1)} %get-tuple-element.182), channel_id=1, source_target_pairs={{0,2},{1,3},{2,0},{3,1},{4,6},{5,7},{6,4},{7,5},{8,10},{9,11},{10,... | collective-permute-start | bytes 4423688 | tf_op jit(solution)/shard_map/ppermute | solution.py:555
  143.0 28.2 %collective-permute-start.18 = (bf16[8,192,384]{2,1,0:T(8,128)(2,1)}, bf16[8,192,384]{2,1,0:T(8,128)(2,1)S(1)}, u32[]{:S(2)}, u32[]{:S(2)}) collective-permute-start(bf16[8,192,384]{2,1,0:T(8,128)(2,1)} %get-tuple-element.180), channel_id=1, source_target_pairs={{0,1},{1,0},{2,3},{3,2},{4,5},{5,4},{6,7},{7,6},{8,9},{9,8},{10,11... | collective-permute-start | bytes 3538952 | tf_op jit(solution)/shard_map/ppermute | solution.py:555
  185.8 18.9 %collective-permute-start.24 = (bf16[4,48,1920]{2,1,0:T(8,128)(2,1)S(1)}, bf16[4,48,1920]{2,1,0:T(8,128)(2,1)S(1)}, u32[]{:S(2)}, u32[]{:S(2)}) collective-permute-start(bf16[4,48,1920]{2,1,0:T(8,128)(2,1)S(1)} %get-tuple-element.195), channel_id=1, source_target_pairs={{0,1},{1,0},{2,3},{3,2},{4,5},{5,4},{6,7},{7,6},{8,9},{9,8},{10,11... | collective-permute-start | bytes 2211848 | tf_op jit(solution)/shard_map/ppermute | solution.py:555
  210.5 49.3 %collective-permute-start.34 = (bf16[256,3072]{1,0:T(8,128)(2,1)}, bf16[256,3072]{1,0:T(8,128)(2,1)}, u32[]{:S(2)}, u32[]{:S(2)}) collective-permute-start(bf16[256,3072]{1,0:T(8,128)(2,1)} %get-tuple-element.227.active_hbm), channel_id=1, source_target_pairs={{0,16},{16,0},{1,17},{17,1},{2,18},{18,2},{3,19},{19,3},{4,20},{20... | collective-permute-start | bytes 4718600 | tf_op jit(solution)/shard_map/ppermute | solution.py:551
  215.5 18.0 %collective-permute-start.28 = (bf16[2,128,768]{2,1,0:T(8,128)(2,1)}, bf16[2,128,768]{2,1,0:T(8,128)(2,1)}, u32[]{:S(2)}, u32[]{:S(2)}) collective-permute-start(bf16[2,128,768]{2,1,0:T(8,128)(2,1)} %dynamic-slice_bitcast_fusion.1), channel_id=1, source_target_pairs={{0,1},{1,0},{2,3},{3,2},{4,5},{5,4},{6,7},{7,6},{8,9},{9,8},{10,11... | collective-permute-start | bytes 1179656 | tf_op jit(solution)/shard_map/ppermute | solution.py:555
  217.8 18.0 %collective-permute-start.29 = (bf16[128,768]{1,0:T(8,128)(2,1)}, bf16[128,768]{1,0:T(8,128)(2,1)S(1)}, u32[]{:S(2)}, u32[]{:S(2)}) collective-permute-start(bf16[128,768]{1,0:T(8,128)(2,1)} %get-tuple-element.321), channel_id=1, source_target_pairs={{2,0},{3,1},{0,3},{1,2},{6,4},{7,5},{4,7},{5,6},{10,8},{11,9},{8,1... | collective-permute-start | bytes 589832 | tf_op jit(solution)/shard_map/ppermute | solution.py:1244
  225.0 24.2 %collective-permute-start.30 = (bf16[128,768]{1,0:T(8,128)(2,1)}, bf16[128,768]{1,0:T(8,128)(2,1)S(1)}, u32[]{:S(2)}, u32[]{:S(2)}) collective-permute-start(bf16[128,768]{1,0:T(8,128)(2,1)} %get-tuple-element.320), channel_id=1, source_target_pairs={{2,3},{3,2},{0,0},{1,1},{6,7},{7,6},{4,4},{5,5},{10,11},{11,10},{8... | collective-permute-start | bytes 589832 | tf_op jit(solution)/shard_map/ppermute | solution.py:1245
  226.6 26.2 %collective-permute-start.33 = (bf16[2,48,3456]{2,1,0:T(8,128)(2,1)S(1)}, bf16[2,48,3456]{2,1,0:T(8,128)(2,1)}, u32[]{:S(2)}, u32[]{:S(2)}) collective-permute-start(bf16[2,48,3456]{2,1,0:T(8,128)(2,1)S(1)} %copy-done.58), channel_id=1, source_target_pairs={{0,4},{4,0},{8,12},{12,8},{1,5},{5,1},{9,13},{13,9},{2,6},{6,2},{1... | collective-permute-start | bytes 1990664 | tf_op jit(solution)/shard_map/ppermute | solution.py:555
  268.8 34.6 %collective-permute-start.39 = (bf16[8,48,1920]{2,1,0:T(8,128)(2,1)}, bf16[8,48,1920]{2,1,0:T(8,128)(2,1)S(1)}, u32[]{:S(2)}, u32[]{:S(2)}) collective-permute-start(bf16[8,48,1920]{2,1,0:T(8,128)(2,1)} %get-tuple-element.238), channel_id=1, source_target_pairs={{0,2},{1,3},{2,0},{3,1},{4,6},{5,7},{6,4},{7,5},{8,10},{9,11},{10,... | collective-permute-start | bytes 4423688 | tf_op jit(solution)/shard_map/ppermute | solution.py:555
  268.8 28.3 %collective-permute-start.38 = (bf16[8,192,384]{2,1,0:T(8,128)(2,1)}, bf16[8,192,384]{2,1,0:T(8,128)(2,1)S(1)}, u32[]{:S(2)}, u32[]{:S(2)}) collective-permute-start(bf16[8,192,384]{2,1,0:T(8,128)(2,1)} %get-tuple-element.236), channel_id=1, source_target_pairs={{0,1},{1,0},{2,3},{3,2},{4,5},{5,4},{6,7},{7,6},{8,9},{9,8},{10,11... | collective-permute-start | bytes 3538952 | tf_op jit(solution)/shard_map/ppermute | solution.py:555
  269.4 26.4 %collective-permute-start.40 = (bf16[48,3456]{1,0:T(8,128)(2,1)S(1)}, bf16[48,3456]{1,0:T(8,128)(2,1)S(1)}, u32[]{:S(2)}, u32[]{:S(2)}) collective-permute-start(bf16[48,3456]{1,0:T(8,128)(2,1)S(1)} %get-tuple-element.240), channel_id=1, source_target_pairs={{0,8},{4,12},{8,0},{12,4},{1,9},{5,13},{9,1},{13,5},{2,10},{6,14},... | collective-permute-start | bytes 995336 | tf_op jit(solution)/shard_map/ppermute | solution.py:555
  272.0 39.9 %collective-permute-start.41 = (bf16[2,48,1152]{2,1,0:T(8,128)(2,1)S(1)}, bf16[2,48,1152]{2,1,0:T(8,128)(2,1)}, u32[]{:S(2)}, u32[]{:S(2)}) collective-permute-start(bf16[2,48,1152]{2,1,0:T(8,128)(2,1)S(1)} %get-tuple-element.245), channel_id=1, source_target_pairs={{0,4},{4,0},{8,12},{12,8},{1,5},{5,1},{9,13},{13,9},{2,6},{6,2},{1... | collective-permute-start | bytes 663560 | tf_op jit(solution)/shard_map/ppermute | solution.py:555
  314.3 18.9 %collective-permute-start.46 = (bf16[4,48,1920]{2,1,0:T(8,128)(2,1)S(1)}, bf16[4,48,1920]{2,1,0:T(8,128)(2,1)S(1)}, u32[]{:S(2)}, u32[]{:S(2)}) collective-permute-start(bf16[4,48,1920]{2,1,0:T(8,128)(2,1)S(1)} %get-tuple-element.258), channel_id=1, source_target_pairs={{0,1},{1,0},{2,3},{3,2},{4,5},{5,4},{6,7},{7,6},{8,9},{9,8},{10,11... | collective-permute-start | bytes 2211848 | tf_op jit(solution)/shard_map/ppermute | solution.py:555
  314.9 16.1 %collective-permute-start.45 = (bf16[4,192,384]{2,1,0:T(8,128)(2,1)S(1)}, bf16[4,192,384]{2,1,0:T(8,128)(2,1)S(1)}, u32[]{:S(2)}, u32[]{:S(2)}) collective-permute-start(bf16[4,192,384]{2,1,0:T(8,128)(2,1)S(1)} %get-tuple-element.256), channel_id=1, source_target_pairs={{0,2},{1,3},{2,0},{3,1},{4,6},{5,7},{6,4},{7,5},{8,10},{9,11},{10,... | collective-permute-start | bytes 1769480 | tf_op jit(solution)/shard_map/ppermute | solution.py:555
  344.1 16.3 %collective-permute-start.51 = (bf16[2,48,3456]{2,1,0:T(8,128)(2,1)}, bf16[2,48,3456]{2,1,0:T(8,128)(2,1)S(1)}, u32[]{:S(2)}, u32[]{:S(2)}) collective-permute-start(bf16[2,48,3456]{2,1,0:T(8,128)(2,1)} %copy-done.59), channel_id=1, source_target_pairs={{0,4},{4,0},{8,12},{12,8},{1,5},{5,1},{9,13},{13,9},{2,6},{6,2},{1... | collective-permute-start | bytes 1990664 | tf_op jit(solution)/shard_map/ppermute | solution.py:555
  345.9 22.4 %collective-permute-start.58 = (f32[26,768]{1,0:T(8,128)}, f32[26,768]{1,0:T(8,128)}, u32[]{:S(2)}, u32[]{:S(2)}) collective-permute-start(f32[26,768]{1,0:T(8,128)} %add_add_fusion.3), channel_id=1, source_target_pairs={{0,2},{1,3},{2,0},{3,1},{4,6},{5,7},{6,4},{7,5},{8,10},{9,11},{10,... | collective-permute-start | bytes 239624 | tf_op jit(solution)/shard_map/ppermute | solution.py:555
  349.9 21.1 %collective-permute-start.52 = (bf16[2,128,768]{2,1,0:T(8,128)(2,1)}, bf16[2,128,768]{2,1,0:T(8,128)(2,1)}, u32[]{:S(2)}, u32[]{:S(2)}) collective-permute-start(bf16[2,128,768]{2,1,0:T(8,128)(2,1)} %dynamic-slice_bitcast_fusion), channel_id=1, source_target_pairs={{0,1},{1,0},{2,3},{3,2},{4,5},{5,4},{6,7},{7,6},{8,9},{9,8},{10,11... | collective-permute-start | bytes 1179656 | tf_op jit(solution)/shard_map/ppermute | solution.py:555
  366.6 24.0 %collective-permute-start.63 = (bf16[48,3456]{1,0:T(8,128)(2,1)}, bf16[48,3456]{1,0:T(8,128)(2,1)S(1)}, u32[]{:S(2)}, u32[]{:S(2)}) collective-permute-start(bf16[48,3456]{1,0:T(8,128)(2,1)} %copy-done.63), channel_id=1, source_target_pairs={{0,8},{4,12},{8,0},{12,4},{1,9},{5,13},{9,1},{13,5},{2,10},{6,14},... | collective-permute-start | bytes 995336 | tf_op jit(solution)/shard_map/ppermute | solution.py:555
  (153 other events, 1156.0 us)

commit v7 on v6

--- a/solution.py
+++ b/solution.py
@@ -143,12 +143,15 @@
             u[pl.ds(pl.multiple_of(step * HEADS * bq + g * bq, bq), bq), :] = part.astype(bf16)
             att = att + part * post[g : g + 1, :]
         att_ref[mine, :] = att.astype(bf16)
+        for i, (x, y) in enumerate(((u, u_hbm), (lse, lse_hbm))):
+            pltpu.make_async_copy(x.at[rows], y.at[rows], sems.at[4 + 2 * step + i]).start()
         return carry
 
     lax.fori_loop(0, 2, rows_step, 0)
-    outs += [pltpu.make_async_copy(u, u_hbm, sems.at[4]), pltpu.make_async_copy(lse, lse_hbm, sems.at[5])]
-    for out in outs[3:]:
-        out.start()
+    for step in range(2):
+        rows = pl.ds(step * HEADS * bq, HEADS * bq)
+        for i, (x, y) in enumerate(((u, u_hbm), (lse, lse_hbm))):
+            outs.append(pltpu.make_async_copy(x.at[rows], y.at[rows], sems.at[4 + 2 * step + i]))
     for out in outs:
         out.wait()
 
@@ -223,7 +226,7 @@
             pltpu.VMEM((HEADS * bq, width), f32),
             pltpu.VMEM((HEADS * bq, 128), f32),
             pltpu.VMEM((HEADS * bq, 128), f32),
-            pltpu.SemaphoreType.DMA((6,)),
+            pltpu.SemaphoreType.DMA((8,)),
         ],
         compiler_params=pltpu.CompilerParams(vmem_limit_bytes=BIG_VMEM),
     )(info, *smalls, *joints, *pieces)

time: 409 us -> 407 us (level)
  Pallas kernels: 188 us -> 196 us
  waiting for transfers between devices: 80.6 us -> 73.3 us
    ppermute x35, waiting for transfers between devices: 66 us -> 58.7 us  [xor_permute(): lax.ppermute(x, axis, [(i, i ^ by) for i in range(lax.axis_size(axis))])]
    pallas_call x2, Pallas kernels: 44.4 us -> 51.1 us  [attend_back(): pl.pallas_call(cost_estimate=SMALL_COST, kernel=functools.partial(attend_...]
  transfers between devices with their start and end apart: 68 -> 68, of which waited for: 32 -> 32; matrix products, arithmetic and copies ran while one was open for 7% -> 7% of each run, Pallas kernels for 30% -> 32%
where the time goes in v7:
time: 407 us; the launch traced here: 401 us
  Pallas kernels  196 us (48%)
  waiting for transfers between devices  73.3 us (18%)
  starting transfers between devices  70.4 us (17%)
  local copies, waits for them, and re-layouts  37.1 us (9%)
  other arithmetic  17.6 us (4%)
  between operations  5.33 us (1%)
    pallas_call x24, Pallas kernels, run(): pl.pallas_call(kernel, cost_estimate=SMALL_COST, grid=(1,), in_specs=[who...  145 us
    ppermute x35, waiting for transfers between devices, xor_permute(): lax.ppermute(x, axis, [(i, i ^ by) for i in range(lax.axis_size(axis))])  58.7 us
    ppermute x35, starting transfers between devices, xor_permute(): lax.ppermute(x, axis, [(i, i ^ by) for i in range(lax.axis_size(axis))])  53.7 us
    pallas_call x2, Pallas kernels, attend_back(): pl.pallas_call(cost_estimate=SMALL_COST, kernel=functools.partial(attend_...  51.1 us
    unnamed x218, local copies, waits for them, and re-layouts  30.2 us
    ppermute x27, waiting for transfers between devices, swap_section(): return lax.ppermute(x, 'section', [(0, 1), (1, 0)])  14.3 us
  transfers between devices with their start and end apart: 68, of which 32 were waited for; matrix products, arithmetic and copies ran while one was open for 7% of the time, Pallas kernels for 32%

profile of v7, /device:TPU:0, one launch (start us, length us, event | category | flops | bytes accessed | tf_op | source)
XLA Modules:
  0.0 401.3 jit_solution(14978004434027735144)
XLA Ops:
  15.4 4.8 %collective-permute-done.6.rest_3_ = bf16[128,768]{1,0:T(8,128)(2,1)S(1)} collective-permute-done((bf16[128,768]{1,0:T(8,128)(2,1)S(1)}, bf16[128,768]{1,0:T(8,128)(2,1)S(1)}, u32[]{:S(2)}, u32[]{:S(2)}) %collective-permute-start.6) | collective-permute-done | bytes 196640 | tf_op jit(solution)/shard_map/ppermute | solution.py:558
  26.3 4.8 %collective-permute-start.1 = (bf16[128,768]{1,0:T(8,128)(2,1)S(1)}, bf16[128,768]{1,0:T(8,128)(2,1)S(1)}, u32[]{:S(2)}, u32[]{:S(2)}) collective-permute-start(bf16[128,768]{1,0:T(8,128)(2,1)S(1)} %get-tuple-element.317), channel_id=1, source_target_pairs={{0,2},{1,3},{3,0},{2,1},{4,6},{5,7},{7,4},{6,5},{8,10},{9,11},{11,... | collective-permute-start | bytes 589832 | tf_op jit(solution)/shard_map/ppermute | solution.py:1240
  33.7 20.7 %shard_map.178 = (bf16[256,768]{1,0:T(8,128)(2,1)}, bf16[256,768]{1,0:T(8,128)(2,1)}, bf16[256,768]{1,0:T(8,128)(2,1)}, bf16[256,768]{1,0:T(8,128)(2,1)}, s32[1]...) custom-call(s32[24]{0:T(128)} %stack.141.info.seat, ...), custom_call_target="tpu_custom_call" | custom-call | tf_op jit(solution)/shard_map/pallas_call | solution.py:190
  59.4 8.5 %shard_map.179 = (bf16[256,768]{1,0:T(8,128)(2,1)S(1)}, f32[256,768]{1,0:T(8,128)}, bf16[256,768]{1,0:T(8,128)(2,1)}, f32[256,3072]{1,0:T(8,128)}, bf16[256,3072]{1,0:T(8,128)(2,1)}, /*index=5*/s32[1]{0:T(128)}) custom-call(s32[24]{0:T(128)S(1)} %copy-done.46, bf16[256,768]{1,0:T(8,128)(2,1)S(1)} %copy-done.13, bf16[256,768]{1,0:T(8,128)(2,1)S(1)} %copy-done.20, ...), custom_call_target="tpu_custom_call" | custom-call | tf_op jit(solution)/shard_map/pallas_call | solution.py:190
  70.3 8.8 %collective-permute-done.11.rest_1_ = bf16[256,768]{1,0:T(8,128)(2,1)S(1)} collective-permute-done((bf16[256,768]{1,0:T(8,128)(2,1)S(1)}, bf16[256,768]{1,0:T(8,128)(2,1)S(1)}, u32[]{:S(2)}, u32[]{:S(2)}) %collective-permute-start.11) | collective-permute-done | bytes 393248 | tf_op jit(solution)/shard_map/ppermute | solution.py:558
  81.6 20.6 %shard_map.180 = (bf16[256,768]{1,0:T(8,128)(2,1)}, bf16[256,768]{1,0:T(8,128)(2,1)}, bf16[256,768]{1,0:T(8,128)(2,1)}, bf16[256,768]{1,0:T(8,128)(2,1)}, s32[1]...) custom-call(s32[24]{0:T(128)} %stack.141.info.seat, ...), custom_call_target="tpu_custom_call" | custom-call | tf_op jit(solution)/shard_map/pallas_call | solution.py:190
  104.3 8.6 %shard_map.181 = (bf16[256,768]{1,0:T(8,128)(2,1)S(1)}, f32[256,768]{1,0:T(8,128)}, bf16[256,768]{1,0:T(8,128)(2,1)}, f32[256,3072]{1,0:T(8,128)}, bf16[256,3072]{1,0:T(8,128)(2,1)}, /*index=5*/s32[1]{0:T(128)}) custom-call(s32[24]{0:T(128)S(1)} %copy-done.47, bf16[256,768]{1,0:T(8,128)(2,1)S(1)} %copy-done.15, bf16[256,768]{1,0:T(8,128)(2,1)S(1)} %copy-done.22, ...), custom_call_target="tpu_custom_call" | custom-call | tf_op jit(solution)/shard_map/pallas_call | solution.py:190
  113.9 9.8 %shard_map.182 = (bf16[256,2304]{1,0:T(8,128)(2,1)S(1)}, bf16[256,2304]{1,0:T(8,128)(2,1)S(1)}, f32[256,768]{1,0:T(8,128)}, bf16[256,768]{1,0:T(8,128)(2,1)S(1)}, f32[1,768]{1,0:T(1,128)S(1)}, /*index=5*/s32[1]{0:T(128)}) custom-call(s32[24]{0:T(128)S(1)} %copy-done.47, bf16[256,768]{1,0:T(8,128)(2,1)S(1)} %pad_maximum_fusion.2.dy_ref, ...), custom_call_target="tpu_custom_call" | custom-call | tf_op jit(solution)/shard_map/pallas_call | solution.py:190
  129.7 8.1 %shard_map.183 = (bf16[8,192,384]{2,1,0:T(8,128)(2,1)}, bf16[8,192,384]{2,1,0:T(8,128)(2,1)}, bf16[8,48,1920]{2,1,0:T(8,128)(2,1)}, bf16[8,48,1920]{2,1,0:T(8,128)(2,1)}, s32[1]{0:T(128)}) custom-call(s32[24]{0:T(128)S(1)} %copy-done.47, bf16[256,3072]{1,0:T(8,128)(2,1)} %get-tuple-element.171.active_hbm, bf16[256,3072]{1,0:T(8,128)(2,1)} %copy-done.69, ...), custom_call_target="tpu_custom_call" | custom-call | tf_op jit(solution)/shard_map/pallas_call | solution.py:190
  141.7 25.6 %shard_map.184 = (bf16[256,768]{1,0:T(8,128)(2,1)}, bf16[1024,768]{1,0:T(8,128)(2,1)}, bf16[1024,768]{1,0:T(8,128)(2,1)}, f32[12,768]{1,0:T(8,128)}, f32[12,768]{1,0:T(8,128)}, /*index=5*/s32[1]{0:T(128)}) custom-call(s32[24]{0:T(128)} %stack.141.info.seat, bf16[256,768]{1,0:T(8,128)(2,1)} %get-tuple-element.164.q_ref, bf16[256,768]{1,0:T(8,128)(2,1)} %copy-done.40, ...), custom_call_target="tpu_custom_call" | custom-call | tf_op jit(solution)/shard_map/pallas_call | solution.py:504
  169.3 4.9 %collective-permute-done.19.refs_5_ = bf16[8,48,1920]{2,1,0:T(8,128)(2,1)S(1)} collective-permute-done((bf16[8,48,1920]{2,1,0:T(8,128)(2,1)}, bf16[8,48,1920]{2,1,0:T(8,128)(2,1)S(1)}, u32[]{:S(2)}, u32[]{:S(2)}) %collective-permute-start.19) | collective-permute-done | bytes 1474592 | tf_op jit(solution)/shard_map/ppermute | solution.py:558
  177.7 4.3 %shard_map.185 = (bf16[4,192,384]{2,1,0:T(8,128)(2,1)S(1)}, bf16[4,192,384]{2,1,0:T(8,128)(2,1)S(1)}, bf16[4,48,1920]{2,1,0:T(8,128)(2,1)S(1)}, bf16[4,48,1920]{...) custom-call(s32[24]{0:T(128)S(1)} %copy-done.48, ...), custom_call_target="tpu_custom_call", output_to_operand_aliasing={{5}: (2, {}), {6}: (3, {})} | custom-call | tf_op jit(solution)/shard_map/pallas_call | solution.py:190
  188.7 8.4 %shard_map.186 = (bf16[512,768]{1,0:T(8,128)(2,1)S(1)}, bf16[512,768]{1,0:T(8,128)(2,1)S(1)}, f32[256,768]{1,0:T(8,128)S(1)}, bf16[8,48,512]{2,1,0:T(8,128)(2,1)...) custom-call(s32[24]{0:T(128)S(1)} %copy-done.48, ...), custom_call_target="tpu_custom_call" | custom-call | tf_op jit(solution)/shard_map/pallas_call | solution.py:190
  197.2 4.2 %collective-permute-done.23.refs_2_ = bf16[4,192,384]{2,1,0:T(8,128)(2,1)S(1)} collective-permute-done((bf16[4,192,384]{2,1,0:T(8,128)(2,1)S(1)}, bf16[4,192,384]{2,1,0:T(8,128)(2,1)S(1)}, u32[]{:S(2)}, u32[]{:S(2)}) %collective-permute-start.23) | collective-permute-done | bytes 589856 | tf_op jit(solution)/shard_map/ppermute | solution.py:558
  204.0 3.4 shard_map.187
  217.8 5.4 %collective-permute-done.26.refs_2_ = bf16[8,48,512]{2,1,0:T(8,128)(2,1)S(1)} collective-permute-done((bf16[8,48,512]{2,1,0:T(8,128)(2,1)}, bf16[8,48,512]{2,1,0:T(8,128)(2,1)S(1)}, u32[]{:S(2)}, u32[]{:S(2)}) %collective-permute-start.26) | collective-permute-done | bytes 393248 | tf_op jit(solution)/shard_map/ppermute | solution.py:558
  237.6 9.8 %shard_map.189 = (bf16[256,2304]{1,0:T(8,128)(2,1)S(1)}, bf16[256,2304]{1,0:T(8,128)(2,1)S(1)}, f32[256,768]{1,0:T(8,128)}, bf16[256,768]{1,0:T(8,128)(2,1)S(1)}, f32[1,768]{1,0:T(1,128)S(1)}, /*index=5*/s32[1]{0:T(128)}) custom-call(s32[24]{0:T(128)S(1)} %copy-done.48, bf16[256,768]{1,0:T(8,128)(2,1)S(1)} %fusion.16.dy_ref, ...), custom_call_target="tpu_custom_call" | custom-call | tf_op jit(solution)/shard_map/pallas_call | solution.py:190
  258.7 8.2 %shard_map.192 = (bf16[8,192,384]{2,1,0:T(8,128)(2,1)}, bf16[8,192,384]{2,1,0:T(8,128)(2,1)}, bf16[8,48,1920]{2,1,0:T(8,128)(2,1)}, bf16[8,48,1920]{2,1,0:T(8,128)(2,1)}, s32[1]{0:T(128)}) custom-call(s32[24]{0:T(128)S(1)} %copy-done.48, bf16[256,3072]{1,0:T(8,128)(2,1)} %get-tuple-element.227.active_hbm, ...), custom_call_target="tpu_custom_call" | custom-call | tf_op jit(solution)/shard_map/pallas_call | solution.py:190
  271.8 25.5 %shard_map.193 = (bf16[256,768]{1,0:T(8,128)(2,1)}, bf16[1024,768]{1,0:T(8,128)(2,1)}, bf16[1024,768]{1,0:T(8,128)(2,1)}, f32[12,768]{1,0:T(8,128)}, f32[12,768]{1,0:T(8,128)}, /*index=5*/s32[1]{0:T(128)}) custom-call(s32[24]{0:T(128)} %stack.141.info.seat, bf16[256,768]{1,0:T(8,128)(2,1)} %get-tuple-element.207.q_ref, bf16[256,768]{1,0:T(8,128)(2,1)} %copy-done.39, ...), custom_call_target="tpu_custom_call" | custom-call | tf_op jit(solution)/shard_map/pallas_call | solution.py:504
  297.3 4.2 %collective-permute-done.39.refs_5_ = bf16[8,48,1920]{2,1,0:T(8,128)(2,1)S(1)} collective-permute-done((bf16[8,48,1920]{2,1,0:T(8,128)(2,1)}, bf16[8,48,1920]{2,1,0:T(8,128)(2,1)S(1)}, u32[]{:S(2)}, u32[]{:S(2)}) %collective-permute-start.39) | collective-permute-done | bytes 1474592 | tf_op jit(solution)/shard_map/ppermute | solution.py:558
  305.1 4.9 %shard_map.194 = (bf16[4,192,384]{2,1,0:T(8,128)(2,1)S(1)}, bf16[4,192,384]{2,1,0:T(8,128)(2,1)S(1)}, bf16[4,48,1920]{2,1,0:T(8,128)(2,1)S(1)}, bf16[4,48,1920]{...) custom-call(s32[24]{0:T(128)S(1)} %copy-done.49, ...), custom_call_target="tpu_custom_call", output_to_operand_aliasing={{6}: (2, {}), {7}: (3, {})} | custom-call | tf_op jit(solution)/shard_map/pallas_call | solution.py:190
  319.0 7.6 %shard_map.196 = (bf16[512,768]{1,0:T(8,128)(2,1)S(1)}, bf16[512,768]{1,0:T(8,128)(2,1)S(1)}, f32[256,768]{1,0:T(8,128)S(1)}, bf16[8,48,512]{2,1,0:T(8,128)(2,1)...) custom-call(s32[24]{0:T(128)S(1)} %copy-done.49, ...), custom_call_target="tpu_custom_call" | custom-call | tf_op jit(solution)/shard_map/pallas_call | solution.py:190
  350.6 3.4 collective-permute-done.49.refs_2_
  388.8 3.5 collective-permute-done.65.refs_4_
  (403 shorter events, 177.9 us)
Async XLA Ops:
  0.7 53.8 %collective-permute-start.10 = (bf16[1,3072,768]{2,1,0:T(8,128)(2,1)}, bf16[1,3072,768]{2,1,0:T(8,128)(2,1)}, u32[]{:S(2)}, u32[]{:S(2)}) collective-permute-start(bf16[1,3072,768]{2,1,0:T(8,128)(2,1)} %down_own.7), channel_id=1, source_target_pairs={{0,16},{16,0},{1,17},{17,1},{2,18},{18,2},{3,19},{19,3},{4,20},{20... | collective-permute-start | bytes 14155784 | tf_op jit(solution)/shard_map/ppermute | solution.py:554
  1.2 53.3 %collective-permute-start.9 = (bf16[1,768,3072]{2,1,0:T(8,128)(2,1)}, bf16[1,768,3072]{2,1,0:T(8,128)(2,1)}, u32[]{:S(2)}, u32[]{:S(2)}) collective-permute-start(bf16[1,768,3072]{2,1,0:T(8,128)(2,1)} %up_own.7), channel_id=1, source_target_pairs={{0,16},{16,0},{1,17},{17,1},{2,18},{18,2},{3,19},{19,3},{4,20},{20... | collective-permute-start | bytes 14155784 | tf_op jit(solution)/shard_map/ppermute | solution.py:554
  1.3 25.1 %collective-permute-start.3 = (bf16[1,768,2304]{2,1,0:T(8,128)(2,1)}, bf16[1,768,2304]{2,1,0:T(8,128)(2,1)}, u32[]{:S(2)}, u32[]{:S(2)}) collective-permute-start(bf16[1,768,2304]{2,1,0:T(8,128)(2,1)} %joint_own.7), channel_id=1, source_target_pairs={{0,16},{16,0},{1,17},{17,1},{2,18},{18,2},{3,19},{19,3},{4,20},{20... | collective-permute-start | bytes 10616840 | tf_op jit(solution)/shard_map/ppermute | solution.py:554
  10.9 43.6 %collective-permute-start.8 = (bf16[1,768,768]{2,1,0:T(8,128)(2,1)}, bf16[1,768,768]{2,1,0:T(8,128)(2,1)S(1)}, u32[]{:S(2)}, u32[]{:S(2)}) collective-permute-start(bf16[1,768,768]{2,1,0:T(8,128)(2,1)} %mixer_own.7), channel_id=1, source_target_pairs={{0,16},{16,0},{1,17},{17,1},{2,18},{18,2},{3,19},{19,3},{4,20},{20... | collective-permute-start | bytes 3538952 | tf_op jit(solution)/shard_map/ppermute | solution.py:554
  24.7 29.7 %collective-permute-start = (bf16[128,768]{1,0:T(8,128)(2,1)}, bf16[128,768]{1,0:T(8,128)(2,1)S(1)}, u32[]{:S(2)}, u32[]{:S(2)}) collective-permute-start(bf16[128,768]{1,0:T(8,128)(2,1)} %get-tuple-element.316), channel_id=1, source_target_pairs={{3,2},{2,3},{0,0},{1,1},{7,6},{6,7},{4,4},{5,5},{11,10},{10,11},{8... | collective-permute-start | bytes 589832 | tf_op jit(solution)/shard_map/ppermute | solution.py:1240
  26.3 28.1 %collective-permute-start.1 = (bf16[128,768]{1,0:T(8,128)(2,1)S(1)}, bf16[128,768]{1,0:T(8,128)(2,1)S(1)}, u32[]{:S(2)}, u32[]{:S(2)}) collective-permute-start(bf16[128,768]{1,0:T(8,128)(2,1)S(1)} %get-tuple-element.317), channel_id=1, source_target_pairs={{0,2},{1,3},{3,0},{2,1},{4,6},{5,7},{7,4},{6,5},{8,10},{9,11},{11,... | collective-permute-start | bytes 589832 | tf_op jit(solution)/shard_map/ppermute | solution.py:1240
  137.8 36.4 %collective-permute-start.19 = (bf16[8,48,1920]{2,1,0:T(8,128)(2,1)}, bf16[8,48,1920]{2,1,0:T(8,128)(2,1)S(1)}, u32[]{:S(2)}, u32[]{:S(2)}) collective-permute-start(bf16[8,48,1920]{2,1,0:T(8,128)(2,1)} %get-tuple-element.182), channel_id=1, source_target_pairs={{0,2},{1,3},{2,0},{3,1},{4,6},{5,7},{6,4},{7,5},{8,10},{9,11},{10,... | collective-permute-start | bytes 4423688 | tf_op jit(solution)/shard_map/ppermute | solution.py:558
  141.2 28.2 %collective-permute-start.18 = (bf16[8,192,384]{2,1,0:T(8,128)(2,1)}, bf16[8,192,384]{2,1,0:T(8,128)(2,1)S(1)}, u32[]{:S(2)}, u32[]{:S(2)}) collective-permute-start(bf16[8,192,384]{2,1,0:T(8,128)(2,1)} %get-tuple-element.180), channel_id=1, source_target_pairs={{0,1},{1,0},{2,3},{3,2},{4,5},{5,4},{6,7},{7,6},{8,9},{9,8},{10,11... | collective-permute-start | bytes 3538952 | tf_op jit(solution)/shard_map/ppermute | solution.py:558
  184.0 19.1 %collective-permute-start.24 = (bf16[4,48,1920]{2,1,0:T(8,128)(2,1)S(1)}, bf16[4,48,1920]{2,1,0:T(8,128)(2,1)S(1)}, u32[]{:S(2)}, u32[]{:S(2)}) collective-permute-start(bf16[4,48,1920]{2,1,0:T(8,128)(2,1)S(1)} %get-tuple-element.195), channel_id=1, source_target_pairs={{0,1},{1,0},{2,3},{3,2},{4,5},{5,4},{6,7},{7,6},{8,9},{9,8},{10,11... | collective-permute-start | bytes 2211848 | tf_op jit(solution)/shard_map/ppermute | solution.py:558
  208.9 49.1 %collective-permute-start.34 = (bf16[256,3072]{1,0:T(8,128)(2,1)}, bf16[256,3072]{1,0:T(8,128)(2,1)}, u32[]{:S(2)}, u32[]{:S(2)}) collective-permute-start(bf16[256,3072]{1,0:T(8,128)(2,1)} %get-tuple-element.227.active_hbm), channel_id=1, source_target_pairs={{0,16},{16,0},{1,17},{17,1},{2,18},{18,2},{3,19},{19,3},{4,20},{20... | collective-permute-start | bytes 4718600 | tf_op jit(solution)/shard_map/ppermute | solution.py:554
  213.7 18.0 %collective-permute-start.28 = (bf16[2,128,768]{2,1,0:T(8,128)(2,1)}, bf16[2,128,768]{2,1,0:T(8,128)(2,1)}, u32[]{:S(2)}, u32[]{:S(2)}) collective-permute-start(bf16[2,128,768]{2,1,0:T(8,128)(2,1)} %dynamic-slice_bitcast_fusion.1), channel_id=1, source_target_pairs={{0,1},{1,0},{2,3},{3,2},{4,5},{5,4},{6,7},{7,6},{8,9},{9,8},{10,11... | collective-permute-start | bytes 1179656 | tf_op jit(solution)/shard_map/ppermute | solution.py:558
  216.0 18.0 %collective-permute-start.29 = (bf16[128,768]{1,0:T(8,128)(2,1)}, bf16[128,768]{1,0:T(8,128)(2,1)S(1)}, u32[]{:S(2)}, u32[]{:S(2)}) collective-permute-start(bf16[128,768]{1,0:T(8,128)(2,1)} %get-tuple-element.321), channel_id=1, source_target_pairs={{2,0},{3,1},{0,3},{1,2},{6,4},{7,5},{4,7},{5,6},{10,8},{11,9},{8,1... | collective-permute-start | bytes 589832 | tf_op jit(solution)/shard_map/ppermute | solution.py:1247
  223.2 24.2 %collective-permute-start.30 = (bf16[128,768]{1,0:T(8,128)(2,1)}, bf16[128,768]{1,0:T(8,128)(2,1)S(1)}, u32[]{:S(2)}, u32[]{:S(2)}) collective-permute-start(bf16[128,768]{1,0:T(8,128)(2,1)} %get-tuple-element.320), channel_id=1, source_target_pairs={{2,3},{3,2},{0,0},{1,1},{6,7},{7,6},{4,4},{5,5},{10,11},{11,10},{8... | collective-permute-start | bytes 589832 | tf_op jit(solution)/shard_map/ppermute | solution.py:1248
  224.8 26.2 %collective-permute-start.33 = (bf16[2,48,3456]{2,1,0:T(8,128)(2,1)S(1)}, bf16[2,48,3456]{2,1,0:T(8,128)(2,1)}, u32[]{:S(2)}, u32[]{:S(2)}) collective-permute-start(bf16[2,48,3456]{2,1,0:T(8,128)(2,1)S(1)} %copy-done.58), channel_id=1, source_target_pairs={{0,4},{4,0},{8,12},{12,8},{1,5},{5,1},{9,13},{13,9},{2,6},{6,2},{1... | collective-permute-start | bytes 1990664 | tf_op jit(solution)/shard_map/ppermute | solution.py:558
  231.7 15.7 %collective-permute-start.32 = (bf16[4,48,640]{2,1,0:T(8,128)(2,1)S(1)}, bf16[4,48,640]{2,1,0:T(8,128)(2,1)S(1)}, u32[]{:S(2)}, u32[]{:S(2)}) collective-permute-start(bf16[4,48,640]{2,1,0:T(8,128)(2,1)S(1)} %get-tuple-element.219), channel_id=1, source_target_pairs={{0,1},{1,0},{2,3},{3,2},{4,5},{5,4},{6,7},{7,6},{8,9},{9,8},{10,11... | collective-permute-start | bytes 737288 | tf_op jit(solution)/shard_map/ppermute | solution.py:558
  266.9 34.6 %collective-permute-start.39 = (bf16[8,48,1920]{2,1,0:T(8,128)(2,1)}, bf16[8,48,1920]{2,1,0:T(8,128)(2,1)S(1)}, u32[]{:S(2)}, u32[]{:S(2)}) collective-permute-start(bf16[8,48,1920]{2,1,0:T(8,128)(2,1)} %get-tuple-element.238), channel_id=1, source_target_pairs={{0,2},{1,3},{2,0},{3,1},{4,6},{5,7},{6,4},{7,5},{8,10},{9,11},{10,... | collective-permute-start | bytes 4423688 | tf_op jit(solution)/shard_map/ppermute | solution.py:558
  267.0 30.3 %collective-permute-start.38 = (bf16[8,192,384]{2,1,0:T(8,128)(2,1)}, bf16[8,192,384]{2,1,0:T(8,128)(2,1)S(1)}, u32[]{:S(2)}, u32[]{:S(2)}) collective-permute-start(bf16[8,192,384]{2,1,0:T(8,128)(2,1)} %get-tuple-element.236), channel_id=1, source_target_pairs={{0,1},{1,0},{2,3},{3,2},{4,5},{5,4},{6,7},{7,6},{8,9},{9,8},{10,11... | collective-permute-start | bytes 3538952 | tf_op jit(solution)/shard_map/ppermute | solution.py:558
  267.6 29.7 %collective-permute-start.40 = (bf16[48,3456]{1,0:T(8,128)(2,1)S(1)}, bf16[48,3456]{1,0:T(8,128)(2,1)S(1)}, u32[]{:S(2)}, u32[]{:S(2)}) collective-permute-start(bf16[48,3456]{1,0:T(8,128)(2,1)S(1)} %get-tuple-element.240), channel_id=1, source_target_pairs={{0,8},{4,12},{8,0},{12,4},{1,9},{5,13},{9,1},{13,5},{2,10},{6,14},... | collective-permute-start | bytes 995336 | tf_op jit(solution)/shard_map/ppermute | solution.py:558
  270.1 39.9 %collective-permute-start.41 = (bf16[2,48,1152]{2,1,0:T(8,128)(2,1)S(1)}, bf16[2,48,1152]{2,1,0:T(8,128)(2,1)}, u32[]{:S(2)}, u32[]{:S(2)}) collective-permute-start(bf16[2,48,1152]{2,1,0:T(8,128)(2,1)S(1)} %get-tuple-element.245), channel_id=1, source_target_pairs={{0,4},{4,0},{8,12},{12,8},{1,5},{5,1},{9,13},{13,9},{2,6},{6,2},{1... | collective-permute-start | bytes 663560 | tf_op jit(solution)/shard_map/ppermute | solution.py:558
  312.5 18.9 %collective-permute-start.46 = (bf16[4,48,1920]{2,1,0:T(8,128)(2,1)S(1)}, bf16[4,48,1920]{2,1,0:T(8,128)(2,1)S(1)}, u32[]{:S(2)}, u32[]{:S(2)}) collective-permute-start(bf16[4,48,1920]{2,1,0:T(8,128)(2,1)S(1)} %get-tuple-element.258), channel_id=1, source_target_pairs={{0,1},{1,0},{2,3},{3,2},{4,5},{5,4},{6,7},{7,6},{8,9},{9,8},{10,11... | collective-permute-start | bytes 2211848 | tf_op jit(solution)/shard_map/ppermute | solution.py:558
  342.3 16.3 %collective-permute-start.51 = (bf16[2,48,3456]{2,1,0:T(8,128)(2,1)}, bf16[2,48,3456]{2,1,0:T(8,128)(2,1)S(1)}, u32[]{:S(2)}, u32[]{:S(2)}) collective-permute-start(bf16[2,48,3456]{2,1,0:T(8,128)(2,1)} %copy-done.59), channel_id=1, source_target_pairs={{0,4},{4,0},{8,12},{12,8},{1,5},{5,1},{9,13},{13,9},{2,6},{6,2},{1... | collective-permute-start | bytes 1990664 | tf_op jit(solution)/shard_map/ppermute | solution.py:558
  344.0 22.4 %collective-permute-start.58 = (f32[26,768]{1,0:T(8,128)}, f32[26,768]{1,0:T(8,128)}, u32[]{:S(2)}, u32[]{:S(2)}) collective-permute-start(f32[26,768]{1,0:T(8,128)} %add_add_fusion.3), channel_id=1, source_target_pairs={{0,2},{1,3},{2,0},{3,1},{4,6},{5,7},{6,4},{7,5},{8,10},{9,11},{10,... | collective-permute-start | bytes 239624 | tf_op jit(solution)/shard_map/ppermute | solution.py:558
  348.1 21.1 %collective-permute-start.52 = (bf16[2,128,768]{2,1,0:T(8,128)(2,1)}, bf16[2,128,768]{2,1,0:T(8,128)(2,1)}, u32[]{:S(2)}, u32[]{:S(2)}) collective-permute-start(bf16[2,128,768]{2,1,0:T(8,128)(2,1)} %dynamic-slice_bitcast_fusion), channel_id=1, source_target_pairs={{0,1},{1,0},{2,3},{3,2},{4,5},{5,4},{6,7},{7,6},{8,9},{9,8},{10,11... | collective-permute-start | bytes 1179656 | tf_op jit(solution)/shard_map/ppermute | solution.py:558
  364.7 24.1 %collective-permute-start.63 = (bf16[48,3456]{1,0:T(8,128)(2,1)}, bf16[48,3456]{1,0:T(8,128)(2,1)S(1)}, u32[]{:S(2)}, u32[]{:S(2)}) collective-permute-start(bf16[48,3456]{1,0:T(8,128)(2,1)} %copy-done.63), channel_id=1, source_target_pairs={{0,8},{4,12},{8,0},{12,4},{1,9},{5,13},{9,1},{13,5},{2,10},{6,14},... | collective-permute-start | bytes 995336 | tf_op jit(solution)/shard_map/ppermute | solution.py:558
  (153 other events, 1153.7 us)
